TPU v7x, 32 devices: a whole 2x2x4 slice. The times are simulated.
32 devices in a mesh: grp: 2 (over x), dom: 16 (over z, y, core).
Axes of the slice: x: 2, y: 2, z: 4, core: 2. Of those that a mesh axis runs over, the one named last changes fastest.
Arguments:
- slabs: bfloat16 [32, 2, 1024, 384], P(('grp', 'dom')), parts along dimension 0, may hold values from -1 to 1
- pair_blocks: int32 [32, 3], P(('grp', 'dom')), parts along dimension 0, may hold values from 0 to 15, as said below
- occ_energy: float32 [32, 2], P('grp'), parts along dimension 0, may hold values from -1.5 to -0.3
- virt_energy: float32 [16384], P('grp'), parts along dimension 0, may hold values from 0.2 to 3
- domain_map: int32 [32, 384], P('grp'), parts along dimension 0, may hold values from 0 to 8191
Outputs:
- residual_slabs: float32 [32, 2, 1024, 384], P(('grp', 'dom')), parts along dimension 0
- metric_gradient: float32 [2048, 1024], P('grp'), parts along dimension 0
There are 2 independent parts, one for each index of `grp`. A program takes and returns all parts, laid end to end along the dimension named above; each array names one. Nothing has to cross between parts.
Inputs may be any that keep to these rules, and one draw needn't show every extreme that they name: `pair_blocks`: each block lists 3 distinct blocks whose index differs from its own by at most 2, possibly itself (a self-pair adds both back-contractions to that block); the first block lists the block 2 above it and the last block the one 2 below it.
All inputs are finite; a program needn't handle non-finite values.
Results may differ from a plain program's by a relative error of at most 0.0015.
Values may be sent and summed in bfloat16 or wider, within the bound.
No kernel may reach another device: no remote copies, remote signals or barrier semaphores. Data moves between devices by JAX's collectives and lax.ppermute only.
A program may use at most 128 MiB of HBM per device.

v0:
```python
import jax
import jax.numpy as jnp
from jax import lax
from jax.sharding import PartitionSpec as P

REACH = 2


def shifted(block, axis, distance):
    devices = range(lax.axis_size(axis))
    route = [(i - distance, i) for i in devices if i - distance in devices]
    return lax.ppermute(block, axis, route)


def pair_amplitude(
    slab_first, slab_partner, energy_first, energy_partner, virt_first, virt_partner
):
    integrals = jnp.einsum(
        "ipa,jpb->iajb", slab_first, slab_partner, preferred_element_type=jnp.float32
    )
    denominator = (
        virt_first[None, :, None, None]
        + virt_partner[None, None, None, :]
        - energy_first[:, None, None, None]
        - energy_partner[None, None, :, None]
    )
    return (-integrals / denominator).astype(jnp.bfloat16)


def shards(slabs, pair_blocks, occ_energy, virt_energy, domain_map):
    my_block = lax.axis_index("dom")
    own_slab = slabs[0]
    nearby = {0: own_slab}
    for distance in range(1, REACH + 1):
        for towards in (1, -1):
            nearby[towards * distance] = shifted(own_slab, "dom", -towards * distance)
    stacked = jnp.stack([nearby[offset] for offset in range(-REACH, REACH + 1)])
    energy_own = occ_energy[my_block]
    virt_own = virt_energy[domain_map[my_block]]
    orbitals, aux_count, virt_count = own_slab.shape
    width = 2 * REACH + 1
    residual = jnp.zeros((orbitals, aux_count, virt_count), jnp.float32)
    outgoing = jnp.zeros((width, orbitals, aux_count, virt_count), jnp.float32)
    for slot_index in range(pair_blocks.shape[1]):
        partner = pair_blocks[0, slot_index]
        position = partner - my_block + REACH
        slab_partner = lax.dynamic_index_in_dim(stacked, position, 0, keepdims=False)
        virt_partner = virt_energy[domain_map[partner]]
        energy_partner = occ_energy[partner]
        amplitude = pair_amplitude(
            own_slab, slab_partner, energy_own, energy_partner, virt_own, virt_partner
        )
        residual = residual + jnp.einsum(
            "iajb,jpb->ipa", amplitude, slab_partner, preferred_element_type=jnp.float32
        )
        partial_sum = jnp.einsum(
            "iajb,ipa->jpb", amplitude, own_slab, preferred_element_type=jnp.float32
        )
        carried = lax.dynamic_index_in_dim(outgoing, position, 0, keepdims=False) + partial_sum
        outgoing = lax.dynamic_update_index_in_dim(outgoing, carried, position, 0)
    for shift_by in range(-REACH, REACH + 1):
        held = outgoing[shift_by + REACH]
        if shift_by != 0:
            held = shifted(held, "dom", shift_by)
        residual = residual + held
    partial_metric = jnp.einsum(
        "ipa,iqa->pq", residual, own_slab.astype(jnp.float32), precision=lax.Precision.HIGHEST
    )
    gradient = lax.psum(partial_metric, "dom") / lax.axis_size("dom")
    return (residual[None], gradient)


def solution(mesh):
    return jax.shard_map(
        shards,
        mesh=mesh,
        in_specs=(
            P(("grp", "dom"), None, None, None),
            P(("grp", "dom"), None),
            P("grp", None),
            P("grp"),
            P("grp", None),
        ),
        out_specs=(P(("grp", "dom"), None, None, None), P("grp", None)),
        check_vma=False,
    )
```

profile of v0, /device:TPU:0, one launch (start us, length us, event | category | flops | bytes accessed | tf_op | source)
XLA Modules:
  0.0 491.4 jit_solution(13441236241615671346)
XLA Ops:
  7.2 0.0 copy-start
  7.2 0.0 all-reduce.2.cloned.1.call-start
  7.2 6.0 %collective-permute-start = (bf16[2,1024,384]{2,1,0:T(8,128)(2,1)}, bf16[2,1024,384]{2,1,0:T(8,128)(2,1)}, u32[]{:S(2)}, u32[]{:S(2)}) collective-permute-start(bf16[2,1024,384]{2,1,0:T(8,128)(2,1)} %bitcast.190), channel_id=1, source_target_pairs={{0,2},{1,3},{2,4},{3,5},{4,6},{5,7},{6,8},{7,9},{8,10},{9,11},{10,... | collective-permute-start | bytes 4718600 | tf_op jit(solution)/shard_map/ppermute | solution.py:12
  13.3 2.6 collective-permute-start.1
  15.9 1.3 collective-permute-start.2
  17.2 1.3 collective-permute-start.3
  18.5 1.4 fusion.52
  27.8 0.9 fusion.42
  28.8 0.0 copy-done
  28.8 2.5 gather_fusion
  31.3 2.5 gather_fusion.1
  33.9 0.0 copy-start.6
  33.9 2.5 gather_fusion.2
  36.4 2.7 gather_fusion.3
  39.2 0.0 copy-done.6
  39.2 0.2 fusion.50
  39.4 0.2 broadcast_add_fusion
  39.6 0.3 broadcast_subtract_fusion
  39.9 57.8 %collective-permute-done = bf16[2,1024,384]{2,1,0:T(8,128)(2,1)} collective-permute-done((bf16[2,1024,384]{2,1,0:T(8,128)(2,1)}, bf16[2,1024,384]{2,1,0:T(8,128)(2,1)}, u32[]{:S(2)}, u32[]{:S(2)}) %collective-permute-start) | collective-permute-done | bytes 1572896 | tf_op jit(solution)/shard_map/ppermute | solution.py:12
  97.8 1.6 bitcast_dynamic-update-slice_fusion.4
  99.3 0.0 copy-start.2
  99.3 0.0 collective-permute-done.1
  99.4 1.8 bitcast_dynamic-update-slice_fusion.3
  101.2 0.0 copy-done.2
  101.2 0.3 constant_dynamic-update-slice_fusion
  101.5 0.0 collective-permute-done.2
  101.5 0.3 bitcast_dynamic-update-slice_fusion.2
  101.9 0.0 collective-permute-done.3
  101.9 0.3 bitcast_dynamic-update-slice_fusion.1
  102.2 0.0 copy-start.4
  102.2 1.5 fusion.12
  103.8 0.0 copy-start.7
  103.8 6.9 %broadcast_in_dim.26 = f32[5,2,1024,384]{3,2,1,0:T(8,128)} broadcast(f32[]{:T(128)} %constant.44.clone.1), dimensions={} | broadcast | bytes 15728644 | tf_op jit(solution)/shard_map/broadcast_in_dim | solution.py:43
  110.7 0.0 copy-done.7
  110.7 3.1 bitcast_dynamic-update-slice_fusion
  113.8 2.1 constant_dynamic-slice_fusion.1
  115.9 1.6 fusion.11
  117.5 0.0 copy-start.5
  117.5 1.0 copy-done.5
  118.5 3.1 fusion.9
  121.6 2.1 constant_dynamic-slice_fusion
  123.7 0.0 copy-done.4
  123.7 1.5 fusion.10
  125.3 3.1 fusion.7
  128.4 8.6 %slice_bitcast_fusion.4 = (f32[2,1024,384]{2,1,0:T(8,128)}, f32[2,1024,384]{2,1,0:T(8,128)S(1)}, f32[2,1024,384]{2,1,0:T(8,128)}, f32[2,1024,384]{2,1,0:T(8,128)}) fusion(f32[5,2,1024,384]{3,2,1,0:T(8,128)} %fusion.7), kind=kLoop, calls=%fused_computation.11 | loop fusion | bytes 25165824 | tf_op jit(solution)/shard_map/squeeze | solution.py:62
  137.0 1.5 collective-permute-start.4
  138.5 1.3 collective-permute-start.5
  139.8 16.9 %collective-permute-start.6 = (f32[2,1024,384]{2,1,0:T(8,128)}, f32[2,1024,384]{2,1,0:T(8,128)S(1)}, u32[]{:S(2)}, u32[]{:S(2)}) collective-permute-start(f32[2,1024,384]{2,1,0:T(8,128)} %get-tuple-element.12), channel_id=1, source_target_pairs={{0,1},{1,2},{2,3},{3,4},{4,5},{5,6},{6,7},{7,8},{8,9},{9,10},{10,1... | collective-permute-start | bytes 9437192 | tf_op jit(solution)/shard_map/ppermute | solution.py:12
  156.7 0.0 copy-start.8
  156.7 5.6 %collective-permute-start.7 = (f32[2,1024,384]{2,1,0:T(8,128)S(1)}, f32[2,1024,384]{2,1,0:T(8,128)S(1)}, u32[]{:S(2)}, u32[]{:S(2)}) collective-permute-start(f32[2,1024,384]{2,1,0:T(8,128)S(1)} %get-tuple-element.11), channel_id=1, source_target_pairs={{0,2},{1,3},{2,4},{3,5},{4,6},{5,7},{6,8},{7,9},{8,10},{9,11},{10,... | collective-permute-start | bytes 9437192 | tf_op jit(solution)/shard_map/ppermute | solution.py:12
  162.3 3.1 fusion.16
  165.4 0.0 copy-done.8
  165.4 2.8 fusion.19
  168.2 55.0 %collective-permute-done.4 = f32[2,1024,384]{2,1,0:T(8,128)S(1)} collective-permute-done((f32[2,1024,384]{2,1,0:T(8,128)}, f32[2,1024,384]{2,1,0:T(8,128)S(1)}, u32[]{:S(2)}, u32[]{:S(2)}) %collective-permute-start.4) | collective-permute-done | bytes 3145760 | tf_op jit(solution)/shard_map/ppermute | solution.py:12
  223.3 0.0 collective-permute-done.5
  223.3 0.0 collective-permute-done.6
  223.3 100.0 %collective-permute-done.7 = f32[2,1024,384]{2,1,0:T(8,128)S(1)} collective-permute-done((f32[2,1024,384]{2,1,0:T(8,128)S(1)}, f32[2,1024,384]{2,1,0:T(8,128)S(1)}, u32[]{:S(2)}, u32[]{:S(2)}) %collective-permute-start.7) | collective-permute-done | bytes 3145760 | tf_op jit(solution)/shard_map/ppermute | solution.py:12
  323.3 4.3 fusion.2
  327.6 0.0 copy-start.3
  327.6 6.7 %convolution_bitcast_fusion = f32[1024,1024]{1,0:T(8,128)} fusion(f32[2,1024,384]{2,1,0:T(8,128)S(1)} %fusion.2, bf16[1,2,1024,384]{3,2,1,0:T(8,128)(2,1)S(1)} %copy-done.2), kind=kOutput, calls=%fused_computation.30 | convolution fusion | flops 9663676416 | bytes 8912896 | tf_op jit(solution)/shard_map/ipa,iqa->pq/dot_general | solution.py:66
  334.3 0.0 all-reduce.2.cloned.1.call-update
  334.3 0.0 copy-start.1
  334.3 145.1 %all-reduce.2.cloned.1.call-done = f32[1024,1024]{1,0:T(8,128)} async-done(((f32[1024,1024]{1,0:T(8,128)}), f32[1024,1024]{1,0:T(8,128)}) %all-reduce.2.cloned.1.call-update) | async-done | bytes 4194320 | tf_op jit(solution)/shard_map/psum | solution.py:69
  479.5 5.0 %broadcast_multiply_fusion = f32[1024,1024]{1,0:T(8,128)} fusion(f32[1024,1024]{1,0:T(8,128)} %all-reduce.2.cloned.1.call-done), kind=kLoop, calls=%fused_computation.31 | loop fusion | flops 1048576 | bytes 8388608 | tf_op jit(solution)/shard_map/div | solution.py:69
  (4 shorter events, 0.0 us)
Async XLA Ops:
  7.2 21.6 %copy-start = (f32[8192]{0:T(1024)S(1)}, f32[8192]{0:T(1024)}, u32[]{:S(2)}) copy-start(f32[8192]{0:T(1024)} %param.8) | copy-start | bytes 98308
  7.2 472.3 %all-reduce.2.cloned.1.call-start = ((), (), s32[]{:S(2)}) async-start(), calls=%async_computation | async-start | bytes 8388608 | tf_op jit(solution)/shard_map/psum | solution.py:69
  7.2 90.5 %collective-permute-start = (bf16[2,1024,384]{2,1,0:T(8,128)(2,1)}, bf16[2,1024,384]{2,1,0:T(8,128)(2,1)}, u32[]{:S(2)}, u32[]{:S(2)}) collective-permute-start(bf16[2,1024,384]{2,1,0:T(8,128)(2,1)} %bitcast.190), channel_id=1, source_target_pairs={{0,2},{1,3},{2,4},{3,5},{4,6},{5,7},{6,8},{7,9},{8,10},{9,11},{10,... | collective-permute-start | bytes 4718600 | tf_op jit(solution)/shard_map/ppermute | solution.py:12
  13.3 86.1 %collective-permute-start.1 = (bf16[2,1024,384]{2,1,0:T(8,128)(2,1)}, bf16[2,1024,384]{2,1,0:T(8,128)(2,1)}, u32[]{:S(2)}, u32[]{:S(2)}) collective-permute-start(bf16[2,1024,384]{2,1,0:T(8,128)(2,1)} %bitcast.191), channel_id=1, source_target_pairs={{0,1},{1,2},{2,3},{3,4},{4,5},{5,6},{6,7},{7,8},{8,9},{9,10},{10,1... | collective-permute-start | bytes 4718600 | tf_op jit(solution)/shard_map/ppermute | solution.py:12
  15.9 85.7 %collective-permute-start.2 = (bf16[2,1024,384]{2,1,0:T(8,128)(2,1)}, bf16[2,1024,384]{2,1,0:T(8,128)(2,1)S(1)}, u32[]{:S(2)}, u32[]{:S(2)}) collective-permute-start(bf16[2,1024,384]{2,1,0:T(8,128)(2,1)} %bitcast.192), channel_id=1, source_target_pairs={{1,0},{2,1},{3,2},{4,3},{5,4},{6,5},{7,6},{8,7},{9,8},{10,9},{11,1... | collective-permute-start | bytes 4718600 | tf_op jit(solution)/shard_map/ppermute | solution.py:12
  17.2 84.7 %collective-permute-start.3 = (bf16[2,1024,384]{2,1,0:T(8,128)(2,1)}, bf16[2,1024,384]{2,1,0:T(8,128)(2,1)S(1)}, u32[]{:S(2)}, u32[]{:S(2)}) collective-permute-start(bf16[2,1024,384]{2,1,0:T(8,128)(2,1)} %bitcast.193), channel_id=1, source_target_pairs={{2,0},{3,1},{4,2},{5,3},{6,4},{7,5},{8,6},{9,7},{10,8},{11,9},{12,... | collective-permute-start | bytes 4718600 | tf_op jit(solution)/shard_map/ppermute | solution.py:12
  33.9 5.3 %copy-start.6 = (f32[16,2]{0,1:T(2,128)S(1)}, f32[16,2]{0,1:T(2,128)}, u32[]{:S(2)}) copy-start(f32[16,2]{0,1:T(2,128)} %param.7) | copy-start | bytes 388
  99.3 1.9 copy-start.2
  102.2 21.5 %copy-start.4 = (bf16[5,2,1024,384]{3,2,1,0:T(8,128)(2,1)}, bf16[5,2,1024,384]{3,2,1,0:T(8,128)(2,1)S(1)}, u32[]{:S(2)}) copy-start(bf16[5,2,1024,384]{3,2,1,0:T(8,128)(2,1)S(1)} %bitcast_dynamic-update-slice_fusion.1) | copy-start | bytes 23592964
  103.8 6.9 %copy-start.7 = (bf16[2,384,2,384]{1,3,0,2:T(8,128)(2,1)}, bf16[2,384,2,384]{1,3,0,2:T(8,128)(2,1)S(1)}, u32[]{:S(2)}) copy-start(bf16[2,384,2,384]{1,3,0,2:T(8,128)(2,1)S(1)} %fusion.12) | copy-start | bytes 3538948
  117.5 1.0 copy-start.5
  137.0 86.2 %collective-permute-start.4 = (f32[2,1024,384]{2,1,0:T(8,128)}, f32[2,1024,384]{2,1,0:T(8,128)S(1)}, u32[]{:S(2)}, u32[]{:S(2)}) collective-permute-start(f32[2,1024,384]{2,1,0:T(8,128)} %get-tuple-element.10), channel_id=1, source_target_pairs={{2,0},{3,1},{4,2},{5,3},{6,4},{7,5},{8,6},{9,7},{10,8},{11,9},{12,... | collective-permute-start | bytes 9437192 | tf_op jit(solution)/shard_map/ppermute | solution.py:12
  138.5 84.7 %collective-permute-start.5 = (f32[2,1024,384]{2,1,0:T(8,128)}, f32[2,1024,384]{2,1,0:T(8,128)S(1)}, u32[]{:S(2)}, u32[]{:S(2)}) collective-permute-start(f32[2,1024,384]{2,1,0:T(8,128)} %get-tuple-element.13), channel_id=1, source_target_pairs={{1,0},{2,1},{3,2},{4,3},{5,4},{6,5},{7,6},{8,7},{9,8},{10,9},{11,1... | collective-permute-start | bytes 9437192 | tf_op jit(solution)/shard_map/ppermute | solution.py:12
  139.8 83.4 %collective-permute-start.6 = (f32[2,1024,384]{2,1,0:T(8,128)}, f32[2,1024,384]{2,1,0:T(8,128)S(1)}, u32[]{:S(2)}, u32[]{:S(2)}) collective-permute-start(f32[2,1024,384]{2,1,0:T(8,128)} %get-tuple-element.12), channel_id=1, source_target_pairs={{0,1},{1,2},{2,3},{3,4},{4,5},{5,6},{6,7},{7,8},{8,9},{9,10},{10,1... | collective-permute-start | bytes 9437192 | tf_op jit(solution)/shard_map/ppermute | solution.py:12
  156.7 8.7 %copy-start.8 = (bf16[2,384,2,384]{1,3,0,2:T(8,128)(2,1)S(1)}, bf16[2,384,2,384]{1,3,0,2:T(8,128)(2,1)}, u32[]{:S(2)}) copy-start(bf16[2,384,2,384]{1,3,0,2:T(8,128)(2,1)} %copy-done.7) | copy-start | bytes 3538948
  156.7 166.6 %collective-permute-start.7 = (f32[2,1024,384]{2,1,0:T(8,128)S(1)}, f32[2,1024,384]{2,1,0:T(8,128)S(1)}, u32[]{:S(2)}, u32[]{:S(2)}) collective-permute-start(f32[2,1024,384]{2,1,0:T(8,128)S(1)} %get-tuple-element.11), channel_id=1, source_target_pairs={{0,2},{1,3},{2,4},{3,5},{4,6},{5,7},{6,8},{7,9},{8,10},{9,11},{10,... | collective-permute-start | bytes 9437192 | tf_op jit(solution)/shard_map/ppermute | solution.py:12
  327.6 6.7 %copy-start.3 = (f32[2,1024,384]{2,1,0:T(8,128)}, f32[2,1024,384]{2,1,0:T(8,128)S(1)}, u32[]{:S(2)}) copy-start(f32[2,1024,384]{2,1,0:T(8,128)S(1)} %fusion.2) | copy-start | bytes 9437188
  334.3 150.2 %copy-start.1 = (f32[8192]{0:T(1024)S(1)}, f32[8192]{0:T(1024)}, u32[]{:S(2)}) copy-start(f32[8192]{0:T(1024)} %param.8) | copy-start | bytes 98308
Sparse Core Ops, SparseCore 0:
  334.4 144.9 all-reduce.1
where the time goes:
time: 492 us; the launch traced here: 491 us
  waiting for transfers between devices  358 us (73%)
  local copies, waits for them, and re-layouts  37.2 us (8%)
  starting transfers between devices  36.5 us (7%)
  matrix products  30.9 us (6%)
  between operations  22.3 us (5%)
  other arithmetic  6.47 us (1%)
    ppermute x8, waiting for transfers between devices, shifted(): return lax.ppermute(block, axis, route)  213 us
    psum x1, waiting for transfers between devices, shards(): gradient = lax.psum(partial_metric, 'dom') / lax.axis_size('dom')  145 us
    ppermute x8, starting transfers between devices, shifted(): return lax.ppermute(block, axis, route)  36.5 us
    dot_general x3, matrix products, shards(): jnp.einsum('iajb,jpb->ipa', amplitude, slab_partner, preferred_element_ty...  10.3 us
  transfers between devices with their start and end apart: 9, of which 4 were waited for; matrix products, arithmetic and copies ran while one was open for 5% of the time, Pallas kernels for 0%

commit v1 on v0

v1 whole, which is shorter than its diff:
```python
import functools

import jax
import jax.numpy as jnp
from jax import lax
from jax.experimental import pallas as pl
from jax.experimental.pallas import tpu as pltpu
from jax.sharding import PartitionSpec as P

VMEM_LIMIT = 60 * 1024 * 1024
TILE = 128
NT = (((1,), (1,)), ((), ()))


def move(x, pairs):
    return lax.ppermute(x, "dom", pairs)


def swapped(x, bit):
    return move(x, [(d, d ^ bit) for d in range(lax.axis_size("dom"))])


def shifted(x, distance):
    devices = range(lax.axis_size("dom"))
    return move(x, [(d, d + distance) for d in devices if d + distance in devices])


def forwarded(x):
    devices = range(lax.axis_size("dom"))
    route = [(d, d - 4 if d & 2 else d + 4) for d in devices]
    return move(x, [(a, b) for a, b in route if b in devices])


def to_sibling(x, own_first):
    devices = range(lax.axis_size("dom"))
    return move(x, [(d, d ^ 1) for d in devices if ((d >> 1) ^ d) & 1 == own_first])


def load(copies, sem):
    started = []
    for at, (src, dst) in enumerate(copies):
        copy = pltpu.make_async_copy(src, dst, sem.at[at])
        copy.start()
        started.append(copy)
    return started


def add_pair(own_t, other, amp, total, own_level, other_level, weight, first):
    integrals = jnp.dot(own_t[...], other[...], preferred_element_type=jnp.float32)
    amp[...] = (integrals * weight / (own_level + other_level)).astype(jnp.bfloat16)
    part = lax.dot_general(other[...], amp[...], NT, preferred_element_type=jnp.float32)
    if first:
        total[...] = part
    else:
        total[...] += part


def near_kernel(own, sib, own_level, levels, weights, own_t_out, total_out, sem, own_s, other, own_t, amp, total):
    virt = own.shape[2]
    copies = load(
        [(x.at[j], s.at[:, pl.ds(j * virt, virt)]) for x, s in ((own, own_s), (sib, other)) for j in range(2)],
        sem,
    )
    for c in copies[:2]:
        c.wait()
    own_t[...] = own_s[...].T
    add_pair(own_t, own_s, amp, total, own_level[...], levels[0:1, :], weights[0:1, :], True)
    for c in copies[2:]:
        c.wait()
    add_pair(own_t, other, amp, total, own_level[...], levels[1:2, :], weights[1:2, :], False)
    own_t_out[...] = own_t[...]
    total_out[...] = total[...]


def far_kernel(pick, own_t, total_in, y00, y01, y10, y11, z00, z01, xy0, xz0, own_level, levels, weights, total_out,
               sem, first, second, amp, total):
    half, virt = y00.shape
    a, b = pl.ds(0, virt), pl.ds(virt, virt)
    top, low = pl.ds(0, half), pl.ds(half, half)
    copies = load(
        [
            (y00, first.at[top, a]), (y01, first.at[low, a]),
            (y10, first.at[top, b]), (y11, first.at[low, b]),
            (z00, second.at[top, a]), (z01, second.at[low, a]),
            (total_in, total),
        ],
        sem,
    )

    @pl.when(pick[0] == 1)
    def _():
        pltpu.make_async_copy(xy0, second.at[:, b], sem.at[7]).start()

    @pl.when(pick[0] != 1)
    def _():
        pltpu.make_async_copy(xz0, second.at[:, b], sem.at[7]).start()

    for c in copies[:4]:
        c.wait()
    copies[6].wait()
    add_pair(own_t, first, amp, total, own_level[...], levels[2:3, :], weights[2:3, :], False)
    for c in copies[4:6]:
        c.wait()
    pltpu.make_async_copy(xz0, second.at[:, b], sem.at[7]).wait()
    add_pair(own_t, second, amp, total, own_level[...], levels[3:4, :], weights[3:4, :], False)
    total_out[...] = total[...]


def last_kernel(pick, own_t, total_in, own, z10, z11, xy1, xz1, own_level, levels, weights, residual, metric,
                sem, own_s, second, amp, total):
    half, virt = z10.shape
    a, b = pl.ds(0, virt), pl.ds(virt, virt)
    top, low = pl.ds(0, half), pl.ds(half, half)

    @pl.when(pick[0] == 1)
    def _():
        pltpu.make_async_copy(xy1, second.at[:, b], sem.at[5]).start()

    @pl.when(pick[0] != 1)
    def _():
        pltpu.make_async_copy(xz1, second.at[:, b], sem.at[5]).start()

    copies = load(
        [
            (z10, second.at[top, a]), (z11, second.at[low, a]), (total_in, total),
            (own.at[0], own_s.at[:, a]), (own.at[1], own_s.at[:, b]),
        ],
        sem,
    )
    copies[0].wait()
    copies[1].wait()
    copies[2].wait()
    pltpu.make_async_copy(xz1, second.at[:, b], sem.at[5]).wait()
    add_pair(own_t, second, amp, total, own_level[...], levels[4:5, :], weights[4:5, :], False)
    outs = load([(total.at[:, a], residual.at[0]), (total.at[:, b], residual.at[1])], sem.at[pl.ds(6, 2)])
    copies[3].wait()
    copies[4].wait()
    high = total[...].astype(jnp.bfloat16)
    rest = (total[...] - high.astype(jnp.float32)).astype(jnp.bfloat16)
    metric[...] = lax.dot_general(high, own_s[...], NT, preferred_element_type=jnp.float32) + lax.dot_general(
        rest, own_s[...], NT, preferred_element_type=jnp.float32
    )
    for c in outs:
        c.wait()


def shards(slabs, pair_blocks, occ_energy, virt_energy, domain_map):
    me = lax.axis_index("dom")
    blocks = lax.axis_size("dom")
    own = slabs[0]
    orbitals, aux, virt = own.shape
    half, wide = aux // 2, orbitals * virt

    sib = swapped(own, 1)
    y = [[swapped(own[j, h * half:(h + 1) * half], 2) for h in range(2)] for j in range(2)]
    near_pairs = {step: shifted(pair_blocks[0], -step) for step in (1, -1, 2, -2)}
    z = [[forwarded(c) for c in row] for row in y]
    from_y = [to_sibling(jnp.concatenate(row), 0) for row in y]
    from_z = [to_sibling(jnp.concatenate(row), 1) for row in z]

    parity, core = (me >> 1) & 1, me & 1
    pick = (parity ^ core).astype(jnp.int32)[None]
    offsets = jnp.stack([0 * me, 1 - 2 * core, 2 - 4 * parity, 4 * parity - 2, 2 * core - 1])
    who = me + offsets
    inside = (who >= 0) & (who < blocks)
    who = jnp.clip(who, 0, blocks - 1)
    listed = jnp.any(pair_blocks[0][None, :] == who[:, None], axis=1) & inside
    theirs = jnp.stack([pair_blocks[0]] + [near_pairs[s] for s in (1, -1, 2, -2)])
    row_at = jnp.stack([0 * me, 1 + core, 3 + parity, 4 - parity, 2 - core])
    lists = jnp.any(theirs[row_at] == me, axis=1) & inside
    count = -(listed.astype(jnp.float32) + lists.astype(jnp.float32))
    level = (virt_energy[domain_map[who]][:, None, :] - occ_energy[who][:, :, None])
    weight = jnp.broadcast_to(count[:, None, None], level.shape)

    def rows(x):
        return jnp.stack([
            x[0].reshape(wide), x[1].reshape(wide), x[2].reshape(wide),
            jnp.concatenate([x[3, 0], x[4, 0]]), jnp.concatenate([x[3, 1], x[4, 1]]),
        ])

    levels, weights = rows(level), rows(weight)
    own_level = level[0].reshape(wide, 1)

    hbm = pl.BlockSpec(memory_space=pl.ANY)
    vmem = pl.BlockSpec(memory_space=pltpu.VMEM)
    smem = pl.BlockSpec(memory_space=pltpu.SMEM)
    f32, bf16 = jnp.float32, jnp.bfloat16
    total_s = pltpu.VMEM((aux, wide), f32)
    slab_s = pltpu.VMEM((aux, wide), bf16)
    amp_s = pltpu.VMEM((wide, wide), bf16)
    params = pltpu.CompilerParams(vmem_limit_bytes=VMEM_LIMIT)
    total_t = jax.ShapeDtypeStruct((aux, wide), f32)
    pair_flops = 4 * aux * wide * wide

    def cost(flops, moved):
        return pl.CostEstimate(flops=flops, bytes_accessed=moved, transcendentals=0)

    own_t, total = pl.pallas_call(
        near_kernel,
        out_shape=(jax.ShapeDtypeStruct((wide, aux), bf16), total_t),
        in_specs=[hbm, hbm, vmem, vmem, vmem],
        out_specs=(vmem, vmem),
        scratch_shapes=[pltpu.SemaphoreType.DMA((4,)), slab_s, slab_s, pltpu.VMEM((wide, aux), bf16), amp_s, total_s],
        compiler_params=params,
        cost_estimate=cost(2 * pair_flops, 10 * aux * wide),
        name="near",
    )(own, sib, own_level, levels, weights)
    total = pl.pallas_call(
        far_kernel,
        out_shape=total_t,
        in_specs=[smem, vmem] + [hbm] * 9 + [vmem] * 3,
        out_specs=vmem,
        scratch_shapes=[pltpu.SemaphoreType.DMA((8,)), slab_s, slab_s, amp_s, total_s],
        compiler_params=params,
        cost_estimate=cost(2 * pair_flops, 14 * aux * wide),
        name="far",
    )(pick, own_t, total, y[0][0], y[0][1], y[1][0], y[1][1], z[0][0], z[0][1], from_y[0], from_z[0],
      own_level, levels, weights)
    residual, partial_metric = pl.pallas_call(
        last_kernel,
        out_shape=(jax.ShapeDtypeStruct(own.shape, f32), jax.ShapeDtypeStruct((aux, aux), f32)),
        in_specs=[smem, vmem] + [hbm] * 6 + [vmem] * 3,
        out_specs=(hbm, vmem),
        scratch_shapes=[pltpu.SemaphoreType.DMA((8,)), slab_s, slab_s, amp_s, total_s],
        compiler_params=params,
        cost_estimate=cost(2 * pair_flops, 14 * aux * wide),
        name="last",
    )(pick, own_t, total, own, z[1][0], z[1][1], from_y[1], from_z[1], own_level, levels, weights)
    gradient = lax.psum(partial_metric, "dom") / blocks
    return residual[None], gradient


def solution(mesh):
    return jax.shard_map(
        shards,
        mesh=mesh,
        in_specs=(
            P(("grp", "dom"), None, None, None),
            P(("grp", "dom"), None),
            P("grp", None),
            P("grp"),
            P("grp", None),
        ),
        out_specs=(P(("grp", "dom"), None, None, None), P("grp", None)),
        check_vma=False,
    )
```

time: 492 us -> 245 us (0.50)
  waiting for transfers between devices: 358 us -> 121 us
  Pallas kernels: 0 us -> 34.5 us
  matrix products: 30.9 us -> 0 us
  local copies, waits for them, and re-layouts: 37.2 us -> 20.1 us
  starting transfers between devices: 36.5 us -> 46.8 us
  between operations: 22.3 us -> 14.5 us
    ppermute x8 -> x17, waiting for transfers between devices: 213 us -> 5.97 us  [move(): return lax.ppermute(x, 'dom', pairs)]
    pallas_call x0 -> x3, Pallas kernels: none -> 34.5 us  [the longest x1 12.7 us: shards(): pl.pallas_call(last_kernel, out_shape=(jax.ShapeDtypeStruct(own.shape, f3...]
    dot_general x10 -> x0, matrix products: 30.9 us -> none  [the longest x3 10.3 us: shards(): jnp.einsum('iajb,jpb->ipa', amplitude, slab_partner, preferred_element_ty...]
    psum x1, waiting for transfers between devices: 145 us -> 115 us  [shards(): gradient = lax.psum(partial_metric, 'dom') / blocks]
    ppermute x8 -> x17, starting transfers between devices: 36.5 us -> 46.8 us  [move(): return lax.ppermute(x, 'dom', pairs)]
    squeeze x1, local copies, waits for them, and re-layouts: 8.64 us -> 1.51 us  [shards(): own[j, h * half:(h + 1) * half]]
    broadcast_in_dim x1, local copies, waits for them, and re-layouts: 6.94 us -> 0.57 us  [shards(): weight = jnp.broadcast_to(count[:, None, None], level.shape)]
    gather x4 -> x5, local copies, waits for them, and re-layouts: 10.3 us -> 12.1 us  [the longest x2 10.4 us: shards(): virt_energy[domain_map[who]][:, None, :] - occ_energy[who][:, :, None]]
  transfers between devices with their start and end apart: 9 -> 18, of which waited for: 4 -> 4; matrix products, arithmetic and copies ran while one was open for 5% -> 9% of each run, Pallas kernels for 0% -> 9%
where the time goes in v1:
time: 245 us; the launch traced here: 244 us
  waiting for transfers between devices  121 us (49%)
  starting transfers between devices  46.8 us (19%)
  Pallas kernels  34.5 us (14%)
  local copies, waits for them, and re-layouts  20.1 us (8%)
  between operations  14.5 us (6%)
  other arithmetic  6.82 us (3%)
    psum x1, waiting for transfers between devices, shards(): gradient = lax.psum(partial_metric, 'dom') / blocks  115 us
    ppermute x17, starting transfers between devices, move(): return lax.ppermute(x, 'dom', pairs)  46.8 us
    pallas_call x1, Pallas kernels, shards(): pl.pallas_call(last_kernel, out_shape=(jax.ShapeDtypeStruct(own.shape, f3...  12.7 us
    pallas_call x1, Pallas kernels, shards(): pl.pallas_call(far_kernel, out_shape=total_t, in_specs=[smem, vmem] + [hb...  11.8 us
    gather x2, local copies, waits for them, and re-layouts, shards(): virt_energy[domain_map[who]][:, None, :] - occ_energy[who][:, :, None]  10.4 us
    pallas_call x1, Pallas kernels, shards(): pl.pallas_call(near_kernel, out_shape=(jax.ShapeDtypeStruct((wide, aux),...  10.1 us
    ppermute x17, waiting for transfers between devices, move(): return lax.ppermute(x, 'dom', pairs)  5.97 us
    div x1, other arithmetic, shards(): gradient = lax.psum(partial_metric, 'dom') / blocks  5.04 us
  transfers between devices with their start and end apart: 18, of which 4 were waited for; matrix products, arithmetic and copies ran while one was open for 9% of the time, Pallas kernels for 9%

profile of v1, /device:TPU:0, one launch (start us, length us, event | category | flops | bytes accessed | tf_op | source)
XLA Modules:
  0.0 243.9 jit_solution(8121838285091550421)
XLA Ops:
  7.2 0.0 copy-start
  7.2 0.0 all-reduce.3.cloned.1.call-start
  7.2 4.9 %collective-permute-start.4 = (s32[3]{0:T(128)}, s32[3]{0:T(128)S(1)}, u32[]{:S(2)}, u32[]{:S(2)}) collective-permute-start(s32[3]{0:T(128)} %bitcast.82), channel_id=1, source_target_pairs={{0,2},{1,3},{2,4},{3,5},{4,6},{5,7},{6,8},{7,9},{8,10},{9,11},{10,... | collective-permute-start | bytes 44 | tf_op jit(solution)/shard_map/ppermute | solution.py:16
  12.1 1.3 collective-permute-start.3
  13.4 0.1 collective-permute-start
  13.5 1.5 slice_bitcast_fusion
  15.0 2.7 %collective-permute-start.6 = (bf16[512,384]{1,0:T(8,128)(2,1)S(1)}, bf16[512,384]{1,0:T(8,128)(2,1)S(1)}, u32[]{:S(2)}, u32[]{:S(2)}) collective-permute-start(bf16[512,384]{1,0:T(8,128)(2,1)S(1)} %get-tuple-element.16), channel_id=1, source_target_pairs={{0,2},{1,3},{2,0},{3,1},{4,6},{5,7},{6,4},{7,5},{8,10},{9,11},{10,... | collective-permute-start | bytes 1179656 | tf_op jit(solution)/shard_map/ppermute | solution.py:16
  17.7 0.1 collective-permute-start.5
  17.8 0.1 stack.85
  17.9 0.1 stack.93
  18.0 0.1 copy.12
  18.1 0.6 gather_fusion.2
  18.7 0.6 gather_fusion
  19.3 0.0 copy-start.9
  19.3 10.4 %gather_fusion.1 = f32[1920]{0:T(1024)S(1)} fusion(f32[8192]{0:T(1024)S(1)} %copy-done, s32[2048]{0:T(1024)S(1)} %pad_clamp_fusion), kind=kCustom, calls=%fused_computation.1 | custom fusion | bytes 23040 | tf_op jit(solution)/shard_map/gather | solution.py:172
  29.7 0.1 broadcast_subtract_fusion
  29.8 0.1 compare_reduce_fusion.1
  30.0 1.0 copy.17
  31.0 0.1 stack.108
  31.1 0.6 stack.88.levels
  31.7 0.1 stack.98
  31.8 0.0 collective-permute-done.4
  31.8 2.1 collective-permute-start.2
  33.9 0.0 collective-permute-done.3
  34.0 1.3 collective-permute-start.1
  35.3 0.0 collective-permute-done.2
  35.3 4.2 %collective-permute-start.8 = (bf16[512,384]{1,0:T(8,128)(2,1)S(1)}, bf16[512,384]{1,0:T(8,128)(2,1)S(1)}, u32[]{:S(2)}, u32[]{:S(2)}) collective-permute-start(bf16[512,384]{1,0:T(8,128)(2,1)S(1)} %get-tuple-element.14), channel_id=1, source_target_pairs={{0,2},{1,3},{2,0},{3,1},{4,6},{5,7},{6,4},{7,5},{8,10},{9,11},{10,... | collective-permute-start | bytes 1179656 | tf_op jit(solution)/shard_map/ppermute | solution.py:16
  39.4 0.0 collective-permute-done.1
  39.4 1.3 collective-permute-start.7
  40.8 0.6 gather_fusion.3
  41.3 0.0 collective-permute-done.6.y01
  41.4 4.5 %collective-permute-start.10 = (bf16[512,384]{1,0:T(8,128)(2,1)S(1)}, bf16[512,384]{1,0:T(8,128)(2,1)S(1)}, u32[]{:S(2)}, u32[]{:S(2)}) collective-permute-start(bf16[512,384]{1,0:T(8,128)(2,1)S(1)} %collective-permute-done.6.y01), channel_id=1, source_target_pairs={{0,4},{1,5},{4,8},{5,9},{6,2},{7,3},{8,12},{9,13},{10,6},{11,7},{1... | collective-permute-start | bytes 1179656 | tf_op jit(solution)/shard_map/ppermute | solution.py:16
  45.9 0.0 collective-permute-done.5.y00
  45.9 0.0 copy-start.3
  45.9 3.5 %collective-permute-start.9 = (bf16[512,384]{1,0:T(8,128)(2,1)S(1)}, bf16[512,384]{1,0:T(8,128)(2,1)S(1)}, u32[]{:S(2)}, u32[]{:S(2)}) collective-permute-start(bf16[512,384]{1,0:T(8,128)(2,1)S(1)} %collective-permute-done.5.y00), channel_id=1, source_target_pairs={{0,4},{1,5},{4,8},{5,9},{6,2},{7,3},{8,12},{9,13},{10,6},{11,7},{1... | collective-permute-start | bytes 1179656 | tf_op jit(solution)/shard_map/ppermute | solution.py:16
  49.4 0.1 compare_reduce_fusion
  49.5 6.5 %collective-permute-start.14 = (bf16[512,384]{1,0:T(8,128)(2,1)S(1)}, bf16[512,384]{1,0:T(8,128)(2,1)}, u32[]{:S(2)}, u32[]{:S(2)}) collective-permute-start(bf16[512,384]{1,0:T(8,128)(2,1)S(1)} %collective-permute-done.8.y11), channel_id=1, source_target_pairs={{0,4},{1,5},{4,8},{5,9},{6,2},{7,3},{8,12},{9,13},{10,6},{11,7},{1... | collective-permute-start | bytes 1179656 | tf_op jit(solution)/shard_map/ppermute | solution.py:16
  56.0 1.7 collective-permute-done.7.y10
  57.7 4.5 %collective-permute-start.13 = (bf16[512,384]{1,0:T(8,128)(2,1)S(1)}, bf16[512,384]{1,0:T(8,128)(2,1)}, u32[]{:S(2)}, u32[]{:S(2)}) collective-permute-start(bf16[512,384]{1,0:T(8,128)(2,1)S(1)} %collective-permute-done.7.y10), channel_id=1, source_target_pairs={{0,4},{1,5},{4,8},{5,9},{6,2},{7,3},{8,12},{9,13},{10,6},{11,7},{1... | collective-permute-start | bytes 1179656 | tf_op jit(solution)/shard_map/ppermute | solution.py:16
  62.2 0.1 pad_maximum_fusion
  62.3 0.0 collective-permute-done.10.z01
  62.3 2.2 collective-permute-start.11
  64.5 0.0 collective-permute-done.9.z00
  64.5 0.1 pad_maximum_fusion.1
  64.7 1.3 collective-permute-start.12
  66.0 0.7 fusion.6
  66.6 0.6 broadcast_in_dim.12
  67.2 0.7 concatenate.60
  67.9 0.6 stack_reshape_squeeze.23
  68.5 0.6 stack_reshape_squeeze.22
  69.1 0.6 stack_reshape_squeeze.21
  69.7 0.6 stack.110.weights
  70.4 0.1 pad_maximum_fusion.2
  70.4 0.7 collective-permute-done.14.z11
  71.2 4.9 %collective-permute-start.15 = (bf16[1024,384]{1,0:T(8,128)(2,1)S(1)}, bf16[1024,384]{1,0:T(8,128)(2,1)}, u32[]{:S(2)}, u32[]{:S(2)}) collective-permute-start(bf16[1024,384]{1,0:T(8,128)(2,1)S(1)} %pad_maximum_fusion.2), channel_id=1, source_target_pairs={{0,1},{3,2},{4,5},{7,6},{8,9},{11,10},{12,13},{15,14},{16,17},{19,... | collective-permute-start | bytes 2359304 | tf_op jit(solution)/shard_map/ppermute | solution.py:16
  76.1 3.5 %collective-permute-done.13.z10 = bf16[512,384]{1,0:T(8,128)(2,1)} collective-permute-done((bf16[512,384]{1,0:T(8,128)(2,1)S(1)}, bf16[512,384]{1,0:T(8,128)(2,1)}, u32[]{:S(2)}, u32[]{:S(2)}) %collective-permute-start.13) | collective-permute-done | bytes 393248 | tf_op jit(solution)/shard_map/ppermute | solution.py:16
  79.6 1.2 pad_maximum_fusion.3
  80.8 1.5 collective-permute-start.16
  82.3 10.1 %near.1 = (bf16[768,1024]{1,0:T(8,128)(2,1)}, f32[1024,768]{1,0:T(8,128)}) custom-call(bf16[2,1024,384]{2,1,0:T(8,128)(2,1)} %bitcast.73, bf16[2,1024,384]{2,1,0:T(8,128)(2,1)} %collective-permute-done.sib, f32[768,1]{1,0:T(8,128)} %bitcast.75, f32[5,768]{1,0:T(8,128)} %stack.88.levels, f32[5,768]{1,0:T(8,128)} %stack.110.weights), custom_call_target="tpu_custom_call" | custom-call | flops 4831838208 | bytes 7864320 | tf_op jit(solution)/shard_map/near/pallas_call | solution.py:198
  92.4 11.8 %far.1.total_in = f32[1024,768]{1,0:T(8,128)} custom-call(s32[1]{0:T(128)} %bitcast.pick, bf16[768,1024]{1,0:T(8,128)(2,1)} %get-tuple-element.6.own_t, f32[1024,768]{1,0:T(8,128)} %get-tuple-element.7.total_in, bf16[512,384]{1,0:T(8,128)(2,1)} %copy-done.3, bf16[512,384]{1,0:T(8,128)(2,1)} %copy-done.2, bf16[512,384]{1,0:T(8,128)(2,1)} %copy-done.5, ...), custom_call_target="tpu_custom_call" | custom-call | flops 4831838208 | bytes 11010048 | tf_op jit(solution)/shard_map/far/pallas_call | solution.py:208
  104.2 12.7 %last.1 = (f32[2,1024,384]{2,1,0:T(8,128)}, f32[1024,1024]{1,0:T(8,128)}) custom-call(s32[1]{0:T(128)} %bitcast.pick, bf16[768,1024]{1,0:T(8,128)(2,1)} %get-tuple-element.6.own_t, f32[1024,768]{1,0:T(8,128)} %far.1.total_in, bf16[2,1024,384]{2,1,0:T(8,128)(2,1)} %bitcast.74, bf16[512,384]{1,0:T(8,128)(2,1)} %collective-permute-done.13.z10, ...), custom_call_target="tpu_custom_call" | custom-call | flops 4831838208 | bytes 11010048 | tf_op jit(solution)/shard_map/last/pallas_call | solution.py:219
  116.9 0.0 all-reduce.3.cloned.1.call-update
  116.9 115.1 %all-reduce.3.cloned.1.call-done = f32[1024,1024]{1,0:T(8,128)} async-done(((f32[1024,1024]{1,0:T(8,128)}), f32[1024,1024]{1,0:T(8,128)}) %all-reduce.3.cloned.1.call-update) | async-done | bytes 4194320 | tf_op jit(solution)/shard_map/psum | solution.py:229
  232.0 5.0 %broadcast_multiply_fusion = f32[1024,1024]{1,0:T(8,128)} fusion(f32[1024,1024]{1,0:T(8,128)} %all-reduce.3.cloned.1.call-done), kind=kLoop, calls=%fused_computation.4 | loop fusion | flops 1048576 | bytes 8388608 | tf_op jit(solution)/shard_map/div | solution.py:229
  (43 shorter events, 0.2 us)
Async XLA Ops:
  7.2 12.1 %copy-start = (f32[8192]{0:T(1024)S(1)}, f32[8192]{0:T(1024)}, u32[]{:S(2)}) copy-start(f32[8192]{0:T(1024)} %param.8) | copy-start | bytes 98308
  7.2 224.8 %all-reduce.3.cloned.1.call-start = ((), (), s32[]{:S(2)}) async-start(), calls=%async_computation | async-start | bytes 8388608 | tf_op jit(solution)/shard_map/psum | solution.py:229
  7.2 24.6 %collective-permute-start.4 = (s32[3]{0:T(128)}, s32[3]{0:T(128)S(1)}, u32[]{:S(2)}, u32[]{:S(2)}) collective-permute-start(s32[3]{0:T(128)} %bitcast.82), channel_id=1, source_target_pairs={{0,2},{1,3},{2,4},{3,5},{4,6},{5,7},{6,8},{7,9},{8,10},{9,11},{10,... | collective-permute-start | bytes 44 | tf_op jit(solution)/shard_map/ppermute | solution.py:16
  12.1 21.8 %collective-permute-start.3 = (s32[3]{0:T(128)}, s32[3]{0:T(128)S(1)}, u32[]{:S(2)}, u32[]{:S(2)}) collective-permute-start(s32[3]{0:T(128)} %bitcast.83), channel_id=1, source_target_pairs={{2,0},{3,1},{4,2},{5,3},{6,4},{7,5},{8,6},{9,7},{10,8},{11,9},{12,... | collective-permute-start | bytes 44 | tf_op jit(solution)/shard_map/ppermute | solution.py:16
  13.4 4.6 %copy-start.8 = (f32[16,2]{0,1:T(2,128)S(1)}, f32[16,2]{0,1:T(2,128)}, u32[]{:S(2)}) copy-start(f32[16,2]{0,1:T(2,128)} %param.7) | copy-start | bytes 388
  13.4 5.3 %copy-start.1 = (s32[16,384]{1,0:T(8,128)S(1)}, s32[16,384]{1,0:T(8,128)}, u32[]{:S(2)}) copy-start(s32[16,384]{1,0:T(8,128)} %param.9) | copy-start | bytes 73732
  13.4 68.9 %collective-permute-start = (bf16[2,1024,384]{2,1,0:T(8,128)(2,1)}, bf16[2,1024,384]{2,1,0:T(8,128)(2,1)}, u32[]{:S(2)}, u32[]{:S(2)}) collective-permute-start(bf16[2,1024,384]{2,1,0:T(8,128)(2,1)} %bitcast.71), channel_id=1, source_target_pairs={{0,1},{1,0},{2,3},{3,2},{4,5},{5,4},{6,7},{7,6},{8,9},{9,8},{10,11... | collective-permute-start | bytes 4718600 | tf_op jit(solution)/shard_map/ppermute | solution.py:16
  15.0 26.3 %collective-permute-start.6 = (bf16[512,384]{1,0:T(8,128)(2,1)S(1)}, bf16[512,384]{1,0:T(8,128)(2,1)S(1)}, u32[]{:S(2)}, u32[]{:S(2)}) collective-permute-start(bf16[512,384]{1,0:T(8,128)(2,1)S(1)} %get-tuple-element.16), channel_id=1, source_target_pairs={{0,2},{1,3},{2,0},{3,1},{4,6},{5,7},{6,4},{7,5},{8,10},{9,11},{10,... | collective-permute-start | bytes 1179656 | tf_op jit(solution)/shard_map/ppermute | solution.py:16
  17.7 28.1 %collective-permute-start.5 = (bf16[512,384]{1,0:T(8,128)(2,1)S(1)}, bf16[512,384]{1,0:T(8,128)(2,1)S(1)}, u32[]{:S(2)}, u32[]{:S(2)}) collective-permute-start(bf16[512,384]{1,0:T(8,128)(2,1)S(1)} %get-tuple-element.17), channel_id=1, source_target_pairs={{0,2},{1,3},{2,0},{3,1},{4,6},{5,7},{6,4},{7,5},{8,10},{9,11},{10,... | collective-permute-start | bytes 1179656 | tf_op jit(solution)/shard_map/ppermute | solution.py:16
  19.3 10.5 %copy-start.9 = (s32[1,3]{1,0:T(1,128)S(1)}, s32[1,3]{1,0:T(1,128)}, u32[]{:S(2)}) copy-start(s32[1,3]{1,0:T(1,128)} %param.6) | copy-start | bytes 40
  31.8 3.4 %collective-permute-start.2 = (s32[3]{0:T(128)S(1)}, s32[3]{0:T(128)S(1)}, u32[]{:S(2)}, u32[]{:S(2)}) collective-permute-start(s32[3]{0:T(128)S(1)} %bitcast.85), channel_id=1, source_target_pairs={{0,1},{1,2},{2,3},{3,4},{4,5},{5,6},{6,7},{7,8},{8,9},{9,10},{10,1... | collective-permute-start | bytes 44 | tf_op jit(solution)/shard_map/ppermute | solution.py:16
  34.0 5.5 %collective-permute-start.1 = (s32[3]{0:T(128)S(1)}, s32[3]{0:T(128)S(1)}, u32[]{:S(2)}, u32[]{:S(2)}) collective-permute-start(s32[3]{0:T(128)S(1)} %bitcast.86), channel_id=1, source_target_pairs={{1,0},{2,1},{3,2},{4,3},{5,4},{6,5},{7,6},{8,7},{9,8},{10,9},{11,1... | collective-permute-start | bytes 44 | tf_op jit(solution)/shard_map/ppermute | solution.py:16
  35.3 14.2 %collective-permute-start.8 = (bf16[512,384]{1,0:T(8,128)(2,1)S(1)}, bf16[512,384]{1,0:T(8,128)(2,1)S(1)}, u32[]{:S(2)}, u32[]{:S(2)}) collective-permute-start(bf16[512,384]{1,0:T(8,128)(2,1)S(1)} %get-tuple-element.14), channel_id=1, source_target_pairs={{0,2},{1,3},{2,0},{3,1},{4,6},{5,7},{6,4},{7,5},{8,10},{9,11},{10,... | collective-permute-start | bytes 1179656 | tf_op jit(solution)/shard_map/ppermute | solution.py:16
  39.4 18.3 %collective-permute-start.7 = (bf16[512,384]{1,0:T(8,128)(2,1)S(1)}, bf16[512,384]{1,0:T(8,128)(2,1)S(1)}, u32[]{:S(2)}, u32[]{:S(2)}) collective-permute-start(bf16[512,384]{1,0:T(8,128)(2,1)S(1)} %get-tuple-element.15), channel_id=1, source_target_pairs={{0,2},{1,3},{2,0},{3,1},{4,6},{5,7},{6,4},{7,5},{8,10},{9,11},{10,... | collective-permute-start | bytes 1179656 | tf_op jit(solution)/shard_map/ppermute | solution.py:16
  41.3 23.3 %copy-start.2 = (bf16[512,384]{1,0:T(8,128)(2,1)}, bf16[512,384]{1,0:T(8,128)(2,1)S(1)}, u32[]{:S(2)}) copy-start(bf16[512,384]{1,0:T(8,128)(2,1)S(1)} %collective-permute-done.6.y01) | copy-start | bytes 1179652
  41.4 21.0 %collective-permute-start.10 = (bf16[512,384]{1,0:T(8,128)(2,1)S(1)}, bf16[512,384]{1,0:T(8,128)(2,1)S(1)}, u32[]{:S(2)}, u32[]{:S(2)}) collective-permute-start(bf16[512,384]{1,0:T(8,128)(2,1)S(1)} %collective-permute-done.6.y01), channel_id=1, source_target_pairs={{0,4},{1,5},{4,8},{5,9},{6,2},{7,3},{8,12},{9,13},{10,6},{11,7},{1... | collective-permute-start | bytes 1179656 | tf_op jit(solution)/shard_map/ppermute | solution.py:16
  45.9 18.8 %copy-start.3 = (bf16[512,384]{1,0:T(8,128)(2,1)}, bf16[512,384]{1,0:T(8,128)(2,1)S(1)}, u32[]{:S(2)}) copy-start(bf16[512,384]{1,0:T(8,128)(2,1)S(1)} %collective-permute-done.5.y00) | copy-start | bytes 1179652
  45.9 18.7 %collective-permute-start.9 = (bf16[512,384]{1,0:T(8,128)(2,1)S(1)}, bf16[512,384]{1,0:T(8,128)(2,1)S(1)}, u32[]{:S(2)}, u32[]{:S(2)}) collective-permute-start(bf16[512,384]{1,0:T(8,128)(2,1)S(1)} %collective-permute-done.5.y00), channel_id=1, source_target_pairs={{0,4},{1,5},{4,8},{5,9},{6,2},{7,3},{8,12},{9,13},{10,6},{11,7},{1... | collective-permute-start | bytes 1179656 | tf_op jit(solution)/shard_map/ppermute | solution.py:16
  49.5 20.8 %copy-start.4 = (bf16[512,384]{1,0:T(8,128)(2,1)}, bf16[512,384]{1,0:T(8,128)(2,1)S(1)}, u32[]{:S(2)}) copy-start(bf16[512,384]{1,0:T(8,128)(2,1)S(1)} %collective-permute-done.8.y11) | copy-start | bytes 1179652
  49.5 21.6 %collective-permute-start.14 = (bf16[512,384]{1,0:T(8,128)(2,1)S(1)}, bf16[512,384]{1,0:T(8,128)(2,1)}, u32[]{:S(2)}, u32[]{:S(2)}) collective-permute-start(bf16[512,384]{1,0:T(8,128)(2,1)S(1)} %collective-permute-done.8.y11), channel_id=1, source_target_pairs={{0,4},{1,5},{4,8},{5,9},{6,2},{7,3},{8,12},{9,13},{10,6},{11,7},{1... | collective-permute-start | bytes 1179656 | tf_op jit(solution)/shard_map/ppermute | solution.py:16
  57.7 12.6 %copy-start.5 = (bf16[512,384]{1,0:T(8,128)(2,1)}, bf16[512,384]{1,0:T(8,128)(2,1)S(1)}, u32[]{:S(2)}) copy-start(bf16[512,384]{1,0:T(8,128)(2,1)S(1)} %collective-permute-done.7.y10) | copy-start | bytes 1179652
  57.7 21.9 %collective-permute-start.13 = (bf16[512,384]{1,0:T(8,128)(2,1)S(1)}, bf16[512,384]{1,0:T(8,128)(2,1)}, u32[]{:S(2)}, u32[]{:S(2)}) collective-permute-start(bf16[512,384]{1,0:T(8,128)(2,1)S(1)} %collective-permute-done.7.y10), channel_id=1, source_target_pairs={{0,4},{1,5},{4,8},{5,9},{6,2},{7,3},{8,12},{9,13},{10,6},{11,7},{1... | collective-permute-start | bytes 1179656 | tf_op jit(solution)/shard_map/ppermute | solution.py:16
  62.3 3.6 %copy-start.6 = (bf16[512,384]{1,0:T(8,128)(2,1)}, bf16[512,384]{1,0:T(8,128)(2,1)S(1)}, u32[]{:S(2)}) copy-start(bf16[512,384]{1,0:T(8,128)(2,1)S(1)} %collective-permute-done.10.z01) | copy-start | bytes 1179652
  62.3 30.0 %collective-permute-start.11 = (bf16[1024,384]{1,0:T(8,128)(2,1)S(1)}, bf16[1024,384]{1,0:T(8,128)(2,1)}, u32[]{:S(2)}, u32[]{:S(2)}) collective-permute-start(bf16[1024,384]{1,0:T(8,128)(2,1)S(1)} %pad_maximum_fusion), channel_id=1, source_target_pairs={{0,1},{3,2},{4,5},{7,6},{8,9},{11,10},{12,13},{15,14},{16,17},{19,... | collective-permute-start | bytes 2359304 | tf_op jit(solution)/shard_map/ppermute | solution.py:16
  64.5 2.1 copy-start.7
  64.7 27.7 %collective-permute-start.12 = (bf16[1024,384]{1,0:T(8,128)(2,1)S(1)}, bf16[1024,384]{1,0:T(8,128)(2,1)}, u32[]{:S(2)}, u32[]{:S(2)}) collective-permute-start(bf16[1024,384]{1,0:T(8,128)(2,1)S(1)} %pad_maximum_fusion.1), channel_id=1, source_target_pairs={{1,0},{2,3},{5,4},{6,7},{9,8},{10,11},{13,12},{14,15},{17,16},{18,... | collective-permute-start | bytes 2359304 | tf_op jit(solution)/shard_map/ppermute | solution.py:16
  71.2 33.0 %collective-permute-start.15 = (bf16[1024,384]{1,0:T(8,128)(2,1)S(1)}, bf16[1024,384]{1,0:T(8,128)(2,1)}, u32[]{:S(2)}, u32[]{:S(2)}) collective-permute-start(bf16[1024,384]{1,0:T(8,128)(2,1)S(1)} %pad_maximum_fusion.2), channel_id=1, source_target_pairs={{0,1},{3,2},{4,5},{7,6},{8,9},{11,10},{12,13},{15,14},{16,17},{19,... | collective-permute-start | bytes 2359304 | tf_op jit(solution)/shard_map/ppermute | solution.py:16
  80.8 23.4 %collective-permute-start.16 = (bf16[1024,384]{1,0:T(8,128)(2,1)S(1)}, bf16[1024,384]{1,0:T(8,128)(2,1)}, u32[]{:S(2)}, u32[]{:S(2)}) collective-permute-start(bf16[1024,384]{1,0:T(8,128)(2,1)S(1)} %pad_maximum_fusion.3), channel_id=1, source_target_pairs={{1,0},{2,3},{5,4},{6,7},{9,8},{10,11},{13,12},{14,15},{17,16},{18,... | collective-permute-start | bytes 2359304 | tf_op jit(solution)/shard_map/ppermute | solution.py:16
Sparse Core Ops, SparseCore 0:
  117.0 114.9 all-reduce.2

commit v2 on v0

v2 whole, which is shorter than its diff:
```python
import functools

import jax
import jax.numpy as jnp
from jax import lax
from jax.experimental import pallas as pl
from jax.experimental.pallas import tpu as pltpu
from jax.sharding import PartitionSpec as P

VMEM_LIMIT = 60 * 1024 * 1024
LANES = 128
BLOCK = 256
PAD = 16
BITS = 14
NT = (((1,), (1,)), ((), ()))
TN = (((0,), (0,)), ((), ()))
F32, BF16, I16, I32 = jnp.float32, jnp.bfloat16, jnp.int16, jnp.int32


def move(x, pairs):
    return lax.ppermute(x, "dom", pairs)


def swapped(x, bits):
    return move(x, [(d, d ^ bits) for d in range(lax.axis_size("dom"))])


def shifted(x, distance):
    devices = range(lax.axis_size("dom"))
    return move(x, [(d, d + distance) for d in devices if d + distance in devices])


def forwarded(x):
    devices = range(lax.axis_size("dom"))
    route = [(d, d - 4 if d & 2 else d + 4) for d in devices]
    return move(x, [(a, b) for a, b in route if b in devices])


def to_sibling(x, kind):
    devices = range(lax.axis_size("dom"))
    return move(x, [(d, d ^ 1) for d in devices if ((d >> 1) ^ d) & 1 == kind])


def begin(copies, sem, at=0):
    started = [pltpu.make_async_copy(a, b, sem.at[at + i]) for i, (a, b) in enumerate(copies)]
    for copy in started:
        copy.start()
    return started


def finish(copies):
    for copy in copies:
        copy.wait()


def place_of(me):
    return (me >> 1) & 1, me & 1, (me >> 2) & 3


def prep_kernel(blocks, me_ref, pairs, up, down, up2, down2, occ, energy, maps, levels, weights):
    me = me_ref[0]
    parity, core, _ = place_of(me)
    virt = maps.shape[1]
    table = energy[...]
    parts = []
    for _ in range(3):
        part = table.astype(BF16)
        parts.append(part)
        table = table - part.astype(F32)
    offsets = (0, 1 - 2 * core, 2 - 4 * parity, 4 * parity - 2, 2 * core - 1)
    row_major = lax.broadcasted_iota(I32, (energy.shape[0], virt), 0)
    lane_major = lax.broadcasted_iota(I32, (LANES, virt), 0)
    slots = pairs.shape[1]
    for at, offset in enumerate(offsets):
        other = me + offset
        inside = jnp.logical_and(other >= 0, other < blocks).astype(I32)
        who = jnp.clip(other, 0, blocks - 1)
        count = 0
        for s in range(slots):
            theirs = pairs[0, s]
            for step, ref in ((1, up), (-1, down), (2, up2), (-2, down2)):
                theirs = jnp.where(offset == step, ref[0, s], theirs)
            count = count + (pairs[0, s] == other).astype(I32) + (theirs == me).astype(I32)
        weight = -(count * inside).astype(F32)
        index = maps[pl.ds(who, 1), :]
        pick = (row_major == index // LANES).astype(F32).astype(BF16)
        rows = sum(lax.dot_general(p, pick, TN, preferred_element_type=F32) for p in parts)
        chosen = jnp.sum(jnp.where(lane_major == index % LANES, rows, 0.0), axis=0, keepdims=True)
        for j in range(2):
            row, col = (at, j * virt) if at < 3 else (3 + j, (at - 3) * virt)
            levels[row:row + 1, col:col + virt] = chosen - occ[who, j]
            weights[row:row + 1, col:col + virt] = jnp.full((1, virt), weight, F32)


def add_pair(own_t, other, amp, given, total, own_level, levels, weights, step, after=None):
    wide = own_t.shape[0]
    for t in range(0, wide, BLOCK):
        s = pl.ds(t, BLOCK)
        integrals = jnp.dot(own_t[s, :], other[...], preferred_element_type=F32)
        gap = own_level[t:t + BLOCK, 0:1] + levels[step:step + 1, :]
        amp[s, :] = (integrals * weights[step:step + 1, :] / gap).astype(BF16)
    if given is not None:
        given()
    for t in range(0, wide, BLOCK):
        s = pl.ds(t, BLOCK)
        part = lax.dot_general(other[...], amp[s, :], NT, preferred_element_type=F32)
        total[:, s] = part if given is None else total[:, s] + part
        if after is not None:
            after(t + BLOCK)


def near_kernel(own, sib, levels, weights, own_t, total_out, sem, own_s, other, amp, total):
    virt = own.shape[2]
    copies = begin(
        [(x.at[j], s.at[:, pl.ds(j * virt, virt)]) for x, s in ((own, own_s), (sib, other)) for j in range(2)],
        sem,
    )
    level = levels[...].T
    finish(copies[:2])
    own_t[...] = own_s[...].T
    add_pair(own_t, own_s, amp, None, total, level, levels, weights, 0)
    finish(copies[2:])
    outs = []

    def after(done):
        s = pl.ds(done - BLOCK, BLOCK)
        outs.extend(begin([(total.at[:, s], total_out.at[:, s])], sem, 4 + len(outs)))

    add_pair(own_t, other, amp, lambda: None, total, level, levels, weights, 1, after)
    finish(outs)


def load_extra(pick, from_y, from_z, dst, sem):
    @pl.when(pick == 1)
    def _():
        pltpu.make_async_copy(from_y, dst, sem).start()

    @pl.when(pick != 1)
    def _():
        pltpu.make_async_copy(from_z, dst, sem).start()

    return pltpu.make_async_copy(from_z, dst, sem)


def far_kernel(me_ref, own_t_in, total_in, y00, y01, y10, y11, z00, z01, xy0, xz0, levels, weights, total_out,
               sem, own_t, first, second, amp, total):
    half, virt = y00.shape
    parity, core, _ = place_of(me_ref[0])
    a, b = pl.ds(0, virt), pl.ds(virt, virt)
    top, low = pl.ds(0, half), pl.ds(half, half)
    copies = begin(
        [
            (own_t_in, own_t),
            (y00, first.at[top, a]), (y01, first.at[low, a]), (y10, first.at[top, b]), (y11, first.at[low, b]),
            (total_in, total), (z00, second.at[top, a]), (z01, second.at[low, a]),
        ],
        sem,
    )
    extra = load_extra(parity ^ core, xy0, xz0, second.at[:, b], sem.at[8])
    level = levels[...].T
    finish(copies[:5])
    add_pair(own_t, first, amp, copies[5].wait, total, level, levels, weights, 2)
    finish(copies[6:])
    extra.wait()
    outs = []

    def after(done):
        s = pl.ds(done - BLOCK, BLOCK)
        outs.extend(begin([(total.at[:, s], total_out.at[:, s])], sem, 9 + len(outs)))

    add_pair(own_t, second, amp, lambda: None, total, level, levels, weights, 3, after)
    finish(outs)


def last_kernel(me_ref, own_t_in, total_in, own, z10, z11, xy1, xz1, levels, weights, residual, keep, send,
                sem, own_t, own_s, second, amp, total, high, rest, packed):
    half, virt = z10.shape
    parity, core, _ = place_of(me_ref[0])
    a, b = pl.ds(0, virt), pl.ds(virt, virt)
    top, low = pl.ds(0, half), pl.ds(half, half)
    copies = begin(
        [
            (own_t_in, own_t), (z10, second.at[top, a]), (z11, second.at[low, a]), (total_in, total),
            (own.at[0], own_s.at[:, a]), (own.at[1], own_s.at[:, b]),
        ],
        sem,
    )
    extra = load_extra(parity ^ core, xy1, xz1, second.at[:, b], sem.at[6])
    level = levels[...].T
    finish(copies[:3])
    extra.wait()
    add_pair(own_t, second, amp, copies[3].wait, total, level, levels, weights, 4)
    outs = begin([(total.at[:, a], residual.at[0]), (total.at[:, b], residual.at[1])], sem, 7)
    finish(copies[4:])
    high[...] = total[...].astype(BF16)
    rest[...] = (total[...] - high[...].astype(F32)).astype(BF16)
    at = 0
    for q in range(0, total.shape[0], BLOCK):
        rows = q + BLOCK
        slab = own_s[q:q + BLOCK, :]
        block = lax.dot_general(high[:rows, :], slab, NT, preferred_element_type=F32)
        block += lax.dot_general(rest[:rows, :], slab, NT, preferred_element_type=F32)
        for c in range(0, BLOCK, LANES):
            upper = q + c + LANES
            packed[at:at + upper, :] = block[:upper, c:c + LANES]
            at += upper
    size = keep.shape[0]
    outs += begin(
        [(packed.at[pl.ds(core * size, size)], keep), (packed.at[pl.ds((1 - core) * size, size)], send)], sem, 9
    )
    finish(outs)


def encode(x, out, row):
    rows = x.shape[0]
    largest = jnp.max(jnp.abs(x), axis=0, keepdims=True)
    power = jnp.floor(jnp.log2(jnp.maximum(largest, 1e-30))) + 1.0
    out[pl.ds(row, rows), :] = jnp.round(x * jnp.exp2(BITS - power)).astype(I32).astype(I16)
    out[pl.ds(row + rows, PAD), :] = jnp.broadcast_to(power, (PAD, LANES)).astype(I32).astype(I16)


def decode(coded):
    rows = coded.shape[0] - PAD
    wide = coded.astype(I32).astype(F32)
    return wide[:rows] * jnp.exp2(wide[rows:rows + 1] - BITS)


def chip_kernel(me_ref, mine, theirs, keep, send):
    parity, _, _ = place_of(me_ref[0])
    size = keep.shape[0]
    piece = size // 4
    at = pl.ds(pl.multiple_of(parity * size, 16), size)
    keep[...] = mine[at, :] + theirs[at, :]
    for t in range(4):
        at = pl.ds(pl.multiple_of((1 - parity) * size + t * piece, 16), piece)
        encode(mine[at, :] + theirs[at, :], send, t * (piece + PAD))


def column_kernel(me_ref, mine, theirs, keep, *sends):
    _, _, z = place_of(me_ref[0])
    piece = keep.shape[0]
    for t in range(4):
        at = pl.ds(pl.multiple_of((z ^ t) * piece, 16), piece)
        coded = theirs[pl.ds(pl.multiple_of((z ^ t) * (piece + PAD), 16), piece + PAD), :]
        value = mine[at, :] + decode(coded)
        if t:
            encode(value, sends[t - 1], 0)
        else:
            keep[...] = value


def sum_kernel(mine, a, b, c, out):
    out[...] = mine[...] + decode(a[...]) + decode(b[...]) + decode(c[...])


def code_kernel(scale, x, out):
    encode(x[...] * scale, out, 0)


def sum_code_kernel(scale, mine, a, b, c, out):
    encode((mine[...] + decode(a[...]) + decode(b[...]) + decode(c[...])) * scale, out, 0)


def spread_kernel(me_ref, a, b, sib_a, sib_b, out, packed):
    parity, core, z = place_of(me_ref[0])
    rows = a.shape[1] - PAD
    for src, half, side in ((a, core, parity), (b, core, 1 - parity), (sib_a, 1 - core, parity), (sib_b, 1 - core, 1 - parity)):
        for t in range(4):
            row = ((half * 2 + side) * 4 + (z ^ t)) * rows
            packed[pl.ds(pl.multiple_of(row, 16), rows), :] = decode(src[t])
    at = 0
    for c in range(0, out.shape[1], LANES):
        out[0:c + LANES, c:c + LANES] = packed[at:at + c + LANES, :]
        for r in range(0, c, LANES):
            out[c:c + LANES, r:r + LANES] = packed[at + r:at + r + LANES, :].T
        at += c + LANES


def shards(slabs, pair_blocks, occ_energy, virt_energy, domain_map):
    blocks = lax.axis_size("dom")
    me = lax.axis_index("dom").astype(I32)[None]
    own = slabs[0]
    orbitals, aux, virt = own.shape
    half, wide = aux // 2, orbitals * virt
    upper = aux * (aux + LANES) // 2 // LANES
    piece = upper // 16

    hbm = pl.BlockSpec(memory_space=pl.ANY)
    vmem = pl.BlockSpec(memory_space=pltpu.VMEM)
    smem = pl.BlockSpec(memory_space=pltpu.SMEM)
    total_s = pltpu.VMEM((aux, wide), F32)
    slab_s = pltpu.VMEM((aux, wide), BF16)
    amp_s = pltpu.VMEM((wide, wide), BF16)
    own_t_s = pltpu.VMEM((wide, aux), BF16)
    total_t = jax.ShapeDtypeStruct((aux, wide), F32)
    pair_flops = 4 * aux * wide * wide

    def kernel(body, name, ins, outs, out_specs, scratch=(), flops=0, moved=0):
        return pl.pallas_call(
            body,
            out_shape=outs,
            in_specs=ins,
            out_specs=out_specs,
            scratch_shapes=scratch,
            compiler_params=pltpu.CompilerParams(vmem_limit_bytes=VMEM_LIMIT),
            cost_estimate=pl.CostEstimate(flops=flops, bytes_accessed=moved, transcendentals=0),
            name=name,
        )

    def dma(n):
        return pltpu.SemaphoreType.DMA((n,))

    def coded(n):
        return jax.ShapeDtypeStruct((n, LANES), I16)

    def plain(n):
        return jax.ShapeDtypeStruct((n, LANES), F32)

    sib = swapped(own, 1)
    y = [[swapped(own[j, h * half:(h + 1) * half], 2) for h in range(2)] for j in range(2)]
    near_pairs = [shifted(pair_blocks, -step) for step in (1, -1, 2, -2)]

    small = jax.ShapeDtypeStruct((8, wide), F32)
    levels, weights = kernel(
        functools.partial(prep_kernel, blocks), "prep", [smem] * 7 + [vmem] * 2, (small, small), (vmem, vmem),
        flops=1000, moved=100000,
    )(me, pair_blocks, *near_pairs, occ_energy, virt_energy.reshape(-1, LANES), domain_map)
    own_t, total = kernel(
        near_kernel, "near", [hbm, hbm, vmem, vmem], (jax.ShapeDtypeStruct((wide, aux), BF16), total_t), (vmem, hbm),
        [dma(7), slab_s, slab_s, amp_s, total_s], 2 * pair_flops, 10 * aux * wide,
    )(own, sib, levels, weights)

    y[0][1], total, own_t = lax.optimization_barrier((y[0][1], total, own_t))
    z = [[forwarded(c) for c in row] for row in y]
    from_y = [to_sibling(jnp.concatenate(row), 0) for row in y]
    from_z = to_sibling(jnp.concatenate(z[0]), 1)
    total = kernel(
        far_kernel, "far", [smem] + [hbm] * 10 + [vmem] * 2, total_t, hbm,
        [dma(12), own_t_s, slab_s, slab_s, amp_s, total_s], 2 * pair_flops, 14 * aux * wide,
    )(me, own_t, total, y[0][0], y[0][1], y[1][0], y[1][1], z[0][0], z[0][1], from_y[0], from_z, levels, weights)
    z[1][0], z[1][1], total = lax.optimization_barrier((z[1][0], z[1][1], total))
    from_z = to_sibling(jnp.concatenate(z[1]), 1)
    residual, keep, send = kernel(
        last_kernel, "last", [smem] + [hbm] * 7 + [vmem] * 2,
        (jax.ShapeDtypeStruct(own.shape, F32), plain(upper // 2), plain(upper // 2)), (hbm,) * 3,
        [dma(11), own_t_s, slab_s, slab_s, amp_s, total_s, slab_s, slab_s, pltpu.VMEM((upper, LANES), F32)],
        2 * pair_flops, 14 * aux * wide,
    )(me, own_t, total, own, z[1][0], z[1][1], from_y[1], from_z, levels, weights)

    got = swapped(send, 1)
    keep, send = kernel(
        chip_kernel, "chip", [smem, vmem, vmem], (plain(upper // 4), coded(4 * (piece + PAD))), (vmem, vmem),
        moved=upper * LANES * 6,
    )(me, keep, got)
    got = swapped(send, 2)
    keep, *sends = kernel(
        column_kernel, "column", [smem, vmem, vmem], (plain(piece),) + (coded(piece + PAD),) * 3, (vmem,) * 4,
        moved=upper * LANES * 2,
    )(me, keep, got)
    got = [swapped(send, 4 * t) for t, send in zip((1, 2, 3), sends)]
    if blocks == 16:
        mine = kernel(
            functools.partial(sum_code_kernel, 1.0 / blocks), "sum_code", [vmem] * 4, coded(piece + PAD), vmem,
            moved=upper * LANES,
        )(keep, *got)
    else:
        value = kernel(sum_kernel, "sum", [vmem] * 4, plain(piece), vmem)(keep, *got)
        bit = 16
        while bit < blocks:
            value = value + swapped(value, bit)
            bit *= 2
        mine = kernel(functools.partial(code_kernel, 1.0 / blocks), "code", [vmem], coded(piece + PAD), vmem)(value)

    column = [mine] + [swapped(mine, 4 * t) for t in (1, 2, 3)]
    across = [swapped(c, 2) for c in column]
    a, b = jnp.stack(column), jnp.stack(across)
    gradient = kernel(
        spread_kernel, "spread", [smem] + [vmem] * 4, jax.ShapeDtypeStruct((aux, aux), F32), vmem,
        [pltpu.VMEM((upper, LANES), F32)], moved=aux * aux * 6,
    )(me, a, b, swapped(a, 1), swapped(b, 1))
    return residual[None], gradient


def solution(mesh):
    return jax.shard_map(
        shards,
        mesh=mesh,
        in_specs=(
            P(("grp", "dom"), None, None, None),
            P(("grp", "dom"), None),
            P("grp", None),
            P("grp"),
            P("grp", None),
        ),
        out_specs=(P(("grp", "dom"), None, None, None), P("grp", None)),
        check_vma=False,
    )
```

time: 492 us -> 165 us (0.34)
  waiting for transfers between devices: 358 us -> 52.4 us
  Pallas kernels: 0 us -> 45.1 us
  matrix products: 30.9 us -> 0 us
  local copies, waits for them, and re-layouts: 37.2 us -> 7.67 us
  between operations: 22.3 us -> 1.12 us
  starting transfers between devices: 36.5 us -> 56.9 us
  other arithmetic: 6.47 us -> 1.25 us
    ppermute x8 -> x31, waiting for transfers between devices: 213 us -> 52.4 us  [move(): return lax.ppermute(x, 'dom', pairs)]
    psum x1 -> x0, waiting for transfers between devices: 145 us -> none  [shards(): gradient = lax.psum(partial_metric, 'dom') / lax.axis_size('dom')]
    pallas_call x0 -> x8, Pallas kernels: none -> 45.1 us  [the longest x1 12.4 us: shards(): kernel(last_kernel, 'last', [smem] + [hbm] * 7 + [vmem] * 2, (jax.ShapeDt...]
    dot_general x10 -> x0, matrix products: 30.9 us -> none  [the longest x3 10.3 us: shards(): jnp.einsum('iajb,jpb->ipa', amplitude, slab_partner, preferred_element_ty...]
    ppermute x8 -> x31, starting transfers between devices: 36.5 us -> 56.9 us  [move(): return lax.ppermute(x, 'dom', pairs)]
    gather x4 -> x0, local copies, waits for them, and re-layouts: 10.3 us -> none  [the longest x3 7.79 us: shards(): virt_partner = virt_energy[domain_map[partner]]]
    squeeze x1, local copies, waits for them, and re-layouts: 8.64 us -> 1.51 us  [shards(): own[j, h * half:(h + 1) * half]]
    broadcast_in_dim x1 -> x0, local copies, waits for them, and re-layouts: 6.94 us -> none  [shards(): outgoing = jnp.zeros((width, orbitals, aux_count, virt_count), jnp.float32)]
  transfers between devices with their start and end apart: 9 -> 31, of which waited for: 4 -> 13; matrix products, arithmetic and copies ran while one was open for 5% -> 2% of each run, Pallas kernels for 0% -> 13%
where the time goes in v2:
time: 165 us; the launch traced here: 164 us
  starting transfers between devices  56.9 us (34%)
  waiting for transfers between devices  52.4 us (32%)
  Pallas kernels  45.1 us (27%)
  local copies, waits for them, and re-layouts  7.67 us (5%)
    ppermute x31, starting transfers between devices, move(): return lax.ppermute(x, 'dom', pairs)  56.9 us
    ppermute x31, waiting for transfers between devices, move(): return lax.ppermute(x, 'dom', pairs)  52.4 us
    pallas_call x1, Pallas kernels, shards(): kernel(last_kernel, 'last', [smem] + [hbm] * 7 + [vmem] * 2, (jax.ShapeDt...  12.4 us
    pallas_call x1, Pallas kernels, shards(): kernel(near_kernel, 'near', [hbm, hbm, vmem, vmem], (jax.ShapeDtypeStruct...  10 us
    pallas_call x1, Pallas kernels, shards(): kernel(far_kernel, 'far', [smem] + [hbm] * 10 + [vmem] * 2, total_t, hbm,...  9.77 us
    unnamed x53, local copies, waits for them, and re-layouts  6.16 us
    pallas_call x1, Pallas kernels, shards(): kernel(spread_kernel, 'spread', [smem] + [vmem] * 4, jax.ShapeDtypeStruct...  4.28 us
  transfers between devices with their start and end apart: 31, of which 13 were waited for; matrix products, arithmetic and copies ran while one was open for 2% of the time, Pallas kernels for 13%

profile of v2, /device:TPU:0, one launch (start us, length us, event | category | flops | bytes accessed | tf_op | source)
XLA Modules:
  0.0 164.4 jit_solution(12476090608073794726)
XLA Ops:
  0.7 0.5 collective-permute-start.1
  1.2 1.5 slice_bitcast_fusion
  2.7 2.6 %collective-permute-start.10 = (bf16[512,384]{1,0:T(8,128)(2,1)S(1)}, bf16[512,384]{1,0:T(8,128)(2,1)S(1)}, u32[]{:S(2)}, u32[]{:S(2)}) collective-permute-start(bf16[512,384]{1,0:T(8,128)(2,1)S(1)} %get-tuple-element.40), channel_id=1, source_target_pairs={{0,2},{1,3},{2,0},{3,1},{4,6},{5,7},{6,4},{7,5},{8,10},{9,11},{10,... | collective-permute-start | bytes 1179656 | tf_op jit(solution)/shard_map/ppermute | solution.py:21
  5.3 1.3 collective-permute-start.2
  6.6 3.0 %collective-permute-start.3 = (s32[1,3]{1,0:T(1,128)S(1)}, s32[1,3]{1,0:T(1,128)S(1)}, u32[]{:S(2)}, u32[]{:S(2)}) collective-permute-start(s32[1,3]{1,0:T(1,128)S(1)} %copy-done.18), channel_id=1, source_target_pairs={{0,1},{1,2},{2,3},{3,4},{4,5},{5,6},{6,7},{7,8},{8,9},{9,10},{10,1... | collective-permute-start | bytes 44 | tf_op jit(solution)/shard_map/ppermute | solution.py:21
  9.6 1.3 collective-permute-start.4
  10.9 0.7 copy.7.occ
  11.6 4.9 %collective-permute-start.5 = (s32[1,3]{1,0:T(1,128)S(1)}, s32[1,3]{1,0:T(1,128)S(1)}, u32[]{:S(2)}, u32[]{:S(2)}) collective-permute-start(s32[1,3]{1,0:T(1,128)S(1)} %copy-done.18), channel_id=1, source_target_pairs={{0,2},{1,3},{2,4},{3,5},{4,6},{5,7},{6,8},{7,9},{8,10},{9,11},{10,... | collective-permute-start | bytes 44 | tf_op jit(solution)/shard_map/ppermute | solution.py:21
  16.6 1.9 %collective-permute-start = (bf16[512,384]{1,0:T(8,128)(2,1)S(1)}, bf16[512,384]{1,0:T(8,128)(2,1)S(1)}, u32[]{:S(2)}, u32[]{:S(2)}) collective-permute-start(bf16[512,384]{1,0:T(8,128)(2,1)S(1)} %get-tuple-element.43), channel_id=1, source_target_pairs={{0,2},{1,3},{2,0},{3,1},{4,6},{5,7},{6,4},{7,5},{8,10},{9,11},{10,... | collective-permute-start | bytes 1179656 | tf_op jit(solution)/shard_map/ppermute | solution.py:21
  18.5 0.6 copy-done.21
  19.1 2.1 %prep.1 = (f32[8,768]{1,0:T(8,128)}, f32[8,768]{1,0:T(8,128)}) custom-call(s32[1]{0:T(128)} %bitcast.me_ref, s32[1,3]{1,0:T(1,128)} %pairs.1, s32[1,3]{1,0:T(1,128)} %copy-done.19, s32[1,3]{1,0:T(1,128)} %copy-done.20, s32[1,3]{1,0:T(1,128)} %copy-done.21, s32[1,3]{1,0:T(1,128)} %copy-done.22, f32[16,2]{1,0:T(8,128)} %copy.7.occ, f32[64,128]{1,0:T(8,128)} %bitcast.32, ...), custom_call_target="tpu_custom_call" | custom-call | flops 1000 | bytes 100000 | tf_op jit(solution)/shard_map/prep/pallas_call | solution.py:324
  21.2 4.7 %collective-permute-start.11 = (bf16[512,384]{1,0:T(8,128)(2,1)S(1)}, bf16[512,384]{1,0:T(8,128)(2,1)S(1)}, u32[]{:S(2)}, u32[]{:S(2)}) collective-permute-start(bf16[512,384]{1,0:T(8,128)(2,1)S(1)} %collective-permute-done.10.y00), channel_id=1, source_target_pairs={{0,4},{1,5},{4,8},{5,9},{6,2},{7,3},{8,12},{9,13},{10,6},{11,7},{1... | collective-permute-start | bytes 1179656 | tf_op jit(solution)/shard_map/ppermute | solution.py:21
  25.9 10.0 %near.1 = (bf16[768,1024]{1,0:T(8,128)(2,1)}, f32[1024,768]{1,0:T(8,128)}) custom-call(bf16[2,1024,384]{2,1,0:T(8,128)(2,1)} %bitcast.22, bf16[2,1024,384]{2,1,0:T(8,128)(2,1)} %collective-permute-done.1.sib, f32[8,768]{1,0:T(8,128)} %get-tuple-element.21.levels, f32[8,768]{1,0:T(8,128)} %get-tuple-element.22.weights), custom_call_target="tpu_custom_call" | custom-call | flops 4831838208 | bytes 7864320 | tf_op jit(solution)/shard_map/near/pallas_call | solution.py:328
  36.0 3.5 %collective-permute-start.12 = (bf16[512,384]{1,0:T(8,128)(2,1)S(1)}, bf16[512,384]{1,0:T(8,128)(2,1)S(1)}, u32[]{:S(2)}, u32[]{:S(2)}) collective-permute-start(bf16[512,384]{1,0:T(8,128)(2,1)S(1)} %collective-permute-done.y01), channel_id=1, source_target_pairs={{0,4},{1,5},{4,8},{5,9},{6,2},{7,3},{8,12},{9,13},{10,6},{11,7},{1... | collective-permute-start | bytes 1179656 | tf_op jit(solution)/shard_map/ppermute | solution.py:21
  39.5 0.1 pad_maximum_fusion
  39.5 2.2 %collective-permute-start.13 = (bf16[1024,384]{1,0:T(8,128)(2,1)S(1)}, bf16[1024,384]{1,0:T(8,128)(2,1)S(1)}, u32[]{:S(2)}, u32[]{:S(2)}) collective-permute-start(bf16[1024,384]{1,0:T(8,128)(2,1)S(1)} %pad_maximum_fusion), channel_id=1, source_target_pairs={{0,1},{3,2},{4,5},{7,6},{8,9},{11,10},{12,13},{15,14},{16,17},{19,... | collective-permute-start | bytes 2359304 | tf_op jit(solution)/shard_map/ppermute | solution.py:21
  41.7 6.7 %collective-permute-done.12.z01 = bf16[512,384]{1,0:T(8,128)(2,1)S(1)} collective-permute-done((bf16[512,384]{1,0:T(8,128)(2,1)S(1)}, bf16[512,384]{1,0:T(8,128)(2,1)S(1)}, u32[]{:S(2)}, u32[]{:S(2)}) %collective-permute-start.12) | collective-permute-done | bytes 393248 | tf_op jit(solution)/shard_map/ppermute | solution.py:21
  48.4 0.1 pad_maximum_fusion.1
  48.5 1.3 collective-permute-start.14
  49.8 1.1 collective-permute-start.6
  50.9 1.0 collective-permute-start.8
  51.9 9.0 %collective-permute-done.6.y10 = bf16[512,384]{1,0:T(8,128)(2,1)S(1)} collective-permute-done((bf16[512,384]{1,0:T(8,128)(2,1)S(1)}, bf16[512,384]{1,0:T(8,128)(2,1)S(1)}, u32[]{:S(2)}, u32[]{:S(2)}) %collective-permute-start.6) | collective-permute-done | bytes 393248 | tf_op jit(solution)/shard_map/ppermute | solution.py:21
  60.9 8.4 %collective-permute-done.8.y11 = bf16[512,384]{1,0:T(8,128)(2,1)S(1)} collective-permute-done((bf16[512,384]{1,0:T(8,128)(2,1)S(1)}, bf16[512,384]{1,0:T(8,128)(2,1)S(1)}, u32[]{:S(2)}, u32[]{:S(2)}) %collective-permute-start.8) | collective-permute-done | bytes 393248 | tf_op jit(solution)/shard_map/ppermute | solution.py:21
  69.3 0.1 pad_maximum_fusion.2
  69.4 2.8 %collective-permute-start.15 = (bf16[1024,384]{1,0:T(8,128)(2,1)S(1)}, bf16[1024,384]{1,0:T(8,128)(2,1)S(1)}, u32[]{:S(2)}, u32[]{:S(2)}) collective-permute-start(bf16[1024,384]{1,0:T(8,128)(2,1)S(1)} %pad_maximum_fusion.2), channel_id=1, source_target_pairs={{0,1},{3,2},{4,5},{7,6},{8,9},{11,10},{12,13},{15,14},{16,17},{19,... | collective-permute-start | bytes 2359304 | tf_op jit(solution)/shard_map/ppermute | solution.py:21
  72.2 4.4 %collective-permute-start.7 = (bf16[512,384]{1,0:T(8,128)(2,1)S(1)}, bf16[512,384]{1,0:T(8,128)(2,1)S(1)}, u32[]{:S(2)}, u32[]{:S(2)}) collective-permute-start(bf16[512,384]{1,0:T(8,128)(2,1)S(1)} %collective-permute-done.6.y10), channel_id=1, source_target_pairs={{0,4},{1,5},{4,8},{5,9},{6,2},{7,3},{8,12},{9,13},{10,6},{11,7},{1... | collective-permute-start | bytes 1179656 | tf_op jit(solution)/shard_map/ppermute | solution.py:21
  76.6 3.7 %collective-permute-start.9 = (bf16[512,384]{1,0:T(8,128)(2,1)S(1)}, bf16[512,384]{1,0:T(8,128)(2,1)S(1)}, u32[]{:S(2)}, u32[]{:S(2)}) collective-permute-start(bf16[512,384]{1,0:T(8,128)(2,1)S(1)} %collective-permute-done.8.y11), channel_id=1, source_target_pairs={{0,4},{1,5},{4,8},{5,9},{6,2},{7,3},{8,12},{9,13},{10,6},{11,7},{1... | collective-permute-start | bytes 1179656 | tf_op jit(solution)/shard_map/ppermute | solution.py:21
  80.3 0.8 copy-done.23
  81.2 9.8 %far.1.total_in = f32[1024,768]{1,0:T(8,128)} custom-call(s32[1]{0:T(128)} %bitcast.me_ref, bf16[768,1024]{1,0:T(8,128)(2,1)} %get-tuple-element.25.own_t_in, f32[1024,768]{1,0:T(8,128)} %get-tuple-element.26.total_in, bf16[512,384]{1,0:T(8,128)(2,1)} %copy-done.3, bf16[512,384]{1,0:T(8,128)(2,1)} %copy-done.4, bf16[512,384]{1,0:T(8,128)(2,1)} %copy-done.9, ...), custom_call_target="tpu_custom_call" | custom-call | flops 4831838208 | bytes 11010048 | tf_op jit(solution)/shard_map/far/pallas_call | solution.py:337
  91.0 1.9 %collective-permute-done.9.z11 = bf16[512,384]{1,0:T(8,128)(2,1)S(1)} collective-permute-done((bf16[512,384]{1,0:T(8,128)(2,1)S(1)}, bf16[512,384]{1,0:T(8,128)(2,1)S(1)}, u32[]{:S(2)}, u32[]{:S(2)}) %collective-permute-start.9) | collective-permute-done | bytes 393248 | tf_op jit(solution)/shard_map/ppermute | solution.py:21
  92.9 0.1 pad_maximum_fusion.3
  93.0 1.5 collective-permute-start.16
  94.5 2.6 %collective-permute-done.16.xz1 = bf16[1024,384]{1,0:T(8,128)(2,1)S(1)} collective-permute-done((bf16[1024,384]{1,0:T(8,128)(2,1)S(1)}, bf16[1024,384]{1,0:T(8,128)(2,1)S(1)}, u32[]{:S(2)}, u32[]{:S(2)}) %collective-permute-start.16) | collective-permute-done | bytes 786464 | tf_op jit(solution)/shard_map/ppermute | solution.py:21
  97.2 0.9 copy-done.25
  98.0 12.4 %last.1 = (f32[2,1024,384]{2,1,0:T(8,128)}, f32[2304,128]{1,0:T(8,128)}, f32[2304,128]{1,0:T(8,128)}) custom-call(s32[1]{0:T(128)} %bitcast.me_ref, bf16[768,1024]{1,0:T(8,128)(2,1)} %get-tuple-element.25.own_t_in, f32[1024,768]{1,0:T(8,128)} %far.1.total_in, bf16[2,1024,384]{2,1,0:T(8,128)(2,1)} %bitcast.23, bf16[512,384]{1,0:T(8,128)(2,1)} %copy-done.7, ...), custom_call_target="tpu_custom_call" | custom-call | flops 4831838208 | bytes 11010048 | tf_op jit(solution)/shard_map/last/pallas_call | solution.py:343
  110.4 0.2 collective-permute-start.17
  110.6 2.9 %collective-permute-done.17.theirs = f32[2304,128]{1,0:T(8,128)S(1)} collective-permute-done((f32[2304,128]{1,0:T(8,128)}, f32[2304,128]{1,0:T(8,128)S(1)}, u32[]{:S(2)}, u32[]{:S(2)}) %collective-permute-start.17) | collective-permute-done | bytes 1179680 | tf_op jit(solution)/shard_map/ppermute | solution.py:21
  113.6 1.0 copy-done.2
  114.6 2.8 %chip.1 = (f32[1152,128]{1,0:T(8,128)}, s16[1216,128]{1,0:T(8,128)(2,1)}) custom-call(s32[1]{0:T(128)} %bitcast.me_ref, f32[2304,128]{1,0:T(8,128)} %get-tuple-element.32.mine, f32[2304,128]{1,0:T(8,128)} %copy-done.2), custom_call_target="tpu_custom_call" | custom-call | bytes 3538944 | tf_op jit(solution)/shard_map/chip/pallas_call | solution.py:351
  117.3 1.5 collective-permute-start.18
  118.9 8.1 %collective-permute-done.18.theirs = s16[1216,128]{1,0:T(8,128)(2,1)S(1)} collective-permute-done((s16[1216,128]{1,0:T(8,128)(2,1)}, s16[1216,128]{1,0:T(8,128)(2,1)S(1)}, u32[]{:S(2)}, u32[]{:S(2)}) %collective-permute-start.18) | collective-permute-done | bytes 311328 | tf_op jit(solution)/shard_map/ppermute | solution.py:21
  127.0 0.7 copy-done.13
  127.7 2.0 %column.1 = (f32[288,128]{1,0:T(8,128)}, s16[304,128]{1,0:T(8,128)(2,1)}, s16[304,128]{1,0:T(8,128)(2,1)}, s16[304,128]{1,0:T(8,128)(2,1)}) custom-call(s32[1]{0:T(128)} %bitcast.me_ref, f32[1152,128]{1,0:T(8,128)} %get-tuple-element.34.mine, s16[1216,128]{1,0:T(8,128)(2,1)} %copy-done.13), custom_call_target="tpu_custom_call" | custom-call | bytes 1179648 | tf_op jit(solution)/shard_map/column/pallas_call | solution.py:356
  129.7 2.5 %collective-permute-start.19 = (s16[304,128]{1,0:T(8,128)(2,1)}, s16[304,128]{1,0:T(8,128)(2,1)S(1)}, u32[]{:S(2)}, u32[]{:S(2)}) collective-permute-start(s16[304,128]{1,0:T(8,128)(2,1)} %get-tuple-element.37), channel_id=1, source_target_pairs={{0,4},{1,5},{2,6},{3,7},{4,0},{5,1},{6,2},{7,3},{8,12},{9,13},{10,... | collective-permute-start | bytes 233480 | tf_op jit(solution)/shard_map/ppermute | solution.py:21
  132.1 1.3 collective-permute-start.20
  133.5 1.2 collective-permute-start.21
  134.6 0.4 collective-permute-done.19.a
  135.1 5.6 %collective-permute-done.20.b = s16[304,128]{1,0:T(8,128)(2,1)S(1)} collective-permute-done((s16[304,128]{1,0:T(8,128)(2,1)}, s16[304,128]{1,0:T(8,128)(2,1)S(1)}, u32[]{:S(2)}, u32[]{:S(2)}) %collective-permute-start.20) | collective-permute-done | bytes 77856 | tf_op jit(solution)/shard_map/ppermute | solution.py:21
  140.7 0.6 copy-done.15
  141.4 1.8 %sum_code.1 = s16[304,128]{1,0:T(8,128)(2,1)} custom-call(f32[288,128]{1,0:T(8,128)} %get-tuple-element.36.mine, s16[304,128]{1,0:T(8,128)(2,1)} %copy-done.14, s16[304,128]{1,0:T(8,128)(2,1)} %copy-done.15, s16[304,128]{1,0:T(8,128)(2,1)} %copy-done.16), custom_call_target="tpu_custom_call" | custom-call | bytes 589824 | tf_op jit(solution)/shard_map/sum_code/pallas_call | solution.py:362
  143.2 1.4 collective-permute-start.22
  144.5 1.4 collective-permute-start.23
  145.9 1.6 collective-permute-start.24
  147.5 0.6 collective-permute-start.25
  148.2 1.4 collective-permute-start.26
  149.6 2.9 %collective-permute-done.23 = s16[304,128]{1,0:T(8,128)(2,1)S(1)} collective-permute-done((s16[304,128]{1,0:T(8,128)(2,1)}, s16[304,128]{1,0:T(8,128)(2,1)S(1)}, u32[]{:S(2)}, u32[]{:S(2)}) %collective-permute-start.23) | collective-permute-done | bytes 77856 | tf_op jit(solution)/shard_map/ppermute | solution.py:21
  152.4 0.8 collective-permute-start.27
  153.3 1.2 collective-permute-start.28
  154.5 0.9 pad_add_fusion.a
  155.5 1.3 collective-permute-done.27
  156.8 0.8 collective-permute-done.28
  157.8 1.6 collective-permute-done.30.sib_b
  159.4 0.7 copy-done.12
  160.1 4.3 %spread.1 = f32[1024,1024]{1,0:T(8,128)} custom-call(s32[1]{0:T(128)} %bitcast.me_ref, s16[4,304,128]{2,1,0:T(8,128)(2,1)} %copy-done, s16[4,304,128]{2,1,0:T(8,128)(2,1)} %copy-done.1, s16[4,304,128]{2,1,0:T(8,128)(2,1)} %copy-done.11, s16[4,304,128]{2,1,0:T(8,128)(2,1)} %copy-done.12), custom_call_target="tpu_custom_call" | custom-call | bytes 6291456 | tf_op jit(solution)/shard_map/spread/pallas_call | solution.py:377
  (66 shorter events, 0.4 us)
Async XLA Ops:
  0.6 4.7 %copy-start.18 = (s32[1,3]{1,0:T(1,128)S(1)}, s32[1,3]{1,0:T(1,128)}, u32[]{:S(2)}) copy-start(s32[1,3]{1,0:T(1,128)} %pairs.1) | copy-start | bytes 40
  0.6 10.3 %copy-start.17 = (f32[16,2]{0,1:T(2,128)S(1)}, f32[16,2]{0,1:T(2,128)}, u32[]{:S(2)}) copy-start(f32[16,2]{0,1:T(2,128)} %param.7) | copy-start | bytes 388
  0.7 25.2 %collective-permute-start.1 = (bf16[2,1024,384]{2,1,0:T(8,128)(2,1)}, bf16[2,1024,384]{2,1,0:T(8,128)(2,1)}, u32[]{:S(2)}, u32[]{:S(2)}) collective-permute-start(bf16[2,1024,384]{2,1,0:T(8,128)(2,1)} %bitcast.20), channel_id=1, source_target_pairs={{0,1},{1,0},{2,3},{3,2},{4,5},{5,4},{6,7},{7,6},{8,9},{9,8},{10,11... | collective-permute-start | bytes 4718600 | tf_op jit(solution)/shard_map/ppermute | solution.py:21
  2.7 18.5 %collective-permute-start.10 = (bf16[512,384]{1,0:T(8,128)(2,1)S(1)}, bf16[512,384]{1,0:T(8,128)(2,1)S(1)}, u32[]{:S(2)}, u32[]{:S(2)}) collective-permute-start(bf16[512,384]{1,0:T(8,128)(2,1)S(1)} %get-tuple-element.40), channel_id=1, source_target_pairs={{0,2},{1,3},{2,0},{3,1},{4,6},{5,7},{6,4},{7,5},{8,10},{9,11},{10,... | collective-permute-start | bytes 1179656 | tf_op jit(solution)/shard_map/ppermute | solution.py:21
  5.3 6.3 %collective-permute-start.2 = (s32[1,3]{1,0:T(1,128)S(1)}, s32[1,3]{1,0:T(1,128)S(1)}, u32[]{:S(2)}, u32[]{:S(2)}) collective-permute-start(s32[1,3]{1,0:T(1,128)S(1)} %copy-done.18), channel_id=1, source_target_pairs={{1,0},{2,1},{3,2},{4,3},{5,4},{6,5},{7,6},{8,7},{9,8},{10,9},{11,1... | collective-permute-start | bytes 44 | tf_op jit(solution)/shard_map/ppermute | solution.py:21
  6.6 10.0 %collective-permute-start.3 = (s32[1,3]{1,0:T(1,128)S(1)}, s32[1,3]{1,0:T(1,128)S(1)}, u32[]{:S(2)}, u32[]{:S(2)}) collective-permute-start(s32[1,3]{1,0:T(1,128)S(1)} %copy-done.18), channel_id=1, source_target_pairs={{0,1},{1,2},{2,3},{3,4},{4,5},{5,6},{6,7},{7,8},{8,9},{9,10},{10,1... | collective-permute-start | bytes 44 | tf_op jit(solution)/shard_map/ppermute | solution.py:21
  9.6 8.9 %collective-permute-start.4 = (s32[1,3]{1,0:T(1,128)S(1)}, s32[1,3]{1,0:T(1,128)S(1)}, u32[]{:S(2)}, u32[]{:S(2)}) collective-permute-start(s32[1,3]{1,0:T(1,128)S(1)} %copy-done.18), channel_id=1, source_target_pairs={{2,0},{3,1},{4,2},{5,3},{6,4},{7,5},{8,6},{9,7},{10,8},{11,9},{12,... | collective-permute-start | bytes 44 | tf_op jit(solution)/shard_map/ppermute | solution.py:21
  11.6 6.9 %copy-start.19 = (s32[1,3]{1,0:T(1,128)}, s32[1,3]{1,0:T(1,128)S(1)}, u32[]{:S(2)}) copy-start(s32[1,3]{1,0:T(1,128)S(1)} %collective-permute-done.2.up) | copy-start | bytes 40
  11.6 6.9 %collective-permute-start.5 = (s32[1,3]{1,0:T(1,128)S(1)}, s32[1,3]{1,0:T(1,128)S(1)}, u32[]{:S(2)}, u32[]{:S(2)}) collective-permute-start(s32[1,3]{1,0:T(1,128)S(1)} %copy-done.18), channel_id=1, source_target_pairs={{0,2},{1,3},{2,4},{3,5},{4,6},{5,7},{6,8},{7,9},{8,10},{9,11},{10,... | collective-permute-start | bytes 44 | tf_op jit(solution)/shard_map/ppermute | solution.py:21
  16.5 2.0 %copy-start.20 = (s32[1,3]{1,0:T(1,128)}, s32[1,3]{1,0:T(1,128)S(1)}, u32[]{:S(2)}) copy-start(s32[1,3]{1,0:T(1,128)S(1)} %collective-permute-done.3.down) | copy-start | bytes 40
  16.6 19.4 %collective-permute-start = (bf16[512,384]{1,0:T(8,128)(2,1)S(1)}, bf16[512,384]{1,0:T(8,128)(2,1)S(1)}, u32[]{:S(2)}, u32[]{:S(2)}) collective-permute-start(bf16[512,384]{1,0:T(8,128)(2,1)S(1)} %get-tuple-element.43), channel_id=1, source_target_pairs={{0,2},{1,3},{2,0},{3,1},{4,6},{5,7},{6,4},{7,5},{8,10},{9,11},{10,... | collective-permute-start | bytes 1179656 | tf_op jit(solution)/shard_map/ppermute | solution.py:21
  18.5 0.6 copy-start.21
  18.5 0.6 copy-start.22
  21.2 18.3 %copy-start.3 = (bf16[512,384]{1,0:T(8,128)(2,1)}, bf16[512,384]{1,0:T(8,128)(2,1)S(1)}, u32[]{:S(2)}) copy-start(bf16[512,384]{1,0:T(8,128)(2,1)S(1)} %collective-permute-done.10.y00) | copy-start | bytes 1179652
  21.2 20.6 %collective-permute-start.11 = (bf16[512,384]{1,0:T(8,128)(2,1)S(1)}, bf16[512,384]{1,0:T(8,128)(2,1)S(1)}, u32[]{:S(2)}, u32[]{:S(2)}) collective-permute-start(bf16[512,384]{1,0:T(8,128)(2,1)S(1)} %collective-permute-done.10.y00), channel_id=1, source_target_pairs={{0,4},{1,5},{4,8},{5,9},{6,2},{7,3},{8,12},{9,13},{10,6},{11,7},{1... | collective-permute-start | bytes 1179656 | tf_op jit(solution)/shard_map/ppermute | solution.py:21
  36.0 12.6 %copy-start.4 = (bf16[512,384]{1,0:T(8,128)(2,1)}, bf16[512,384]{1,0:T(8,128)(2,1)S(1)}, u32[]{:S(2)}) copy-start(bf16[512,384]{1,0:T(8,128)(2,1)S(1)} %collective-permute-done.y01) | copy-start | bytes 1179652
  36.0 12.5 %collective-permute-start.12 = (bf16[512,384]{1,0:T(8,128)(2,1)S(1)}, bf16[512,384]{1,0:T(8,128)(2,1)S(1)}, u32[]{:S(2)}, u32[]{:S(2)}) collective-permute-start(bf16[512,384]{1,0:T(8,128)(2,1)S(1)} %collective-permute-done.y01), channel_id=1, source_target_pairs={{0,4},{1,5},{4,8},{5,9},{6,2},{7,3},{8,12},{9,13},{10,6},{11,7},{1... | collective-permute-start | bytes 1179656 | tf_op jit(solution)/shard_map/ppermute | solution.py:21
  39.5 40.7 %collective-permute-start.13 = (bf16[1024,384]{1,0:T(8,128)(2,1)S(1)}, bf16[1024,384]{1,0:T(8,128)(2,1)S(1)}, u32[]{:S(2)}, u32[]{:S(2)}) collective-permute-start(bf16[1024,384]{1,0:T(8,128)(2,1)S(1)} %pad_maximum_fusion), channel_id=1, source_target_pairs={{0,1},{3,2},{4,5},{7,6},{8,9},{11,10},{12,13},{15,14},{16,17},{19,... | collective-permute-start | bytes 2359304 | tf_op jit(solution)/shard_map/ppermute | solution.py:21
  41.7 27.7 %copy-start.5 = (bf16[512,384]{1,0:T(8,128)(2,1)}, bf16[512,384]{1,0:T(8,128)(2,1)S(1)}, u32[]{:S(2)}) copy-start(bf16[512,384]{1,0:T(8,128)(2,1)S(1)} %collective-permute-done.11.z00) | copy-start | bytes 1179652
  48.4 21.0 %copy-start.6 = (bf16[512,384]{1,0:T(8,128)(2,1)}, bf16[512,384]{1,0:T(8,128)(2,1)S(1)}, u32[]{:S(2)}) copy-start(bf16[512,384]{1,0:T(8,128)(2,1)S(1)} %collective-permute-done.12.z01) | copy-start | bytes 1179652
  48.5 31.8 %collective-permute-start.14 = (bf16[1024,384]{1,0:T(8,128)(2,1)S(1)}, bf16[1024,384]{1,0:T(8,128)(2,1)}, u32[]{:S(2)}, u32[]{:S(2)}) collective-permute-start(bf16[1024,384]{1,0:T(8,128)(2,1)S(1)} %pad_maximum_fusion.1), channel_id=1, source_target_pairs={{1,0},{2,3},{5,4},{6,7},{9,8},{10,11},{13,12},{14,15},{17,16},{18,... | collective-permute-start | bytes 2359304 | tf_op jit(solution)/shard_map/ppermute | solution.py:21
  49.8 11.1 %collective-permute-start.6 = (bf16[512,384]{1,0:T(8,128)(2,1)S(1)}, bf16[512,384]{1,0:T(8,128)(2,1)S(1)}, u32[]{:S(2)}, u32[]{:S(2)}) collective-permute-start(bf16[512,384]{1,0:T(8,128)(2,1)S(1)} %get-tuple-element.42), channel_id=1, source_target_pairs={{0,2},{1,3},{2,0},{3,1},{4,6},{5,7},{6,4},{7,5},{8,10},{9,11},{10,... | collective-permute-start | bytes 1179656 | tf_op jit(solution)/shard_map/ppermute | solution.py:21
  50.9 18.4 %collective-permute-start.8 = (bf16[512,384]{1,0:T(8,128)(2,1)S(1)}, bf16[512,384]{1,0:T(8,128)(2,1)S(1)}, u32[]{:S(2)}, u32[]{:S(2)}) collective-permute-start(bf16[512,384]{1,0:T(8,128)(2,1)S(1)} %get-tuple-element.41), channel_id=1, source_target_pairs={{0,2},{1,3},{2,0},{3,1},{4,6},{5,7},{6,4},{7,5},{8,10},{9,11},{10,... | collective-permute-start | bytes 1179656 | tf_op jit(solution)/shard_map/ppermute | solution.py:21
  60.9 19.4 %copy-start.9 = (bf16[512,384]{1,0:T(8,128)(2,1)}, bf16[512,384]{1,0:T(8,128)(2,1)S(1)}, u32[]{:S(2)}) copy-start(bf16[512,384]{1,0:T(8,128)(2,1)S(1)} %collective-permute-done.6.y10) | copy-start | bytes 1179652
  69.3 11.0 %copy-start.10 = (bf16[512,384]{1,0:T(8,128)(2,1)}, bf16[512,384]{1,0:T(8,128)(2,1)S(1)}, u32[]{:S(2)}) copy-start(bf16[512,384]{1,0:T(8,128)(2,1)S(1)} %collective-permute-done.8.y11) | copy-start | bytes 1179652
  69.4 25.1 %collective-permute-start.15 = (bf16[1024,384]{1,0:T(8,128)(2,1)S(1)}, bf16[1024,384]{1,0:T(8,128)(2,1)S(1)}, u32[]{:S(2)}, u32[]{:S(2)}) collective-permute-start(bf16[1024,384]{1,0:T(8,128)(2,1)S(1)} %pad_maximum_fusion.2), channel_id=1, source_target_pairs={{0,1},{3,2},{4,5},{7,6},{8,9},{11,10},{12,13},{15,14},{16,17},{19,... | collective-permute-start | bytes 2359304 | tf_op jit(solution)/shard_map/ppermute | solution.py:21
  72.2 18.8 %collective-permute-start.7 = (bf16[512,384]{1,0:T(8,128)(2,1)S(1)}, bf16[512,384]{1,0:T(8,128)(2,1)S(1)}, u32[]{:S(2)}, u32[]{:S(2)}) collective-permute-start(bf16[512,384]{1,0:T(8,128)(2,1)S(1)} %collective-permute-done.6.y10), channel_id=1, source_target_pairs={{0,4},{1,5},{4,8},{5,9},{6,2},{7,3},{8,12},{9,13},{10,6},{11,7},{1... | collective-permute-start | bytes 1179656 | tf_op jit(solution)/shard_map/ppermute | solution.py:21
  76.6 16.3 %collective-permute-start.9 = (bf16[512,384]{1,0:T(8,128)(2,1)S(1)}, bf16[512,384]{1,0:T(8,128)(2,1)S(1)}, u32[]{:S(2)}, u32[]{:S(2)}) collective-permute-start(bf16[512,384]{1,0:T(8,128)(2,1)S(1)} %collective-permute-done.8.y11), channel_id=1, source_target_pairs={{0,4},{1,5},{4,8},{5,9},{6,2},{7,3},{8,12},{9,13},{10,6},{11,7},{1... | collective-permute-start | bytes 1179656 | tf_op jit(solution)/shard_map/ppermute | solution.py:21
  80.3 0.9 copy-start.23
  91.0 6.2 %copy-start.7 = (bf16[512,384]{1,0:T(8,128)(2,1)}, bf16[512,384]{1,0:T(8,128)(2,1)S(1)}, u32[]{:S(2)}) copy-start(bf16[512,384]{1,0:T(8,128)(2,1)S(1)} %collective-permute-done.7.z10) | copy-start | bytes 1179652
  92.9 4.3 %copy-start.8 = (bf16[512,384]{1,0:T(8,128)(2,1)}, bf16[512,384]{1,0:T(8,128)(2,1)S(1)}, u32[]{:S(2)}) copy-start(bf16[512,384]{1,0:T(8,128)(2,1)S(1)} %collective-permute-done.9.z11) | copy-start | bytes 1179652
  93.0 4.2 %collective-permute-start.16 = (bf16[1024,384]{1,0:T(8,128)(2,1)S(1)}, bf16[1024,384]{1,0:T(8,128)(2,1)S(1)}, u32[]{:S(2)}, u32[]{:S(2)}) collective-permute-start(bf16[1024,384]{1,0:T(8,128)(2,1)S(1)} %pad_maximum_fusion.3), channel_id=1, source_target_pairs={{1,0},{2,3},{5,4},{6,7},{9,8},{10,11},{13,12},{14,15},{17,16},{18,... | collective-permute-start | bytes 2359304 | tf_op jit(solution)/shard_map/ppermute | solution.py:21
  94.5 2.7 %copy-start.24 = (bf16[1024,384]{1,0:T(8,128)(2,1)}, bf16[1024,384]{1,0:T(8,128)(2,1)S(1)}, u32[]{:S(2)}) copy-start(bf16[1024,384]{1,0:T(8,128)(2,1)S(1)} %collective-permute-done.15.xy1) | copy-start | bytes 2359300
  97.1 0.9 copy-start.25
  110.4 3.1 %collective-permute-start.17 = (f32[2304,128]{1,0:T(8,128)}, f32[2304,128]{1,0:T(8,128)S(1)}, u32[]{:S(2)}, u32[]{:S(2)}) collective-permute-start(f32[2304,128]{1,0:T(8,128)} %get-tuple-element.33), channel_id=1, source_target_pairs={{0,1},{1,0},{2,3},{3,2},{4,5},{5,4},{6,7},{7,6},{8,9},{9,8},{10,11... | collective-permute-start | bytes 3538952 | tf_op jit(solution)/shard_map/ppermute | solution.py:21
  113.6 1.0 copy-start.2
  117.3 9.6 %collective-permute-start.18 = (s16[1216,128]{1,0:T(8,128)(2,1)}, s16[1216,128]{1,0:T(8,128)(2,1)S(1)}, u32[]{:S(2)}, u32[]{:S(2)}) collective-permute-start(s16[1216,128]{1,0:T(8,128)(2,1)} %get-tuple-element.35), channel_id=1, source_target_pairs={{0,2},{1,3},{2,0},{3,1},{4,6},{5,7},{6,4},{7,5},{8,10},{9,11},{10,... | collective-permute-start | bytes 933896 | tf_op jit(solution)/shard_map/ppermute | solution.py:21
  127.0 0.7 copy-start.13
  129.7 5.4 %collective-permute-start.19 = (s16[304,128]{1,0:T(8,128)(2,1)}, s16[304,128]{1,0:T(8,128)(2,1)S(1)}, u32[]{:S(2)}, u32[]{:S(2)}) collective-permute-start(s16[304,128]{1,0:T(8,128)(2,1)} %get-tuple-element.37), channel_id=1, source_target_pairs={{0,4},{1,5},{2,6},{3,7},{4,0},{5,1},{6,2},{7,3},{8,12},{9,13},{10,... | collective-permute-start | bytes 233480 | tf_op jit(solution)/shard_map/ppermute | solution.py:21
  132.1 8.6 %collective-permute-start.20 = (s16[304,128]{1,0:T(8,128)(2,1)}, s16[304,128]{1,0:T(8,128)(2,1)S(1)}, u32[]{:S(2)}, u32[]{:S(2)}) collective-permute-start(s16[304,128]{1,0:T(8,128)(2,1)} %get-tuple-element.38), channel_id=1, source_target_pairs={{0,8},{1,9},{2,10},{3,11},{4,12},{5,13},{6,14},{7,15},{8,0},{9,1},... | collective-permute-start | bytes 233480 | tf_op jit(solution)/shard_map/ppermute | solution.py:21
  133.5 7.3 %collective-permute-start.21 = (s16[304,128]{1,0:T(8,128)(2,1)}, s16[304,128]{1,0:T(8,128)(2,1)S(1)}, u32[]{:S(2)}, u32[]{:S(2)}) collective-permute-start(s16[304,128]{1,0:T(8,128)(2,1)} %get-tuple-element.39), channel_id=1, source_target_pairs={{0,12},{1,13},{2,14},{3,15},{4,8},{5,9},{6,10},{7,11},{8,4},{9,5},... | collective-permute-start | bytes 233480 | tf_op jit(solution)/shard_map/ppermute | solution.py:21
  135.1 5.7 %copy-start.14 = (s16[304,128]{1,0:T(8,128)(2,1)}, s16[304,128]{1,0:T(8,128)(2,1)S(1)}, u32[]{:S(2)}) copy-start(s16[304,128]{1,0:T(8,128)(2,1)S(1)} %collective-permute-done.19.a) | copy-start | bytes 233476
  140.7 0.6 copy-start.15
  140.7 0.7 copy-start.16
  143.2 5.0 %collective-permute-start.22 = (s16[304,128]{1,0:T(8,128)(2,1)}, s16[304,128]{1,0:T(8,128)(2,1)S(1)}, u32[]{:S(2)}, u32[]{:S(2)}) collective-permute-start(s16[304,128]{1,0:T(8,128)(2,1)} %sum_code.1), channel_id=1, source_target_pairs={{0,4},{1,5},{2,6},{3,7},{4,0},{5,1},{6,2},{7,3},{8,12},{9,13},{10,... | collective-permute-start | bytes 233480 | tf_op jit(solution)/shard_map/ppermute | solution.py:21
  144.5 7.9 %collective-permute-start.23 = (s16[304,128]{1,0:T(8,128)(2,1)}, s16[304,128]{1,0:T(8,128)(2,1)S(1)}, u32[]{:S(2)}, u32[]{:S(2)}) collective-permute-start(s16[304,128]{1,0:T(8,128)(2,1)} %sum_code.1), channel_id=1, source_target_pairs={{0,8},{1,9},{2,10},{3,11},{4,12},{5,13},{6,14},{7,15},{8,0},{9,1},... | collective-permute-start | bytes 233480 | tf_op jit(solution)/shard_map/ppermute | solution.py:21
  145.9 7.3 %collective-permute-start.24 = (s16[304,128]{1,0:T(8,128)(2,1)}, s16[304,128]{1,0:T(8,128)(2,1)S(1)}, u32[]{:S(2)}, u32[]{:S(2)}) collective-permute-start(s16[304,128]{1,0:T(8,128)(2,1)} %sum_code.1), channel_id=1, source_target_pairs={{0,12},{1,13},{2,14},{3,15},{4,8},{5,9},{6,10},{7,11},{8,4},{9,5},... | collective-permute-start | bytes 233480 | tf_op jit(solution)/shard_map/ppermute | solution.py:21
  147.5 7.9 %collective-permute-start.25 = (s16[304,128]{1,0:T(8,128)(2,1)}, s16[304,128]{1,0:T(8,128)(2,1)S(1)}, u32[]{:S(2)}, u32[]{:S(2)}) collective-permute-start(s16[304,128]{1,0:T(8,128)(2,1)} %sum_code.1), channel_id=1, source_target_pairs={{0,2},{1,3},{2,0},{3,1},{4,6},{5,7},{6,4},{7,5},{8,10},{9,11},{10,... | collective-permute-start | bytes 233480 | tf_op jit(solution)/shard_map/ppermute | solution.py:21
  148.2 7.3 %collective-permute-start.26 = (s16[304,128]{1,0:T(8,128)(2,1)S(1)}, s16[304,128]{1,0:T(8,128)(2,1)S(1)}, u32[]{:S(2)}, u32[]{:S(2)}) collective-permute-start(s16[304,128]{1,0:T(8,128)(2,1)S(1)} %collective-permute-done.22), channel_id=1, source_target_pairs={{0,2},{1,3},{2,0},{3,1},{4,6},{5,7},{6,4},{7,5},{8,10},{9,11},{10,... | collective-permute-start | bytes 233480 | tf_op jit(solution)/shard_map/ppermute | solution.py:21
  152.4 4.4 %collective-permute-start.27 = (s16[304,128]{1,0:T(8,128)(2,1)S(1)}, s16[304,128]{1,0:T(8,128)(2,1)S(1)}, u32[]{:S(2)}, u32[]{:S(2)}) collective-permute-start(s16[304,128]{1,0:T(8,128)(2,1)S(1)} %collective-permute-done.23), channel_id=1, source_target_pairs={{0,2},{1,3},{2,0},{3,1},{4,6},{5,7},{6,4},{7,5},{8,10},{9,11},{10,... | collective-permute-start | bytes 233480 | tf_op jit(solution)/shard_map/ppermute | solution.py:21
  153.3 4.4 %collective-permute-start.28 = (s16[304,128]{1,0:T(8,128)(2,1)S(1)}, s16[304,128]{1,0:T(8,128)(2,1)S(1)}, u32[]{:S(2)}, u32[]{:S(2)}) collective-permute-start(s16[304,128]{1,0:T(8,128)(2,1)S(1)} %collective-permute-done.24), channel_id=1, source_target_pairs={{0,2},{1,3},{2,0},{3,1},{4,6},{5,7},{6,4},{7,5},{8,10},{9,11},{10,... | collective-permute-start | bytes 233480 | tf_op jit(solution)/shard_map/ppermute | solution.py:21
  155.4 4.0 %copy-start = (s16[4,304,128]{2,1,0:T(8,128)(2,1)}, s16[4,304,128]{2,1,0:T(8,128)(2,1)S(1)}, u32[]{:S(2)}) copy-start(s16[4,304,128]{2,1,0:T(8,128)(2,1)S(1)} %pad_add_fusion.a) | copy-start | bytes 933892
  155.4 2.4 %collective-permute-start.29 = (s16[4,304,128]{2,1,0:T(8,128)(2,1)S(1)}, s16[4,304,128]{2,1,0:T(8,128)(2,1)S(1)}, u32[]{:S(2)}, u32[]{:S(2)}) collective-permute-start(s16[4,304,128]{2,1,0:T(8,128)(2,1)S(1)} %pad_add_fusion.a), channel_id=1, source_target_pairs={{0,1},{1,0},{2,3},{3,2},{4,5},{5,4},{6,7},{7,6},{8,9},{9,8},{10,11... | collective-permute-start | bytes 933896 | tf_op jit(solution)/shard_map/ppermute | solution.py:21
  157.7 1.7 %copy-start.1 = (s16[4,304,128]{2,1,0:T(8,128)(2,1)}, s16[4,304,128]{2,1,0:T(8,128)(2,1)S(1)}, u32[]{:S(2)}) copy-start(s16[4,304,128]{2,1,0:T(8,128)(2,1)S(1)} %pad_add_fusion.1.b) | copy-start | bytes 933892
  157.7 1.7 %collective-permute-start.30 = (s16[4,304,128]{2,1,0:T(8,128)(2,1)S(1)}, s16[4,304,128]{2,1,0:T(8,128)(2,1)S(1)}, u32[]{:S(2)}, u32[]{:S(2)}) collective-permute-start(s16[4,304,128]{2,1,0:T(8,128)(2,1)S(1)} %pad_add_fusion.1.b), channel_id=1, source_target_pairs={{0,1},{1,0},{2,3},{3,2},{4,5},{5,4},{6,7},{7,6},{8,9},{9,8},{10,11... | collective-permute-start | bytes 933896 | tf_op jit(solution)/shard_map/ppermute | solution.py:21
  157.8 1.6 copy-start.11
  159.4 0.7 copy-start.12

commit v3 on v2

v3 whole, which is shorter than its diff:
```python
import functools

import jax
import jax.numpy as jnp
from jax import lax
from jax.experimental import pallas as pl
from jax.experimental.pallas import tpu as pltpu
from jax.sharding import PartitionSpec as P

LARGE_LIMIT = 28 * 1024 * 1024
SMALL_LIMIT = 16 * 1024 * 1024
LANES = 128
BLOCK = 256
PAD = 16
GROUP = 32
BITS = 14
NT = (((1,), (1,)), ((), ()))
TN = (((0,), (0,)), ((), ()))
F32, BF16, I16, I32 = jnp.float32, jnp.bfloat16, jnp.int16, jnp.int32


def move(x, pairs):
    return lax.ppermute(x, "dom", pairs)


def swapped(x, bits):
    return move(x, [(d, d ^ bits) for d in range(lax.axis_size("dom"))])


def forwarded(x):
    devices = range(lax.axis_size("dom"))
    route = [(d, d - 4 if d & 2 else d + 4) for d in devices]
    return move(x, [(a, b) for a, b in route if b in devices])


def to_sibling(x, kind):
    devices = range(lax.axis_size("dom"))
    return move(x, [(d, d ^ 1) for d in devices if ((d >> 1) ^ d) & 1 == kind])


def begin(copies, sem, at=0):
    started = [pltpu.make_async_copy(a, b, sem.at[at + i]) for i, (a, b) in enumerate(copies)]
    for copy in started:
        copy.start()
    return started


def finish(copies):
    for copy in copies:
        copy.wait()


def place_of(me):
    return (me >> 1) & 1, me & 1, (me >> 2) & 3


def offsets_of(me):
    parity, core, _ = place_of(me)
    return 0, 1 - 2 * core, 2 - 4 * parity, 4 * parity - 2, 2 * core - 1


OWN, SIB, Y, Z, X = range(5)
STEPS = (((OWN, 0), (OWN, 1)), ((SIB, 0), (SIB, 1)), ((Y, 0), (Z, 0)), ((X, 0), (Y, 1)), ((Z, 1), (X, 1)))


def prep_kernel(blocks, me_ref, pairs, sib_pairs, occ, energy, maps, levels, weights):
    me = me_ref[0]
    virt = maps.shape[1]
    table = energy[...]
    parts = []
    for _ in range(3):
        part = table.astype(BF16)
        parts.append(part)
        table = table - part.astype(F32)
    row_major = lax.broadcasted_iota(I32, (energy.shape[0], virt), 0)
    lane_major = lax.broadcasted_iota(I32, (LANES, virt), 0)
    for block, offset in enumerate(offsets_of(me)):
        other = me + offset
        who = jnp.clip(other, 0, blocks - 1)
        count = 0
        for s in range(pairs.shape[1]):
            count = count + (pairs[0, s] == other).astype(I32)
            if block in (OWN, SIB):
                count = count + ((pairs, sib_pairs)[block][0, s] == me).astype(I32)
        index = maps[pl.ds(who, 1), :]
        pick = (row_major == index // LANES).astype(F32).astype(BF16)
        rows = sum(lax.dot_general(p, pick, TN, preferred_element_type=F32) for p in parts)
        chosen = jnp.sum(jnp.where(lane_major == index % LANES, rows, 0.0), axis=0, keepdims=True)
        for step, halves in enumerate(STEPS):
            for side, (which, j) in enumerate(halves):
                if which == block:
                    at = pl.ds(side * virt, virt)
                    levels[step:step + 1, at] = chosen - occ[who, j]
                    weights[step:step + 1, at] = jnp.full((1, virt), -count.astype(F32), F32)


def add_pair(own_t, other, amp, total, own_level, level, weight, first):
    wide = own_t.shape[0]
    for t in range(0, wide, BLOCK):
        s = pl.ds(t, BLOCK)
        integrals = jnp.dot(own_t[s, :], other[...], preferred_element_type=F32)
        amp[s, :] = (integrals * weight / (own_level[t:t + BLOCK, 0:1] + level)).astype(BF16)
    for t in range(0, wide, BLOCK):
        s = pl.ds(t, BLOCK)
        part = lax.dot_general(other[...], amp[s, :], NT, preferred_element_type=F32)
        total[:, s] = part if first else total[:, s] + part


def split_kernel(me_ref, pairs, own, *rest):
    parts, sem = rest[:-1], rest[-1]
    per = len(parts) // 2
    rows, virt = parts[1].shape
    copies = begin(
        [(own.at[i // per, pl.ds(i % per * rows, rows)], part.at[pl.ds(0, rows)]) for i, part in enumerate(parts)], sem
    )
    lane = lax.broadcasted_iota(I32, (PAD, virt), 1)
    listed = jnp.full((PAD, virt), 100, I32)
    for s in range(pairs.shape[1]):
        listed = jnp.where(lane == s, pairs[0, s] - me_ref[0], listed)
    parts[0][rows:, :] = listed.astype(F32).astype(BF16)
    finish(copies)


def near_kernel(own, sib, levels, weights, own_t, total, sem, own_s, other, amp):
    virt = own.shape[2]
    copies = begin(
        [(x.at[j], s.at[:, pl.ds(j * virt, virt)]) for x, s in ((own, own_s), (sib, other)) for j in range(2)],
        sem,
    )
    level = levels[...].T
    finish(copies[:2])
    own_t[...] = own_s[...].T
    add_pair(own_t, own_s, amp, total, level, levels[0:1, :], weights[0:1, :], True)
    finish(copies[2:])
    add_pair(own_t, other, amp, total, level, levels[1:2, :], weights[1:2, :], False)


def fetch(plan, step, me, refs, other):
    parity, core, _ = place_of(me)
    along_y = (parity ^ core) == 1
    counts = []
    for side, (rows, (name, at)) in enumerate(plan):
        virt = other.shape[1] // 2
        columns = slice(side * virt, (side + 1) * virt)

        def copy(ref_name, first, n, to):
            other[to:to + n, columns] = refs[ref_name][first:first + n, :]

        for source, first, n, to in rows:
            if isinstance(source, str):
                copy(source, first, n, to)
            else:
                pl.when(along_y)(functools.partial(copy, source[0][0], source[0][1], n, to))
                pl.when(jnp.logical_not(along_y))(functools.partial(copy, source[1][0], source[1][1], n, to))
        if isinstance(name, str):
            listed = refs[name][at:at + PAD, :].astype(F32)
        else:
            listed = jnp.where(
                along_y, refs[name[0]][at:at + PAD, :].astype(F32), refs[name[1]][at:at + PAD, :].astype(F32)
            )
        wanted = -offsets_of(me)[STEPS[step][side][0]]
        hits = jnp.where(listed[0:1, :] == wanted.astype(F32), 1.0, 0.0)
        counts.append(jnp.broadcast_to(jnp.sum(hits, axis=1, keepdims=True), (1, virt)))
    return jnp.concatenate(counts, axis=1)


def far_kernel(plan, names, step, me_ref, own_t, total_in, levels, weights, *rest):
    refs = dict(zip(names, rest))
    total, other, amp = rest[len(names):]
    weight = weights[step:step + 1, :] - fetch(plan, step, me_ref[0], refs, other)
    add_pair(own_t, other, amp, total, levels[...].T, levels[step:step + 1, :], weight, False)


def last_kernel(plan, names, step, me_ref, own_t, total_in, levels, weights, own, *rest):
    refs = dict(zip(names, rest))
    total, residual, keep, send, sem, other, amp, own_s, high, low, packed = rest[len(names):]
    me = me_ref[0]
    core = me & 1
    virt = own.shape[2]
    a, b = pl.ds(0, virt), pl.ds(virt, virt)
    copies = begin([(own.at[0], own_s.at[:, a]), (own.at[1], own_s.at[:, b])], sem)
    weight = weights[step:step + 1, :] - fetch(plan, step, me, refs, other)
    add_pair(own_t, other, amp, total, levels[...].T, levels[step:step + 1, :], weight, False)
    outs = begin([(total.at[:, a], residual.at[0]), (total.at[:, b], residual.at[1])], sem, 2)
    finish(copies)
    high[...] = total[...].astype(BF16)
    low[...] = (total[...] - high[...].astype(F32)).astype(BF16)
    at = 0
    for q in range(0, total.shape[0], BLOCK):
        rows = q + BLOCK
        slab = own_s[q:q + BLOCK, :]
        block = lax.dot_general(high[:rows, :], slab, NT, preferred_element_type=F32)
        block += lax.dot_general(low[:rows, :], slab, NT, preferred_element_type=F32)
        for c in range(0, BLOCK, LANES):
            upper = q + c + LANES
            packed[at:at + upper, :] = block[:upper, c:c + LANES]
            at += upper
    size = keep.shape[0]
    keep[...] = packed[pl.ds(pl.multiple_of(core * size, 16), size), :]
    send[...] = packed[pl.ds(pl.multiple_of((1 - core) * size, 16), size), :]
    finish(outs)


def encode(x, out, row):
    rows = x.shape[0]
    groups = x.reshape(rows // GROUP, GROUP, LANES)
    largest = jnp.max(jnp.abs(groups), axis=1)
    power = jnp.floor(jnp.log2(jnp.maximum(largest, 1e-30))) + 1.0
    unit = jnp.exp2(BITS - power)
    for g in range(rows // GROUP):
        whole = jnp.round(groups[g] * unit[g:g + 1, :]).astype(I32)
        out[pl.ds(row + g * GROUP, GROUP), :] = whole.astype(I16)
    pad = jnp.zeros((PAD - rows // GROUP, LANES), F32)
    out[pl.ds(row + rows, PAD), :] = jnp.concatenate([power, pad]).astype(I32).astype(I16)


def decode(coded):
    rows = coded.shape[0] - PAD
    wide = coded.astype(I32).astype(F32)
    unit = jnp.exp2(wide[rows:] - BITS)
    return jnp.concatenate(
        [wide[g * GROUP:(g + 1) * GROUP] * unit[g:g + 1, :] for g in range(rows // GROUP)]
    )


def chip_kernel(me_ref, mine, theirs, keep, send):
    parity, _, _ = place_of(me_ref[0])
    size = keep.shape[0]
    piece = size // 4
    at = pl.ds(pl.multiple_of(parity * size, 16), size)
    keep[...] = mine[at, :] + theirs[at, :]
    for t in range(4):
        at = pl.ds(pl.multiple_of((1 - parity) * size + t * piece, 16), piece)
        encode(mine[at, :] + theirs[at, :], send, t * (piece + PAD))


def column_kernel(me_ref, mine, theirs, keep, *sends):
    _, _, z = place_of(me_ref[0])
    piece = keep.shape[0]
    for t in range(4):
        at = pl.ds(pl.multiple_of((z ^ t) * piece, 16), piece)
        coded = theirs[pl.ds(pl.multiple_of((z ^ t) * (piece + PAD), 16), piece + PAD), :]
        value = mine[at, :] + decode(coded)
        if t:
            encode(value, sends[t - 1], 0)
        else:
            keep[...] = value


def sum_kernel(mine, a, b, c, out):
    out[...] = mine[...] + decode(a[...]) + decode(b[...]) + decode(c[...])


def code_kernel(scale, x, out):
    encode(x[...] * scale, out, 0)


def sum_code_kernel(scale, mine, a, b, c, out):
    encode((mine[...] + decode(a[...]) + decode(b[...]) + decode(c[...])) * scale, out, 0)


def spread_kernel(me_ref, a, b, sib_a, sib_b, out, sem, packed, square):
    parity, core, z = place_of(me_ref[0])
    rows = a.shape[1] - PAD
    for src, half, side in ((a, core, parity), (b, core, 1 - parity), (sib_a, 1 - core, parity), (sib_b, 1 - core, 1 - parity)):
        for t in range(4):
            row = ((half * 2 + side) * 4 + (z ^ t)) * rows
            packed[pl.ds(pl.multiple_of(row, 16), rows), :] = decode(src[t])
    copies = []
    at = packed.shape[0]
    for c in range(out.shape[1] - LANES, -1, -LANES):
        at -= c + LANES
        square[0:c + LANES, c:c + LANES] = packed[at:at + c + LANES, :]
        for r in range(0, c, LANES):
            square[c:c + LANES, r:r + LANES] = packed[at + r:at + r + LANES, :].T
        done = pl.ds(c, LANES)
        copies += begin([(square.at[done], out.at[done])], sem, len(copies))
    finish(copies)


def shards(slabs, pair_blocks, occ_energy, virt_energy, domain_map):
    blocks = lax.axis_size("dom")
    me = lax.axis_index("dom").astype(I32)[None]
    own = slabs[0]
    orbitals, aux, virt = own.shape
    wide = orbitals * virt
    upper = aux * (aux + LANES) // 2 // LANES
    piece = upper // 16

    hbm = pl.BlockSpec(memory_space=pl.ANY)
    vmem = pl.BlockSpec(memory_space=pltpu.VMEM)
    smem = pl.BlockSpec(memory_space=pltpu.SMEM)
    slab_s = pltpu.VMEM((aux, wide), BF16)
    amp_s = pltpu.VMEM((wide, wide), BF16)
    total_t = jax.ShapeDtypeStruct((aux, wide), F32)

    def kernel(body, name, ins, outs, out_specs, scratch=(), limit=SMALL_LIMIT, aliases={}, flops=1):
        return pl.pallas_call(
            body,
            out_shape=outs,
            in_specs=ins,
            out_specs=out_specs,
            scratch_shapes=scratch,
            compiler_params=pltpu.CompilerParams(vmem_limit_bytes=limit),
            cost_estimate=pl.CostEstimate(flops=flops, bytes_accessed=1, transcendentals=0),
            input_output_aliases=aliases,
            name=name,
        )

    def dma(n):
        return pltpu.SemaphoreType.DMA((n,))

    def coded(n):
        return jax.ShapeDtypeStruct((n, LANES), I16)

    def plain(n):
        return jax.ShapeDtypeStruct((n, LANES), F32)

    half = aux // 2
    sib, sib_pairs = swapped(own, 1), swapped(pair_blocks, 1)
    parts = kernel(
        split_kernel, "split", [smem, smem, hbm],
        [jax.ShapeDtypeStruct((half + (0 if i else PAD), virt), BF16) for i in range(4)], [vmem] * 4, [dma(4)],
    )(me, pair_blocks, own)
    y = [swapped(parts[0], 2)]
    sib, part = lax.optimization_barrier((sib, parts[1]))
    y.append(swapped(part, 2))

    small = jax.ShapeDtypeStruct((8, wide), F32)
    levels, weights = kernel(
        functools.partial(prep_kernel, blocks), "prep", [smem] * 4 + [vmem] * 2, (small, small), (vmem, vmem),
    )(me, pair_blocks, sib_pairs, occ_energy, virt_energy.reshape(-1, LANES), domain_map)
    own_t, total = kernel(
        near_kernel, "near", [hbm, hbm, vmem, vmem], (jax.ShapeDtypeStruct((wide, aux), BF16), total_t), (vmem, vmem),
        [dma(4), slab_s, slab_s, amp_s], LARGE_LIMIT, flops=int(5e10),
    )(own, sib, levels, weights)
    y[0], total, own_t, part = lax.optimization_barrier((y[0], total, own_t, parts[2]))
    y.append(swapped(part, 2))
    y[1], part = lax.optimization_barrier((y[1], parts[3]))
    y.append(swapped(part, 2))

    z = [forwarded(part) for part in y]
    z[0], z[1], y[2], y[3] = lax.optimization_barrier((z[0], z[1], y[2], y[3]))
    arrays = {f"y{i}": part for i, part in enumerate(y)}
    arrays |= {f"z{i}": part for i, part in enumerate(z)}
    arrays["sy0"] = to_sibling(jnp.concatenate(y[:2]), 0)
    arrays["sz0"] = to_sibling(jnp.concatenate(z[:2]), 1)
    arrays["sy2"] = to_sibling(jnp.concatenate(y[2:]), 0)

    def own_core(name, j):
        return [(f"{name}{2 * j + h}", 0, half, h * half) for h in range(2)], (f"{name}0", half)

    def other_core(j):
        if j:
            rows = [((("sy2", h * half), (f"sz{2 + h}", 0)), 0, half, h * half) for h in range(2)]
        else:
            rows = [((("sy0", at), ("sz0", at)), 0, half, to) for at, to in ((0, 0), (half + PAD, half))]
        return rows, (("sy0", "sz0"), half)

    def names_in(plan):
        names = []
        for rows, (name, _) in plan:
            for source in [r[0] for r in rows]:
                names += [source] if isinstance(source, str) else [n for n, _ in source]
            names += [name] if isinstance(name, str) else name
        return list(dict.fromkeys(names))

    def pair_step(body, name, step, given=(), outs=(), out_specs=(), scratch=()):
        plan = [other_core(j) if which == X else own_core("y" if which == Y else "z", j) for which, j in STEPS[step]]
        names = names_in(plan)
        return kernel(
            functools.partial(body, plan, names, step), name,
            [smem] + [vmem] * 4 + [hbm] * len(given) + [vmem] * len(names),
            (total_t, *outs), (vmem, *out_specs), scratch, LARGE_LIMIT, {2: 0}, int(1e10),
        )(me, own_t, total, levels, weights, *given, *[arrays[n] for n in names])

    (total,) = pair_step(far_kernel, "far2", 2, scratch=[slab_s, amp_s])
    (total,) = pair_step(far_kernel, "far3", 3, scratch=[slab_s, amp_s])
    z[2], z[3], total = lax.optimization_barrier((z[2], z[3], total))
    arrays["z2"], arrays["z3"] = z[2], z[3]
    arrays["sz2"], arrays["sz3"] = to_sibling(z[2], 1), to_sibling(z[3], 1)
    _, residual, keep, send = pair_step(
        last_kernel, "last", 4, (own,),
        (jax.ShapeDtypeStruct(own.shape, F32), plain(upper // 2), plain(upper // 2)), (hbm, vmem, vmem),
        [dma(4), slab_s, amp_s, slab_s, slab_s, slab_s, pltpu.VMEM((upper, LANES), F32)],
    )

    got = swapped(send, 1)
    keep, send = kernel(
        chip_kernel, "chip", [smem, vmem, vmem], (plain(upper // 4), coded(4 * (piece + PAD))), (vmem, vmem),
    )(me, keep, got)
    got = swapped(send, 2)
    keep, *sends = kernel(
        column_kernel, "column", [smem, vmem, vmem], (plain(piece),) + (coded(piece + PAD),) * 3, (vmem,) * 4,
    )(me, keep, got)
    got = [swapped(send, 4 * t) for t, send in zip((1, 2, 3), sends)]
    if blocks == 16:
        mine = kernel(
            functools.partial(sum_code_kernel, 1.0 / blocks), "sum_code", [vmem] * 4, coded(piece + PAD), vmem,
        )(keep, *got)
    else:
        value = kernel(sum_kernel, "sum", [vmem] * 4, plain(piece), vmem)(keep, *got)
        bit = 16
        while bit < blocks:
            value = value + swapped(value, bit)
            bit *= 2
        mine = kernel(functools.partial(code_kernel, 1.0 / blocks), "code", [vmem], coded(piece + PAD), vmem)(value)

    column = [mine] + [swapped(mine, 4 * t) for t in (1, 2, 3)]
    across = [swapped(c, 2) for c in column]
    a, b = jnp.stack(column), jnp.stack(across)
    gradient = kernel(
        spread_kernel, "spread", [smem] + [vmem] * 4, jax.ShapeDtypeStruct((aux, aux), F32), hbm,
        [dma(aux // LANES), pltpu.VMEM((upper, LANES), F32), pltpu.VMEM((aux, aux), F32)],
    )(me, a, b, swapped(a, 1), swapped(b, 1))
    return residual[None], gradient


def solution(mesh):
    return jax.shard_map(
        shards,
        mesh=mesh,
        in_specs=(
            P(("grp", "dom"), None, None, None),
            P(("grp", "dom"), None),
            P("grp", None),
            P("grp"),
            P("grp", None),
        ),
        out_specs=(P(("grp", "dom"), None, None, None), P("grp", None)),
        check_vma=False,
    )
```

time: 165 us -> 115 us (0.70)
  Pallas kernels: 45.1 us -> 24.4 us
  starting transfers between devices: 56.9 us -> 43.7 us
  waiting for transfers between devices: 52.4 us -> 39.4 us
  local copies, waits for them, and re-layouts: 7.67 us -> 5.71 us
    ppermute x31 -> x29, starting transfers between devices: 56.9 us -> 43.7 us  [move(): return lax.ppermute(x, 'dom', pairs)]
    ppermute x31 -> x29, waiting for transfers between devices: 52.4 us -> 39.4 us  [move(): return lax.ppermute(x, 'dom', pairs)]
    pallas_call x3 -> x5, Pallas kernels: 24.2 us -> 15.5 us  [the longest x3 12.9 us: pair_step(): kernel(functools.partial(body, plan, names, step), name, [smem] + [vmem]...]
    pallas_call x1, Pallas kernels: 10 us -> 5.73 us  [shards(): kernel(near_kernel, 'near', [hbm, hbm, vmem, vmem], (jax.ShapeDtypeStruct...]
    pallas_call x1, Pallas kernels: 2.77 us -> 0.25 us  [shards(): kernel(chip_kernel, 'chip', [smem, vmem, vmem], (plain(upper // 4), coded...]
    pallas_call x1, Pallas kernels: 1.99 us -> 0.22 us  [shards(): kernel(column_kernel, 'column', [smem, vmem, vmem], (plain(piece),) + (co...]
    pallas_call x1, Pallas kernels: 4.28 us -> 2.56 us  [shards(): kernel(spread_kernel, 'spread', [smem] + [vmem] * 4, jax.ShapeDtypeStruct...]
    pallas_call x1, Pallas kernels: 1.78 us -> 0.12 us  [shards(): kernel(functools.partial(sum_code_kernel, 1.0 / blocks), 'sum_code', [vme...]
  transfers between devices with their start and end apart: 31 -> 29, of which waited for: 13 -> 17; matrix products, arithmetic and copies ran while one was open for 2% -> 1% of each run, Pallas kernels for 13% -> 12%
where the time goes in v3:
time: 115 us; the launch traced here: 114 us
  starting transfers between devices  43.7 us (38%)
  waiting for transfers between devices  39.4 us (34%)
  Pallas kernels  24.4 us (21%)
  local copies, waits for them, and re-layouts  5.71 us (5%)
    ppermute x29, starting transfers between devices, move(): return lax.ppermute(x, 'dom', pairs)  43.7 us
    ppermute x29, waiting for transfers between devices, move(): return lax.ppermute(x, 'dom', pairs)  39.4 us
    pallas_call x3, Pallas kernels, pair_step(): kernel(functools.partial(body, plan, names, step), name, [smem] + [vmem]...  12.9 us
    pallas_call x1, Pallas kernels, shards(): kernel(near_kernel, 'near', [hbm, hbm, vmem, vmem], (jax.ShapeDtypeStruct...  5.73 us
    unnamed x15, local copies, waits for them, and re-layouts  5.71 us
    pallas_call x1, Pallas kernels, shards(): kernel(spread_kernel, 'spread', [smem] + [vmem] * 4, jax.ShapeDtypeStruct...  2.56 us
  transfers between devices with their start and end apart: 29, of which 17 were waited for; matrix products, arithmetic and copies ran while one was open for 1% of the time, Pallas kernels for 12%

profile of v3, /device:TPU:0, one launch (start us, length us, event | category | flops | bytes accessed | tf_op | source)
XLA Modules:
  0.0 114.5 jit_solution(17963347017540847714)
XLA Ops:
  0.6 0.5 collective-permute-start.1
  1.1 0.1 collective-permute-start.2
  1.2 1.4 %copy-done = bf16[1,2,1024,384]{3,2,1,0:T(8,128)(2,1)S(1)} copy-done((bf16[1,2,1024,384]{3,2,1,0:T(8,128)(2,1)S(1)}, bf16[1,2,1024,384]{3,2,1,0:T(8,128)(2,1)}, u32[]{:S(2)}) %copy-start) | copy-done | bytes 1572888
  2.6 0.7 copy-done.4
  3.3 1.3 %split.1 = (bf16[528,384]{1,0:T(8,128)(2,1)S(1)}, bf16[512,384]{1,0:T(8,128)(2,1)S(1)}, bf16[512,384]{1,0:T(8,128)(2,1)S(1)}, bf16[512,384]{1,0:T(8,128)(2,1)S(1)}) custom-call(s32[1]{0:T(128)} %bitcast.me_ref, s32[1,3]{1,0:T(1,128)S(1)} %copy-done.4, bf16[2,1024,384]{2,1,0:T(8,128)(2,1)S(1)} %bitcast.13), custom_call_target="tpu_custom_call" | custom-call | flops 1 | bytes 1 | tf_op jit(solution)/shard_map/split/pallas_call | solution.py:321
  4.7 0.7 copy-done.6
  5.4 2.9 %collective-permute-start = (bf16[528,384]{1,0:T(8,128)(2,1)S(1)}, bf16[528,384]{1,0:T(8,128)(2,1)S(1)}, u32[]{:S(2)}, u32[]{:S(2)}) collective-permute-start(bf16[528,384]{1,0:T(8,128)(2,1)S(1)} %get-tuple-element.34), channel_id=1, source_target_pairs={{0,2},{1,3},{2,0},{3,1},{4,6},{5,7},{6,4},{7,5},{8,10},{9,11},{10,... | collective-permute-start | bytes 1216520 | tf_op jit(solution)/shard_map/ppermute | solution.py:23
  8.3 0.8 copy.10.occ
  9.1 0.8 copy-done.2
  9.9 0.7 copy-done.3
  10.6 0.7 copy-done.5
  11.2 1.3 %prep.1 = (f32[8,768]{1,0:T(8,128)S(1)}, f32[8,768]{1,0:T(8,128)S(1)}) custom-call(s32[1]{0:T(128)} %bitcast.me_ref, s32[1,3]{1,0:T(1,128)S(1)} %copy-done.5, s32[1,3]{1,0:T(1,128)S(1)} %collective-permute-done.2.sib_pairs, f32[16,2]{1,0:T(8,128)S(1)} %copy.10.occ, f32[64,128]{1,0:T(8,128)S(1)} %bitcast.17, s32[16,384]{1,0:T(8,128)S(1)} %copy-done.3), custom_call_target="tpu_custom_call" | custom-call | flops 1 | bytes 1 | tf_op jit(solution)/shard_map/prep/pallas_call | solution.py:330
  12.5 0.1 collective-permute-start.5
  12.6 5.7 %near.1 = (bf16[768,1024]{1,0:T(8,128)(2,1)S(1)}, f32[1024,768]{1,0:T(8,128)S(1)}) custom-call(bf16[2,1024,384]{2,1,0:T(8,128)(2,1)S(1)} %bitcast.14, bf16[2,1024,384]{2,1,0:T(8,128)(2,1)} %collective-permute-done.1.sib, f32[8,768]{1,0:T(8,128)S(1)} %get-tuple-element.37.levels, f32[8,768]{1,0:T(8,128)S(1)} %get-tuple-element.38.weights), custom_call_target="tpu_custom_call" | custom-call | flops 49999998976 | bytes 1 | tf_op jit(solution)/shard_map/near/pallas_call | solution.py:333
  18.4 0.1 collective-permute-done.rest_0_.rest_4_
  18.5 4.0 %collective-permute-start.8 = (bf16[528,384]{1,0:T(8,128)(2,1)S(1)}, bf16[528,384]{1,0:T(8,128)(2,1)S(1)}, u32[]{:S(2)}, u32[]{:S(2)}) collective-permute-start(bf16[528,384]{1,0:T(8,128)(2,1)S(1)} %collective-permute-done.rest_0_.rest_4_), channel_id=1, source_target_pairs={{0,4},{1,5},{4,8},{5,9},{6,2},{7,3},{8,12},{9,13},{10,6},{11,7},{1... | collective-permute-start | bytes 1216520 | tf_op jit(solution)/shard_map/ppermute | solution.py:23
  22.6 0.1 collective-permute-start.3
  22.6 4.3 %collective-permute-done.5.rest_1_ = bf16[512,384]{1,0:T(8,128)(2,1)S(1)} collective-permute-done((bf16[512,384]{1,0:T(8,128)(2,1)}, bf16[512,384]{1,0:T(8,128)(2,1)S(1)}, u32[]{:S(2)}, u32[]{:S(2)}) %collective-permute-start.5) | collective-permute-done | bytes 393248 | tf_op jit(solution)/shard_map/ppermute | solution.py:23
  26.9 2.1 %collective-permute-start.6 = (bf16[512,384]{1,0:T(8,128)(2,1)S(1)}, bf16[512,384]{1,0:T(8,128)(2,1)S(1)}, u32[]{:S(2)}, u32[]{:S(2)}) collective-permute-start(bf16[512,384]{1,0:T(8,128)(2,1)S(1)} %get-tuple-element.46), channel_id=1, source_target_pairs={{0,2},{1,3},{2,0},{3,1},{4,6},{5,7},{6,4},{7,5},{8,10},{9,11},{10,... | collective-permute-start | bytes 1179656 | tf_op jit(solution)/shard_map/ppermute | solution.py:23
  29.0 3.5 %collective-permute-start.9 = (bf16[512,384]{1,0:T(8,128)(2,1)S(1)}, bf16[512,384]{1,0:T(8,128)(2,1)S(1)}, u32[]{:S(2)}, u32[]{:S(2)}) collective-permute-start(bf16[512,384]{1,0:T(8,128)(2,1)S(1)} %collective-permute-done.5.rest_1_), channel_id=1, source_target_pairs={{0,4},{1,5},{4,8},{5,9},{6,2},{7,3},{8,12},{9,13},{10,6},{11,7},{1... | collective-permute-start | bytes 1179656 | tf_op jit(solution)/shard_map/ppermute | solution.py:23
  32.5 0.1 pad_maximum_fusion
  32.6 1.3 %collective-permute-start.10 = (bf16[1040,384]{1,0:T(8,128)(2,1)S(1)}, bf16[1040,384]{1,0:T(8,128)(2,1)S(1)}, u32[]{:S(2)}, u32[]{:S(2)}) collective-permute-start(bf16[1040,384]{1,0:T(8,128)(2,1)S(1)} %pad_maximum_fusion), channel_id=1, source_target_pairs={{0,1},{3,2},{4,5},{7,6},{8,9},{11,10},{12,13},{15,14},{16,17},{19,... | collective-permute-start | bytes 2396168 | tf_op jit(solution)/shard_map/ppermute | solution.py:23
  33.9 1.4 %collective-permute-done.3.rest_2_ = bf16[512,384]{1,0:T(8,128)(2,1)S(1)} collective-permute-done((bf16[512,384]{1,0:T(8,128)(2,1)S(1)}, bf16[512,384]{1,0:T(8,128)(2,1)S(1)}, u32[]{:S(2)}, u32[]{:S(2)}) %collective-permute-start.3) | collective-permute-done | bytes 393248 | tf_op jit(solution)/shard_map/ppermute | solution.py:23
  35.4 4.0 %collective-permute-start.4 = (bf16[512,384]{1,0:T(8,128)(2,1)S(1)}, bf16[512,384]{1,0:T(8,128)(2,1)S(1)}, u32[]{:S(2)}, u32[]{:S(2)}) collective-permute-start(bf16[512,384]{1,0:T(8,128)(2,1)S(1)} %collective-permute-done.3.rest_2_), channel_id=1, source_target_pairs={{0,4},{1,5},{4,8},{5,9},{6,2},{7,3},{8,12},{9,13},{10,6},{11,7},{1... | collective-permute-start | bytes 1179656 | tf_op jit(solution)/shard_map/ppermute | solution.py:23
  39.4 3.8 %collective-permute-done.6.rest_3_ = bf16[512,384]{1,0:T(8,128)(2,1)S(1)} collective-permute-done((bf16[512,384]{1,0:T(8,128)(2,1)S(1)}, bf16[512,384]{1,0:T(8,128)(2,1)S(1)}, u32[]{:S(2)}, u32[]{:S(2)}) %collective-permute-start.6) | collective-permute-done | bytes 393248 | tf_op jit(solution)/shard_map/ppermute | solution.py:23
  43.2 0.1 pad_maximum_fusion.2
  43.3 1.5 %collective-permute-start.12 = (bf16[1024,384]{1,0:T(8,128)(2,1)S(1)}, bf16[1024,384]{1,0:T(8,128)(2,1)S(1)}, u32[]{:S(2)}, u32[]{:S(2)}) collective-permute-start(bf16[1024,384]{1,0:T(8,128)(2,1)S(1)} %pad_maximum_fusion.2), channel_id=1, source_target_pairs={{0,1},{3,2},{4,5},{7,6},{8,9},{11,10},{12,13},{15,14},{16,17},{19,... | collective-permute-start | bytes 2359304 | tf_op jit(solution)/shard_map/ppermute | solution.py:23
  44.8 0.1 pad_maximum_fusion.1
  44.9 1.3 %collective-permute-start.11 = (bf16[1040,384]{1,0:T(8,128)(2,1)S(1)}, bf16[1040,384]{1,0:T(8,128)(2,1)S(1)}, u32[]{:S(2)}, u32[]{:S(2)}) collective-permute-start(bf16[1040,384]{1,0:T(8,128)(2,1)S(1)} %pad_maximum_fusion.1), channel_id=1, source_target_pairs={{1,0},{2,3},{5,4},{6,7},{9,8},{10,11},{13,12},{14,15},{17,16},{18,... | collective-permute-start | bytes 2396168 | tf_op jit(solution)/shard_map/ppermute | solution.py:23
  46.2 3.6 %collective-permute-start.7 = (bf16[512,384]{1,0:T(8,128)(2,1)S(1)}, bf16[512,384]{1,0:T(8,128)(2,1)S(1)}, u32[]{:S(2)}, u32[]{:S(2)}) collective-permute-start(bf16[512,384]{1,0:T(8,128)(2,1)S(1)} %collective-permute-done.6.rest_3_), channel_id=1, source_target_pairs={{0,4},{1,5},{4,8},{5,9},{6,2},{7,3},{8,12},{9,13},{10,6},{11,7},{1... | collective-permute-start | bytes 1179656 | tf_op jit(solution)/shard_map/ppermute | solution.py:23
  49.8 2.7 %far2.1.total_in = f32[1024,768]{1,0:T(8,128)S(1)} custom-call(s32[1]{0:T(128)} %bitcast.me_ref, bf16[768,1024]{1,0:T(8,128)(2,1)S(1)} %get-tuple-element.42.own_t, f32[1024,768]{1,0:T(8,128)S(1)} %get-tuple-element.47.total_in, f32[8,768]{1,0:T(8,128)S(1)} %get-tuple-element.37.levels, ...), custom_call_target="tpu_custom_call", output_to_operand_aliasing={{}: (2, {})} | custom-call | flops 10000000000 | bytes 1 | tf_op jit(solution)/shard_map/far2/pallas_call | solution.py:371
  52.5 2.8 %far3.1.total_in = f32[1024,768]{1,0:T(8,128)S(1)} custom-call(s32[1]{0:T(128)} %bitcast.me_ref, bf16[768,1024]{1,0:T(8,128)(2,1)S(1)} %get-tuple-element.42.own_t, f32[1024,768]{1,0:T(8,128)S(1)} %far2.1.total_in, f32[8,768]{1,0:T(8,128)S(1)} %get-tuple-element.37.levels, f32[8,768]{1,0:T(8,128)S(1)} %get-tuple-element.38.weights, ...), custom_call_target="tpu_custom_call", output_to_operand_aliasing={{}: (2, {})} | custom-call | flops 10000000000 | bytes 1 | tf_op jit(solution)/shard_map/far3/pallas_call | solution.py:371
  55.4 3.7 %collective-permute-done.7.rest_1_ = bf16[512,384]{1,0:T(8,128)(2,1)S(1)} collective-permute-done((bf16[512,384]{1,0:T(8,128)(2,1)S(1)}, bf16[512,384]{1,0:T(8,128)(2,1)S(1)}, u32[]{:S(2)}, u32[]{:S(2)}) %collective-permute-start.7) | collective-permute-done | bytes 393248 | tf_op jit(solution)/shard_map/ppermute | solution.py:23
  59.1 1.3 %collective-permute-start.13 = (bf16[512,384]{1,0:T(8,128)(2,1)S(1)}, bf16[512,384]{1,0:T(8,128)(2,1)S(1)}, u32[]{:S(2)}, u32[]{:S(2)}) collective-permute-start(bf16[512,384]{1,0:T(8,128)(2,1)S(1)} %collective-permute-done.4.rest_0_), channel_id=1, source_target_pairs={{1,0},{2,3},{5,4},{6,7},{9,8},{10,11},{13,12},{14,15},{17,16},{18,... | collective-permute-start | bytes 1179656 | tf_op jit(solution)/shard_map/ppermute | solution.py:23
  60.3 1.5 %collective-permute-start.14 = (bf16[512,384]{1,0:T(8,128)(2,1)S(1)}, bf16[512,384]{1,0:T(8,128)(2,1)S(1)}, u32[]{:S(2)}, u32[]{:S(2)}) collective-permute-start(bf16[512,384]{1,0:T(8,128)(2,1)S(1)} %collective-permute-done.7.rest_1_), channel_id=1, source_target_pairs={{1,0},{2,3},{5,4},{6,7},{9,8},{10,11},{13,12},{14,15},{17,16},{18,... | collective-permute-start | bytes 1179656 | tf_op jit(solution)/shard_map/ppermute | solution.py:23
  61.8 0.8 collective-permute-done.13.rest_4_
  62.7 1.3 %collective-permute-done.14.rest_5_ = bf16[512,384]{1,0:T(8,128)(2,1)S(1)} collective-permute-done((bf16[512,384]{1,0:T(8,128)(2,1)S(1)}, bf16[512,384]{1,0:T(8,128)(2,1)S(1)}, u32[]{:S(2)}, u32[]{:S(2)}) %collective-permute-start.14) | collective-permute-done | bytes 393248 | tf_op jit(solution)/shard_map/ppermute | solution.py:23
  64.0 7.3 %last.1 = (f32[1024,768]{1,0:T(8,128)S(1)}, f32[2,1024,384]{2,1,0:T(8,128)}, f32[2304,128]{1,0:T(8,128)S(1)}, f32[2304,128]{1,0:T(8,128)S(1)}) custom-call(s32[1]{0:T(128)} %bitcast.me_ref, bf16[768,1024]{1,0:T(8,128)(2,1)S(1)} %get-tuple-element.42.own_t, f32[1024,768]{1,0:T(8,128)S(1)} %far3.1.total_in, ...), custom_call_target="tpu_custom_call", output_to_operand_aliasing={{0}: (2, {})} | custom-call | flops 10000000000 | bytes 1 | tf_op jit(solution)/shard_map/last/pallas_call | solution.py:371
  71.3 0.2 collective-permute-start.15
  71.5 2.7 %collective-permute-done.15.theirs = f32[2304,128]{1,0:T(8,128)S(1)} collective-permute-done((f32[2304,128]{1,0:T(8,128)S(1)}, f32[2304,128]{1,0:T(8,128)S(1)}, u32[]{:S(2)}, u32[]{:S(2)}) %collective-permute-start.15) | collective-permute-done | bytes 1179680 | tf_op jit(solution)/shard_map/ppermute | solution.py:23
  74.2 0.3 chip.1
  74.5 1.9 %collective-permute-start.16 = (s16[1216,128]{1,0:T(8,128)(2,1)S(1)}, s16[1216,128]{1,0:T(8,128)(2,1)S(1)}, u32[]{:S(2)}, u32[]{:S(2)}) collective-permute-start(s16[1216,128]{1,0:T(8,128)(2,1)S(1)} %get-tuple-element.61), channel_id=1, source_target_pairs={{0,2},{1,3},{2,0},{3,1},{4,6},{5,7},{6,4},{7,5},{8,10},{9,11},{10,... | collective-permute-start | bytes 933896 | tf_op jit(solution)/shard_map/ppermute | solution.py:23
  76.4 7.9 %collective-permute-done.16.theirs = s16[1216,128]{1,0:T(8,128)(2,1)S(1)} collective-permute-done((s16[1216,128]{1,0:T(8,128)(2,1)S(1)}, s16[1216,128]{1,0:T(8,128)(2,1)S(1)}, u32[]{:S(2)}, u32[]{:S(2)}) %collective-permute-start.16) | collective-permute-done | bytes 311328 | tf_op jit(solution)/shard_map/ppermute | solution.py:23
  84.3 0.2 column.1
  84.5 2.2 %collective-permute-start.17 = (s16[304,128]{1,0:T(8,128)(2,1)S(1)}, s16[304,128]{1,0:T(8,128)(2,1)S(1)}, u32[]{:S(2)}, u32[]{:S(2)}) collective-permute-start(s16[304,128]{1,0:T(8,128)(2,1)S(1)} %get-tuple-element.63), channel_id=1, source_target_pairs={{0,4},{1,5},{2,6},{3,7},{4,0},{5,1},{6,2},{7,3},{8,12},{9,13},{10,... | collective-permute-start | bytes 233480 | tf_op jit(solution)/shard_map/ppermute | solution.py:23
  86.7 2.6 %collective-permute-start.18 = (s16[304,128]{1,0:T(8,128)(2,1)S(1)}, s16[304,128]{1,0:T(8,128)(2,1)S(1)}, u32[]{:S(2)}, u32[]{:S(2)}) collective-permute-start(s16[304,128]{1,0:T(8,128)(2,1)S(1)} %get-tuple-element.64), channel_id=1, source_target_pairs={{0,8},{1,9},{2,10},{3,11},{4,12},{5,13},{6,14},{7,15},{8,0},{9,1},... | collective-permute-start | bytes 233480 | tf_op jit(solution)/shard_map/ppermute | solution.py:23
  89.3 4.9 %collective-permute-done.18.b = s16[304,128]{1,0:T(8,128)(2,1)S(1)} collective-permute-done((s16[304,128]{1,0:T(8,128)(2,1)S(1)}, s16[304,128]{1,0:T(8,128)(2,1)S(1)}, u32[]{:S(2)}, u32[]{:S(2)}) %collective-permute-start.18) | collective-permute-done | bytes 77856 | tf_op jit(solution)/shard_map/ppermute | solution.py:23
  94.2 1.4 %collective-permute-done.19.c = s16[304,128]{1,0:T(8,128)(2,1)S(1)} collective-permute-done((s16[304,128]{1,0:T(8,128)(2,1)S(1)}, s16[304,128]{1,0:T(8,128)(2,1)S(1)}, u32[]{:S(2)}, u32[]{:S(2)}) %collective-permute-start.19) | collective-permute-done | bytes 77856 | tf_op jit(solution)/shard_map/ppermute | solution.py:23
  95.6 0.1 sum_code.1
  95.7 2.0 %collective-permute-start.22 = (s16[304,128]{1,0:T(8,128)(2,1)S(1)}, s16[304,128]{1,0:T(8,128)(2,1)S(1)}, u32[]{:S(2)}, u32[]{:S(2)}) collective-permute-start(s16[304,128]{1,0:T(8,128)(2,1)S(1)} %sum_code.1), channel_id=1, source_target_pairs={{0,12},{1,13},{2,14},{3,15},{4,8},{5,9},{6,10},{7,11},{8,4},{9,5},... | collective-permute-start | bytes 233480 | tf_op jit(solution)/shard_map/ppermute | solution.py:23
  97.8 0.4 collective-permute-start.21
  98.1 2.1 %collective-permute-start.20 = (s16[304,128]{1,0:T(8,128)(2,1)S(1)}, s16[304,128]{1,0:T(8,128)(2,1)S(1)}, u32[]{:S(2)}, u32[]{:S(2)}) collective-permute-start(s16[304,128]{1,0:T(8,128)(2,1)S(1)} %sum_code.1), channel_id=1, source_target_pairs={{0,4},{1,5},{2,6},{3,7},{4,0},{5,1},{6,2},{7,3},{8,12},{9,13},{10,... | collective-permute-start | bytes 233480 | tf_op jit(solution)/shard_map/ppermute | solution.py:23
  100.2 0.9 collective-permute-start.23
  101.1 1.0 collective-permute-done.22
  102.1 1.5 %collective-permute-start.26 = (s16[304,128]{1,0:T(8,128)(2,1)S(1)}, s16[304,128]{1,0:T(8,128)(2,1)S(1)}, u32[]{:S(2)}, u32[]{:S(2)}) collective-permute-start(s16[304,128]{1,0:T(8,128)(2,1)S(1)} %collective-permute-done.22), channel_id=1, source_target_pairs={{0,2},{1,3},{2,0},{3,1},{4,6},{5,7},{6,4},{7,5},{8,10},{9,11},{10,... | collective-permute-start | bytes 233480 | tf_op jit(solution)/shard_map/ppermute | solution.py:23
  103.6 0.2 collective-permute-done.21
  103.8 1.9 %collective-permute-start.25 = (s16[304,128]{1,0:T(8,128)(2,1)S(1)}, s16[304,128]{1,0:T(8,128)(2,1)S(1)}, u32[]{:S(2)}, u32[]{:S(2)}) collective-permute-start(s16[304,128]{1,0:T(8,128)(2,1)S(1)} %collective-permute-done.21), channel_id=1, source_target_pairs={{0,2},{1,3},{2,0},{3,1},{4,6},{5,7},{6,4},{7,5},{8,10},{9,11},{10,... | collective-permute-start | bytes 233480 | tf_op jit(solution)/shard_map/ppermute | solution.py:23
  105.7 0.2 collective-permute-start.24
  106.0 1.2 %collective-permute-done.26 = s16[304,128]{1,0:T(8,128)(2,1)S(1)} collective-permute-done((s16[304,128]{1,0:T(8,128)(2,1)S(1)}, s16[304,128]{1,0:T(8,128)(2,1)S(1)}, u32[]{:S(2)}, u32[]{:S(2)}) %collective-permute-start.26) | collective-permute-done | bytes 77856 | tf_op jit(solution)/shard_map/ppermute | solution.py:23
  107.2 1.0 collective-permute-done.25
  108.2 1.9 %collective-permute-done.24 = s16[304,128]{1,0:T(8,128)(2,1)S(1)} collective-permute-done((s16[304,128]{1,0:T(8,128)(2,1)S(1)}, s16[304,128]{1,0:T(8,128)(2,1)S(1)}, u32[]{:S(2)}, u32[]{:S(2)}) %collective-permute-start.24) | collective-permute-done | bytes 77856 | tf_op jit(solution)/shard_map/ppermute | solution.py:23
  110.1 0.1 collective-permute-start.28
  110.2 1.6 %collective-permute-done.28.sib_b = s16[4,304,128]{2,1,0:T(8,128)(2,1)S(1)} collective-permute-done((s16[4,304,128]{2,1,0:T(8,128)(2,1)S(1)}, s16[4,304,128]{2,1,0:T(8,128)(2,1)S(1)}, u32[]{:S(2)}, u32[]{:S(2)}) %collective-permute-start.28) | collective-permute-done | bytes 311328 | tf_op jit(solution)/shard_map/ppermute | solution.py:23
  111.8 2.6 %spread.1 = f32[1024,1024]{1,0:T(8,128)} custom-call(s32[1]{0:T(128)} %bitcast.me_ref, s16[4,304,128]{2,1,0:T(8,128)(2,1)S(1)} %pad_add_fusion.a, s16[4,304,128]{2,1,0:T(8,128)(2,1)S(1)} %pad_add_fusion.1.b, s16[4,304,128]{2,1,0:T(8,128)(2,1)S(1)} %collective-permute-done.27.sib_a, s16[4,304,128]{2,1,0:T(8,128)(2,1)S(1)} %collective-permute-done.28.sib_b), custom_call_target="tpu_custom_call" | custom-call | flops 1 | bytes 1 | tf_op jit(solution)/shard_map/spread/pallas_call | solution.py:412
  (24 shorter events, 0.2 us)
Async XLA Ops:
  0.6 11.9 %collective-permute-start.1 = (bf16[2,1024,384]{2,1,0:T(8,128)(2,1)}, bf16[2,1024,384]{2,1,0:T(8,128)(2,1)}, u32[]{:S(2)}, u32[]{:S(2)}) collective-permute-start(bf16[2,1024,384]{2,1,0:T(8,128)(2,1)} %bitcast.12), channel_id=1, source_target_pairs={{0,1},{1,0},{2,3},{3,2},{4,5},{5,4},{6,7},{7,6},{8,9},{9,8},{10,11... | collective-permute-start | bytes 4718600 | tf_op jit(solution)/shard_map/ppermute | solution.py:23
  1.1 7.9 %collective-permute-start.2 = (s32[1,3]{1,0:T(1,128)}, s32[1,3]{1,0:T(1,128)S(1)}, u32[]{:S(2)}, u32[]{:S(2)}) collective-permute-start(s32[1,3]{1,0:T(1,128)} %pairs.3), channel_id=1, source_target_pairs={{0,1},{1,0},{2,3},{3,2},{4,5},{5,4},{6,7},{7,6},{8,9},{9,8},{10,11... | collective-permute-start | bytes 44 | tf_op jit(solution)/shard_map/ppermute | solution.py:23
  1.2 1.4 %copy-start = (bf16[1,2,1024,384]{3,2,1,0:T(8,128)(2,1)S(1)}, bf16[1,2,1024,384]{3,2,1,0:T(8,128)(2,1)}, u32[]{:S(2)}) copy-start(bf16[1,2,1024,384]{3,2,1,0:T(8,128)(2,1)} %param.5) | copy-start | bytes 4718596
  2.6 0.7 copy-start.4
  3.3 9.3 %copy-start.1 = (bf16[1,2,1024,384]{3,2,1,0:T(8,128)(2,1)S(1)}, bf16[1,2,1024,384]{3,2,1,0:T(8,128)(2,1)}, u32[]{:S(2)}) copy-start(bf16[1,2,1024,384]{3,2,1,0:T(8,128)(2,1)} %param.5) | copy-start | bytes 4718596
  4.6 0.7 copy-start.6
  5.4 13.1 %collective-permute-start = (bf16[528,384]{1,0:T(8,128)(2,1)S(1)}, bf16[528,384]{1,0:T(8,128)(2,1)S(1)}, u32[]{:S(2)}, u32[]{:S(2)}) collective-permute-start(bf16[528,384]{1,0:T(8,128)(2,1)S(1)} %get-tuple-element.34), channel_id=1, source_target_pairs={{0,2},{1,3},{2,0},{3,1},{4,6},{5,7},{6,4},{7,5},{8,10},{9,11},{10,... | collective-permute-start | bytes 1216520 | tf_op jit(solution)/shard_map/ppermute | solution.py:23
  9.1 0.8 copy-start.2
  9.8 0.7 copy-start.3
  10.6 0.7 copy-start.5
  12.5 14.4 %collective-permute-start.5 = (bf16[512,384]{1,0:T(8,128)(2,1)}, bf16[512,384]{1,0:T(8,128)(2,1)S(1)}, u32[]{:S(2)}, u32[]{:S(2)}) collective-permute-start(bf16[512,384]{1,0:T(8,128)(2,1)} %copy-done.6), channel_id=1, source_target_pairs={{0,2},{1,3},{2,0},{3,1},{4,6},{5,7},{6,4},{7,5},{8,10},{9,11},{10,... | collective-permute-start | bytes 1179656 | tf_op jit(solution)/shard_map/ppermute | solution.py:23
  18.5 20.9 %collective-permute-start.8 = (bf16[528,384]{1,0:T(8,128)(2,1)S(1)}, bf16[528,384]{1,0:T(8,128)(2,1)S(1)}, u32[]{:S(2)}, u32[]{:S(2)}) collective-permute-start(bf16[528,384]{1,0:T(8,128)(2,1)S(1)} %collective-permute-done.rest_0_.rest_4_), channel_id=1, source_target_pairs={{0,4},{1,5},{4,8},{5,9},{6,2},{7,3},{8,12},{9,13},{10,6},{11,7},{1... | collective-permute-start | bytes 1216520 | tf_op jit(solution)/shard_map/ppermute | solution.py:23
  22.6 12.8 %collective-permute-start.3 = (bf16[512,384]{1,0:T(8,128)(2,1)S(1)}, bf16[512,384]{1,0:T(8,128)(2,1)S(1)}, u32[]{:S(2)}, u32[]{:S(2)}) collective-permute-start(bf16[512,384]{1,0:T(8,128)(2,1)S(1)} %get-tuple-element.43), channel_id=1, source_target_pairs={{0,2},{1,3},{2,0},{3,1},{4,6},{5,7},{6,4},{7,5},{8,10},{9,11},{10,... | collective-permute-start | bytes 1179656 | tf_op jit(solution)/shard_map/ppermute | solution.py:23
  26.9 16.3 %collective-permute-start.6 = (bf16[512,384]{1,0:T(8,128)(2,1)S(1)}, bf16[512,384]{1,0:T(8,128)(2,1)S(1)}, u32[]{:S(2)}, u32[]{:S(2)}) collective-permute-start(bf16[512,384]{1,0:T(8,128)(2,1)S(1)} %get-tuple-element.46), channel_id=1, source_target_pairs={{0,2},{1,3},{2,0},{3,1},{4,6},{5,7},{6,4},{7,5},{8,10},{9,11},{10,... | collective-permute-start | bytes 1179656 | tf_op jit(solution)/shard_map/ppermute | solution.py:23
  29.0 14.2 %collective-permute-start.9 = (bf16[512,384]{1,0:T(8,128)(2,1)S(1)}, bf16[512,384]{1,0:T(8,128)(2,1)S(1)}, u32[]{:S(2)}, u32[]{:S(2)}) collective-permute-start(bf16[512,384]{1,0:T(8,128)(2,1)S(1)} %collective-permute-done.5.rest_1_), channel_id=1, source_target_pairs={{0,4},{1,5},{4,8},{5,9},{6,2},{7,3},{8,12},{9,13},{10,6},{11,7},{1... | collective-permute-start | bytes 1179656 | tf_op jit(solution)/shard_map/ppermute | solution.py:23
  32.6 19.9 %collective-permute-start.10 = (bf16[1040,384]{1,0:T(8,128)(2,1)S(1)}, bf16[1040,384]{1,0:T(8,128)(2,1)S(1)}, u32[]{:S(2)}, u32[]{:S(2)}) collective-permute-start(bf16[1040,384]{1,0:T(8,128)(2,1)S(1)} %pad_maximum_fusion), channel_id=1, source_target_pairs={{0,1},{3,2},{4,5},{7,6},{8,9},{11,10},{12,13},{15,14},{16,17},{19,... | collective-permute-start | bytes 2396168 | tf_op jit(solution)/shard_map/ppermute | solution.py:23
  35.4 20.0 %collective-permute-start.4 = (bf16[512,384]{1,0:T(8,128)(2,1)S(1)}, bf16[512,384]{1,0:T(8,128)(2,1)S(1)}, u32[]{:S(2)}, u32[]{:S(2)}) collective-permute-start(bf16[512,384]{1,0:T(8,128)(2,1)S(1)} %collective-permute-done.3.rest_2_), channel_id=1, source_target_pairs={{0,4},{1,5},{4,8},{5,9},{6,2},{7,3},{8,12},{9,13},{10,6},{11,7},{1... | collective-permute-start | bytes 1179656 | tf_op jit(solution)/shard_map/ppermute | solution.py:23
  43.3 18.5 %collective-permute-start.12 = (bf16[1024,384]{1,0:T(8,128)(2,1)S(1)}, bf16[1024,384]{1,0:T(8,128)(2,1)S(1)}, u32[]{:S(2)}, u32[]{:S(2)}) collective-permute-start(bf16[1024,384]{1,0:T(8,128)(2,1)S(1)} %pad_maximum_fusion.2), channel_id=1, source_target_pairs={{0,1},{3,2},{4,5},{7,6},{8,9},{11,10},{12,13},{15,14},{16,17},{19,... | collective-permute-start | bytes 2359304 | tf_op jit(solution)/shard_map/ppermute | solution.py:23
  44.9 7.6 %collective-permute-start.11 = (bf16[1040,384]{1,0:T(8,128)(2,1)S(1)}, bf16[1040,384]{1,0:T(8,128)(2,1)S(1)}, u32[]{:S(2)}, u32[]{:S(2)}) collective-permute-start(bf16[1040,384]{1,0:T(8,128)(2,1)S(1)} %pad_maximum_fusion.1), channel_id=1, source_target_pairs={{1,0},{2,3},{5,4},{6,7},{9,8},{10,11},{13,12},{14,15},{17,16},{18,... | collective-permute-start | bytes 2396168 | tf_op jit(solution)/shard_map/ppermute | solution.py:23
  46.2 12.8 %collective-permute-start.7 = (bf16[512,384]{1,0:T(8,128)(2,1)S(1)}, bf16[512,384]{1,0:T(8,128)(2,1)S(1)}, u32[]{:S(2)}, u32[]{:S(2)}) collective-permute-start(bf16[512,384]{1,0:T(8,128)(2,1)S(1)} %collective-permute-done.6.rest_3_), channel_id=1, source_target_pairs={{0,4},{1,5},{4,8},{5,9},{6,2},{7,3},{8,12},{9,13},{10,6},{11,7},{1... | collective-permute-start | bytes 1179656 | tf_op jit(solution)/shard_map/ppermute | solution.py:23
  59.1 3.6 %collective-permute-start.13 = (bf16[512,384]{1,0:T(8,128)(2,1)S(1)}, bf16[512,384]{1,0:T(8,128)(2,1)S(1)}, u32[]{:S(2)}, u32[]{:S(2)}) collective-permute-start(bf16[512,384]{1,0:T(8,128)(2,1)S(1)} %collective-permute-done.4.rest_0_), channel_id=1, source_target_pairs={{1,0},{2,3},{5,4},{6,7},{9,8},{10,11},{13,12},{14,15},{17,16},{18,... | collective-permute-start | bytes 1179656 | tf_op jit(solution)/shard_map/ppermute | solution.py:23
  60.3 3.6 %collective-permute-start.14 = (bf16[512,384]{1,0:T(8,128)(2,1)S(1)}, bf16[512,384]{1,0:T(8,128)(2,1)S(1)}, u32[]{:S(2)}, u32[]{:S(2)}) collective-permute-start(bf16[512,384]{1,0:T(8,128)(2,1)S(1)} %collective-permute-done.7.rest_1_), channel_id=1, source_target_pairs={{1,0},{2,3},{5,4},{6,7},{9,8},{10,11},{13,12},{14,15},{17,16},{18,... | collective-permute-start | bytes 1179656 | tf_op jit(solution)/shard_map/ppermute | solution.py:23
  71.3 2.9 %collective-permute-start.15 = (f32[2304,128]{1,0:T(8,128)S(1)}, f32[2304,128]{1,0:T(8,128)S(1)}, u32[]{:S(2)}, u32[]{:S(2)}) collective-permute-start(f32[2304,128]{1,0:T(8,128)S(1)} %get-tuple-element.59), channel_id=1, source_target_pairs={{0,1},{1,0},{2,3},{3,2},{4,5},{5,4},{6,7},{7,6},{8,9},{9,8},{10,11... | collective-permute-start | bytes 3538952 | tf_op jit(solution)/shard_map/ppermute | solution.py:23
  74.5 9.8 %collective-permute-start.16 = (s16[1216,128]{1,0:T(8,128)(2,1)S(1)}, s16[1216,128]{1,0:T(8,128)(2,1)S(1)}, u32[]{:S(2)}, u32[]{:S(2)}) collective-permute-start(s16[1216,128]{1,0:T(8,128)(2,1)S(1)} %get-tuple-element.61), channel_id=1, source_target_pairs={{0,2},{1,3},{2,0},{3,1},{4,6},{5,7},{6,4},{7,5},{8,10},{9,11},{10,... | collective-permute-start | bytes 933896 | tf_op jit(solution)/shard_map/ppermute | solution.py:23
  84.5 4.8 %collective-permute-start.17 = (s16[304,128]{1,0:T(8,128)(2,1)S(1)}, s16[304,128]{1,0:T(8,128)(2,1)S(1)}, u32[]{:S(2)}, u32[]{:S(2)}) collective-permute-start(s16[304,128]{1,0:T(8,128)(2,1)S(1)} %get-tuple-element.63), channel_id=1, source_target_pairs={{0,4},{1,5},{2,6},{3,7},{4,0},{5,1},{6,2},{7,3},{8,12},{9,13},{10,... | collective-permute-start | bytes 233480 | tf_op jit(solution)/shard_map/ppermute | solution.py:23
  86.7 7.5 %collective-permute-start.18 = (s16[304,128]{1,0:T(8,128)(2,1)S(1)}, s16[304,128]{1,0:T(8,128)(2,1)S(1)}, u32[]{:S(2)}, u32[]{:S(2)}) collective-permute-start(s16[304,128]{1,0:T(8,128)(2,1)S(1)} %get-tuple-element.64), channel_id=1, source_target_pairs={{0,8},{1,9},{2,10},{3,11},{4,12},{5,13},{6,14},{7,15},{8,0},{9,1},... | collective-permute-start | bytes 233480 | tf_op jit(solution)/shard_map/ppermute | solution.py:23
  89.3 6.3 %collective-permute-start.19 = (s16[304,128]{1,0:T(8,128)(2,1)S(1)}, s16[304,128]{1,0:T(8,128)(2,1)S(1)}, u32[]{:S(2)}, u32[]{:S(2)}) collective-permute-start(s16[304,128]{1,0:T(8,128)(2,1)S(1)} %get-tuple-element.65), channel_id=1, source_target_pairs={{0,12},{1,13},{2,14},{3,15},{4,8},{5,9},{6,10},{7,11},{8,4},{9,5},... | collective-permute-start | bytes 233480 | tf_op jit(solution)/shard_map/ppermute | solution.py:23
  95.7 6.3 %collective-permute-start.22 = (s16[304,128]{1,0:T(8,128)(2,1)S(1)}, s16[304,128]{1,0:T(8,128)(2,1)S(1)}, u32[]{:S(2)}, u32[]{:S(2)}) collective-permute-start(s16[304,128]{1,0:T(8,128)(2,1)S(1)} %sum_code.1), channel_id=1, source_target_pairs={{0,12},{1,13},{2,14},{3,15},{4,8},{5,9},{6,10},{7,11},{8,4},{9,5},... | collective-permute-start | bytes 233480 | tf_op jit(solution)/shard_map/ppermute | solution.py:23
  97.8 6.1 %collective-permute-start.21 = (s16[304,128]{1,0:T(8,128)(2,1)S(1)}, s16[304,128]{1,0:T(8,128)(2,1)S(1)}, u32[]{:S(2)}, u32[]{:S(2)}) collective-permute-start(s16[304,128]{1,0:T(8,128)(2,1)S(1)} %sum_code.1), channel_id=1, source_target_pairs={{0,8},{1,9},{2,10},{3,11},{4,12},{5,13},{6,14},{7,15},{8,0},{9,1},... | collective-permute-start | bytes 233480 | tf_op jit(solution)/shard_map/ppermute | solution.py:23
  98.1 7.5 %collective-permute-start.20 = (s16[304,128]{1,0:T(8,128)(2,1)S(1)}, s16[304,128]{1,0:T(8,128)(2,1)S(1)}, u32[]{:S(2)}, u32[]{:S(2)}) collective-permute-start(s16[304,128]{1,0:T(8,128)(2,1)S(1)} %sum_code.1), channel_id=1, source_target_pairs={{0,4},{1,5},{2,6},{3,7},{4,0},{5,1},{6,2},{7,3},{8,12},{9,13},{10,... | collective-permute-start | bytes 233480 | tf_op jit(solution)/shard_map/ppermute | solution.py:23
  100.2 5.8 %collective-permute-start.23 = (s16[304,128]{1,0:T(8,128)(2,1)S(1)}, s16[304,128]{1,0:T(8,128)(2,1)S(1)}, u32[]{:S(2)}, u32[]{:S(2)}) collective-permute-start(s16[304,128]{1,0:T(8,128)(2,1)S(1)} %sum_code.1), channel_id=1, source_target_pairs={{0,2},{1,3},{2,0},{3,1},{4,6},{5,7},{6,4},{7,5},{8,10},{9,11},{10,... | collective-permute-start | bytes 233480 | tf_op jit(solution)/shard_map/ppermute | solution.py:23
  102.1 5.1 %collective-permute-start.26 = (s16[304,128]{1,0:T(8,128)(2,1)S(1)}, s16[304,128]{1,0:T(8,128)(2,1)S(1)}, u32[]{:S(2)}, u32[]{:S(2)}) collective-permute-start(s16[304,128]{1,0:T(8,128)(2,1)S(1)} %collective-permute-done.22), channel_id=1, source_target_pairs={{0,2},{1,3},{2,0},{3,1},{4,6},{5,7},{6,4},{7,5},{8,10},{9,11},{10,... | collective-permute-start | bytes 233480 | tf_op jit(solution)/shard_map/ppermute | solution.py:23
  103.8 4.4 %collective-permute-start.25 = (s16[304,128]{1,0:T(8,128)(2,1)S(1)}, s16[304,128]{1,0:T(8,128)(2,1)S(1)}, u32[]{:S(2)}, u32[]{:S(2)}) collective-permute-start(s16[304,128]{1,0:T(8,128)(2,1)S(1)} %collective-permute-done.21), channel_id=1, source_target_pairs={{0,2},{1,3},{2,0},{3,1},{4,6},{5,7},{6,4},{7,5},{8,10},{9,11},{10,... | collective-permute-start | bytes 233480 | tf_op jit(solution)/shard_map/ppermute | solution.py:23
  105.7 4.4 %collective-permute-start.24 = (s16[304,128]{1,0:T(8,128)(2,1)S(1)}, s16[304,128]{1,0:T(8,128)(2,1)S(1)}, u32[]{:S(2)}, u32[]{:S(2)}) collective-permute-start(s16[304,128]{1,0:T(8,128)(2,1)S(1)} %collective-permute-done.20), channel_id=1, source_target_pairs={{0,2},{1,3},{2,0},{3,1},{4,6},{5,7},{6,4},{7,5},{8,10},{9,11},{10,... | collective-permute-start | bytes 233480 | tf_op jit(solution)/shard_map/ppermute | solution.py:23
  105.9 4.3 %collective-permute-start.27 = (s16[4,304,128]{2,1,0:T(8,128)(2,1)S(1)}, s16[4,304,128]{2,1,0:T(8,128)(2,1)S(1)}, u32[]{:S(2)}, u32[]{:S(2)}) collective-permute-start(s16[4,304,128]{2,1,0:T(8,128)(2,1)S(1)} %pad_add_fusion.a), channel_id=1, source_target_pairs={{0,1},{1,0},{2,3},{3,2},{4,5},{5,4},{6,7},{7,6},{8,9},{9,8},{10,11... | collective-permute-start | bytes 933896 | tf_op jit(solution)/shard_map/ppermute | solution.py:23
  110.1 1.7 %collective-permute-start.28 = (s16[4,304,128]{2,1,0:T(8,128)(2,1)S(1)}, s16[4,304,128]{2,1,0:T(8,128)(2,1)S(1)}, u32[]{:S(2)}, u32[]{:S(2)}) collective-permute-start(s16[4,304,128]{2,1,0:T(8,128)(2,1)S(1)} %pad_add_fusion.1.b), channel_id=1, source_target_pairs={{0,1},{1,0},{2,3},{3,2},{4,5},{5,4},{6,7},{7,6},{8,9},{9,8},{10,11... | collective-permute-start | bytes 933896 | tf_op jit(solution)/shard_map/ppermute | solution.py:23

commit v4 on v3

--- a/solution.py
+++ b/solution.py
@@ -12,6 +12,7 @@
 LANES = 128
 BLOCK = 256
 PAD = 16
+PER = 2
 GROUP = 32
 BITS = 14
 NT = (((1,), (1,)), ((), ()))
@@ -63,15 +64,18 @@
 STEPS = (((OWN, 0), (OWN, 1)), ((SIB, 0), (SIB, 1)), ((Y, 0), (Z, 0)), ((X, 0), (Y, 1)), ((Z, 1), (X, 1)))
 
 
-def prep_kernel(blocks, me_ref, pairs, sib_pairs, occ, energy, maps, levels, weights):
+def prep_kernel(blocks, me_ref, pairs, sib_pairs, occ_in, energy_in, maps_in, levels, weights, sem, occ, energy, maps):
+    copies = begin([(occ_in, occ), (energy_in, energy), (maps_in, maps)], sem)
     me = me_ref[0]
     virt = maps.shape[1]
+    finish(copies)
     table = energy[...]
     parts = []
     for _ in range(3):
         part = table.astype(BF16)
         parts.append(part)
         table = table - part.astype(F32)
+    block_major = lax.broadcasted_iota(I32, occ.shape, 1)
     row_major = lax.broadcasted_iota(I32, (energy.shape[0], virt), 0)
     lane_major = lax.broadcasted_iota(I32, (LANES, virt), 0)
     for block, offset in enumerate(offsets_of(me)):
@@ -82,6 +86,7 @@
             count = count + (pairs[0, s] == other).astype(I32)
             if block in (OWN, SIB):
                 count = count + ((pairs, sib_pairs)[block][0, s] == me).astype(I32)
+        occupied = jnp.sum(jnp.where(block_major == who, occ[...], 0.0), axis=1, keepdims=True)
         index = maps[pl.ds(who, 1), :]
         pick = (row_major == index // LANES).astype(F32).astype(BF16)
         rows = sum(lax.dot_general(p, pick, TN, preferred_element_type=F32) for p in parts)
@@ -90,11 +95,11 @@
             for side, (which, j) in enumerate(halves):
                 if which == block:
                     at = pl.ds(side * virt, virt)
-                    levels[step:step + 1, at] = chosen - occ[who, j]
+                    levels[step:step + 1, at] = chosen - occupied[j:j + 1, :]
                     weights[step:step + 1, at] = jnp.full((1, virt), -count.astype(F32), F32)
 
 
-def add_pair(own_t, other, amp, total, own_level, level, weight, first):
+def add_pair(own_t, other, amp, total, own_level, level, weight, first, halves=None):
     wide = own_t.shape[0]
     for t in range(0, wide, BLOCK):
         s = pl.ds(t, BLOCK)
@@ -103,16 +108,20 @@
     for t in range(0, wide, BLOCK):
         s = pl.ds(t, BLOCK)
         part = lax.dot_general(other[...], amp[s, :], NT, preferred_element_type=F32)
-        total[:, s] = part if first else total[:, s] + part
-
-
-def split_kernel(me_ref, pairs, own, *rest):
+        value = part if first else total[:, s] + part
+        total[:, s] = value
+        if halves is not None:
+            high = value.astype(BF16)
+            halves[0][:, s] = high
+            halves[1][:, s] = (value - high.astype(F32)).astype(BF16)
+
+
+def split_kernel(places, me_ref, pairs, own, *rest):
     parts, sem = rest[:-1], rest[-1]
-    per = len(parts) // 2
-    rows, virt = parts[1].shape
     copies = begin(
-        [(own.at[i // per, pl.ds(i % per * rows, rows)], part.at[pl.ds(0, rows)]) for i, part in enumerate(parts)], sem
+        [(own.at[j, pl.ds(a, n)], part.at[pl.ds(0, n)]) for (j, a, n), part in zip(places, parts)], sem
     )
+    rows, virt = parts[0].shape[0] - PAD, parts[0].shape[1]
     lane = lax.broadcasted_iota(I32, (PAD, virt), 1)
     listed = jnp.full((PAD, virt), 100, I32)
     for s in range(pairs.shape[1]):
@@ -121,17 +130,20 @@
     finish(copies)
 
 
-def near_kernel(own, sib, levels, weights, own_t, total, sem, own_s, other, amp):
+def own_kernel(own, levels, weights, own_t, total, sem, own_s, amp):
     virt = own.shape[2]
-    copies = begin(
-        [(x.at[j], s.at[:, pl.ds(j * virt, virt)]) for x, s in ((own, own_s), (sib, other)) for j in range(2)],
-        sem,
-    )
+    copies = begin([(own.at[j], own_s.at[:, pl.ds(j * virt, virt)]) for j in range(2)], sem)
     level = levels[...].T
-    finish(copies[:2])
+    finish(copies)
     own_t[...] = own_s[...].T
     add_pair(own_t, own_s, amp, total, level, levels[0:1, :], weights[0:1, :], True)
-    finish(copies[2:])
+
+
+def sib_kernel(own_t, total_in, sib, levels, weights, total, sem, other, amp):
+    virt = sib.shape[2]
+    copies = begin([(sib.at[j], other.at[:, pl.ds(j * virt, virt)]) for j in range(2)], sem)
+    level = levels[...].T
+    finish(copies)
     add_pair(own_t, other, amp, total, level, levels[1:2, :], weights[1:2, :], False)
 
 
@@ -173,18 +185,16 @@
 
 def last_kernel(plan, names, step, me_ref, own_t, total_in, levels, weights, own, *rest):
     refs = dict(zip(names, rest))
-    total, residual, keep, send, sem, other, amp, own_s, high, low, packed = rest[len(names):]
+    total, residual, *quarters, sem, other, amp, own_s, high, low, packed = rest[len(names):]
     me = me_ref[0]
-    core = me & 1
+    parity, core, _ = place_of(me)
     virt = own.shape[2]
     a, b = pl.ds(0, virt), pl.ds(virt, virt)
-    copies = begin([(own.at[0], own_s.at[:, a]), (own.at[1], own_s.at[:, b])], sem)
+    for j, at in enumerate((a, b)):
+        own_s[:, at] = own[j]
     weight = weights[step:step + 1, :] - fetch(plan, step, me, refs, other)
-    add_pair(own_t, other, amp, total, levels[...].T, levels[step:step + 1, :], weight, False)
-    outs = begin([(total.at[:, a], residual.at[0]), (total.at[:, b], residual.at[1])], sem, 2)
-    finish(copies)
-    high[...] = total[...].astype(BF16)
-    low[...] = (total[...] - high[...].astype(F32)).astype(BF16)
+    add_pair(own_t, other, amp, total, levels[...].T, levels[step:step + 1, :], weight, False, (high, low))
+    outs = begin([(total.at[:, a], residual.at[0]), (total.at[:, b], residual.at[1])], sem)
     at = 0
     for q in range(0, total.shape[0], BLOCK):
         rows = q + BLOCK
@@ -195,9 +205,10 @@
             upper = q + c + LANES
             packed[at:at + upper, :] = block[:upper, c:c + LANES]
             at += upper
-    size = keep.shape[0]
-    keep[...] = packed[pl.ds(pl.multiple_of(core * size, 16), size), :]
-    send[...] = packed[pl.ds(pl.multiple_of((1 - core) * size, 16), size), :]
+    size = quarters[0].shape[0]
+    where = ((core, 1 - parity), (core, parity), (1 - core, 1 - parity), (1 - core, parity))
+    for out, (half, side) in zip(quarters, where):
+        out[...] = packed[pl.ds(pl.multiple_of((2 * half + side) * size, 16), size), :]
     finish(outs)
 
 
@@ -223,24 +234,20 @@
     )
 
 
-def chip_kernel(me_ref, mine, theirs, keep, send):
-    parity, _, _ = place_of(me_ref[0])
-    size = keep.shape[0]
-    piece = size // 4
-    at = pl.ds(pl.multiple_of(parity * size, 16), size)
-    keep[...] = mine[at, :] + theirs[at, :]
+def chip_kernel(mine, theirs, send):
+    piece = mine.shape[0] // 4
     for t in range(4):
-        at = pl.ds(pl.multiple_of((1 - parity) * size + t * piece, 16), piece)
+        at = pl.ds(t * piece, piece)
         encode(mine[at, :] + theirs[at, :], send, t * (piece + PAD))
 
 
-def column_kernel(me_ref, mine, theirs, keep, *sends):
+def column_kernel(me_ref, mine, theirs, across, keep, *sends):
     _, _, z = place_of(me_ref[0])
     piece = keep.shape[0]
     for t in range(4):
         at = pl.ds(pl.multiple_of((z ^ t) * piece, 16), piece)
-        coded = theirs[pl.ds(pl.multiple_of((z ^ t) * (piece + PAD), 16), piece + PAD), :]
-        value = mine[at, :] + decode(coded)
+        coded = across[pl.ds(pl.multiple_of((z ^ t) * (piece + PAD), 16), piece + PAD), :]
+        value = mine[at, :] + theirs[at, :] + decode(coded)
         if t:
             encode(value, sends[t - 1], 0)
         else:
@@ -316,46 +323,70 @@
     def plain(n):
         return jax.ShapeDtypeStruct((n, LANES), F32)
 
-    half = aux // 2
-    sib, sib_pairs = swapped(own, 1), swapped(pair_blocks, 1)
-    parts = kernel(
-        split_kernel, "split", [smem, smem, hbm],
-        [jax.ShapeDtypeStruct((half + (0 if i else PAD), virt), BF16) for i in range(4)], [vmem] * 4, [dma(4)],
-    )(me, pair_blocks, own)
-    y = [swapped(parts[0], 2)]
+    cuts = [[at * aux // PER + (PAD if at and at < PER and not j else 0) for at in range(PER + 1)] for j in range(orbitals)]
+    places = [(j, a, b - a) for j in range(orbitals) for a, b in zip(cuts[j], cuts[j][1:])]
+    count = len(places)
+    part = own[0, :places[0][2]]
+    y = [swapped(part, 2)]
+    sib_pairs = swapped(pair_blocks, 1)
+    later, part = lax.optimization_barrier((own, part))
+    sib = swapped(later, 1)
+    parts = [None, *kernel(
+        functools.partial(split_kernel, places[1:]), "split", [smem, smem, hbm],
+        [jax.ShapeDtypeStruct((n + (0 if i else PAD), virt), BF16) for i, (_, _, n) in enumerate(places[1:])],
+        [vmem] * (count - 1), [dma(count - 1)],
+    )(me, pair_blocks, later)]
+
+    small = jax.ShapeDtypeStruct((8, wide), F32)
+    energy = virt_energy.reshape(-1, LANES)
+    levels, weights = kernel(
+        functools.partial(prep_kernel, blocks), "prep", [smem] * 3 + [hbm] * 3, (small, small), (vmem, vmem),
+        [dma(3), pltpu.VMEM((orbitals, blocks), F32), pltpu.VMEM(energy.shape, F32), pltpu.VMEM(domain_map.shape, I32)],
+    )(me, pair_blocks, sib_pairs, occ_energy.T, energy, domain_map)
+    sib, near_own = lax.optimization_barrier((sib, own))
+    own_t, total = kernel(
+        own_kernel, "own", [hbm, vmem, vmem], (jax.ShapeDtypeStruct((wide, aux), BF16), total_t), (vmem, vmem),
+        [dma(2), slab_s, amp_s], LARGE_LIMIT, flops=int(2e10),
+    )(near_own, levels, weights)
     sib, part = lax.optimization_barrier((sib, parts[1]))
     y.append(swapped(part, 2))
-
-    small = jax.ShapeDtypeStruct((8, wide), F32)
-    levels, weights = kernel(
-        functools.partial(prep_kernel, blocks), "prep", [smem] * 4 + [vmem] * 2, (small, small), (vmem, vmem),
-    )(me, pair_blocks, sib_pairs, occ_energy, virt_energy.reshape(-1, LANES), domain_map)
-    own_t, total = kernel(
-        near_kernel, "near", [hbm, hbm, vmem, vmem], (jax.ShapeDtypeStruct((wide, aux), BF16), total_t), (vmem, vmem),
-        [dma(4), slab_s, slab_s, amp_s], LARGE_LIMIT, flops=int(5e10),
-    )(own, sib, levels, weights)
-    y[0], total, own_t, part = lax.optimization_barrier((y[0], total, own_t, parts[2]))
+    y[0], total, own_t, sib, part = lax.optimization_barrier((y[0], total, own_t, sib, parts[2]))
     y.append(swapped(part, 2))
-    y[1], part = lax.optimization_barrier((y[1], parts[3]))
+    z = [forwarded(y[0])]
+    total = kernel(
+        sib_kernel, "sib", [vmem, vmem, hbm, vmem, vmem], total_t, vmem, [dma(2), slab_s, amp_s], LARGE_LIMIT, {1: 0},
+        int(1e10),
+    )(own_t, total, sib, levels, weights)
+    y[1], total, part = lax.optimization_barrier((y[1], total, parts[3]))
     y.append(swapped(part, 2))
-
-    z = [forwarded(part) for part in y]
-    z[0], z[1], y[2], y[3] = lax.optimization_barrier((z[0], z[1], y[2], y[3]))
+    z.append(forwarded(y[1]))
+    for i in range(4, count):
+        y[i - 2], part, _ = lax.optimization_barrier((y[i - 2], parts[i], y[i - 3]))
+        y.append(swapped(part, 2))
+        z.append(forwarded(y[i - 2]))
+    y[-2], z[0] = lax.optimization_barrier((y[-2], z[0]))
+    z.append(forwarded(y[-2]))
+
     arrays = {f"y{i}": part for i, part in enumerate(y)}
     arrays |= {f"z{i}": part for i, part in enumerate(z)}
-    arrays["sy0"] = to_sibling(jnp.concatenate(y[:2]), 0)
-    arrays["sz0"] = to_sibling(jnp.concatenate(z[:2]), 1)
-    arrays["sy2"] = to_sibling(jnp.concatenate(y[2:]), 0)
+    arrays["sy0"] = to_sibling(jnp.concatenate(y[:PER]), 0)
+    arrays["sz0"] = to_sibling(jnp.concatenate(z[:PER]), 1)
 
     def own_core(name, j):
-        return [(f"{name}{2 * j + h}", 0, half, h * half) for h in range(2)], (f"{name}0", half)
+        rows = [(f"{name}{i}", 0, n, to) for i, (k, to, n) in enumerate(places) if k == j]
+        return rows, (f"{name}1", places[1][2])
 
     def other_core(j):
-        if j:
-            rows = [((("sy2", h * half), (f"sz{2 + h}", 0)), 0, half, h * half) for h in range(2)]
-        else:
-            rows = [((("sy0", at), ("sz0", at)), 0, half, to) for at, to in ((0, 0), (half + PAD, half))]
-        return rows, (("sy0", "sz0"), half)
+        rows = []
+        for h, (_, to, n) in enumerate(places[j * PER:(j + 1) * PER]):
+            if not j:
+                at = to + (PAD if h > 1 else 0)
+                rows.append(((("sy0", at), ("sz0", at)), 0, n, to))
+            elif h < PER - 1:
+                rows.append(((("sy1", to), ("sz1", to)), 0, n, to))
+            else:
+                rows.append(((("sy1", to), ("sz2", 0)), 0, n, to))
+        return rows, (("sy0", "sz0"), places[0][2] + places[1][2])
 
     def names_in(plan):
         names = []
@@ -365,34 +396,41 @@
             names += [name] if isinstance(name, str) else name
         return list(dict.fromkeys(names))
 
-    def pair_step(body, name, step, given=(), outs=(), out_specs=(), scratch=()):
+    def pair_step(body, name, step, given=(), outs=(), out_specs=(), scratch=(), flops=1):
         plan = [other_core(j) if which == X else own_core("y" if which == Y else "z", j) for which, j in STEPS[step]]
         names = names_in(plan)
         return kernel(
             functools.partial(body, plan, names, step), name,
-            [smem] + [vmem] * 4 + [hbm] * len(given) + [vmem] * len(names),
-            (total_t, *outs), (vmem, *out_specs), scratch, LARGE_LIMIT, {2: 0}, int(1e10),
+            [smem] + [vmem] * (4 + len(given) + len(names)),
+            (total_t, *outs), (vmem, *out_specs), scratch, LARGE_LIMIT, {2: 0}, flops,
         )(me, own_t, total, levels, weights, *given, *[arrays[n] for n in names])
 
-    (total,) = pair_step(far_kernel, "far2", 2, scratch=[slab_s, amp_s])
-    (total,) = pair_step(far_kernel, "far3", 3, scratch=[slab_s, amp_s])
-    z[2], z[3], total = lax.optimization_barrier((z[2], z[3], total))
-    arrays["z2"], arrays["z3"] = z[2], z[3]
-    arrays["sz2"], arrays["sz3"] = to_sibling(z[2], 1), to_sibling(z[3], 1)
-    _, residual, keep, send = pair_step(
+    z.append(forwarded(y[-1]))
+    y[-1], total = lax.optimization_barrier((y[-1], total))
+    arrays[f"y{count - 1}"] = y[-1]
+    (total,) = pair_step(far_kernel, "far2", 2, scratch=[slab_s, amp_s], flops=int(1e10))
+    (total,) = pair_step(far_kernel, "far3", 3, scratch=[slab_s, amp_s], flops=1)
+    total, *late = lax.optimization_barrier((total, *y[PER:], *z[PER:-1]))
+    y[PER:], z[PER:-1] = late[:PER], late[PER:]
+    arrays["sy1"] = to_sibling(jnp.concatenate(y[PER:]), 0)
+    arrays["sz1"] = to_sibling(jnp.concatenate(z[PER:-1]), 1)
+    z[-1], total, arrays["sz1"] = lax.optimization_barrier((z[-1], total, arrays["sz1"]))
+    arrays["sz2"] = to_sibling(z[-1], 1)
+    arrays |= {f"z{i}": part for i, part in enumerate(z)}
+    _, residual, *quarters = pair_step(
         last_kernel, "last", 4, (own,),
-        (jax.ShapeDtypeStruct(own.shape, F32), plain(upper // 2), plain(upper // 2)), (hbm, vmem, vmem),
-        [dma(4), slab_s, amp_s, slab_s, slab_s, slab_s, pltpu.VMEM((upper, LANES), F32)],
+        (jax.ShapeDtypeStruct(own.shape, F32),) + (plain(upper // 4),) * 4, (hbm,) + (vmem,) * 4,
+        [dma(2), slab_s, amp_s, slab_s, slab_s, slab_s, pltpu.VMEM((upper, LANES), F32)],
     )
 
-    got = swapped(send, 1)
-    keep, send = kernel(
-        chip_kernel, "chip", [smem, vmem, vmem], (plain(upper // 4), coded(4 * (piece + PAD))), (vmem, vmem),
-    )(me, keep, got)
-    got = swapped(send, 2)
+    got = swapped(quarters[2], 1)
+    got, send = lax.optimization_barrier((got, quarters[3]))
+    got_own = swapped(send, 1)
+    send = kernel(chip_kernel, "chip", [vmem, vmem], coded(4 * (piece + PAD)), vmem)(quarters[0], got)
+    across = swapped(send, 2)
     keep, *sends = kernel(
-        column_kernel, "column", [smem, vmem, vmem], (plain(piece),) + (coded(piece + PAD),) * 3, (vmem,) * 4,
-    )(me, keep, got)
+        column_kernel, "column", [smem, vmem, vmem, vmem], (plain(piece),) + (coded(piece + PAD),) * 3, (vmem,) * 4,
+    )(me, quarters[1], got_own, across)
     got = [swapped(send, 4 * t) for t, send in zip((1, 2, 3), sends)]
     if blocks == 16:
         mine = kernel(

time: 115 us -> 107 us (0.930)
  waiting for transfers between devices: 39.4 us -> 35.6 us
  local copies, waits for them, and re-layouts: 5.71 us -> 3.14 us
    ppermute x29 -> x30, waiting for transfers between devices: 39.4 us -> 35.6 us  [move(): return lax.ppermute(x, 'dom', pairs)]
    unnamed x15 -> x12, local copies, waits for them, and re-layouts: 5.71 us -> 2.08 us
    ppermute x29 -> x30, starting transfers between devices: 43.7 us -> 42.9 us  [move(): return lax.ppermute(x, 'dom', pairs)]
    pallas_call x5 -> x6, Pallas kernels: 8.81 us -> 8.92 us  [the longest x1 3.07 us: shards(): kernel(own_kernel, 'own', [hbm, vmem, vmem], (jax.ShapeDtypeStruct((wide,...]
  transfers between devices with their start and end apart: 29 -> 30, of which waited for: 17 -> 14; matrix products, arithmetic and copies ran while one was open for 1% -> 0% of each run, Pallas kernels for 12% -> 13%
where the time goes in v4:
time: 107 us
  starting transfers between devices  42.9 us (40%)
  waiting for transfers between devices  35.6 us (33%)
  Pallas kernels  23.8 us (22%)
  local copies, waits for them, and re-layouts  3.14 us (3%)
  between operations  1.12 us (1%)
    ppermute x30, starting transfers between devices, move(): return lax.ppermute(x, 'dom', pairs)  42.9 us
    ppermute x30, waiting for transfers between devices, move(): return lax.ppermute(x, 'dom', pairs)  35.6 us
    pallas_call x3, Pallas kernels, pair_step(): kernel(functools.partial(body, plan, names, step), name, [smem] + [vmem]...  12.2 us
    pallas_call x1, Pallas kernels, shards(): kernel(own_kernel, 'own', [hbm, vmem, vmem], (jax.ShapeDtypeStruct((wide,...  3.07 us
    pallas_call x1, Pallas kernels, shards(): kernel(sib_kernel, 'sib', [vmem, vmem, hbm, vmem, vmem], total_t, vmem, [...  3.03 us
    pallas_call x1, Pallas kernels, shards(): kernel(spread_kernel, 'spread', [smem] + [vmem] * 4, jax.ShapeDtypeStruct...  2.56 us
  transfers between devices with their start and end apart: 30, of which 14 were waited for; matrix products, arithmetic and copies ran while one was open for 0% of the time, Pallas kernels for 13%

profile of v4, /device:TPU:0, one launch (start us, length us, event | category | flops | bytes accessed | tf_op | source)
XLA Modules:
  0.0 106.9 jit_solution(12897757029221778267)
XLA Ops:
  0.7 1.1 slice_bitcast_fusion
  1.7 0.5 collective-permute-start.1
  2.2 2.6 %collective-permute-start = (bf16[528,384]{1,0:T(8,128)(2,1)S(1)}, bf16[528,384]{1,0:T(8,128)(2,1)S(1)}, u32[]{:S(2)}, u32[]{:S(2)}) collective-permute-start(bf16[528,384]{1,0:T(8,128)(2,1)S(1)} %slice_bitcast_fusion), channel_id=1, source_target_pairs={{0,2},{1,3},{2,0},{3,1},{4,6},{5,7},{6,4},{7,5},{8,10},{9,11},{10,... | collective-permute-start | bytes 1216520 | tf_op jit(solution)/shard_map/ppermute | solution.py:24
  4.8 0.2 collective-permute-start.2
  5.0 1.4 %copy-done = bf16[1,2,1024,384]{3,2,1,0:T(8,128)(2,1)S(1)} copy-done((bf16[1,2,1024,384]{3,2,1,0:T(8,128)(2,1)S(1)}, bf16[1,2,1024,384]{3,2,1,0:T(8,128)(2,1)}, u32[]{:S(2)}) %copy-start) | copy-done | bytes 1572888
  6.4 0.7 copy-done.4
  7.1 1.1 %split.1 = (bf16[512,384]{1,0:T(8,128)(2,1)S(1)}, bf16[512,384]{1,0:T(8,128)(2,1)S(1)}, bf16[512,384]{1,0:T(8,128)(2,1)S(1)}) custom-call(s32[1]{0:T(128)} %bitcast.me_ref, s32[1,3]{1,0:T(1,128)S(1)} %copy-done.4, bf16[2,1024,384]{2,1,0:T(8,128)(2,1)S(1)} %bitcast.17), custom_call_target="tpu_custom_call" | custom-call | flops 1 | bytes 1 | tf_op jit(solution)/shard_map/split/pallas_call | solution.py:334
  8.2 0.0 collective-permute-done.2.sib_pairs
  8.2 1.3 %prep.1 = (f32[8,768]{1,0:T(8,128)S(1)}, f32[8,768]{1,0:T(8,128)S(1)}) custom-call(s32[1]{0:T(128)} %bitcast.me_ref, s32[1,3]{1,0:T(1,128)S(1)} %copy-done.4, s32[1,3]{1,0:T(1,128)S(1)} %collective-permute-done.2.sib_pairs, f32[2,16]{1,0:T(2,128)S(1)} %bitcast.22, f32[64,128]{1,0:T(8,128)S(1)} %bitcast.21, s32[16,384]{1,0:T(8,128)S(1)} %copy-done.3), custom_call_target="tpu_custom_call" | custom-call | flops 1 | bytes 1 | tf_op jit(solution)/shard_map/prep/pallas_call | solution.py:342
  9.5 0.0 collective-permute-done.1.sib
  9.5 0.3 collective-permute-start.3
  9.9 3.1 %own.1 = (bf16[768,1024]{1,0:T(8,128)(2,1)S(1)}, f32[1024,768]{1,0:T(8,128)S(1)}) custom-call(bf16[2,1024,384]{2,1,0:T(8,128)(2,1)S(1)} %bitcast.18, f32[8,768]{1,0:T(8,128)S(1)} %get-tuple-element.46.levels, f32[8,768]{1,0:T(8,128)S(1)} %get-tuple-element.47.weights), custom_call_target="tpu_custom_call" | custom-call | flops 20000000000 | bytes 1 | tf_op jit(solution)/shard_map/own/pallas_call | solution.py:347
  12.9 2.1 %collective-permute-done.rest_0_ = bf16[528,384]{1,0:T(8,128)(2,1)S(1)} collective-permute-done((bf16[528,384]{1,0:T(8,128)(2,1)S(1)}, bf16[528,384]{1,0:T(8,128)(2,1)S(1)}, u32[]{:S(2)}, u32[]{:S(2)}) %collective-permute-start) | collective-permute-done | bytes 405536 | tf_op jit(solution)/shard_map/ppermute | solution.py:24
  15.1 1.9 %collective-permute-start.6 = (bf16[512,384]{1,0:T(8,128)(2,1)S(1)}, bf16[512,384]{1,0:T(8,128)(2,1)S(1)}, u32[]{:S(2)}, u32[]{:S(2)}) collective-permute-start(bf16[512,384]{1,0:T(8,128)(2,1)S(1)} %get-tuple-element.64), channel_id=1, source_target_pairs={{0,2},{1,3},{2,0},{3,1},{4,6},{5,7},{6,4},{7,5},{8,10},{9,11},{10,... | collective-permute-start | bytes 1179656 | tf_op jit(solution)/shard_map/ppermute | solution.py:24
  17.0 3.5 %collective-permute-start.7 = (bf16[528,384]{1,0:T(8,128)(2,1)S(1)}, bf16[528,384]{1,0:T(8,128)(2,1)S(1)}, u32[]{:S(2)}, u32[]{:S(2)}) collective-permute-start(bf16[528,384]{1,0:T(8,128)(2,1)S(1)} %collective-permute-done.rest_0_), channel_id=1, source_target_pairs={{0,4},{1,5},{4,8},{5,9},{6,2},{7,3},{8,12},{9,13},{10,6},{11,7},{1... | collective-permute-start | bytes 1216520 | tf_op jit(solution)/shard_map/ppermute | solution.py:24
  20.5 3.0 %sib.1.total_in = f32[1024,768]{1,0:T(8,128)S(1)} custom-call(bf16[768,1024]{1,0:T(8,128)(2,1)S(1)} %get-tuple-element.54.own_t, f32[1024,768]{1,0:T(8,128)S(1)} %get-tuple-element.56.total_in, bf16[2,1024,384]{2,1,0:T(8,128)(2,1)S(1)} %collective-permute-done.1.sib, f32[8,768]{1,0:T(8,128)S(1)} %get-tuple-element.46.levels, ...), custom_call_target="tpu_custom_call", output_to_operand_aliasing={{}: (1, {})} | custom-call | flops 10000000000 | bytes 1 | tf_op jit(solution)/shard_map/sib/pallas_call | solution.py:356
  23.6 1.9 %collective-permute-start.4 = (bf16[512,384]{1,0:T(8,128)(2,1)S(1)}, bf16[512,384]{1,0:T(8,128)(2,1)S(1)}, u32[]{:S(2)}, u32[]{:S(2)}) collective-permute-start(bf16[512,384]{1,0:T(8,128)(2,1)S(1)} %get-tuple-element.59), channel_id=1, source_target_pairs={{0,2},{1,3},{2,0},{3,1},{4,6},{5,7},{6,4},{7,5},{8,10},{9,11},{10,... | collective-permute-start | bytes 1179656 | tf_op jit(solution)/shard_map/ppermute | solution.py:24
  25.4 3.5 %collective-permute-start.8 = (bf16[512,384]{1,0:T(8,128)(2,1)S(1)}, bf16[512,384]{1,0:T(8,128)(2,1)S(1)}, u32[]{:S(2)}, u32[]{:S(2)}) collective-permute-start(bf16[512,384]{1,0:T(8,128)(2,1)S(1)} %collective-permute-done.3.rest_1_.rest_4_), channel_id=1, source_target_pairs={{0,4},{1,5},{4,8},{5,9},{6,2},{7,3},{8,12},{9,13},{10,6},{11,7},{1... | collective-permute-start | bytes 1179656 | tf_op jit(solution)/shard_map/ppermute | solution.py:24
  28.9 0.1 pad_maximum_fusion
  29.0 1.3 %collective-permute-start.9 = (bf16[1040,384]{1,0:T(8,128)(2,1)S(1)}, bf16[1040,384]{1,0:T(8,128)(2,1)S(1)}, u32[]{:S(2)}, u32[]{:S(2)}) collective-permute-start(bf16[1040,384]{1,0:T(8,128)(2,1)S(1)} %pad_maximum_fusion), channel_id=1, source_target_pairs={{0,1},{3,2},{4,5},{7,6},{8,9},{11,10},{12,13},{15,14},{16,17},{19,... | collective-permute-start | bytes 2396168 | tf_op jit(solution)/shard_map/ppermute | solution.py:24
  30.4 1.5 %collective-permute-done.6.rest_2_ = bf16[512,384]{1,0:T(8,128)(2,1)S(1)} collective-permute-done((bf16[512,384]{1,0:T(8,128)(2,1)S(1)}, bf16[512,384]{1,0:T(8,128)(2,1)S(1)}, u32[]{:S(2)}, u32[]{:S(2)}) %collective-permute-start.6) | collective-permute-done | bytes 393248 | tf_op jit(solution)/shard_map/ppermute | solution.py:24
  31.9 3.9 %collective-permute-start.11 = (bf16[512,384]{1,0:T(8,128)(2,1)S(1)}, bf16[512,384]{1,0:T(8,128)(2,1)S(1)}, u32[]{:S(2)}, u32[]{:S(2)}) collective-permute-start(bf16[512,384]{1,0:T(8,128)(2,1)S(1)} %collective-permute-done.6.rest_2_), channel_id=1, source_target_pairs={{0,4},{1,5},{4,8},{5,9},{6,2},{7,3},{8,12},{9,13},{10,6},{11,7},{1... | collective-permute-start | bytes 1179656 | tf_op jit(solution)/shard_map/ppermute | solution.py:24
  35.9 4.2 %collective-permute-done.4.rest_3_ = bf16[512,384]{1,0:T(8,128)(2,1)S(1)} collective-permute-done((bf16[512,384]{1,0:T(8,128)(2,1)S(1)}, bf16[512,384]{1,0:T(8,128)(2,1)S(1)}, u32[]{:S(2)}, u32[]{:S(2)}) %collective-permute-start.4) | collective-permute-done | bytes 393248 | tf_op jit(solution)/shard_map/ppermute | solution.py:24
  40.1 0.1 pad_maximum_fusion.1
  40.2 1.3 %collective-permute-start.10 = (bf16[1040,384]{1,0:T(8,128)(2,1)S(1)}, bf16[1040,384]{1,0:T(8,128)(2,1)S(1)}, u32[]{:S(2)}, u32[]{:S(2)}) collective-permute-start(bf16[1040,384]{1,0:T(8,128)(2,1)S(1)} %pad_maximum_fusion.1), channel_id=1, source_target_pairs={{1,0},{2,3},{5,4},{6,7},{9,8},{10,11},{13,12},{14,15},{17,16},{18,... | collective-permute-start | bytes 2396168 | tf_op jit(solution)/shard_map/ppermute | solution.py:24
  41.5 3.7 %collective-permute-start.5 = (bf16[512,384]{1,0:T(8,128)(2,1)S(1)}, bf16[512,384]{1,0:T(8,128)(2,1)S(1)}, u32[]{:S(2)}, u32[]{:S(2)}) collective-permute-start(bf16[512,384]{1,0:T(8,128)(2,1)S(1)} %collective-permute-done.4.rest_3_), channel_id=1, source_target_pairs={{0,4},{1,5},{4,8},{5,9},{6,2},{7,3},{8,12},{9,13},{10,6},{11,7},{1... | collective-permute-start | bytes 1179656 | tf_op jit(solution)/shard_map/ppermute | solution.py:24
  45.2 2.7 %far2.1.total_in = f32[1024,768]{1,0:T(8,128)S(1)} custom-call(s32[1]{0:T(128)} %bitcast.me_ref, bf16[768,1024]{1,0:T(8,128)(2,1)S(1)} %get-tuple-element.54.own_t, f32[1024,768]{1,0:T(8,128)S(1)} %sib.1.total_in, f32[8,768]{1,0:T(8,128)S(1)} %get-tuple-element.46.levels, f32[8,768]{1,0:T(8,128)S(1)} %get-tuple-element.47.weights, ...), custom_call_target="tpu_custom_call", output_to_operand_aliasing={{}: (2, {})} | custom-call | flops 10000000000 | bytes 1 | tf_op jit(solution)/shard_map/far2/pallas_call | solution.py:402
  47.9 2.8 %far3.1.total_in = f32[1024,768]{1,0:T(8,128)S(1)} custom-call(s32[1]{0:T(128)} %bitcast.me_ref, bf16[768,1024]{1,0:T(8,128)(2,1)S(1)} %get-tuple-element.54.own_t, f32[1024,768]{1,0:T(8,128)S(1)} %far2.1.total_in, f32[8,768]{1,0:T(8,128)S(1)} %get-tuple-element.46.levels, f32[8,768]{1,0:T(8,128)S(1)} %get-tuple-element.47.weights, ...), custom_call_target="tpu_custom_call", output_to_operand_aliasing={{}: (2, {})} | custom-call | flops 1 | bytes 1 | tf_op jit(solution)/shard_map/far3/pallas_call | solution.py:402
  50.8 1.5 %collective-permute-start.12 = (bf16[512,384]{1,0:T(8,128)(2,1)S(1)}, bf16[512,384]{1,0:T(8,128)(2,1)S(1)}, u32[]{:S(2)}, u32[]{:S(2)}) collective-permute-start(bf16[512,384]{1,0:T(8,128)(2,1)S(1)} %collective-permute-done.11.rest_0_), channel_id=1, source_target_pairs={{1,0},{2,3},{5,4},{6,7},{9,8},{10,11},{13,12},{14,15},{17,16},{18,... | collective-permute-start | bytes 1179656 | tf_op jit(solution)/shard_map/ppermute | solution.py:24
  52.3 0.1 pad_maximum_fusion.2
  52.3 3.1 %collective-permute-start.13 = (bf16[1024,384]{1,0:T(8,128)(2,1)S(1)}, bf16[1024,384]{1,0:T(8,128)(2,1)S(1)}, u32[]{:S(2)}, u32[]{:S(2)}) collective-permute-start(bf16[1024,384]{1,0:T(8,128)(2,1)S(1)} %pad_maximum_fusion.2), channel_id=1, source_target_pairs={{0,1},{3,2},{4,5},{7,6},{8,9},{11,10},{12,13},{15,14},{16,17},{19,... | collective-permute-start | bytes 2359304 | tf_op jit(solution)/shard_map/ppermute | solution.py:24
  55.5 1.3 %collective-permute-start.14 = (bf16[512,384]{1,0:T(8,128)(2,1)S(1)}, bf16[512,384]{1,0:T(8,128)(2,1)S(1)}, u32[]{:S(2)}, u32[]{:S(2)}) collective-permute-start(bf16[512,384]{1,0:T(8,128)(2,1)S(1)} %collective-permute-done.5.rest_1_), channel_id=1, source_target_pairs={{1,0},{2,3},{5,4},{6,7},{9,8},{10,11},{13,12},{14,15},{17,16},{18,... | collective-permute-start | bytes 1179656 | tf_op jit(solution)/shard_map/ppermute | solution.py:24
  56.8 2.3 %collective-permute-done.14.rest_5_ = bf16[512,384]{1,0:T(8,128)(2,1)S(1)} collective-permute-done((bf16[512,384]{1,0:T(8,128)(2,1)S(1)}, bf16[512,384]{1,0:T(8,128)(2,1)S(1)}, u32[]{:S(2)}, u32[]{:S(2)}) %collective-permute-start.14) | collective-permute-done | bytes 393248 | tf_op jit(solution)/shard_map/ppermute | solution.py:24
  59.1 6.7 %last.1 = (f32[1024,768]{1,0:T(8,128)S(1)}, f32[2,1024,384]{2,1,0:T(8,128)}, f32[1152,128]{1,0:T(8,128)S(1)}, f32[1152,128]{1,0:T(8,128)S(1)}, f32[1152,128]{1,0:T(8,128)S(1)}, /*index=5*/f32[1152,128]{1,0:T(8,128)S(1)}) custom-call(s32[1]{0:T(128)} %bitcast.me_ref, bf16[768,1024]{1,0:T(8,128)(2,1)S(1)} %get-tuple-element.54.own_t, ...), custom_call_target="tpu_custom_call", output_to_operand_aliasing={{0}: (2, {})} | custom-call | flops 1 | bytes 1 | tf_op jit(solution)/shard_map/last/pallas_call | solution.py:402
  65.8 0.2 collective-permute-start.15
  66.0 1.9 %collective-permute-done.15.theirs = f32[1152,128]{1,0:T(8,128)S(1)} collective-permute-done((f32[1152,128]{1,0:T(8,128)S(1)}, f32[1152,128]{1,0:T(8,128)S(1)}, u32[]{:S(2)}, u32[]{:S(2)}) %collective-permute-start.15) | collective-permute-done | bytes 589856 | tf_op jit(solution)/shard_map/ppermute | solution.py:24
  67.9 0.1 collective-permute-start.16
  68.0 0.2 chip.1
  68.2 0.1 collective-permute-start.17
  68.3 9.6 %collective-permute-done.17.across = s16[1216,128]{1,0:T(8,128)(2,1)S(1)} collective-permute-done((s16[1216,128]{1,0:T(8,128)(2,1)S(1)}, s16[1216,128]{1,0:T(8,128)(2,1)S(1)}, u32[]{:S(2)}, u32[]{:S(2)}) %collective-permute-start.17) | collective-permute-done | bytes 311328 | tf_op jit(solution)/shard_map/ppermute | solution.py:24
  77.9 0.2 column.1
  78.2 1.6 %collective-permute-start.18 = (s16[304,128]{1,0:T(8,128)(2,1)S(1)}, s16[304,128]{1,0:T(8,128)(2,1)S(1)}, u32[]{:S(2)}, u32[]{:S(2)}) collective-permute-start(s16[304,128]{1,0:T(8,128)(2,1)S(1)} %get-tuple-element.83), channel_id=1, source_target_pairs={{0,4},{1,5},{2,6},{3,7},{4,0},{5,1},{6,2},{7,3},{8,12},{9,13},{10,... | collective-permute-start | bytes 233480 | tf_op jit(solution)/shard_map/ppermute | solution.py:24
  79.8 2.5 %collective-permute-start.19 = (s16[304,128]{1,0:T(8,128)(2,1)S(1)}, s16[304,128]{1,0:T(8,128)(2,1)S(1)}, u32[]{:S(2)}, u32[]{:S(2)}) collective-permute-start(s16[304,128]{1,0:T(8,128)(2,1)S(1)} %get-tuple-element.84), channel_id=1, source_target_pairs={{0,8},{1,9},{2,10},{3,11},{4,12},{5,13},{6,14},{7,15},{8,0},{9,1},... | collective-permute-start | bytes 233480 | tf_op jit(solution)/shard_map/ppermute | solution.py:24
  82.3 0.3 collective-permute-start.20
  82.6 0.0 collective-permute-done.18.a
  82.6 4.9 %collective-permute-done.19.b = s16[304,128]{1,0:T(8,128)(2,1)S(1)} collective-permute-done((s16[304,128]{1,0:T(8,128)(2,1)S(1)}, s16[304,128]{1,0:T(8,128)(2,1)S(1)}, u32[]{:S(2)}, u32[]{:S(2)}) %collective-permute-start.19) | collective-permute-done | bytes 77856 | tf_op jit(solution)/shard_map/ppermute | solution.py:24
  87.6 1.0 collective-permute-done.20.c
  88.6 0.1 sum_code.1
  88.8 2.3 %collective-permute-start.23 = (s16[304,128]{1,0:T(8,128)(2,1)S(1)}, s16[304,128]{1,0:T(8,128)(2,1)S(1)}, u32[]{:S(2)}, u32[]{:S(2)}) collective-permute-start(s16[304,128]{1,0:T(8,128)(2,1)S(1)} %sum_code.1), channel_id=1, source_target_pairs={{0,12},{1,13},{2,14},{3,15},{4,8},{5,9},{6,10},{7,11},{8,4},{9,5},... | collective-permute-start | bytes 233480 | tf_op jit(solution)/shard_map/ppermute | solution.py:24
  91.1 0.4 collective-permute-start.22
  91.5 1.7 %collective-permute-start.21 = (s16[304,128]{1,0:T(8,128)(2,1)S(1)}, s16[304,128]{1,0:T(8,128)(2,1)S(1)}, u32[]{:S(2)}, u32[]{:S(2)}) collective-permute-start(s16[304,128]{1,0:T(8,128)(2,1)S(1)} %sum_code.1), channel_id=1, source_target_pairs={{0,4},{1,5},{2,6},{3,7},{4,0},{5,1},{6,2},{7,3},{8,12},{9,13},{10,... | collective-permute-start | bytes 233480 | tf_op jit(solution)/shard_map/ppermute | solution.py:24
  93.2 0.3 collective-permute-start.24
  93.5 2.0 %collective-permute-done.23 = s16[304,128]{1,0:T(8,128)(2,1)S(1)} collective-permute-done((s16[304,128]{1,0:T(8,128)(2,1)S(1)}, s16[304,128]{1,0:T(8,128)(2,1)S(1)}, u32[]{:S(2)}, u32[]{:S(2)}) %collective-permute-start.23) | collective-permute-done | bytes 77856 | tf_op jit(solution)/shard_map/ppermute | solution.py:24
  95.5 0.6 collective-permute-start.27
  96.1 1.2 %collective-permute-done.22 = s16[304,128]{1,0:T(8,128)(2,1)S(1)} collective-permute-done((s16[304,128]{1,0:T(8,128)(2,1)S(1)}, s16[304,128]{1,0:T(8,128)(2,1)S(1)}, u32[]{:S(2)}, u32[]{:S(2)}) %collective-permute-start.22) | collective-permute-done | bytes 77856 | tf_op jit(solution)/shard_map/ppermute | solution.py:24
  97.3 0.5 collective-permute-start.26
  97.8 1.5 %collective-permute-start.25 = (s16[304,128]{1,0:T(8,128)(2,1)S(1)}, s16[304,128]{1,0:T(8,128)(2,1)S(1)}, u32[]{:S(2)}, u32[]{:S(2)}) collective-permute-start(s16[304,128]{1,0:T(8,128)(2,1)S(1)} %collective-permute-done.21), channel_id=1, source_target_pairs={{0,2},{1,3},{2,0},{3,1},{4,6},{5,7},{6,4},{7,5},{8,10},{9,11},{10,... | collective-permute-start | bytes 233480 | tf_op jit(solution)/shard_map/ppermute | solution.py:24
  99.3 0.1 collective-permute-start.28
  99.4 0.5 collective-permute-done.27
  99.9 1.8 %collective-permute-done.26 = s16[304,128]{1,0:T(8,128)(2,1)S(1)} collective-permute-done((s16[304,128]{1,0:T(8,128)(2,1)S(1)}, s16[304,128]{1,0:T(8,128)(2,1)S(1)}, u32[]{:S(2)}, u32[]{:S(2)}) %collective-permute-start.26) | collective-permute-done | bytes 77856 | tf_op jit(solution)/shard_map/ppermute | solution.py:24
  101.7 0.8 collective-permute-done.25
  102.5 0.1 collective-permute-start.29
  102.6 1.6 %collective-permute-done.29.sib_b = s16[4,304,128]{2,1,0:T(8,128)(2,1)S(1)} collective-permute-done((s16[4,304,128]{2,1,0:T(8,128)(2,1)S(1)}, s16[4,304,128]{2,1,0:T(8,128)(2,1)S(1)}, u32[]{:S(2)}, u32[]{:S(2)}) %collective-permute-start.29) | collective-permute-done | bytes 311328 | tf_op jit(solution)/shard_map/ppermute | solution.py:24
  104.2 2.6 %spread.1 = f32[1024,1024]{1,0:T(8,128)} custom-call(s32[1]{0:T(128)} %bitcast.me_ref, s16[4,304,128]{2,1,0:T(8,128)(2,1)S(1)} %pad_add_fusion.a, s16[4,304,128]{2,1,0:T(8,128)(2,1)S(1)} %pad_add_fusion.1.b, s16[4,304,128]{2,1,0:T(8,128)(2,1)S(1)} %collective-permute-done.28.sib_a, s16[4,304,128]{2,1,0:T(8,128)(2,1)S(1)} %collective-permute-done.29.sib_b), custom_call_target="tpu_custom_call" | custom-call | flops 1 | bytes 1 | tf_op jit(solution)/shard_map/spread/pallas_call | solution.py:450
  (25 shorter events, 0.1 us)
Async XLA Ops:
  0.6 7.6 %copy-start.3 = (s32[16,384]{1,0:T(8,128)S(1)}, s32[16,384]{1,0:T(8,128)}, u32[]{:S(2)}) copy-start(s32[16,384]{1,0:T(8,128)} %maps_in.1) | copy-start | bytes 73732
  0.6 7.6 %copy-start.2 = (f32[8192]{0:T(1024)S(1)}, f32[8192]{0:T(1024)}, u32[]{:S(2)}) copy-start(f32[8192]{0:T(1024)} %param.8) | copy-start | bytes 98308
  0.7 7.6 %copy-start.5 = (f32[16,2]{0,1:T(2,128)S(1)}, f32[16,2]{0,1:T(2,128)}, u32[]{:S(2)}) copy-start(f32[16,2]{0,1:T(2,128)} %param.7) | copy-start | bytes 388
  1.7 7.8 %collective-permute-start.1 = (bf16[2,1024,384]{2,1,0:T(8,128)(2,1)}, bf16[2,1024,384]{2,1,0:T(8,128)(2,1)S(1)}, u32[]{:S(2)}, u32[]{:S(2)}) collective-permute-start(bf16[2,1024,384]{2,1,0:T(8,128)(2,1)} %bitcast.16), channel_id=1, source_target_pairs={{0,1},{1,0},{2,3},{3,2},{4,5},{5,4},{6,7},{7,6},{8,9},{9,8},{10,11... | collective-permute-start | bytes 4718600 | tf_op jit(solution)/shard_map/ppermute | solution.py:24
  2.2 12.8 %collective-permute-start = (bf16[528,384]{1,0:T(8,128)(2,1)S(1)}, bf16[528,384]{1,0:T(8,128)(2,1)S(1)}, u32[]{:S(2)}, u32[]{:S(2)}) collective-permute-start(bf16[528,384]{1,0:T(8,128)(2,1)S(1)} %slice_bitcast_fusion), channel_id=1, source_target_pairs={{0,2},{1,3},{2,0},{3,1},{4,6},{5,7},{6,4},{7,5},{8,10},{9,11},{10,... | collective-permute-start | bytes 1216520 | tf_op jit(solution)/shard_map/ppermute | solution.py:24
  4.8 3.4 %collective-permute-start.2 = (s32[1,3]{1,0:T(1,128)}, s32[1,3]{1,0:T(1,128)S(1)}, u32[]{:S(2)}, u32[]{:S(2)}) collective-permute-start(s32[1,3]{1,0:T(1,128)} %pairs.3), channel_id=1, source_target_pairs={{0,1},{1,0},{2,3},{3,2},{4,5},{5,4},{6,7},{7,6},{8,9},{9,8},{10,11... | collective-permute-start | bytes 44 | tf_op jit(solution)/shard_map/ppermute | solution.py:24
  5.0 1.4 %copy-start = (bf16[1,2,1024,384]{3,2,1,0:T(8,128)(2,1)S(1)}, bf16[1,2,1024,384]{3,2,1,0:T(8,128)(2,1)}, u32[]{:S(2)}) copy-start(bf16[1,2,1024,384]{3,2,1,0:T(8,128)(2,1)} %param.5) | copy-start | bytes 4718596
  6.4 0.7 copy-start.4
  7.1 2.8 %copy-start.1 = (bf16[1,2,1024,384]{3,2,1,0:T(8,128)(2,1)S(1)}, bf16[1,2,1024,384]{3,2,1,0:T(8,128)(2,1)}, u32[]{:S(2)}) copy-start(bf16[1,2,1024,384]{3,2,1,0:T(8,128)(2,1)} %param.5) | copy-start | bytes 4718596
  9.5 14.0 %collective-permute-start.3 = (bf16[512,384]{1,0:T(8,128)(2,1)S(1)}, bf16[512,384]{1,0:T(8,128)(2,1)S(1)}, u32[]{:S(2)}, u32[]{:S(2)}) collective-permute-start(bf16[512,384]{1,0:T(8,128)(2,1)S(1)} %get-tuple-element.55), channel_id=1, source_target_pairs={{0,2},{1,3},{2,0},{3,1},{4,6},{5,7},{6,4},{7,5},{8,10},{9,11},{10,... | collective-permute-start | bytes 1179656 | tf_op jit(solution)/shard_map/ppermute | solution.py:24
  15.1 16.9 %collective-permute-start.6 = (bf16[512,384]{1,0:T(8,128)(2,1)S(1)}, bf16[512,384]{1,0:T(8,128)(2,1)S(1)}, u32[]{:S(2)}, u32[]{:S(2)}) collective-permute-start(bf16[512,384]{1,0:T(8,128)(2,1)S(1)} %get-tuple-element.64), channel_id=1, source_target_pairs={{0,2},{1,3},{2,0},{3,1},{4,6},{5,7},{6,4},{7,5},{8,10},{9,11},{10,... | collective-permute-start | bytes 1179656 | tf_op jit(solution)/shard_map/ppermute | solution.py:24
  17.0 14.9 %collective-permute-start.7 = (bf16[528,384]{1,0:T(8,128)(2,1)S(1)}, bf16[528,384]{1,0:T(8,128)(2,1)S(1)}, u32[]{:S(2)}, u32[]{:S(2)}) collective-permute-start(bf16[528,384]{1,0:T(8,128)(2,1)S(1)} %collective-permute-done.rest_0_), channel_id=1, source_target_pairs={{0,4},{1,5},{4,8},{5,9},{6,2},{7,3},{8,12},{9,13},{10,6},{11,7},{1... | collective-permute-start | bytes 1216520 | tf_op jit(solution)/shard_map/ppermute | solution.py:24
  23.6 16.5 %collective-permute-start.4 = (bf16[512,384]{1,0:T(8,128)(2,1)S(1)}, bf16[512,384]{1,0:T(8,128)(2,1)S(1)}, u32[]{:S(2)}, u32[]{:S(2)}) collective-permute-start(bf16[512,384]{1,0:T(8,128)(2,1)S(1)} %get-tuple-element.59), channel_id=1, source_target_pairs={{0,2},{1,3},{2,0},{3,1},{4,6},{5,7},{6,4},{7,5},{8,10},{9,11},{10,... | collective-permute-start | bytes 1179656 | tf_op jit(solution)/shard_map/ppermute | solution.py:24
  25.4 14.6 %collective-permute-start.8 = (bf16[512,384]{1,0:T(8,128)(2,1)S(1)}, bf16[512,384]{1,0:T(8,128)(2,1)S(1)}, u32[]{:S(2)}, u32[]{:S(2)}) collective-permute-start(bf16[512,384]{1,0:T(8,128)(2,1)S(1)} %collective-permute-done.3.rest_1_.rest_4_), channel_id=1, source_target_pairs={{0,4},{1,5},{4,8},{5,9},{6,2},{7,3},{8,12},{9,13},{10,6},{11,7},{1... | collective-permute-start | bytes 1179656 | tf_op jit(solution)/shard_map/ppermute | solution.py:24
  29.0 18.9 %collective-permute-start.9 = (bf16[1040,384]{1,0:T(8,128)(2,1)S(1)}, bf16[1040,384]{1,0:T(8,128)(2,1)S(1)}, u32[]{:S(2)}, u32[]{:S(2)}) collective-permute-start(bf16[1040,384]{1,0:T(8,128)(2,1)S(1)} %pad_maximum_fusion), channel_id=1, source_target_pairs={{0,1},{3,2},{4,5},{7,6},{8,9},{11,10},{12,13},{15,14},{16,17},{19,... | collective-permute-start | bytes 2396168 | tf_op jit(solution)/shard_map/ppermute | solution.py:24
  31.9 18.8 %collective-permute-start.11 = (bf16[512,384]{1,0:T(8,128)(2,1)S(1)}, bf16[512,384]{1,0:T(8,128)(2,1)S(1)}, u32[]{:S(2)}, u32[]{:S(2)}) collective-permute-start(bf16[512,384]{1,0:T(8,128)(2,1)S(1)} %collective-permute-done.6.rest_2_), channel_id=1, source_target_pairs={{0,4},{1,5},{4,8},{5,9},{6,2},{7,3},{8,12},{9,13},{10,6},{11,7},{1... | collective-permute-start | bytes 1179656 | tf_op jit(solution)/shard_map/ppermute | solution.py:24
  40.2 7.8 %collective-permute-start.10 = (bf16[1040,384]{1,0:T(8,128)(2,1)S(1)}, bf16[1040,384]{1,0:T(8,128)(2,1)S(1)}, u32[]{:S(2)}, u32[]{:S(2)}) collective-permute-start(bf16[1040,384]{1,0:T(8,128)(2,1)S(1)} %pad_maximum_fusion.1), channel_id=1, source_target_pairs={{1,0},{2,3},{5,4},{6,7},{9,8},{10,11},{13,12},{14,15},{17,16},{18,... | collective-permute-start | bytes 2396168 | tf_op jit(solution)/shard_map/ppermute | solution.py:24
  41.5 14.0 %collective-permute-start.5 = (bf16[512,384]{1,0:T(8,128)(2,1)S(1)}, bf16[512,384]{1,0:T(8,128)(2,1)S(1)}, u32[]{:S(2)}, u32[]{:S(2)}) collective-permute-start(bf16[512,384]{1,0:T(8,128)(2,1)S(1)} %collective-permute-done.4.rest_3_), channel_id=1, source_target_pairs={{0,4},{1,5},{4,8},{5,9},{6,2},{7,3},{8,12},{9,13},{10,6},{11,7},{1... | collective-permute-start | bytes 1179656 | tf_op jit(solution)/shard_map/ppermute | solution.py:24
  50.8 4.7 %collective-permute-start.12 = (bf16[512,384]{1,0:T(8,128)(2,1)S(1)}, bf16[512,384]{1,0:T(8,128)(2,1)S(1)}, u32[]{:S(2)}, u32[]{:S(2)}) collective-permute-start(bf16[512,384]{1,0:T(8,128)(2,1)S(1)} %collective-permute-done.11.rest_0_), channel_id=1, source_target_pairs={{1,0},{2,3},{5,4},{6,7},{9,8},{10,11},{13,12},{14,15},{17,16},{18,... | collective-permute-start | bytes 1179656 | tf_op jit(solution)/shard_map/ppermute | solution.py:24
  52.3 6.7 %collective-permute-start.13 = (bf16[1024,384]{1,0:T(8,128)(2,1)S(1)}, bf16[1024,384]{1,0:T(8,128)(2,1)S(1)}, u32[]{:S(2)}, u32[]{:S(2)}) collective-permute-start(bf16[1024,384]{1,0:T(8,128)(2,1)S(1)} %pad_maximum_fusion.2), channel_id=1, source_target_pairs={{0,1},{3,2},{4,5},{7,6},{8,9},{11,10},{12,13},{15,14},{16,17},{19,... | collective-permute-start | bytes 2359304 | tf_op jit(solution)/shard_map/ppermute | solution.py:24
  55.5 3.6 %collective-permute-start.14 = (bf16[512,384]{1,0:T(8,128)(2,1)S(1)}, bf16[512,384]{1,0:T(8,128)(2,1)S(1)}, u32[]{:S(2)}, u32[]{:S(2)}) collective-permute-start(bf16[512,384]{1,0:T(8,128)(2,1)S(1)} %collective-permute-done.5.rest_1_), channel_id=1, source_target_pairs={{1,0},{2,3},{5,4},{6,7},{9,8},{10,11},{13,12},{14,15},{17,16},{18,... | collective-permute-start | bytes 1179656 | tf_op jit(solution)/shard_map/ppermute | solution.py:24
  65.8 2.1 %collective-permute-start.15 = (f32[1152,128]{1,0:T(8,128)S(1)}, f32[1152,128]{1,0:T(8,128)S(1)}, u32[]{:S(2)}, u32[]{:S(2)}) collective-permute-start(f32[1152,128]{1,0:T(8,128)S(1)} %get-tuple-element.77), channel_id=1, source_target_pairs={{0,1},{1,0},{2,3},{3,2},{4,5},{5,4},{6,7},{7,6},{8,9},{9,8},{10,11... | collective-permute-start | bytes 1769480 | tf_op jit(solution)/shard_map/ppermute | solution.py:24
  67.9 10.0 %collective-permute-start.16 = (f32[1152,128]{1,0:T(8,128)S(1)}, f32[1152,128]{1,0:T(8,128)S(1)}, u32[]{:S(2)}, u32[]{:S(2)}) collective-permute-start(f32[1152,128]{1,0:T(8,128)S(1)} %get-tuple-element.79), channel_id=1, source_target_pairs={{0,1},{1,0},{2,3},{3,2},{4,5},{5,4},{6,7},{7,6},{8,9},{9,8},{10,11... | collective-permute-start | bytes 1769480 | tf_op jit(solution)/shard_map/ppermute | solution.py:24
  68.2 9.7 %collective-permute-start.17 = (s16[1216,128]{1,0:T(8,128)(2,1)S(1)}, s16[1216,128]{1,0:T(8,128)(2,1)S(1)}, u32[]{:S(2)}, u32[]{:S(2)}) collective-permute-start(s16[1216,128]{1,0:T(8,128)(2,1)S(1)} %chip.1), channel_id=1, source_target_pairs={{0,2},{1,3},{2,0},{3,1},{4,6},{5,7},{6,4},{7,5},{8,10},{9,11},{10,... | collective-permute-start | bytes 933896 | tf_op jit(solution)/shard_map/ppermute | solution.py:24
  78.2 4.5 %collective-permute-start.18 = (s16[304,128]{1,0:T(8,128)(2,1)S(1)}, s16[304,128]{1,0:T(8,128)(2,1)S(1)}, u32[]{:S(2)}, u32[]{:S(2)}) collective-permute-start(s16[304,128]{1,0:T(8,128)(2,1)S(1)} %get-tuple-element.83), channel_id=1, source_target_pairs={{0,4},{1,5},{2,6},{3,7},{4,0},{5,1},{6,2},{7,3},{8,12},{9,13},{10,... | collective-permute-start | bytes 233480 | tf_op jit(solution)/shard_map/ppermute | solution.py:24
  79.8 7.8 %collective-permute-start.19 = (s16[304,128]{1,0:T(8,128)(2,1)S(1)}, s16[304,128]{1,0:T(8,128)(2,1)S(1)}, u32[]{:S(2)}, u32[]{:S(2)}) collective-permute-start(s16[304,128]{1,0:T(8,128)(2,1)S(1)} %get-tuple-element.84), channel_id=1, source_target_pairs={{0,8},{1,9},{2,10},{3,11},{4,12},{5,13},{6,14},{7,15},{8,0},{9,1},... | collective-permute-start | bytes 233480 | tf_op jit(solution)/shard_map/ppermute | solution.py:24
  82.3 6.3 %collective-permute-start.20 = (s16[304,128]{1,0:T(8,128)(2,1)S(1)}, s16[304,128]{1,0:T(8,128)(2,1)S(1)}, u32[]{:S(2)}, u32[]{:S(2)}) collective-permute-start(s16[304,128]{1,0:T(8,128)(2,1)S(1)} %get-tuple-element.85), channel_id=1, source_target_pairs={{0,12},{1,13},{2,14},{3,15},{4,8},{5,9},{6,10},{7,11},{8,4},{9,5},... | collective-permute-start | bytes 233480 | tf_op jit(solution)/shard_map/ppermute | solution.py:24
  88.8 6.7 %collective-permute-start.23 = (s16[304,128]{1,0:T(8,128)(2,1)S(1)}, s16[304,128]{1,0:T(8,128)(2,1)S(1)}, u32[]{:S(2)}, u32[]{:S(2)}) collective-permute-start(s16[304,128]{1,0:T(8,128)(2,1)S(1)} %sum_code.1), channel_id=1, source_target_pairs={{0,12},{1,13},{2,14},{3,15},{4,8},{5,9},{6,10},{7,11},{8,4},{9,5},... | collective-permute-start | bytes 233480 | tf_op jit(solution)/shard_map/ppermute | solution.py:24
  91.1 6.2 %collective-permute-start.22 = (s16[304,128]{1,0:T(8,128)(2,1)S(1)}, s16[304,128]{1,0:T(8,128)(2,1)S(1)}, u32[]{:S(2)}, u32[]{:S(2)}) collective-permute-start(s16[304,128]{1,0:T(8,128)(2,1)S(1)} %sum_code.1), channel_id=1, source_target_pairs={{0,8},{1,9},{2,10},{3,11},{4,12},{5,13},{6,14},{7,15},{8,0},{9,1},... | collective-permute-start | bytes 233480 | tf_op jit(solution)/shard_map/ppermute | solution.py:24
  91.5 6.3 %collective-permute-start.21 = (s16[304,128]{1,0:T(8,128)(2,1)S(1)}, s16[304,128]{1,0:T(8,128)(2,1)S(1)}, u32[]{:S(2)}, u32[]{:S(2)}) collective-permute-start(s16[304,128]{1,0:T(8,128)(2,1)S(1)} %sum_code.1), channel_id=1, source_target_pairs={{0,4},{1,5},{2,6},{3,7},{4,0},{5,1},{6,2},{7,3},{8,12},{9,13},{10,... | collective-permute-start | bytes 233480 | tf_op jit(solution)/shard_map/ppermute | solution.py:24
  93.2 6.2 %collective-permute-start.24 = (s16[304,128]{1,0:T(8,128)(2,1)S(1)}, s16[304,128]{1,0:T(8,128)(2,1)S(1)}, u32[]{:S(2)}, u32[]{:S(2)}) collective-permute-start(s16[304,128]{1,0:T(8,128)(2,1)S(1)} %sum_code.1), channel_id=1, source_target_pairs={{0,2},{1,3},{2,0},{3,1},{4,6},{5,7},{6,4},{7,5},{8,10},{9,11},{10,... | collective-permute-start | bytes 233480 | tf_op jit(solution)/shard_map/ppermute | solution.py:24
  95.5 4.4 %collective-permute-start.27 = (s16[304,128]{1,0:T(8,128)(2,1)S(1)}, s16[304,128]{1,0:T(8,128)(2,1)S(1)}, u32[]{:S(2)}, u32[]{:S(2)}) collective-permute-start(s16[304,128]{1,0:T(8,128)(2,1)S(1)} %collective-permute-done.23), channel_id=1, source_target_pairs={{0,2},{1,3},{2,0},{3,1},{4,6},{5,7},{6,4},{7,5},{8,10},{9,11},{10,... | collective-permute-start | bytes 233480 | tf_op jit(solution)/shard_map/ppermute | solution.py:24
  97.3 4.4 %collective-permute-start.26 = (s16[304,128]{1,0:T(8,128)(2,1)S(1)}, s16[304,128]{1,0:T(8,128)(2,1)S(1)}, u32[]{:S(2)}, u32[]{:S(2)}) collective-permute-start(s16[304,128]{1,0:T(8,128)(2,1)S(1)} %collective-permute-done.22), channel_id=1, source_target_pairs={{0,2},{1,3},{2,0},{3,1},{4,6},{5,7},{6,4},{7,5},{8,10},{9,11},{10,... | collective-permute-start | bytes 233480 | tf_op jit(solution)/shard_map/ppermute | solution.py:24
  97.8 4.7 %collective-permute-start.25 = (s16[304,128]{1,0:T(8,128)(2,1)S(1)}, s16[304,128]{1,0:T(8,128)(2,1)S(1)}, u32[]{:S(2)}, u32[]{:S(2)}) collective-permute-start(s16[304,128]{1,0:T(8,128)(2,1)S(1)} %collective-permute-done.21), channel_id=1, source_target_pairs={{0,2},{1,3},{2,0},{3,1},{4,6},{5,7},{6,4},{7,5},{8,10},{9,11},{10,... | collective-permute-start | bytes 233480 | tf_op jit(solution)/shard_map/ppermute | solution.py:24
  99.3 3.3 %collective-permute-start.28 = (s16[4,304,128]{2,1,0:T(8,128)(2,1)S(1)}, s16[4,304,128]{2,1,0:T(8,128)(2,1)S(1)}, u32[]{:S(2)}, u32[]{:S(2)}) collective-permute-start(s16[4,304,128]{2,1,0:T(8,128)(2,1)S(1)} %pad_add_fusion.a), channel_id=1, source_target_pairs={{0,1},{1,0},{2,3},{3,2},{4,5},{5,4},{6,7},{7,6},{8,9},{9,8},{10,11... | collective-permute-start | bytes 933896 | tf_op jit(solution)/shard_map/ppermute | solution.py:24
  102.5 1.7 %collective-permute-start.29 = (s16[4,304,128]{2,1,0:T(8,128)(2,1)S(1)}, s16[4,304,128]{2,1,0:T(8,128)(2,1)S(1)}, u32[]{:S(2)}, u32[]{:S(2)}) collective-permute-start(s16[4,304,128]{2,1,0:T(8,128)(2,1)S(1)} %pad_add_fusion.1.b), channel_id=1, source_target_pairs={{0,1},{1,0},{2,3},{3,2},{4,5},{5,4},{6,7},{7,6},{8,9},{9,8},{10,11... | collective-permute-start | bytes 933896 | tf_op jit(solution)/shard_map/ppermute | solution.py:24

commit v5 on v4

--- a/solution.py
+++ b/solution.py
@@ -34,11 +34,6 @@
     return move(x, [(a, b) for a, b in route if b in devices])
 
 
-def to_sibling(x, kind):
-    devices = range(lax.axis_size("dom"))
-    return move(x, [(d, d ^ 1) for d in devices if ((d >> 1) ^ d) & 1 == kind])
-
-
 def begin(copies, sem, at=0):
     started = [pltpu.make_async_copy(a, b, sem.at[at + i]) for i, (a, b) in enumerate(copies)]
     for copy in started:
@@ -61,7 +56,7 @@
 
 
 OWN, SIB, Y, Z, X = range(5)
-STEPS = (((OWN, 0), (OWN, 1)), ((SIB, 0), (SIB, 1)), ((Y, 0), (Z, 0)), ((X, 0), (Y, 1)), ((Z, 1), (X, 1)))
+STEPS = (((OWN, 0), (OWN, 1)), ((SIB, 0), (SIB, 1)), ((Y, 0), (Y, 1)), ((Z, 0), (X, 0)), ((Z, 1), (X, 1)))
 
 
 def prep_kernel(blocks, me_ref, pairs, sib_pairs, occ_in, energy_in, maps_in, levels, weights, sem, occ, energy, maps):
@@ -99,7 +94,7 @@
                     weights[step:step + 1, at] = jnp.full((1, virt), -count.astype(F32), F32)
 
 
-def add_pair(own_t, other, amp, total, own_level, level, weight, first, halves=None):
+def add_pair(own_t, other, amp, total, own_level, level, weight, first, halves=None, near=None):
     wide = own_t.shape[0]
     for t in range(0, wide, BLOCK):
         s = pl.ds(t, BLOCK)
@@ -109,7 +104,7 @@
         s = pl.ds(t, BLOCK)
         part = lax.dot_general(other[...], amp[s, :], NT, preferred_element_type=F32)
         value = part if first else total[:, s] + part
-        total[:, s] = value
+        total[:, s] = value if near is None else value + near[:, s]
         if halves is not None:
             high = value.astype(BF16)
             halves[0][:, s] = high
@@ -130,7 +125,7 @@
     finish(copies)
 
 
-def own_kernel(own, levels, weights, own_t, total, sem, own_s, amp):
+def own_kernel(own, levels, weights, own_t, own_s, total, sem, amp):
     virt = own.shape[2]
     copies = begin([(own.at[j], own_s.at[:, pl.ds(j * virt, virt)]) for j in range(2)], sem)
     level = levels[...].T
@@ -148,68 +143,104 @@
 
 
 def fetch(plan, step, me, refs, other):
-    parity, core, _ = place_of(me)
-    along_y = (parity ^ core) == 1
     counts = []
     for side, (rows, (name, at)) in enumerate(plan):
         virt = other.shape[1] // 2
-        columns = slice(side * virt, (side + 1) * virt)
-
-        def copy(ref_name, first, n, to):
-            other[to:to + n, columns] = refs[ref_name][first:first + n, :]
-
         for source, first, n, to in rows:
-            if isinstance(source, str):
-                copy(source, first, n, to)
-            else:
-                pl.when(along_y)(functools.partial(copy, source[0][0], source[0][1], n, to))
-                pl.when(jnp.logical_not(along_y))(functools.partial(copy, source[1][0], source[1][1], n, to))
-        if isinstance(name, str):
-            listed = refs[name][at:at + PAD, :].astype(F32)
-        else:
-            listed = jnp.where(
-                along_y, refs[name[0]][at:at + PAD, :].astype(F32), refs[name[1]][at:at + PAD, :].astype(F32)
-            )
+            other[to:to + n, side * virt:(side + 1) * virt] = refs[source][first:first + n, :]
         wanted = -offsets_of(me)[STEPS[step][side][0]]
-        hits = jnp.where(listed[0:1, :] == wanted.astype(F32), 1.0, 0.0)
+        hits = jnp.where(refs[name][at:at + PAD, :].astype(F32)[0:1, :] == wanted.astype(F32), 1.0, 0.0)
         counts.append(jnp.broadcast_to(jnp.sum(hits, axis=1, keepdims=True), (1, virt)))
     return jnp.concatenate(counts, axis=1)
 
 
-def far_kernel(plan, names, step, me_ref, own_t, total_in, levels, weights, *rest):
+def first_far_kernel(plan, names, step, me_ref, own_t, levels, weights, *rest):
+    refs = dict(zip(names, rest))
+    total, other, amp = rest[len(names):]
+    weight = weights[step:step + 1, :] - fetch(plan, step, me_ref[0], refs, other)
+    add_pair(own_t, other, amp, total, levels[...].T, levels[step:step + 1, :], weight, True)
+
+
+def far_kernel(plan, names, step, me_ref, own_t, levels, weights, total_in, *rest):
     refs = dict(zip(names, rest))
     total, other, amp = rest[len(names):]
     weight = weights[step:step + 1, :] - fetch(plan, step, me_ref[0], refs, other)
     add_pair(own_t, other, amp, total, levels[...].T, levels[step:step + 1, :], weight, False)
 
 
-def last_kernel(plan, names, step, me_ref, own_t, total_in, levels, weights, own, *rest):
-    refs = dict(zip(names, rest))
-    total, residual, *quarters, sem, other, amp, own_s, high, low, packed = rest[len(names):]
-    me = me_ref[0]
-    parity, core, _ = place_of(me)
-    virt = own.shape[2]
-    a, b = pl.ds(0, virt), pl.ds(virt, virt)
-    for j, at in enumerate((a, b)):
-        own_s[:, at] = own[j]
-    weight = weights[step:step + 1, :] - fetch(plan, step, me, refs, other)
-    add_pair(own_t, other, amp, total, levels[...].T, levels[step:step + 1, :], weight, False, (high, low))
-    outs = begin([(total.at[:, a], residual.at[0]), (total.at[:, b], residual.at[1])], sem)
-    at = 0
-    for q in range(0, total.shape[0], BLOCK):
+def near_metric_kernel(me_ref, total, own_s, keep, away, *rest):
+    *sends, high, low, packed = rest
+    parity, core, _ = place_of(me_ref[0])
+    high[...] = total[...].astype(BF16)
+    low[...] = (total[...] - high[...].astype(F32)).astype(BF16)
+    aux = total.shape[0]
+    half, quarter = aux // 2, aux // 4
+    plane = packed.shape[0] // 2
+    square = plane - half // LANES * quarter
+    for q in range(0, aux, BLOCK):
         rows = q + BLOCK
         slab = own_s[q:q + BLOCK, :]
         block = lax.dot_general(high[:rows, :], slab, NT, preferred_element_type=F32)
         block += lax.dot_general(low[:rows, :], slab, NT, preferred_element_type=F32)
+        for c in range(q, q + BLOCK, LANES):
+            column = block[:, c - q:c - q + LANES]
+            base, side = (half, 1) if c >= half else (0, 0)
+            k = (c - base) // LANES
+            at = side * plane + k * (k + 1) // 2 * LANES
+            packed[at:at + (k + 1) * LANES, :] = column[base:c + LANES, :]
+            if side:
+                for s in range(2):
+                    at = s * plane + square + k * quarter
+                    packed[at:at + quarter, :] = column[s * quarter:(s + 1) * quarter, :]
+    size = plane // 2
+
+    def part(side, which):
+        return packed[pl.ds(pl.multiple_of((2 * side + which) * size, 16), size), :]
+
+    keep[...] = part(parity, core)
+    away[...] = part(1 - parity, core)
+    given = [part(1 - parity, 1 - core), part(parity, 1 - core)]
+    piece = size // 4
+    for send, x in zip(sends, given):
+        for t in range(4):
+            encode(x[t * piece:(t + 1) * piece, :], send, t * (piece + PAD))
+
+
+def last_kernel(plan, names, step, me_ref, own_t, levels, weights, total_in, own_s, near, *rest):
+    refs = dict(zip(names, rest))
+    total, residual, keep, send, sem, other, amp, high, low, packed = rest[len(names):]
+    me = me_ref[0]
+    parity, core, _ = place_of(me)
+    aux, wide = total.shape
+    virt = wide // 2
+    weight = weights[step:step + 1, :] - fetch(plan, step, me, refs, other)
+    add_pair(own_t, other, amp, total, levels[...].T, levels[step:step + 1, :], weight, False, (high, low), near)
+    copies = begin([(total.at[:, pl.ds(j * virt, virt)], residual.at[j]) for j in range(2)], sem)
+    half, quarter = aux // 2, aux // 4
+
+    def both(first, n, q):
+        rows, columns = pl.ds(pl.multiple_of(first, 16), n), pl.ds(pl.multiple_of(q, 16), BLOCK)
+        pairs = ((high, own_s), (low, own_s), (own_s, high), (own_s, low))
+        return sum(
+            lax.dot_general(a[rows, :], b[columns, :], NT, preferred_element_type=F32) for a, b in pairs
+        )
+
+    at = 0
+    for q in range(0, half, BLOCK):
+        block = both(parity * half, q + BLOCK, parity * half + q)
         for c in range(0, BLOCK, LANES):
             upper = q + c + LANES
             packed[at:at + upper, :] = block[:upper, c:c + LANES]
             at += upper
-    size = quarters[0].shape[0]
-    where = ((core, 1 - parity), (core, parity), (1 - core, 1 - parity), (1 - core, parity))
-    for out, (half, side) in zip(quarters, where):
-        out[...] = packed[pl.ds(pl.multiple_of((2 * half + side) * size, 16), size), :]
-    finish(outs)
+    for q in range(half, aux, BLOCK):
+        block = both(parity * quarter, quarter, q)
+        for c in range(0, BLOCK, LANES):
+            packed[at:at + quarter, :] = block[:, c:c + LANES]
+            at += quarter
+    size = keep.shape[0]
+    keep[...] = packed[pl.ds(pl.multiple_of(core * size, 16), size), :]
+    send[...] = packed[pl.ds(pl.multiple_of((1 - core) * size, 16), size), :]
+    finish(copies)
 
 
 def encode(x, out, row):
@@ -234,20 +265,21 @@
     )
 
 
-def chip_kernel(mine, theirs, send):
-    piece = mine.shape[0] // 4
+def chip_kernel(keep_in, away, got_away, got_keep, keep, send):
+    piece = keep.shape[0] // 4
     for t in range(4):
-        at = pl.ds(t * piece, piece)
-        encode(mine[at, :] + theirs[at, :], send, t * (piece + PAD))
-
-
-def column_kernel(me_ref, mine, theirs, across, keep, *sends):
+        at, coded = pl.ds(t * piece, piece), pl.ds(t * (piece + PAD), piece + PAD)
+        encode(away[at, :] + decode(got_away[coded, :]), send, t * (piece + PAD))
+        keep[at, :] = keep_in[at, :] + decode(got_keep[coded, :])
+
+
+def column_kernel(me_ref, mine, theirs, near, across, keep, *sends):
     _, _, z = place_of(me_ref[0])
     piece = keep.shape[0]
     for t in range(4):
         at = pl.ds(pl.multiple_of((z ^ t) * piece, 16), piece)
         coded = across[pl.ds(pl.multiple_of((z ^ t) * (piece + PAD), 16), piece + PAD), :]
-        value = mine[at, :] + theirs[at, :] + decode(coded)
+        value = (mine[at, :] + theirs[at, :]) + (near[at, :] + decode(coded))
         if t:
             encode(value, sends[t - 1], 0)
         else:
@@ -269,19 +301,34 @@
 def spread_kernel(me_ref, a, b, sib_a, sib_b, out, sem, packed, square):
     parity, core, z = place_of(me_ref[0])
     rows = a.shape[1] - PAD
-    for src, half, side in ((a, core, parity), (b, core, 1 - parity), (sib_a, 1 - core, parity), (sib_b, 1 - core, 1 - parity)):
+    aux = out.shape[1]
+    half, quarter = aux // 2, aux // 4
+    plane = packed.shape[0] // 2
+    sources = ((a, core, parity), (b, core, 1 - parity), (sib_a, 1 - core, parity), (sib_b, 1 - core, 1 - parity))
+    for src, which, side in sources:
         for t in range(4):
-            row = ((half * 2 + side) * 4 + (z ^ t)) * rows
+            row = ((side * 2 + which) * 4 + (z ^ t)) * rows
             packed[pl.ds(pl.multiple_of(row, 16), rows), :] = decode(src[t])
+    for side in range(2):
+        at = side * plane + plane - half // LANES * quarter
+        for c in range(half, aux, LANES):
+            first = side * quarter
+            square[first:first + quarter, c:c + LANES] = packed[at:at + quarter, :]
+            for r in range(0, quarter, LANES):
+                square[c:c + LANES, first + r:first + r + LANES] = packed[at + r:at + r + LANES, :].T
+            at += quarter
     copies = []
-    at = packed.shape[0]
-    for c in range(out.shape[1] - LANES, -1, -LANES):
-        at -= c + LANES
-        square[0:c + LANES, c:c + LANES] = packed[at:at + c + LANES, :]
-        for r in range(0, c, LANES):
-            square[c:c + LANES, r:r + LANES] = packed[at + r:at + r + LANES, :].T
-        done = pl.ds(c, LANES)
-        copies += begin([(square.at[done], out.at[done])], sem, len(copies))
+    for side in range(2):
+        at = side * plane + plane - half // LANES * quarter
+        base = side * half
+        for c in range(half - LANES, -1, -LANES):
+            at -= c + LANES
+            columns = slice(base + c, base + c + LANES)
+            square[base:base + c + LANES, columns] = packed[at:at + c + LANES, :]
+            for r in range(0, c, LANES):
+                square[columns, base + r:base + r + LANES] = packed[at + r:at + r + LANES, :].T
+            done = pl.ds(base + c, LANES)
+            copies += begin([(square.at[done], out.at[done])], sem, len(copies))
     finish(copies)
 
 
@@ -344,9 +391,10 @@
         [dma(3), pltpu.VMEM((orbitals, blocks), F32), pltpu.VMEM(energy.shape, F32), pltpu.VMEM(domain_map.shape, I32)],
     )(me, pair_blocks, sib_pairs, occ_energy.T, energy, domain_map)
     sib, near_own = lax.optimization_barrier((sib, own))
-    own_t, total = kernel(
-        own_kernel, "own", [hbm, vmem, vmem], (jax.ShapeDtypeStruct((wide, aux), BF16), total_t), (vmem, vmem),
-        [dma(2), slab_s, amp_s], LARGE_LIMIT, flops=int(2e10),
+    own_t, own_s, total = kernel(
+        own_kernel, "own", [hbm, vmem, vmem],
+        (jax.ShapeDtypeStruct((wide, aux), BF16), jax.ShapeDtypeStruct((aux, wide), BF16), total_t), (vmem,) * 3,
+        [dma(2), amp_s], LARGE_LIMIT, flops=int(2e10),
     )(near_own, levels, weights)
     sib, part = lax.optimization_barrier((sib, parts[1]))
     y.append(swapped(part, 2))
@@ -367,70 +415,73 @@
     y[-2], z[0] = lax.optimization_barrier((y[-2], z[0]))
     z.append(forwarded(y[-2]))
 
+    y[-2], near = lax.optimization_barrier((y[-2], total))
+    keep, away, *sends = kernel(
+        near_metric_kernel, "near_metric", [smem, vmem, vmem], (plain(upper // 4),) * 2 + (coded(4 * (piece + PAD)),) * 2,
+        (vmem,) * 4, [slab_s, slab_s, pltpu.VMEM((upper, LANES), F32)], LARGE_LIMIT, flops=int(1e10),
+    )(me, near, own_s)
+    got = [swapped(send, 1) for send in sends]
+    y[-1], *got = lax.optimization_barrier((y[-1], *got))
+    z.append(forwarded(y[-1]))
+    keep, send = kernel(
+        chip_kernel, "chip", [vmem] * 4, (plain(upper // 4), coded(4 * (piece + PAD))), (vmem, vmem),
+    )(keep, away, *got)
+    across = swapped(send, 2)
+    y[-1], own_t, keep = lax.optimization_barrier((y[-1], own_t, keep))
+
+    gives_y = ((me[0] >> 1) ^ me[0]) & 1 == 0
+
+    def given(rows_y, rows_z):
+        return swapped(jnp.where(gives_y, jnp.concatenate(rows_y), jnp.concatenate(rows_z)), 1)
+
     arrays = {f"y{i}": part for i, part in enumerate(y)}
     arrays |= {f"z{i}": part for i, part in enumerate(z)}
-    arrays["sy0"] = to_sibling(jnp.concatenate(y[:PER]), 0)
-    arrays["sz0"] = to_sibling(jnp.concatenate(z[:PER]), 1)
-
-    def own_core(name, j):
-        rows = [(f"{name}{i}", 0, n, to) for i, (k, to, n) in enumerate(places) if k == j]
-        return rows, (f"{name}1", places[1][2])
-
-    def other_core(j):
-        rows = []
-        for h, (_, to, n) in enumerate(places[j * PER:(j + 1) * PER]):
-            if not j:
-                at = to + (PAD if h > 1 else 0)
-                rows.append(((("sy0", at), ("sz0", at)), 0, n, to))
-            elif h < PER - 1:
-                rows.append(((("sy1", to), ("sz1", to)), 0, n, to))
-            else:
-                rows.append(((("sy1", to), ("sz2", 0)), 0, n, to))
-        return rows, (("sy0", "sz0"), places[0][2] + places[1][2])
-
-    def names_in(plan):
-        names = []
-        for rows, (name, _) in plan:
-            for source in [r[0] for r in rows]:
-                names += [source] if isinstance(source, str) else [n for n, _ in source]
-            names += [name] if isinstance(name, str) else name
-        return list(dict.fromkeys(names))
-
-    def pair_step(body, name, step, given=(), outs=(), out_specs=(), scratch=(), flops=1):
-        plan = [other_core(j) if which == X else own_core("y" if which == Y else "z", j) for which, j in STEPS[step]]
-        names = names_in(plan)
+    arrays["x0"] = given(y[:PER], z[:PER])
+
+    def half_of(which, j):
+        name = "y" if which == Y else "z"
+        if which != X:
+            rows = [(f"{name}{i}", 0, n, to) for i, (k, to, n) in enumerate(places) if k == j]
+            return rows, (f"{name}1", places[1][2])
+        if j:
+            cut = places[-1][1]
+            rows = [("x1", 0, cut // 2, 0), ("x2", 0, cut // 2, cut // 2), ("x3", 0, aux - cut, cut)]
+        else:
+            cut = places[0][2] + places[1][2]
+            rows = [("x0", 0, cut, 0)] + ([("x0", cut + PAD, aux - cut, cut)] if cut < aux else [])
+        return rows, ("x0", places[0][2] + places[1][2])
+
+    def pair_step(body, name, step, before=(), outs=(), out_specs=(), scratch=(), flops=1):
+        plan = [half_of(*half) for half in STEPS[step]]
+        names = list(dict.fromkeys(n for rows, (at, _) in plan for n in [r[0] for r in rows] + [at]))
         return kernel(
             functools.partial(body, plan, names, step), name,
-            [smem] + [vmem] * (4 + len(given) + len(names)),
-            (total_t, *outs), (vmem, *out_specs), scratch, LARGE_LIMIT, {2: 0}, flops,
-        )(me, own_t, total, levels, weights, *given, *[arrays[n] for n in names])
-
-    z.append(forwarded(y[-1]))
-    y[-1], total = lax.optimization_barrier((y[-1], total))
-    arrays[f"y{count - 1}"] = y[-1]
-    (total,) = pair_step(far_kernel, "far2", 2, scratch=[slab_s, amp_s], flops=int(1e10))
-    (total,) = pair_step(far_kernel, "far3", 3, scratch=[slab_s, amp_s], flops=1)
-    total, *late = lax.optimization_barrier((total, *y[PER:], *z[PER:-1]))
-    y[PER:], z[PER:-1] = late[:PER], late[PER:]
-    arrays["sy1"] = to_sibling(jnp.concatenate(y[PER:]), 0)
-    arrays["sz1"] = to_sibling(jnp.concatenate(z[PER:-1]), 1)
-    z[-1], total, arrays["sz1"] = lax.optimization_barrier((z[-1], total, arrays["sz1"]))
-    arrays["sz2"] = to_sibling(z[-1], 1)
-    arrays |= {f"z{i}": part for i, part in enumerate(z)}
-    _, residual, *quarters = pair_step(
-        last_kernel, "last", 4, (own,),
-        (jax.ShapeDtypeStruct(own.shape, F32),) + (plain(upper // 4),) * 4, (hbm,) + (vmem,) * 4,
-        [dma(2), slab_s, amp_s, slab_s, slab_s, slab_s, pltpu.VMEM((upper, LANES), F32)],
+            [smem] + [vmem] * (3 + len(before) + len(names)),
+            (total_t, *outs), (vmem, *out_specs), scratch, LARGE_LIMIT, {4: 0} if before else {}, flops,
+        )(me, own_t, levels, weights, *before, *[arrays[n] for n in names])
+
+    (total,) = pair_step(first_far_kernel, "far2", 2, scratch=[slab_s, amp_s], flops=int(1e10))
+    (total,) = pair_step(far_kernel, "far3", 3, (total,), scratch=[slab_s, amp_s], flops=1)
+    total, *late = lax.optimization_barrier((total, *y[PER:-1], *z[PER:-1]))
+    early = [jnp.where(gives_y, a, b) for a, b in zip(late[:PER - 1], late[PER - 1:])]
+    early = jnp.concatenate(early)
+    middle = early.shape[0] // 2
+    arrays["x1"], arrays["x2"] = swapped(early[:middle], 1), swapped(early[middle:], 1)
+    z[-1], total, arrays["x1"], arrays["x2"], across = lax.optimization_barrier(
+        (z[-1], total, arrays["x1"], arrays["x2"], across)
     )
-
-    got = swapped(quarters[2], 1)
-    got, send = lax.optimization_barrier((got, quarters[3]))
-    got_own = swapped(send, 1)
-    send = kernel(chip_kernel, "chip", [vmem, vmem], coded(4 * (piece + PAD)), vmem)(quarters[0], got)
-    across = swapped(send, 2)
+    arrays[f"z{count - 1}"] = z[-1]
+    arrays["x3"] = given(y[-1:], z[-1:])
+    _, residual, mine, send = pair_step(
+        last_kernel, "last", 4, (total, own_s, near),
+        (jax.ShapeDtypeStruct(own.shape, F32), plain(upper // 4), plain(upper // 4)), (hbm, vmem, vmem),
+        [dma(2), slab_s, amp_s, slab_s, slab_s, pltpu.VMEM((upper // 2, LANES), F32)],
+    )
+
+    got = swapped(send, 1)
     keep, *sends = kernel(
-        column_kernel, "column", [smem, vmem, vmem, vmem], (plain(piece),) + (coded(piece + PAD),) * 3, (vmem,) * 4,
-    )(me, quarters[1], got_own, across)
+        column_kernel, "column", [smem] + [vmem] * 4, (plain(piece),) + (coded(piece + PAD),) * 3, (vmem,) * 4,
+    )(me, mine, got, keep, across)
     got = [swapped(send, 4 * t) for t, send in zip((1, 2, 3), sends)]
     if blocks == 16:
         mine = kernel(

time: 107 us -> 101 us (0.944)
  waiting for transfers between devices: 35.6 us -> 25.2 us
  Pallas kernels: 23.8 us -> 30.5 us
  starting transfers between devices: 42.9 us -> 36.7 us
  other arithmetic: 0.3 us -> 2.48 us
  local copies, waits for them, and re-layouts: 3.14 us -> 4.39 us
    ppermute x30, waiting for transfers between devices: 35.6 us -> 25.2 us  [move(): return lax.ppermute(x, 'dom', pairs)]
    ppermute x30, starting transfers between devices: 42.9 us -> 36.7 us  [move(): return lax.ppermute(x, 'dom', pairs)]
    pallas_call x2 -> x3, Pallas kernels: 0.44 us -> 5.19 us  [the longest x1 3.51 us: shards(): kernel(near_metric_kernel, 'near_metric', [smem, vmem, vmem], (plain(uppe...]
    select_n x0 -> x3, other arithmetic: none -> 2.43 us  [the longest x2 2.36 us: given(): jnp.where(gives_y, jnp.concatenate(rows_y), jnp.concatenate(rows_z))]
    unnamed x12 -> x42, local copies, waits for them, and re-layouts: 2.08 us -> 3.28 us
  transfers between devices with their start and end apart: 30 -> 30, of which waited for: 14 -> 14; matrix products, arithmetic and copies ran while one was open for 0% -> 1% of each run, Pallas kernels for 13% -> 20%
where the time goes in v5:
time: 101 us; the launch traced here: 100 us
  starting transfers between devices  36.7 us (36%)
  Pallas kernels  30.5 us (30%)
  waiting for transfers between devices  25.2 us (25%)
  local copies, waits for them, and re-layouts  4.39 us (4%)
  other arithmetic  2.48 us (2%)
  between operations  1.24 us (1%)
    ppermute x30, starting transfers between devices, move(): return lax.ppermute(x, 'dom', pairs)  36.7 us
    ppermute x30, waiting for transfers between devices, move(): return lax.ppermute(x, 'dom', pairs)  25.2 us
    pallas_call x3, Pallas kernels, pair_step(): kernel(functools.partial(body, plan, names, step), name, [smem] + [vmem]...  13.2 us
    pallas_call x1, Pallas kernels, shards(): kernel(near_metric_kernel, 'near_metric', [smem, vmem, vmem], (plain(uppe...  3.51 us
    unnamed x42, local copies, waits for them, and re-layouts  3.28 us
    pallas_call x1, Pallas kernels, shards(): kernel(own_kernel, 'own', [hbm, vmem, vmem], (jax.ShapeDtypeStruct((wide,...  3.01 us
    pallas_call x1, Pallas kernels, shards(): kernel(sib_kernel, 'sib', [vmem, vmem, hbm, vmem, vmem], total_t, vmem, [...  2.97 us
    pallas_call x1, Pallas kernels, shards(): kernel(spread_kernel, 'spread', [smem] + [vmem] * 4, jax.ShapeDtypeStruct...  2.81 us
  transfers between devices with their start and end apart: 30, of which 14 were waited for; matrix products, arithmetic and copies ran while one was open for 1% of the time, Pallas kernels for 20%

profile of v5, /device:TPU:0, one launch (start us, length us, event | category | flops | bytes accessed | tf_op | source)
XLA Modules:
  0.0 100.4 jit_solution(18052983924629723017)
XLA Ops:
  0.7 1.1 %slice_bitcast_fusion = bf16[528,384]{1,0:T(8,128)(2,1)S(1)} fusion(bf16[2,1024,384]{2,1,0:T(8,128)(2,1)} %bitcast.15), kind=kLoop, calls=%fused_computation.1 | loop fusion | bytes 811008 | tf_op jit(solution)/shard_map/squeeze | solution.py:376
  1.7 0.5 collective-permute-start
  2.3 2.6 %collective-permute-start.2 = (bf16[528,384]{1,0:T(8,128)(2,1)S(1)}, bf16[528,384]{1,0:T(8,128)(2,1)S(1)}, u32[]{:S(2)}, u32[]{:S(2)}) collective-permute-start(bf16[528,384]{1,0:T(8,128)(2,1)S(1)} %slice_bitcast_fusion), channel_id=1, source_target_pairs={{0,2},{1,3},{2,0},{3,1},{4,6},{5,7},{6,4},{7,5},{8,10},{9,11},{10,... | collective-permute-start | bytes 1216520 | tf_op jit(solution)/shard_map/ppermute | solution.py:24
  4.9 0.2 collective-permute-start.3
  5.0 1.4 %copy-done.2 = bf16[1,2,1024,384]{3,2,1,0:T(8,128)(2,1)S(1)} copy-done((bf16[1,2,1024,384]{3,2,1,0:T(8,128)(2,1)S(1)}, bf16[1,2,1024,384]{3,2,1,0:T(8,128)(2,1)}, u32[]{:S(2)}) %copy-start.2) | copy-done | bytes 1572888
  6.4 0.7 copy-done.16
  7.1 1.9 %split.1 = (bf16[512,384]{1,0:T(8,128)(2,1)S(1)}, bf16[512,384]{1,0:T(8,128)(2,1)S(1)}, bf16[512,384]{1,0:T(8,128)(2,1)}) custom-call(s32[1]{0:T(128)} %bitcast.me_ref, s32[1,3]{1,0:T(1,128)S(1)} %copy-done.16, bf16[2,1024,384]{2,1,0:T(8,128)(2,1)S(1)} %bitcast.17), custom_call_target="tpu_custom_call" | custom-call | flops 1 | bytes 1 | tf_op jit(solution)/shard_map/split/pallas_call | solution.py:381
  9.0 1.3 %prep.1 = (f32[8,768]{1,0:T(8,128)S(1)}, f32[8,768]{1,0:T(8,128)S(1)}) custom-call(s32[1]{0:T(128)} %bitcast.me_ref, s32[1,3]{1,0:T(1,128)S(1)} %copy-done.17, s32[1,3]{1,0:T(1,128)S(1)} %collective-permute-done.3.sib_pairs, f32[2,16]{1,0:T(2,128)S(1)} %bitcast.21, f32[64,128]{1,0:T(8,128)S(1)} %bitcast.20, s32[16,384]{1,0:T(8,128)S(1)} %copy-done.15), custom_call_target="tpu_custom_call" | custom-call | flops 1 | bytes 1 | tf_op jit(solution)/shard_map/prep/pallas_call | solution.py:389
  10.3 0.0 copy-start.19
  10.3 1.1 %copy-done.19 = bf16[2,1024,384]{2,1,0:T(8,128)(2,1)} copy-done((bf16[2,1024,384]{2,1,0:T(8,128)(2,1)}, bf16[2,1024,384]{2,1,0:T(8,128)(2,1)S(1)}, u32[]{:S(2)}) %copy-start.19) | copy-done | bytes 1572888
  11.4 0.3 collective-permute-start.1
  11.7 3.0 %own.1 = (bf16[768,1024]{1,0:T(8,128)(2,1)S(1)}, bf16[1024,768]{1,0:T(8,128)(2,1)S(1)}, f32[1024,768]{1,0:T(8,128)S(1)}) custom-call(bf16[2,1024,384]{2,1,0:T(8,128)(2,1)S(1)} %bitcast.18, f32[8,768]{1,0:T(8,128)S(1)} %get-tuple-element.59.levels, f32[8,768]{1,0:T(8,128)S(1)} %get-tuple-element.60.weights), custom_call_target="tpu_custom_call" | custom-call | flops 20000000000 | bytes 1 | tf_op jit(solution)/shard_map/own/pallas_call | solution.py:394
  14.7 0.0 copy-start.4
  14.8 0.3 collective-permute-done.2.rest_0_
  15.1 1.9 %collective-permute-start.5 = (bf16[512,384]{1,0:T(8,128)(2,1)S(1)}, bf16[512,384]{1,0:T(8,128)(2,1)S(1)}, u32[]{:S(2)}, u32[]{:S(2)}) collective-permute-start(bf16[512,384]{1,0:T(8,128)(2,1)S(1)} %get-tuple-element.70), channel_id=1, source_target_pairs={{0,2},{1,3},{2,0},{3,1},{4,6},{5,7},{6,4},{7,5},{8,10},{9,11},{10,... | collective-permute-start | bytes 1179656 | tf_op jit(solution)/shard_map/ppermute | solution.py:24
  17.0 3.5 %collective-permute-start.6 = (bf16[528,384]{1,0:T(8,128)(2,1)S(1)}, bf16[528,384]{1,0:T(8,128)(2,1)S(1)}, u32[]{:S(2)}, u32[]{:S(2)}) collective-permute-start(bf16[528,384]{1,0:T(8,128)(2,1)S(1)} %collective-permute-done.2.rest_0_), channel_id=1, source_target_pairs={{0,4},{1,5},{4,8},{5,9},{6,2},{7,3},{8,12},{9,13},{10,6},{11,7},{1... | collective-permute-start | bytes 1216520 | tf_op jit(solution)/shard_map/ppermute | solution.py:24
  20.6 3.0 %sib.1.total.near = f32[1024,768]{1,0:T(8,128)S(1)} custom-call(bf16[768,1024]{1,0:T(8,128)(2,1)S(1)} %get-tuple-element.84.own_t, f32[1024,768]{1,0:T(8,128)S(1)} %get-tuple-element.66.total_in, bf16[2,1024,384]{2,1,0:T(8,128)(2,1)S(1)} %copy-done.20, f32[8,768]{1,0:T(8,128)S(1)} %get-tuple-element.59.levels, ...), custom_call_target="tpu_custom_call", output_to_operand_aliasing={{}: (1, {})} | custom-call | flops 10000000000 | bytes 1 | tf_op jit(solution)/shard_map/sib/pallas_call | solution.py:404
  23.6 0.1 collective-permute-done.1.rest_1_
  23.6 1.9 %collective-permute-start.4 = (bf16[512,384]{1,0:T(8,128)(2,1)}, bf16[512,384]{1,0:T(8,128)(2,1)}, u32[]{:S(2)}, u32[]{:S(2)}) collective-permute-start(bf16[512,384]{1,0:T(8,128)(2,1)} %get-tuple-element.69), channel_id=1, source_target_pairs={{0,2},{1,3},{2,0},{3,1},{4,6},{5,7},{6,4},{7,5},{8,10},{9,11},{10,... | collective-permute-start | bytes 1179656 | tf_op jit(solution)/shard_map/ppermute | solution.py:24
  25.6 3.5 %collective-permute-start.10 = (bf16[512,384]{1,0:T(8,128)(2,1)}, bf16[512,384]{1,0:T(8,128)(2,1)S(1)}, u32[]{:S(2)}, u32[]{:S(2)}) collective-permute-start(bf16[512,384]{1,0:T(8,128)(2,1)} %collective-permute-done.1.rest_1_), channel_id=1, source_target_pairs={{0,4},{1,5},{4,8},{5,9},{6,2},{7,3},{8,12},{9,13},{10,6},{11,7},{1... | collective-permute-start | bytes 1179656 | tf_op jit(solution)/shard_map/ppermute | solution.py:24
  29.1 2.9 %collective-permute-done.5.rest_2_ = bf16[512,384]{1,0:T(8,128)(2,1)S(1)} collective-permute-done((bf16[512,384]{1,0:T(8,128)(2,1)S(1)}, bf16[512,384]{1,0:T(8,128)(2,1)S(1)}, u32[]{:S(2)}, u32[]{:S(2)}) %collective-permute-start.5) | collective-permute-done | bytes 393248 | tf_op jit(solution)/shard_map/ppermute | solution.py:24
  31.9 3.5 %near_metric.1 = (f32[1152,128]{1,0:T(8,128)S(1)}, f32[1152,128]{1,0:T(8,128)S(1)}, s16[1216,128]{1,0:T(8,128)(2,1)}, s16[1216,128]{1,0:T(8,128)(2,1)}) custom-call(s32[1]{0:T(128)} %bitcast.me_ref, f32[1024,768]{1,0:T(8,128)S(1)} %sib.1.total.near, bf16[1024,768]{1,0:T(8,128)(2,1)S(1)} %get-tuple-element.75.own_s), custom_call_target="tpu_custom_call" | custom-call | flops 10000000000 | bytes 1 | tf_op jit(solution)/shard_map/near_metric/pallas_call | solution.py:419
  35.5 0.5 collective-permute-start.8
  36.0 4.0 %collective-permute-start.12 = (bf16[512,384]{1,0:T(8,128)(2,1)}, bf16[512,384]{1,0:T(8,128)(2,1)S(1)}, u32[]{:S(2)}, u32[]{:S(2)}) collective-permute-start(bf16[512,384]{1,0:T(8,128)(2,1)} %copy-done.8), channel_id=1, source_target_pairs={{0,4},{1,5},{4,8},{5,9},{6,2},{7,3},{8,12},{9,13},{10,6},{11,7},{1... | collective-permute-start | bytes 1179656 | tf_op jit(solution)/shard_map/ppermute | solution.py:24
  40.1 1.3 %maximum_select_fusion = bf16[1040,384]{1,0:T(8,128)(2,1)S(1)} fusion(bf16[512,384]{1,0:T(8,128)(2,1)} %collective-permute-done.1.rest_1_, bf16[528,384]{1,0:T(8,128)(2,1)} %copy-done.6, bf16[512,384]{1,0:T(8,128)(2,1)S(1)} %collective-permute-done.10.rest_1_.rest_2_, bf16[528,384]{1,0:T(8,128)(2,1)S(1)} %collective-permute-done.6.rest_0_, pred[]{:T(512)S(6)} %eq.3), kind=kLoop, calls=%fused_computation | loop fusion | flops 3594240 | bytes 2396161 | tf_op jit(solution)/shard_map/jit(_where)/select_n | solution.py:435
  41.4 0.1 collective-permute-start.11
  41.5 3.7 %collective-permute-start.9 = (bf16[512,384]{1,0:T(8,128)(2,1)}, bf16[512,384]{1,0:T(8,128)(2,1)S(1)}, u32[]{:S(2)}, u32[]{:S(2)}) collective-permute-start(bf16[512,384]{1,0:T(8,128)(2,1)} %collective-permute-done.4.rest_3_), channel_id=1, source_target_pairs={{0,4},{1,5},{4,8},{5,9},{6,2},{7,3},{8,12},{9,13},{10,6},{11,7},{1... | collective-permute-start | bytes 1179656 | tf_op jit(solution)/shard_map/ppermute | solution.py:24
  45.2 1.4 %chip.1 = (f32[1152,128]{1,0:T(8,128)S(1)}, s16[1216,128]{1,0:T(8,128)(2,1)S(1)}) custom-call(f32[1152,128]{1,0:T(8,128)S(1)} %get-tuple-element.79.keep_in, f32[1152,128]{1,0:T(8,128)S(1)} %get-tuple-element.80.away, s16[1216,128]{1,0:T(8,128)(2,1)} %collective-permute-done.7.got_away, s16[1216,128]{1,0:T(8,128)(2,1)} %collective-permute-done.8.got_keep), custom_call_target="tpu_custom_call" | custom-call | flops 1 | bytes 1 | tf_op jit(solution)/shard_map/chip/pallas_call | solution.py:426
  46.6 0.1 collective-permute-start.15
  46.7 3.8 %far2.1.total_in = f32[1024,768]{1,0:T(8,128)S(1)} custom-call(s32[1]{0:T(128)} %bitcast.me_ref, bf16[768,1024]{1,0:T(8,128)(2,1)S(1)} %get-tuple-element.84.own_t, f32[8,768]{1,0:T(8,128)S(1)} %copy-done.11, f32[8,768]{1,0:T(8,128)S(1)} %copy-done.13, bf16[528,384]{1,0:T(8,128)(2,1)S(1)} %copy-done.7, bf16[512,384]{1,0:T(8,128)(2,1)} %collective-permute-done.1.rest_1_, ...), custom_call_target="tpu_custom_call" | custom-call | flops 10000000000 | bytes 1 | tf_op jit(solution)/shard_map/far2/pallas_call | solution.py:457
  50.5 2.7 %far3.1.total_in = f32[1024,768]{1,0:T(8,128)S(1)} custom-call(s32[1]{0:T(128)} %bitcast.me_ref, bf16[768,1024]{1,0:T(8,128)(2,1)S(1)} %get-tuple-element.84.own_t, f32[8,768]{1,0:T(8,128)S(1)} %copy-done.11, f32[8,768]{1,0:T(8,128)S(1)} %copy-done.13, f32[1024,768]{1,0:T(8,128)S(1)} %far2.1.total_in, ...), custom_call_target="tpu_custom_call", output_to_operand_aliasing={{}: (4, {})} | custom-call | flops 1 | bytes 1 | tf_op jit(solution)/shard_map/far3/pallas_call | solution.py:457
  53.2 0.1 broadcast_select_fusion.1
  53.3 0.3 collective-permute-start.14
  53.6 0.3 collective-permute-start.13
  53.9 2.2 %collective-permute-done.15.across = s16[1216,128]{1,0:T(8,128)(2,1)S(1)} collective-permute-done((s16[1216,128]{1,0:T(8,128)(2,1)S(1)}, s16[1216,128]{1,0:T(8,128)(2,1)S(1)}, u32[]{:S(2)}, u32[]{:S(2)}) %collective-permute-start.15) | collective-permute-done | bytes 311328 | tf_op jit(solution)/shard_map/ppermute | solution.py:24
  56.1 1.3 %collective-permute-done.9.rest_1_ = bf16[512,384]{1,0:T(8,128)(2,1)S(1)} collective-permute-done((bf16[512,384]{1,0:T(8,128)(2,1)}, bf16[512,384]{1,0:T(8,128)(2,1)S(1)}, u32[]{:S(2)}, u32[]{:S(2)}) %collective-permute-start.9) | collective-permute-done | bytes 393248 | tf_op jit(solution)/shard_map/ppermute | solution.py:24
  57.4 1.0 %broadcast_select_fusion = bf16[512,384]{1,0:T(8,128)(2,1)S(1)} fusion(bf16[512,384]{1,0:T(8,128)(2,1)} %collective-permute-done.4.rest_3_, bf16[512,384]{1,0:T(8,128)(2,1)S(1)} %collective-permute-done.9.rest_1_, pred[]{:T(512)S(6)} %eq.3), kind=kLoop, calls=%fused_computation.2 | loop fusion | flops 196608 | bytes 1179649 | tf_op jit(solution)/shard_map/jit(_where)/select_n | solution.py:435
  58.4 0.1 collective-permute-start.16
  58.5 1.7 %collective-permute-done.16.rest_5_ = bf16[512,384]{1,0:T(8,128)(2,1)S(1)} collective-permute-done((bf16[512,384]{1,0:T(8,128)(2,1)S(1)}, bf16[512,384]{1,0:T(8,128)(2,1)S(1)}, u32[]{:S(2)}, u32[]{:S(2)}) %collective-permute-start.16) | collective-permute-done | bytes 393248 | tf_op jit(solution)/shard_map/ppermute | solution.py:24
  60.2 6.8 %last.1 = (f32[1024,768]{1,0:T(8,128)S(1)}, f32[2,1024,384]{2,1,0:T(8,128)}, f32[1152,128]{1,0:T(8,128)S(1)}, f32[1152,128]{1,0:T(8,128)S(1)}) custom-call(s32[1]{0:T(128)} %bitcast.me_ref, bf16[768,1024]{1,0:T(8,128)(2,1)S(1)} %get-tuple-element.84.own_t, f32[8,768]{1,0:T(8,128)S(1)} %copy-done.11, ...), custom_call_target="tpu_custom_call", output_to_operand_aliasing={{0}: (4, {})} | custom-call | flops 1 | bytes 1 | tf_op jit(solution)/shard_map/last/pallas_call | solution.py:457
  67.0 0.2 collective-permute-start.17
  67.2 1.9 %collective-permute-done.17.theirs = f32[1152,128]{1,0:T(8,128)S(1)} collective-permute-done((f32[1152,128]{1,0:T(8,128)S(1)}, f32[1152,128]{1,0:T(8,128)S(1)}, u32[]{:S(2)}, u32[]{:S(2)}) %collective-permute-start.17) | collective-permute-done | bytes 589856 | tf_op jit(solution)/shard_map/ppermute | solution.py:24
  69.1 0.3 column.1
  69.3 2.4 %collective-permute-start.18 = (s16[304,128]{1,0:T(8,128)(2,1)S(1)}, s16[304,128]{1,0:T(8,128)(2,1)S(1)}, u32[]{:S(2)}, u32[]{:S(2)}) collective-permute-start(s16[304,128]{1,0:T(8,128)(2,1)S(1)} %get-tuple-element.103), channel_id=1, source_target_pairs={{0,4},{1,5},{2,6},{3,7},{4,0},{5,1},{6,2},{7,3},{8,12},{9,13},{10,... | collective-permute-start | bytes 233480 | tf_op jit(solution)/shard_map/ppermute | solution.py:24
  71.8 2.6 %collective-permute-start.19 = (s16[304,128]{1,0:T(8,128)(2,1)S(1)}, s16[304,128]{1,0:T(8,128)(2,1)S(1)}, u32[]{:S(2)}, u32[]{:S(2)}) collective-permute-start(s16[304,128]{1,0:T(8,128)(2,1)S(1)} %get-tuple-element.104), channel_id=1, source_target_pairs={{0,8},{1,9},{2,10},{3,11},{4,12},{5,13},{6,14},{7,15},{8,0},{9,1},... | collective-permute-start | bytes 233480 | tf_op jit(solution)/shard_map/ppermute | solution.py:24
  74.4 0.1 collective-permute-done.18.a
  74.5 6.5 %collective-permute-done.19.b = s16[304,128]{1,0:T(8,128)(2,1)S(1)} collective-permute-done((s16[304,128]{1,0:T(8,128)(2,1)S(1)}, s16[304,128]{1,0:T(8,128)(2,1)S(1)}, u32[]{:S(2)}, u32[]{:S(2)}) %collective-permute-start.19) | collective-permute-done | bytes 77856 | tf_op jit(solution)/shard_map/ppermute | solution.py:24
  81.0 0.1 sum_code.1
  81.1 2.6 %collective-permute-start.23 = (s16[304,128]{1,0:T(8,128)(2,1)S(1)}, s16[304,128]{1,0:T(8,128)(2,1)S(1)}, u32[]{:S(2)}, u32[]{:S(2)}) collective-permute-start(s16[304,128]{1,0:T(8,128)(2,1)S(1)} %sum_code.1), channel_id=1, source_target_pairs={{0,12},{1,13},{2,14},{3,15},{4,8},{5,9},{6,10},{7,11},{8,4},{9,5},... | collective-permute-start | bytes 233480 | tf_op jit(solution)/shard_map/ppermute | solution.py:24
  83.6 0.5 collective-permute-start.22
  84.1 1.4 %collective-permute-start.21 = (s16[304,128]{1,0:T(8,128)(2,1)S(1)}, s16[304,128]{1,0:T(8,128)(2,1)S(1)}, u32[]{:S(2)}, u32[]{:S(2)}) collective-permute-start(s16[304,128]{1,0:T(8,128)(2,1)S(1)} %sum_code.1), channel_id=1, source_target_pairs={{0,4},{1,5},{2,6},{3,7},{4,0},{5,1},{6,2},{7,3},{8,12},{9,13},{10,... | collective-permute-start | bytes 233480 | tf_op jit(solution)/shard_map/ppermute | solution.py:24
  85.5 0.6 collective-permute-start.24
  86.1 1.9 %collective-permute-done.23 = s16[304,128]{1,0:T(8,128)(2,1)S(1)} collective-permute-done((s16[304,128]{1,0:T(8,128)(2,1)S(1)}, s16[304,128]{1,0:T(8,128)(2,1)S(1)}, u32[]{:S(2)}, u32[]{:S(2)}) %collective-permute-start.23) | collective-permute-done | bytes 77856 | tf_op jit(solution)/shard_map/ppermute | solution.py:24
  88.1 0.8 collective-permute-start.27
  88.8 1.5 %collective-permute-done.22 = s16[304,128]{1,0:T(8,128)(2,1)S(1)} collective-permute-done((s16[304,128]{1,0:T(8,128)(2,1)S(1)}, s16[304,128]{1,0:T(8,128)(2,1)S(1)}, u32[]{:S(2)}, u32[]{:S(2)}) %collective-permute-start.22) | collective-permute-done | bytes 77856 | tf_op jit(solution)/shard_map/ppermute | solution.py:24
  90.3 1.0 collective-permute-start.26
  91.3 1.0 %collective-permute-start.25 = (s16[304,128]{1,0:T(8,128)(2,1)S(1)}, s16[304,128]{1,0:T(8,128)(2,1)S(1)}, u32[]{:S(2)}, u32[]{:S(2)}) collective-permute-start(s16[304,128]{1,0:T(8,128)(2,1)S(1)} %collective-permute-done.21), channel_id=1, source_target_pairs={{0,2},{1,3},{2,0},{3,1},{4,6},{5,7},{6,4},{7,5},{8,10},{9,11},{10,... | collective-permute-start | bytes 233480 | tf_op jit(solution)/shard_map/ppermute | solution.py:24
  92.4 0.1 collective-permute-start.28
  92.5 0.8 collective-permute-done.27
  93.3 1.6 %collective-permute-done.26 = s16[304,128]{1,0:T(8,128)(2,1)S(1)} collective-permute-done((s16[304,128]{1,0:T(8,128)(2,1)S(1)}, s16[304,128]{1,0:T(8,128)(2,1)S(1)}, u32[]{:S(2)}, u32[]{:S(2)}) %collective-permute-start.26) | collective-permute-done | bytes 77856 | tf_op jit(solution)/shard_map/ppermute | solution.py:24
  94.9 0.8 collective-permute-done.25
  95.7 0.1 collective-permute-start.29
  95.8 1.6 %collective-permute-done.29.sib_b = s16[4,304,128]{2,1,0:T(8,128)(2,1)S(1)} collective-permute-done((s16[4,304,128]{2,1,0:T(8,128)(2,1)S(1)}, s16[4,304,128]{2,1,0:T(8,128)(2,1)S(1)}, u32[]{:S(2)}, u32[]{:S(2)}) %collective-permute-start.29) | collective-permute-done | bytes 311328 | tf_op jit(solution)/shard_map/ppermute | solution.py:24
  97.4 2.8 %spread.1 = f32[1024,1024]{1,0:T(8,128)} custom-call(s32[1]{0:T(128)} %bitcast.me_ref, s16[4,304,128]{2,1,0:T(8,128)(2,1)S(1)} %pad_add_fusion.a, s16[4,304,128]{2,1,0:T(8,128)(2,1)S(1)} %pad_add_fusion.1.b, s16[4,304,128]{2,1,0:T(8,128)(2,1)S(1)} %collective-permute-done.28.sib_a, s16[4,304,128]{2,1,0:T(8,128)(2,1)S(1)} %collective-permute-done.29.sib_b), custom_call_target="tpu_custom_call" | custom-call | flops 1 | bytes 1 | tf_op jit(solution)/shard_map/spread/pallas_call | solution.py:501
  (57 shorter events, 0.2 us)
Async XLA Ops:
  0.6 8.3 %copy-start.17 = (s32[1,3]{1,0:T(1,128)S(1)}, s32[1,3]{1,0:T(1,128)}, u32[]{:S(2)}) copy-start(s32[1,3]{1,0:T(1,128)} %pairs.3) | copy-start | bytes 40
  0.6 8.3 %copy-start.15 = (s32[16,384]{1,0:T(8,128)S(1)}, s32[16,384]{1,0:T(8,128)}, u32[]{:S(2)}) copy-start(s32[16,384]{1,0:T(8,128)} %maps_in.1) | copy-start | bytes 73732
  0.7 8.3 %copy-start.14 = (f32[8192]{0:T(1024)S(1)}, f32[8192]{0:T(1024)}, u32[]{:S(2)}) copy-start(f32[8192]{0:T(1024)} %param.8) | copy-start | bytes 98308
  0.7 8.3 %copy-start.18 = (f32[16,2]{0,1:T(2,128)S(1)}, f32[16,2]{0,1:T(2,128)}, u32[]{:S(2)}) copy-start(f32[16,2]{0,1:T(2,128)} %param.7) | copy-start | bytes 388
  1.7 8.6 %collective-permute-start = (bf16[2,1024,384]{2,1,0:T(8,128)(2,1)}, bf16[2,1024,384]{2,1,0:T(8,128)(2,1)S(1)}, u32[]{:S(2)}, u32[]{:S(2)}) collective-permute-start(bf16[2,1024,384]{2,1,0:T(8,128)(2,1)} %bitcast.16), channel_id=1, source_target_pairs={{0,1},{1,0},{2,3},{3,2},{4,5},{5,4},{6,7},{7,6},{8,9},{9,8},{10,11... | collective-permute-start | bytes 4718600 | tf_op jit(solution)/shard_map/ppermute | solution.py:24
  2.3 12.8 %collective-permute-start.2 = (bf16[528,384]{1,0:T(8,128)(2,1)S(1)}, bf16[528,384]{1,0:T(8,128)(2,1)S(1)}, u32[]{:S(2)}, u32[]{:S(2)}) collective-permute-start(bf16[528,384]{1,0:T(8,128)(2,1)S(1)} %slice_bitcast_fusion), channel_id=1, source_target_pairs={{0,2},{1,3},{2,0},{3,1},{4,6},{5,7},{6,4},{7,5},{8,10},{9,11},{10,... | collective-permute-start | bytes 1216520 | tf_op jit(solution)/shard_map/ppermute | solution.py:24
  4.9 4.1 %collective-permute-start.3 = (s32[1,3]{1,0:T(1,128)}, s32[1,3]{1,0:T(1,128)S(1)}, u32[]{:S(2)}, u32[]{:S(2)}) collective-permute-start(s32[1,3]{1,0:T(1,128)} %pairs.3), channel_id=1, source_target_pairs={{0,1},{1,0},{2,3},{3,2},{4,5},{5,4},{6,7},{7,6},{8,9},{9,8},{10,11... | collective-permute-start | bytes 44 | tf_op jit(solution)/shard_map/ppermute | solution.py:24
  5.0 1.4 %copy-start.2 = (bf16[1,2,1024,384]{3,2,1,0:T(8,128)(2,1)S(1)}, bf16[1,2,1024,384]{3,2,1,0:T(8,128)(2,1)}, u32[]{:S(2)}) copy-start(bf16[1,2,1024,384]{3,2,1,0:T(8,128)(2,1)} %param.5) | copy-start | bytes 4718596
  6.4 0.7 copy-start.16
  7.1 4.6 %copy-start.3 = (bf16[1,2,1024,384]{3,2,1,0:T(8,128)(2,1)S(1)}, bf16[1,2,1024,384]{3,2,1,0:T(8,128)(2,1)}, u32[]{:S(2)}) copy-start(bf16[1,2,1024,384]{3,2,1,0:T(8,128)(2,1)} %param.5) | copy-start | bytes 4718596
  10.3 10.3 %copy-start.10 = (f32[8,768]{1,0:T(8,128)}, f32[8,768]{1,0:T(8,128)S(1)}, u32[]{:S(2)}) copy-start(f32[8,768]{1,0:T(8,128)S(1)} %get-tuple-element.59.levels) | copy-start | bytes 73732
  10.3 10.3 %copy-start.12 = (f32[8,768]{1,0:T(8,128)}, f32[8,768]{1,0:T(8,128)S(1)}, u32[]{:S(2)}) copy-start(f32[8,768]{1,0:T(8,128)S(1)} %get-tuple-element.60.weights) | copy-start | bytes 73732
  10.3 1.1 %copy-start.19 = (bf16[2,1024,384]{2,1,0:T(8,128)(2,1)}, bf16[2,1024,384]{2,1,0:T(8,128)(2,1)S(1)}, u32[]{:S(2)}) copy-start(bf16[2,1024,384]{2,1,0:T(8,128)(2,1)S(1)} %collective-permute-done.sib) | copy-start | bytes 4718596
  11.4 12.2 %collective-permute-start.1 = (bf16[512,384]{1,0:T(8,128)(2,1)S(1)}, bf16[512,384]{1,0:T(8,128)(2,1)}, u32[]{:S(2)}, u32[]{:S(2)}) collective-permute-start(bf16[512,384]{1,0:T(8,128)(2,1)S(1)} %get-tuple-element.57), channel_id=1, source_target_pairs={{0,2},{1,3},{2,0},{3,1},{4,6},{5,7},{6,4},{7,5},{8,10},{9,11},{10,... | collective-permute-start | bytes 1179656 | tf_op jit(solution)/shard_map/ppermute | solution.py:24
  11.7 8.8 %copy-start.20 = (bf16[2,1024,384]{2,1,0:T(8,128)(2,1)S(1)}, bf16[2,1024,384]{2,1,0:T(8,128)(2,1)}, u32[]{:S(2)}) copy-start(bf16[2,1024,384]{2,1,0:T(8,128)(2,1)} %copy-done.19) | copy-start | bytes 4718596
  14.7 17.2 %copy-start.4 = (bf16[1024,768]{1,0:T(8,128)(2,1)}, bf16[1024,768]{1,0:T(8,128)(2,1)S(1)}, u32[]{:S(2)}) copy-start(bf16[1024,768]{1,0:T(8,128)(2,1)S(1)} %get-tuple-element.75.own_s) | copy-start | bytes 4718596
  15.1 8.5 %copy-start.6 = (bf16[528,384]{1,0:T(8,128)(2,1)}, bf16[528,384]{1,0:T(8,128)(2,1)S(1)}, u32[]{:S(2)}) copy-start(bf16[528,384]{1,0:T(8,128)(2,1)S(1)} %collective-permute-done.2.rest_0_) | copy-start | bytes 1216516
  15.1 16.9 %collective-permute-start.5 = (bf16[512,384]{1,0:T(8,128)(2,1)S(1)}, bf16[512,384]{1,0:T(8,128)(2,1)S(1)}, u32[]{:S(2)}, u32[]{:S(2)}) collective-permute-start(bf16[512,384]{1,0:T(8,128)(2,1)S(1)} %get-tuple-element.70), channel_id=1, source_target_pairs={{0,2},{1,3},{2,0},{3,1},{4,6},{5,7},{6,4},{7,5},{8,10},{9,11},{10,... | collective-permute-start | bytes 1179656 | tf_op jit(solution)/shard_map/ppermute | solution.py:24
  17.0 14.9 %collective-permute-start.6 = (bf16[528,384]{1,0:T(8,128)(2,1)S(1)}, bf16[528,384]{1,0:T(8,128)(2,1)S(1)}, u32[]{:S(2)}, u32[]{:S(2)}) collective-permute-start(bf16[528,384]{1,0:T(8,128)(2,1)S(1)} %collective-permute-done.2.rest_0_), channel_id=1, source_target_pairs={{0,4},{1,5},{4,8},{5,9},{6,2},{7,3},{8,12},{9,13},{10,6},{11,7},{1... | collective-permute-start | bytes 1216520 | tf_op jit(solution)/shard_map/ppermute | solution.py:24
  23.6 11.9 %copy-start = (f32[1024,768]{1,0:T(8,128)}, f32[1024,768]{1,0:T(8,128)S(1)}, u32[]{:S(2)}) copy-start(f32[1024,768]{1,0:T(8,128)S(1)} %sib.1.total.near) | copy-start | bytes 9437188
  23.6 17.9 %collective-permute-start.4 = (bf16[512,384]{1,0:T(8,128)(2,1)}, bf16[512,384]{1,0:T(8,128)(2,1)}, u32[]{:S(2)}, u32[]{:S(2)}) collective-permute-start(bf16[512,384]{1,0:T(8,128)(2,1)} %get-tuple-element.69), channel_id=1, source_target_pairs={{0,2},{1,3},{2,0},{3,1},{4,6},{5,7},{6,4},{7,5},{8,10},{9,11},{10,... | collective-permute-start | bytes 1179656 | tf_op jit(solution)/shard_map/ppermute | solution.py:24
  25.6 14.5 %collective-permute-start.10 = (bf16[512,384]{1,0:T(8,128)(2,1)}, bf16[512,384]{1,0:T(8,128)(2,1)S(1)}, u32[]{:S(2)}, u32[]{:S(2)}) collective-permute-start(bf16[512,384]{1,0:T(8,128)(2,1)} %collective-permute-done.1.rest_1_), channel_id=1, source_target_pairs={{0,4},{1,5},{4,8},{5,9},{6,2},{7,3},{8,12},{9,13},{10,6},{11,7},{1... | collective-permute-start | bytes 1179656 | tf_op jit(solution)/shard_map/ppermute | solution.py:24
  31.9 3.5 %copy-start.8 = (bf16[512,384]{1,0:T(8,128)(2,1)}, bf16[512,384]{1,0:T(8,128)(2,1)S(1)}, u32[]{:S(2)}) copy-start(bf16[512,384]{1,0:T(8,128)(2,1)S(1)} %collective-permute-done.5.rest_2_) | copy-start | bytes 1179652
  35.5 6.0 %collective-permute-start.7 = (s16[1216,128]{1,0:T(8,128)(2,1)}, s16[1216,128]{1,0:T(8,128)(2,1)}, u32[]{:S(2)}, u32[]{:S(2)}) collective-permute-start(s16[1216,128]{1,0:T(8,128)(2,1)} %get-tuple-element.76), channel_id=1, source_target_pairs={{0,1},{1,0},{2,3},{3,2},{4,5},{5,4},{6,7},{7,6},{8,9},{9,8},{10,11... | collective-permute-start | bytes 933896 | tf_op jit(solution)/shard_map/ppermute | solution.py:24
  35.5 6.0 %collective-permute-start.8 = (s16[1216,128]{1,0:T(8,128)(2,1)}, s16[1216,128]{1,0:T(8,128)(2,1)}, u32[]{:S(2)}, u32[]{:S(2)}) collective-permute-start(s16[1216,128]{1,0:T(8,128)(2,1)} %get-tuple-element.77), channel_id=1, source_target_pairs={{0,1},{1,0},{2,3},{3,2},{4,5},{5,4},{6,7},{7,6},{8,9},{9,8},{10,11... | collective-permute-start | bytes 933896 | tf_op jit(solution)/shard_map/ppermute | solution.py:24
  36.0 10.7 %copy-start.7 = (bf16[528,384]{1,0:T(8,128)(2,1)S(1)}, bf16[528,384]{1,0:T(8,128)(2,1)}, u32[]{:S(2)}) copy-start(bf16[528,384]{1,0:T(8,128)(2,1)} %copy-done.6) | copy-start | bytes 1216516
  36.0 10.7 %copy-start.9 = (bf16[512,384]{1,0:T(8,128)(2,1)S(1)}, bf16[512,384]{1,0:T(8,128)(2,1)}, u32[]{:S(2)}) copy-start(bf16[512,384]{1,0:T(8,128)(2,1)} %copy-done.8) | copy-start | bytes 1179652
  36.0 10.7 %copy-start.11 = (f32[8,768]{1,0:T(8,128)S(1)}, f32[8,768]{1,0:T(8,128)}, u32[]{:S(2)}) copy-start(f32[8,768]{1,0:T(8,128)} %copy-done.10) | copy-start | bytes 73732
  36.0 10.7 %copy-start.13 = (f32[8,768]{1,0:T(8,128)S(1)}, f32[8,768]{1,0:T(8,128)}, u32[]{:S(2)}) copy-start(f32[8,768]{1,0:T(8,128)} %copy-done.12) | copy-start | bytes 73732
  36.0 17.2 %collective-permute-start.12 = (bf16[512,384]{1,0:T(8,128)(2,1)}, bf16[512,384]{1,0:T(8,128)(2,1)S(1)}, u32[]{:S(2)}, u32[]{:S(2)}) collective-permute-start(bf16[512,384]{1,0:T(8,128)(2,1)} %copy-done.8), channel_id=1, source_target_pairs={{0,4},{1,5},{4,8},{5,9},{6,2},{7,3},{8,12},{9,13},{10,6},{11,7},{1... | collective-permute-start | bytes 1179656 | tf_op jit(solution)/shard_map/ppermute | solution.py:24
  41.4 9.1 %collective-permute-start.11 = (bf16[1040,384]{1,0:T(8,128)(2,1)S(1)}, bf16[1040,384]{1,0:T(8,128)(2,1)S(1)}, u32[]{:S(2)}, u32[]{:S(2)}) collective-permute-start(bf16[1040,384]{1,0:T(8,128)(2,1)S(1)} %maximum_select_fusion), channel_id=1, source_target_pairs={{0,1},{1,0},{2,3},{3,2},{4,5},{5,4},{6,7},{7,6},{8,9},{9,8},{10,11... | collective-permute-start | bytes 2396168 | tf_op jit(solution)/shard_map/ppermute | solution.py:24
  41.5 15.9 %collective-permute-start.9 = (bf16[512,384]{1,0:T(8,128)(2,1)}, bf16[512,384]{1,0:T(8,128)(2,1)S(1)}, u32[]{:S(2)}, u32[]{:S(2)}) collective-permute-start(bf16[512,384]{1,0:T(8,128)(2,1)} %collective-permute-done.4.rest_3_), channel_id=1, source_target_pairs={{0,4},{1,5},{4,8},{5,9},{6,2},{7,3},{8,12},{9,13},{10,6},{11,7},{1... | collective-permute-start | bytes 1179656 | tf_op jit(solution)/shard_map/ppermute | solution.py:24
  46.6 9.5 %collective-permute-start.15 = (s16[1216,128]{1,0:T(8,128)(2,1)S(1)}, s16[1216,128]{1,0:T(8,128)(2,1)S(1)}, u32[]{:S(2)}, u32[]{:S(2)}) collective-permute-start(s16[1216,128]{1,0:T(8,128)(2,1)S(1)} %get-tuple-element.92), channel_id=1, source_target_pairs={{0,2},{1,3},{2,0},{3,1},{4,6},{5,7},{6,4},{7,5},{8,10},{9,11},{10,... | collective-permute-start | bytes 933896 | tf_op jit(solution)/shard_map/ppermute | solution.py:24
  50.5 9.7 %copy-start.5 = (bf16[1024,768]{1,0:T(8,128)(2,1)S(1)}, bf16[1024,768]{1,0:T(8,128)(2,1)}, u32[]{:S(2)}) copy-start(bf16[1024,768]{1,0:T(8,128)(2,1)} %copy-done.4) | copy-start | bytes 4718596
  53.2 7.0 %copy-start.1 = (f32[1024,768]{1,0:T(8,128)S(1)}, f32[1024,768]{1,0:T(8,128)}, u32[]{:S(2)}) copy-start(f32[1024,768]{1,0:T(8,128)} %copy-done) | copy-start | bytes 9437188
  53.3 4.1 %collective-permute-start.14 = (bf16[256,384]{1,0:T(8,128)(2,1)S(1)}, bf16[256,384]{1,0:T(8,128)(2,1)S(1)}, u32[]{:S(2)}, u32[]{:S(2)}) collective-permute-start(bf16[256,384]{1,0:T(8,128)(2,1)S(1)} %get-tuple-element.106), channel_id=1, source_target_pairs={{0,1},{1,0},{2,3},{3,2},{4,5},{5,4},{6,7},{7,6},{8,9},{9,8},{10,11... | collective-permute-start | bytes 589832 | tf_op jit(solution)/shard_map/ppermute | solution.py:24
  53.6 3.8 %collective-permute-start.13 = (bf16[256,384]{1,0:T(8,128)(2,1)S(1)}, bf16[256,384]{1,0:T(8,128)(2,1)S(1)}, u32[]{:S(2)}, u32[]{:S(2)}) collective-permute-start(bf16[256,384]{1,0:T(8,128)(2,1)S(1)} %get-tuple-element.107), channel_id=1, source_target_pairs={{0,1},{1,0},{2,3},{3,2},{4,5},{5,4},{6,7},{7,6},{8,9},{9,8},{10,11... | collective-permute-start | bytes 589832 | tf_op jit(solution)/shard_map/ppermute | solution.py:24
  58.4 1.8 %collective-permute-start.16 = (bf16[512,384]{1,0:T(8,128)(2,1)S(1)}, bf16[512,384]{1,0:T(8,128)(2,1)S(1)}, u32[]{:S(2)}, u32[]{:S(2)}) collective-permute-start(bf16[512,384]{1,0:T(8,128)(2,1)S(1)} %broadcast_select_fusion), channel_id=1, source_target_pairs={{0,1},{1,0},{2,3},{3,2},{4,5},{5,4},{6,7},{7,6},{8,9},{9,8},{10,11... | collective-permute-start | bytes 1179656 | tf_op jit(solution)/shard_map/ppermute | solution.py:24
  67.0 2.1 %collective-permute-start.17 = (f32[1152,128]{1,0:T(8,128)S(1)}, f32[1152,128]{1,0:T(8,128)S(1)}, u32[]{:S(2)}, u32[]{:S(2)}) collective-permute-start(f32[1152,128]{1,0:T(8,128)S(1)} %get-tuple-element.99), channel_id=1, source_target_pairs={{0,1},{1,0},{2,3},{3,2},{4,5},{5,4},{6,7},{7,6},{8,9},{9,8},{10,11... | collective-permute-start | bytes 1769480 | tf_op jit(solution)/shard_map/ppermute | solution.py:24
  69.3 5.1 %collective-permute-start.18 = (s16[304,128]{1,0:T(8,128)(2,1)S(1)}, s16[304,128]{1,0:T(8,128)(2,1)S(1)}, u32[]{:S(2)}, u32[]{:S(2)}) collective-permute-start(s16[304,128]{1,0:T(8,128)(2,1)S(1)} %get-tuple-element.103), channel_id=1, source_target_pairs={{0,4},{1,5},{2,6},{3,7},{4,0},{5,1},{6,2},{7,3},{8,12},{9,13},{10,... | collective-permute-start | bytes 233480 | tf_op jit(solution)/shard_map/ppermute | solution.py:24
  71.8 9.2 %collective-permute-start.19 = (s16[304,128]{1,0:T(8,128)(2,1)S(1)}, s16[304,128]{1,0:T(8,128)(2,1)S(1)}, u32[]{:S(2)}, u32[]{:S(2)}) collective-permute-start(s16[304,128]{1,0:T(8,128)(2,1)S(1)} %get-tuple-element.104), channel_id=1, source_target_pairs={{0,8},{1,9},{2,10},{3,11},{4,12},{5,13},{6,14},{7,15},{8,0},{9,1},... | collective-permute-start | bytes 233480 | tf_op jit(solution)/shard_map/ppermute | solution.py:24
  74.4 6.6 %collective-permute-start.20 = (s16[304,128]{1,0:T(8,128)(2,1)S(1)}, s16[304,128]{1,0:T(8,128)(2,1)S(1)}, u32[]{:S(2)}, u32[]{:S(2)}) collective-permute-start(s16[304,128]{1,0:T(8,128)(2,1)S(1)} %get-tuple-element.105), channel_id=1, source_target_pairs={{0,12},{1,13},{2,14},{3,15},{4,8},{5,9},{6,10},{7,11},{8,4},{9,5},... | collective-permute-start | bytes 233480 | tf_op jit(solution)/shard_map/ppermute | solution.py:24
  81.1 7.0 %collective-permute-start.23 = (s16[304,128]{1,0:T(8,128)(2,1)S(1)}, s16[304,128]{1,0:T(8,128)(2,1)S(1)}, u32[]{:S(2)}, u32[]{:S(2)}) collective-permute-start(s16[304,128]{1,0:T(8,128)(2,1)S(1)} %sum_code.1), channel_id=1, source_target_pairs={{0,12},{1,13},{2,14},{3,15},{4,8},{5,9},{6,10},{7,11},{8,4},{9,5},... | collective-permute-start | bytes 233480 | tf_op jit(solution)/shard_map/ppermute | solution.py:24
  83.6 6.7 %collective-permute-start.22 = (s16[304,128]{1,0:T(8,128)(2,1)S(1)}, s16[304,128]{1,0:T(8,128)(2,1)S(1)}, u32[]{:S(2)}, u32[]{:S(2)}) collective-permute-start(s16[304,128]{1,0:T(8,128)(2,1)S(1)} %sum_code.1), channel_id=1, source_target_pairs={{0,8},{1,9},{2,10},{3,11},{4,12},{5,13},{6,14},{7,15},{8,0},{9,1},... | collective-permute-start | bytes 233480 | tf_op jit(solution)/shard_map/ppermute | solution.py:24
  84.1 7.2 %collective-permute-start.21 = (s16[304,128]{1,0:T(8,128)(2,1)S(1)}, s16[304,128]{1,0:T(8,128)(2,1)S(1)}, u32[]{:S(2)}, u32[]{:S(2)}) collective-permute-start(s16[304,128]{1,0:T(8,128)(2,1)S(1)} %sum_code.1), channel_id=1, source_target_pairs={{0,4},{1,5},{2,6},{3,7},{4,0},{5,1},{6,2},{7,3},{8,12},{9,13},{10,... | collective-permute-start | bytes 233480 | tf_op jit(solution)/shard_map/ppermute | solution.py:24
  85.5 6.9 %collective-permute-start.24 = (s16[304,128]{1,0:T(8,128)(2,1)S(1)}, s16[304,128]{1,0:T(8,128)(2,1)S(1)}, u32[]{:S(2)}, u32[]{:S(2)}) collective-permute-start(s16[304,128]{1,0:T(8,128)(2,1)S(1)} %sum_code.1), channel_id=1, source_target_pairs={{0,2},{1,3},{2,0},{3,1},{4,6},{5,7},{6,4},{7,5},{8,10},{9,11},{10,... | collective-permute-start | bytes 233480 | tf_op jit(solution)/shard_map/ppermute | solution.py:24
  88.1 5.2 %collective-permute-start.27 = (s16[304,128]{1,0:T(8,128)(2,1)S(1)}, s16[304,128]{1,0:T(8,128)(2,1)S(1)}, u32[]{:S(2)}, u32[]{:S(2)}) collective-permute-start(s16[304,128]{1,0:T(8,128)(2,1)S(1)} %collective-permute-done.23), channel_id=1, source_target_pairs={{0,2},{1,3},{2,0},{3,1},{4,6},{5,7},{6,4},{7,5},{8,10},{9,11},{10,... | collective-permute-start | bytes 233480 | tf_op jit(solution)/shard_map/ppermute | solution.py:24
  90.3 4.6 %collective-permute-start.26 = (s16[304,128]{1,0:T(8,128)(2,1)S(1)}, s16[304,128]{1,0:T(8,128)(2,1)S(1)}, u32[]{:S(2)}, u32[]{:S(2)}) collective-permute-start(s16[304,128]{1,0:T(8,128)(2,1)S(1)} %collective-permute-done.22), channel_id=1, source_target_pairs={{0,2},{1,3},{2,0},{3,1},{4,6},{5,7},{6,4},{7,5},{8,10},{9,11},{10,... | collective-permute-start | bytes 233480 | tf_op jit(solution)/shard_map/ppermute | solution.py:24
  91.3 4.4 %collective-permute-start.25 = (s16[304,128]{1,0:T(8,128)(2,1)S(1)}, s16[304,128]{1,0:T(8,128)(2,1)S(1)}, u32[]{:S(2)}, u32[]{:S(2)}) collective-permute-start(s16[304,128]{1,0:T(8,128)(2,1)S(1)} %collective-permute-done.21), channel_id=1, source_target_pairs={{0,2},{1,3},{2,0},{3,1},{4,6},{5,7},{6,4},{7,5},{8,10},{9,11},{10,... | collective-permute-start | bytes 233480 | tf_op jit(solution)/shard_map/ppermute | solution.py:24
  92.4 3.4 %collective-permute-start.28 = (s16[4,304,128]{2,1,0:T(8,128)(2,1)S(1)}, s16[4,304,128]{2,1,0:T(8,128)(2,1)S(1)}, u32[]{:S(2)}, u32[]{:S(2)}) collective-permute-start(s16[4,304,128]{2,1,0:T(8,128)(2,1)S(1)} %pad_add_fusion.a), channel_id=1, source_target_pairs={{0,1},{1,0},{2,3},{3,2},{4,5},{5,4},{6,7},{7,6},{8,9},{9,8},{10,11... | collective-permute-start | bytes 933896 | tf_op jit(solution)/shard_map/ppermute | solution.py:24
  95.7 1.7 %collective-permute-start.29 = (s16[4,304,128]{2,1,0:T(8,128)(2,1)S(1)}, s16[4,304,128]{2,1,0:T(8,128)(2,1)S(1)}, u32[]{:S(2)}, u32[]{:S(2)}) collective-permute-start(s16[4,304,128]{2,1,0:T(8,128)(2,1)S(1)} %pad_add_fusion.1.b), channel_id=1, source_target_pairs={{0,1},{1,0},{2,3},{3,2},{4,5},{5,4},{6,7},{7,6},{8,9},{9,8},{10,11... | collective-permute-start | bytes 933896 | tf_op jit(solution)/shard_map/ppermute | solution.py:24

commit v6 on v5

--- a/solution.py
+++ b/solution.py
@@ -7,8 +7,8 @@
 from jax.experimental.pallas import tpu as pltpu
 from jax.sharding import PartitionSpec as P
 
-LARGE_LIMIT = 28 * 1024 * 1024
-SMALL_LIMIT = 16 * 1024 * 1024
+LARGE_LIMIT = 16 * 1024 * 1024
+SMALL_LIMIT = 8 * 1024 * 1024
 LANES = 128
 BLOCK = 256
 PAD = 16
@@ -376,7 +376,8 @@
     part = own[0, :places[0][2]]
     y = [swapped(part, 2)]
     sib_pairs = swapped(pair_blocks, 1)
-    later, part = lax.optimization_barrier((own, part))
+    gives_y = ((me[0] >> 1) ^ me[0]) & 1 == 0
+    later, part, gives_y = lax.optimization_barrier((own, part, gives_y))
     sib = swapped(later, 1)
     parts = [None, *kernel(
         functools.partial(split_kernel, places[1:]), "split", [smem, smem, hbm],
@@ -423,13 +424,12 @@
     got = [swapped(send, 1) for send in sends]
     y[-1], *got = lax.optimization_barrier((y[-1], *got))
     z.append(forwarded(y[-1]))
+    y[-1], keep, away = lax.optimization_barrier((y[-1], keep, away))
     keep, send = kernel(
         chip_kernel, "chip", [vmem] * 4, (plain(upper // 4), coded(4 * (piece + PAD))), (vmem, vmem),
     )(keep, away, *got)
     across = swapped(send, 2)
-    y[-1], own_t, keep = lax.optimization_barrier((y[-1], own_t, keep))
-
-    gives_y = ((me[0] >> 1) ^ me[0]) & 1 == 0
+    (y[-1], own_t, keep), z[PER:-1] = lax.optimization_barrier(((y[-1], own_t, keep), z[PER:-1]))
 
     def given(rows_y, rows_z):
         return swapped(jnp.where(gives_y, jnp.concatenate(rows_y), jnp.concatenate(rows_z)), 1)

time: 101 us -> 96.1 us (0.951)
  Pallas kernels: 30.5 us -> 26.6 us
  waiting for transfers between devices: 25.2 us -> 28.5 us
  other arithmetic: 2.48 us -> 0.39 us
  local copies, waits for them, and re-layouts: 4.39 us -> 3.17 us
    ppermute x30, waiting for transfers between devices: 25.2 us -> 28.5 us  [move(): return lax.ppermute(x, 'dom', pairs)]
    select_n x2, other arithmetic: 2.36 us -> 0.27 us  [given(): jnp.where(gives_y, jnp.concatenate(rows_y), jnp.concatenate(rows_z))]
    pallas_call x3, Pallas kernels: 13.2 us -> 12 us  [pair_step(): kernel(functools.partial(body, plan, names, step), name, [smem] + [vmem]...]
    unnamed x42 -> x12, local copies, waits for them, and re-layouts: 3.28 us -> 2.08 us
    pallas_call x1, Pallas kernels: 1.41 us -> 0.34 us  [shards(): kernel(chip_kernel, 'chip', [vmem] * 4, (plain(upper // 4), coded(4 * (pi...]
  transfers between devices with their start and end apart: 30 -> 30, of which waited for: 14 -> 15; matrix products, arithmetic and copies ran while one was open for 1% -> 0% of each run, Pallas kernels for 20% -> 17%
where the time goes in v6:
time: 96.1 us; the launch traced here: 95.8 us
  starting transfers between devices  36.1 us (38%)
  waiting for transfers between devices  28.5 us (30%)
  Pallas kernels  26.6 us (28%)
  local copies, waits for them, and re-layouts  3.17 us (3%)
  between operations  1.1 us (1%)
    ppermute x30, starting transfers between devices, move(): return lax.ppermute(x, 'dom', pairs)  36.1 us
    ppermute x30, waiting for transfers between devices, move(): return lax.ppermute(x, 'dom', pairs)  28.5 us
    pallas_call x3, Pallas kernels, pair_step(): kernel(functools.partial(body, plan, names, step), name, [smem] + [vmem]...  12 us
    pallas_call x1, Pallas kernels, shards(): kernel(own_kernel, 'own', [hbm, vmem, vmem], (jax.ShapeDtypeStruct((wide,...  3.01 us
    pallas_call x1, Pallas kernels, shards(): kernel(sib_kernel, 'sib', [vmem, vmem, hbm, vmem, vmem], total_t, vmem, [...  2.97 us
    pallas_call x1, Pallas kernels, shards(): kernel(spread_kernel, 'spread', [smem] + [vmem] * 4, jax.ShapeDtypeStruct...  2.81 us
    pallas_call x1, Pallas kernels, shards(): kernel(near_metric_kernel, 'near_metric', [smem, vmem, vmem], (plain(uppe...  2.71 us
    unnamed x12, local copies, waits for them, and re-layouts  2.08 us
  transfers between devices with their start and end apart: 30, of which 15 were waited for; matrix products, arithmetic and copies ran while one was open for 0% of the time, Pallas kernels for 17%

profile of v6, /device:TPU:0, one launch (start us, length us, event | category | flops | bytes accessed | tf_op | source)
XLA Modules:
  0.0 95.8 jit_solution(883663336316079862)
XLA Ops:
  0.7 1.1 %slice_bitcast_fusion = bf16[528,384]{1,0:T(8,128)(2,1)S(1)} fusion(bf16[2,1024,384]{2,1,0:T(8,128)(2,1)} %bitcast.15), kind=kLoop, calls=%fused_computation.1 | loop fusion | bytes 811008 | tf_op jit(solution)/shard_map/squeeze | solution.py:376
  1.7 0.5 collective-permute-start
  2.2 2.6 %collective-permute-start.2 = (bf16[528,384]{1,0:T(8,128)(2,1)S(1)}, bf16[528,384]{1,0:T(8,128)(2,1)S(1)}, u32[]{:S(2)}, u32[]{:S(2)}) collective-permute-start(bf16[528,384]{1,0:T(8,128)(2,1)S(1)} %slice_bitcast_fusion), channel_id=1, source_target_pairs={{0,2},{1,3},{2,0},{3,1},{4,6},{5,7},{6,4},{7,5},{8,10},{9,11},{10,... | collective-permute-start | bytes 1216520 | tf_op jit(solution)/shard_map/ppermute | solution.py:24
  4.8 0.2 collective-permute-start.3
  5.0 1.4 %copy-done = bf16[1,2,1024,384]{3,2,1,0:T(8,128)(2,1)S(1)} copy-done((bf16[1,2,1024,384]{3,2,1,0:T(8,128)(2,1)S(1)}, bf16[1,2,1024,384]{3,2,1,0:T(8,128)(2,1)}, u32[]{:S(2)}) %copy-start) | copy-done | bytes 1572888
  6.4 0.7 copy-done.4
  7.1 1.1 %split.1 = (bf16[512,384]{1,0:T(8,128)(2,1)S(1)}, bf16[512,384]{1,0:T(8,128)(2,1)S(1)}, bf16[512,384]{1,0:T(8,128)(2,1)S(1)}) custom-call(s32[1]{0:T(128)} %bitcast.me_ref, s32[1,3]{1,0:T(1,128)S(1)} %copy-done.4, bf16[2,1024,384]{2,1,0:T(8,128)(2,1)S(1)} %bitcast.17), custom_call_target="tpu_custom_call" | custom-call | flops 1 | bytes 1 | tf_op jit(solution)/shard_map/split/pallas_call | solution.py:382
  8.2 0.0 collective-permute-done.3.sib_pairs
  8.2 1.3 %prep.1 = (f32[8,768]{1,0:T(8,128)S(1)}, f32[8,768]{1,0:T(8,128)S(1)}) custom-call(s32[1]{0:T(128)} %bitcast.me_ref, s32[1,3]{1,0:T(1,128)S(1)} %copy-done.4, s32[1,3]{1,0:T(1,128)S(1)} %collective-permute-done.3.sib_pairs, f32[2,16]{1,0:T(2,128)S(1)} %bitcast.21, f32[64,128]{1,0:T(8,128)S(1)} %bitcast.20, s32[16,384]{1,0:T(8,128)S(1)} %copy-done.3), custom_call_target="tpu_custom_call" | custom-call | flops 1 | bytes 1 | tf_op jit(solution)/shard_map/prep/pallas_call | solution.py:390
  9.5 0.3 collective-permute-start.1
  9.9 3.0 %own.1 = (bf16[768,1024]{1,0:T(8,128)(2,1)S(1)}, bf16[1024,768]{1,0:T(8,128)(2,1)S(1)}, f32[1024,768]{1,0:T(8,128)S(1)}) custom-call(bf16[2,1024,384]{2,1,0:T(8,128)(2,1)S(1)} %bitcast.18, f32[8,768]{1,0:T(8,128)S(1)} %get-tuple-element.64.levels, f32[8,768]{1,0:T(8,128)S(1)} %get-tuple-element.65.weights), custom_call_target="tpu_custom_call" | custom-call | flops 20000000000 | bytes 1 | tf_op jit(solution)/shard_map/own/pallas_call | solution.py:395
  12.9 2.2 %collective-permute-done.2.rest_0_ = bf16[528,384]{1,0:T(8,128)(2,1)S(1)} collective-permute-done((bf16[528,384]{1,0:T(8,128)(2,1)S(1)}, bf16[528,384]{1,0:T(8,128)(2,1)S(1)}, u32[]{:S(2)}, u32[]{:S(2)}) %collective-permute-start.2) | collective-permute-done | bytes 405536 | tf_op jit(solution)/shard_map/ppermute | solution.py:24
  15.1 1.9 %collective-permute-start.5 = (bf16[512,384]{1,0:T(8,128)(2,1)S(1)}, bf16[512,384]{1,0:T(8,128)(2,1)S(1)}, u32[]{:S(2)}, u32[]{:S(2)}) collective-permute-start(bf16[512,384]{1,0:T(8,128)(2,1)S(1)} %get-tuple-element.75), channel_id=1, source_target_pairs={{0,2},{1,3},{2,0},{3,1},{4,6},{5,7},{6,4},{7,5},{8,10},{9,11},{10,... | collective-permute-start | bytes 1179656 | tf_op jit(solution)/shard_map/ppermute | solution.py:24
  17.0 3.5 %collective-permute-start.6 = (bf16[528,384]{1,0:T(8,128)(2,1)S(1)}, bf16[528,384]{1,0:T(8,128)(2,1)S(1)}, u32[]{:S(2)}, u32[]{:S(2)}) collective-permute-start(bf16[528,384]{1,0:T(8,128)(2,1)S(1)} %collective-permute-done.2.rest_0_), channel_id=1, source_target_pairs={{0,4},{1,5},{4,8},{5,9},{6,2},{7,3},{8,12},{9,13},{10,6},{11,7},{1... | collective-permute-start | bytes 1216520 | tf_op jit(solution)/shard_map/ppermute | solution.py:24
  20.5 3.0 %sib.1.total.near = f32[1024,768]{1,0:T(8,128)S(1)} custom-call(bf16[768,1024]{1,0:T(8,128)(2,1)S(1)} %get-tuple-element.92.own_t, f32[1024,768]{1,0:T(8,128)S(1)} %get-tuple-element.71.total_in, bf16[2,1024,384]{2,1,0:T(8,128)(2,1)S(1)} %collective-permute-done.sib, f32[8,768]{1,0:T(8,128)S(1)} %get-tuple-element.64.levels, ...), custom_call_target="tpu_custom_call", output_to_operand_aliasing={{}: (1, {})} | custom-call | flops 10000000000 | bytes 1 | tf_op jit(solution)/shard_map/sib/pallas_call | solution.py:405
  23.5 0.0 collective-permute-done.1.rest_1_
  23.5 1.9 %collective-permute-start.4 = (bf16[512,384]{1,0:T(8,128)(2,1)S(1)}, bf16[512,384]{1,0:T(8,128)(2,1)S(1)}, u32[]{:S(2)}, u32[]{:S(2)}) collective-permute-start(bf16[512,384]{1,0:T(8,128)(2,1)S(1)} %get-tuple-element.74), channel_id=1, source_target_pairs={{0,2},{1,3},{2,0},{3,1},{4,6},{5,7},{6,4},{7,5},{8,10},{9,11},{10,... | collective-permute-start | bytes 1179656 | tf_op jit(solution)/shard_map/ppermute | solution.py:24
  25.4 3.5 %collective-permute-start.11 = (bf16[512,384]{1,0:T(8,128)(2,1)S(1)}, bf16[512,384]{1,0:T(8,128)(2,1)S(1)}, u32[]{:S(2)}, u32[]{:S(2)}) collective-permute-start(bf16[512,384]{1,0:T(8,128)(2,1)S(1)} %collective-permute-done.1.rest_1_), channel_id=1, source_target_pairs={{0,4},{1,5},{4,8},{5,9},{6,2},{7,3},{8,12},{9,13},{10,6},{11,7},{1... | collective-permute-start | bytes 1179656 | tf_op jit(solution)/shard_map/ppermute | solution.py:24
  28.9 3.0 %collective-permute-done.5.rest_2_ = bf16[512,384]{1,0:T(8,128)(2,1)S(1)} collective-permute-done((bf16[512,384]{1,0:T(8,128)(2,1)S(1)}, bf16[512,384]{1,0:T(8,128)(2,1)S(1)}, u32[]{:S(2)}, u32[]{:S(2)}) %collective-permute-start.5) | collective-permute-done | bytes 393248 | tf_op jit(solution)/shard_map/ppermute | solution.py:24
  31.9 3.9 %collective-permute-start.9 = (bf16[512,384]{1,0:T(8,128)(2,1)S(1)}, bf16[512,384]{1,0:T(8,128)(2,1)S(1)}, u32[]{:S(2)}, u32[]{:S(2)}) collective-permute-start(bf16[512,384]{1,0:T(8,128)(2,1)S(1)} %collective-permute-done.5.rest_2_), channel_id=1, source_target_pairs={{0,4},{1,5},{4,8},{5,9},{6,2},{7,3},{8,12},{9,13},{10,6},{11,7},{1... | collective-permute-start | bytes 1179656 | tf_op jit(solution)/shard_map/ppermute | solution.py:24
  35.9 2.7 %near_metric.1 = (f32[1152,128]{1,0:T(8,128)S(1)}, f32[1152,128]{1,0:T(8,128)S(1)}, s16[1216,128]{1,0:T(8,128)(2,1)S(1)}, s16[1216,128]{1,0:T(8,128)(2,1)S(1)}) custom-call(s32[1]{0:T(128)} %bitcast.me_ref, f32[1024,768]{1,0:T(8,128)S(1)} %sib.1.total.near, bf16[1024,768]{1,0:T(8,128)(2,1)S(1)} %get-tuple-element.80.own_s), custom_call_target="tpu_custom_call" | custom-call | flops 10000000000 | bytes 1 | tf_op jit(solution)/shard_map/near_metric/pallas_call | solution.py:420
  38.6 0.1 collective-permute-start.7
  38.7 0.5 collective-permute-start.8
  39.2 0.2 maximum_select_fusion
  39.4 0.1 collective-permute-start.12
  39.5 0.7 collective-permute-done.7.got_away
  40.2 0.4 collective-permute-done.8.got_keep
  40.7 3.7 %collective-permute-start.10 = (bf16[512,384]{1,0:T(8,128)(2,1)S(1)}, bf16[512,384]{1,0:T(8,128)(2,1)S(1)}, u32[]{:S(2)}, u32[]{:S(2)}) collective-permute-start(bf16[512,384]{1,0:T(8,128)(2,1)S(1)} %collective-permute-done.4.rest_3_), channel_id=1, source_target_pairs={{0,4},{1,5},{4,8},{5,9},{6,2},{7,3},{8,12},{9,13},{10,6},{11,7},{1... | collective-permute-start | bytes 1179656 | tf_op jit(solution)/shard_map/ppermute | solution.py:24
  44.4 0.3 chip.1
  44.7 0.1 collective-permute-start.15
  44.8 0.9 collective-permute-done.9.rest_0_
  45.7 2.6 %far2.1.total_in = f32[1024,768]{1,0:T(8,128)S(1)} custom-call(s32[1]{0:T(128)} %bitcast.me_ref, bf16[768,1024]{1,0:T(8,128)(2,1)S(1)} %get-tuple-element.92.own_t, f32[8,768]{1,0:T(8,128)S(1)} %get-tuple-element.64.levels, f32[8,768]{1,0:T(8,128)S(1)} %get-tuple-element.65.weights, bf16[528,384]{1,0:T(8,128)(2,1)S(1)} %collective-permute-done.2.rest_0_, ...), custom_call_target="tpu_custom_call" | custom-call | flops 10000000000 | bytes 1 | tf_op jit(solution)/shard_map/far2/pallas_call | solution.py:457
  48.3 2.7 %far3.1.total_in = f32[1024,768]{1,0:T(8,128)S(1)} custom-call(s32[1]{0:T(128)} %bitcast.me_ref, bf16[768,1024]{1,0:T(8,128)(2,1)S(1)} %get-tuple-element.92.own_t, f32[8,768]{1,0:T(8,128)S(1)} %get-tuple-element.64.levels, f32[8,768]{1,0:T(8,128)S(1)} %get-tuple-element.65.weights, f32[1024,768]{1,0:T(8,128)S(1)} %far2.1.total_in, ...), custom_call_target="tpu_custom_call", output_to_operand_aliasing={{}: (4, {})} | custom-call | flops 1 | bytes 1 | tf_op jit(solution)/shard_map/far3/pallas_call | solution.py:457
  51.0 0.1 broadcast_select_fusion.1
  51.1 0.1 collective-permute-start.14
  51.2 0.5 collective-permute-start.13
  51.7 2.2 %collective-permute-done.15.across = s16[1216,128]{1,0:T(8,128)(2,1)S(1)} collective-permute-done((s16[1216,128]{1,0:T(8,128)(2,1)S(1)}, s16[1216,128]{1,0:T(8,128)(2,1)S(1)}, u32[]{:S(2)}, u32[]{:S(2)}) %collective-permute-start.15) | collective-permute-done | bytes 311328 | tf_op jit(solution)/shard_map/ppermute | solution.py:24
  53.9 0.1 broadcast_select_fusion
  54.0 0.1 collective-permute-start.16
  54.1 1.7 %collective-permute-done.16.rest_5_ = bf16[512,384]{1,0:T(8,128)(2,1)S(1)} collective-permute-done((bf16[512,384]{1,0:T(8,128)(2,1)S(1)}, bf16[512,384]{1,0:T(8,128)(2,1)S(1)}, u32[]{:S(2)}, u32[]{:S(2)}) %collective-permute-start.16) | collective-permute-done | bytes 393248 | tf_op jit(solution)/shard_map/ppermute | solution.py:24
  55.8 6.7 %last.1 = (f32[1024,768]{1,0:T(8,128)S(1)}, f32[2,1024,384]{2,1,0:T(8,128)}, f32[1152,128]{1,0:T(8,128)S(1)}, f32[1152,128]{1,0:T(8,128)S(1)}) custom-call(s32[1]{0:T(128)} %bitcast.me_ref, bf16[768,1024]{1,0:T(8,128)(2,1)S(1)} %get-tuple-element.92.own_t, f32[8,768]{1,0:T(8,128)S(1)} %get-tuple-element.64.levels, ...), custom_call_target="tpu_custom_call", output_to_operand_aliasing={{0}: (4, {})} | custom-call | flops 1 | bytes 1 | tf_op jit(solution)/shard_map/last/pallas_call | solution.py:457
  62.5 0.2 collective-permute-start.17
  62.7 1.9 %collective-permute-done.17.theirs = f32[1152,128]{1,0:T(8,128)S(1)} collective-permute-done((f32[1152,128]{1,0:T(8,128)S(1)}, f32[1152,128]{1,0:T(8,128)S(1)}, u32[]{:S(2)}, u32[]{:S(2)}) %collective-permute-start.17) | collective-permute-done | bytes 589856 | tf_op jit(solution)/shard_map/ppermute | solution.py:24
  64.5 0.3 column.1
  64.8 2.1 %collective-permute-start.18 = (s16[304,128]{1,0:T(8,128)(2,1)S(1)}, s16[304,128]{1,0:T(8,128)(2,1)S(1)}, u32[]{:S(2)}, u32[]{:S(2)}) collective-permute-start(s16[304,128]{1,0:T(8,128)(2,1)S(1)} %get-tuple-element.113), channel_id=1, source_target_pairs={{0,4},{1,5},{2,6},{3,7},{4,0},{5,1},{6,2},{7,3},{8,12},{9,13},{10,... | collective-permute-start | bytes 233480 | tf_op jit(solution)/shard_map/ppermute | solution.py:24
  66.9 2.8 %collective-permute-start.19 = (s16[304,128]{1,0:T(8,128)(2,1)S(1)}, s16[304,128]{1,0:T(8,128)(2,1)S(1)}, u32[]{:S(2)}, u32[]{:S(2)}) collective-permute-start(s16[304,128]{1,0:T(8,128)(2,1)S(1)} %get-tuple-element.114), channel_id=1, source_target_pairs={{0,8},{1,9},{2,10},{3,11},{4,12},{5,13},{6,14},{7,15},{8,0},{9,1},... | collective-permute-start | bytes 233480 | tf_op jit(solution)/shard_map/ppermute | solution.py:24
  69.8 6.5 %collective-permute-done.19.b = s16[304,128]{1,0:T(8,128)(2,1)S(1)} collective-permute-done((s16[304,128]{1,0:T(8,128)(2,1)S(1)}, s16[304,128]{1,0:T(8,128)(2,1)S(1)}, u32[]{:S(2)}, u32[]{:S(2)}) %collective-permute-start.19) | collective-permute-done | bytes 77856 | tf_op jit(solution)/shard_map/ppermute | solution.py:24
  76.2 0.1 sum_code.1
  76.4 2.7 %collective-permute-start.23 = (s16[304,128]{1,0:T(8,128)(2,1)S(1)}, s16[304,128]{1,0:T(8,128)(2,1)S(1)}, u32[]{:S(2)}, u32[]{:S(2)}) collective-permute-start(s16[304,128]{1,0:T(8,128)(2,1)S(1)} %sum_code.1), channel_id=1, source_target_pairs={{0,12},{1,13},{2,14},{3,15},{4,8},{5,9},{6,10},{7,11},{8,4},{9,5},... | collective-permute-start | bytes 233480 | tf_op jit(solution)/shard_map/ppermute | solution.py:24
  79.0 0.4 collective-permute-start.22
  79.4 1.4 %collective-permute-start.21 = (s16[304,128]{1,0:T(8,128)(2,1)S(1)}, s16[304,128]{1,0:T(8,128)(2,1)S(1)}, u32[]{:S(2)}, u32[]{:S(2)}) collective-permute-start(s16[304,128]{1,0:T(8,128)(2,1)S(1)} %sum_code.1), channel_id=1, source_target_pairs={{0,4},{1,5},{2,6},{3,7},{4,0},{5,1},{6,2},{7,3},{8,12},{9,13},{10,... | collective-permute-start | bytes 233480 | tf_op jit(solution)/shard_map/ppermute | solution.py:24
  80.8 0.4 collective-permute-start.24
  81.2 2.2 %collective-permute-done.23 = s16[304,128]{1,0:T(8,128)(2,1)S(1)} collective-permute-done((s16[304,128]{1,0:T(8,128)(2,1)S(1)}, s16[304,128]{1,0:T(8,128)(2,1)S(1)}, u32[]{:S(2)}, u32[]{:S(2)}) %collective-permute-start.23) | collective-permute-done | bytes 77856 | tf_op jit(solution)/shard_map/ppermute | solution.py:24
  83.4 0.4 collective-permute-start.27
  83.9 1.8 %collective-permute-done.22 = s16[304,128]{1,0:T(8,128)(2,1)S(1)} collective-permute-done((s16[304,128]{1,0:T(8,128)(2,1)S(1)}, s16[304,128]{1,0:T(8,128)(2,1)S(1)}, u32[]{:S(2)}, u32[]{:S(2)}) %collective-permute-start.22) | collective-permute-done | bytes 77856 | tf_op jit(solution)/shard_map/ppermute | solution.py:24
  85.7 0.5 collective-permute-start.26
  86.3 1.5 %collective-permute-start.25 = (s16[304,128]{1,0:T(8,128)(2,1)S(1)}, s16[304,128]{1,0:T(8,128)(2,1)S(1)}, u32[]{:S(2)}, u32[]{:S(2)}) collective-permute-start(s16[304,128]{1,0:T(8,128)(2,1)S(1)} %collective-permute-done.21), channel_id=1, source_target_pairs={{0,2},{1,3},{2,0},{3,1},{4,6},{5,7},{6,4},{7,5},{8,10},{9,11},{10,... | collective-permute-start | bytes 233480 | tf_op jit(solution)/shard_map/ppermute | solution.py:24
  87.8 0.1 collective-permute-start.28
  87.9 0.8 collective-permute-done.27
  88.7 1.7 %collective-permute-done.26 = s16[304,128]{1,0:T(8,128)(2,1)S(1)} collective-permute-done((s16[304,128]{1,0:T(8,128)(2,1)S(1)}, s16[304,128]{1,0:T(8,128)(2,1)S(1)}, u32[]{:S(2)}, u32[]{:S(2)}) %collective-permute-start.26) | collective-permute-done | bytes 77856 | tf_op jit(solution)/shard_map/ppermute | solution.py:24
  90.3 0.8 collective-permute-done.25
  91.2 0.1 collective-permute-start.29
  91.3 1.6 %collective-permute-done.29.sib_b = s16[4,304,128]{2,1,0:T(8,128)(2,1)S(1)} collective-permute-done((s16[4,304,128]{2,1,0:T(8,128)(2,1)S(1)}, s16[4,304,128]{2,1,0:T(8,128)(2,1)S(1)}, u32[]{:S(2)}, u32[]{:S(2)}) %collective-permute-start.29) | collective-permute-done | bytes 311328 | tf_op jit(solution)/shard_map/ppermute | solution.py:24
  92.9 2.8 %spread.1 = f32[1024,1024]{1,0:T(8,128)} custom-call(s32[1]{0:T(128)} %bitcast.me_ref, s16[4,304,128]{2,1,0:T(8,128)(2,1)S(1)} %pad_add_fusion.a, s16[4,304,128]{2,1,0:T(8,128)(2,1)S(1)} %pad_add_fusion.1.b, s16[4,304,128]{2,1,0:T(8,128)(2,1)S(1)} %collective-permute-done.28.sib_a, s16[4,304,128]{2,1,0:T(8,128)(2,1)S(1)} %collective-permute-done.29.sib_b), custom_call_target="tpu_custom_call" | custom-call | flops 1 | bytes 1 | tf_op jit(solution)/shard_map/spread/pallas_call | solution.py:501
  (27 shorter events, 0.2 us)
Async XLA Ops:
  0.6 7.6 %copy-start.3 = (s32[16,384]{1,0:T(8,128)S(1)}, s32[16,384]{1,0:T(8,128)}, u32[]{:S(2)}) copy-start(s32[16,384]{1,0:T(8,128)} %maps_in.1) | copy-start | bytes 73732
  0.6 7.6 %copy-start.2 = (f32[8192]{0:T(1024)S(1)}, f32[8192]{0:T(1024)}, u32[]{:S(2)}) copy-start(f32[8192]{0:T(1024)} %param.8) | copy-start | bytes 98308
  0.7 7.6 %copy-start.5 = (f32[16,2]{0,1:T(2,128)S(1)}, f32[16,2]{0,1:T(2,128)}, u32[]{:S(2)}) copy-start(f32[16,2]{0,1:T(2,128)} %param.7) | copy-start | bytes 388
  1.7 7.8 %collective-permute-start = (bf16[2,1024,384]{2,1,0:T(8,128)(2,1)}, bf16[2,1024,384]{2,1,0:T(8,128)(2,1)S(1)}, u32[]{:S(2)}, u32[]{:S(2)}) collective-permute-start(bf16[2,1024,384]{2,1,0:T(8,128)(2,1)} %bitcast.16), channel_id=1, source_target_pairs={{0,1},{1,0},{2,3},{3,2},{4,5},{5,4},{6,7},{7,6},{8,9},{9,8},{10,11... | collective-permute-start | bytes 4718600 | tf_op jit(solution)/shard_map/ppermute | solution.py:24
  2.2 12.8 %collective-permute-start.2 = (bf16[528,384]{1,0:T(8,128)(2,1)S(1)}, bf16[528,384]{1,0:T(8,128)(2,1)S(1)}, u32[]{:S(2)}, u32[]{:S(2)}) collective-permute-start(bf16[528,384]{1,0:T(8,128)(2,1)S(1)} %slice_bitcast_fusion), channel_id=1, source_target_pairs={{0,2},{1,3},{2,0},{3,1},{4,6},{5,7},{6,4},{7,5},{8,10},{9,11},{10,... | collective-permute-start | bytes 1216520 | tf_op jit(solution)/shard_map/ppermute | solution.py:24
  4.8 3.4 %collective-permute-start.3 = (s32[1,3]{1,0:T(1,128)}, s32[1,3]{1,0:T(1,128)S(1)}, u32[]{:S(2)}, u32[]{:S(2)}) collective-permute-start(s32[1,3]{1,0:T(1,128)} %pairs.3), channel_id=1, source_target_pairs={{0,1},{1,0},{2,3},{3,2},{4,5},{5,4},{6,7},{7,6},{8,9},{9,8},{10,11... | collective-permute-start | bytes 44 | tf_op jit(solution)/shard_map/ppermute | solution.py:24
  5.0 1.4 %copy-start = (bf16[1,2,1024,384]{3,2,1,0:T(8,128)(2,1)S(1)}, bf16[1,2,1024,384]{3,2,1,0:T(8,128)(2,1)}, u32[]{:S(2)}) copy-start(bf16[1,2,1024,384]{3,2,1,0:T(8,128)(2,1)} %param.5) | copy-start | bytes 4718596
  6.4 0.7 copy-start.4
  7.1 2.8 %copy-start.1 = (bf16[1,2,1024,384]{3,2,1,0:T(8,128)(2,1)S(1)}, bf16[1,2,1024,384]{3,2,1,0:T(8,128)(2,1)}, u32[]{:S(2)}) copy-start(bf16[1,2,1024,384]{3,2,1,0:T(8,128)(2,1)} %param.5) | copy-start | bytes 4718596
  9.5 14.0 %collective-permute-start.1 = (bf16[512,384]{1,0:T(8,128)(2,1)S(1)}, bf16[512,384]{1,0:T(8,128)(2,1)S(1)}, u32[]{:S(2)}, u32[]{:S(2)}) collective-permute-start(bf16[512,384]{1,0:T(8,128)(2,1)S(1)} %get-tuple-element.62), channel_id=1, source_target_pairs={{0,2},{1,3},{2,0},{3,1},{4,6},{5,7},{6,4},{7,5},{8,10},{9,11},{10,... | collective-permute-start | bytes 1179656 | tf_op jit(solution)/shard_map/ppermute | solution.py:24
  15.1 16.9 %collective-permute-start.5 = (bf16[512,384]{1,0:T(8,128)(2,1)S(1)}, bf16[512,384]{1,0:T(8,128)(2,1)S(1)}, u32[]{:S(2)}, u32[]{:S(2)}) collective-permute-start(bf16[512,384]{1,0:T(8,128)(2,1)S(1)} %get-tuple-element.75), channel_id=1, source_target_pairs={{0,2},{1,3},{2,0},{3,1},{4,6},{5,7},{6,4},{7,5},{8,10},{9,11},{10,... | collective-permute-start | bytes 1179656 | tf_op jit(solution)/shard_map/ppermute | solution.py:24
  17.0 14.9 %collective-permute-start.6 = (bf16[528,384]{1,0:T(8,128)(2,1)S(1)}, bf16[528,384]{1,0:T(8,128)(2,1)S(1)}, u32[]{:S(2)}, u32[]{:S(2)}) collective-permute-start(bf16[528,384]{1,0:T(8,128)(2,1)S(1)} %collective-permute-done.2.rest_0_), channel_id=1, source_target_pairs={{0,4},{1,5},{4,8},{5,9},{6,2},{7,3},{8,12},{9,13},{10,6},{11,7},{1... | collective-permute-start | bytes 1216520 | tf_op jit(solution)/shard_map/ppermute | solution.py:24
  23.5 17.2 %collective-permute-start.4 = (bf16[512,384]{1,0:T(8,128)(2,1)S(1)}, bf16[512,384]{1,0:T(8,128)(2,1)S(1)}, u32[]{:S(2)}, u32[]{:S(2)}) collective-permute-start(bf16[512,384]{1,0:T(8,128)(2,1)S(1)} %get-tuple-element.74), channel_id=1, source_target_pairs={{0,2},{1,3},{2,0},{3,1},{4,6},{5,7},{6,4},{7,5},{8,10},{9,11},{10,... | collective-permute-start | bytes 1179656 | tf_op jit(solution)/shard_map/ppermute | solution.py:24
  25.4 13.7 %collective-permute-start.11 = (bf16[512,384]{1,0:T(8,128)(2,1)S(1)}, bf16[512,384]{1,0:T(8,128)(2,1)S(1)}, u32[]{:S(2)}, u32[]{:S(2)}) collective-permute-start(bf16[512,384]{1,0:T(8,128)(2,1)S(1)} %collective-permute-done.1.rest_1_), channel_id=1, source_target_pairs={{0,4},{1,5},{4,8},{5,9},{6,2},{7,3},{8,12},{9,13},{10,6},{11,7},{1... | collective-permute-start | bytes 1179656 | tf_op jit(solution)/shard_map/ppermute | solution.py:24
  31.9 13.7 %collective-permute-start.9 = (bf16[512,384]{1,0:T(8,128)(2,1)S(1)}, bf16[512,384]{1,0:T(8,128)(2,1)S(1)}, u32[]{:S(2)}, u32[]{:S(2)}) collective-permute-start(bf16[512,384]{1,0:T(8,128)(2,1)S(1)} %collective-permute-done.5.rest_2_), channel_id=1, source_target_pairs={{0,4},{1,5},{4,8},{5,9},{6,2},{7,3},{8,12},{9,13},{10,6},{11,7},{1... | collective-permute-start | bytes 1179656 | tf_op jit(solution)/shard_map/ppermute | solution.py:24
  38.6 1.7 %collective-permute-start.7 = (s16[1216,128]{1,0:T(8,128)(2,1)S(1)}, s16[1216,128]{1,0:T(8,128)(2,1)S(1)}, u32[]{:S(2)}, u32[]{:S(2)}) collective-permute-start(s16[1216,128]{1,0:T(8,128)(2,1)S(1)} %get-tuple-element.81), channel_id=1, source_target_pairs={{0,1},{1,0},{2,3},{3,2},{4,5},{5,4},{6,7},{7,6},{8,9},{9,8},{10,11... | collective-permute-start | bytes 933896 | tf_op jit(solution)/shard_map/ppermute | solution.py:24
  38.7 2.0 %collective-permute-start.8 = (s16[1216,128]{1,0:T(8,128)(2,1)S(1)}, s16[1216,128]{1,0:T(8,128)(2,1)S(1)}, u32[]{:S(2)}, u32[]{:S(2)}) collective-permute-start(s16[1216,128]{1,0:T(8,128)(2,1)S(1)} %get-tuple-element.82), channel_id=1, source_target_pairs={{0,1},{1,0},{2,3},{3,2},{4,5},{5,4},{6,7},{7,6},{8,9},{9,8},{10,11... | collective-permute-start | bytes 933896 | tf_op jit(solution)/shard_map/ppermute | solution.py:24
  39.4 8.9 %collective-permute-start.12 = (bf16[1040,384]{1,0:T(8,128)(2,1)S(1)}, bf16[1040,384]{1,0:T(8,128)(2,1)S(1)}, u32[]{:S(2)}, u32[]{:S(2)}) collective-permute-start(bf16[1040,384]{1,0:T(8,128)(2,1)S(1)} %maximum_select_fusion), channel_id=1, source_target_pairs={{0,1},{1,0},{2,3},{3,2},{4,5},{5,4},{6,7},{7,6},{8,9},{9,8},{10,11... | collective-permute-start | bytes 2396168 | tf_op jit(solution)/shard_map/ppermute | solution.py:24
  40.7 13.2 %collective-permute-start.10 = (bf16[512,384]{1,0:T(8,128)(2,1)S(1)}, bf16[512,384]{1,0:T(8,128)(2,1)S(1)}, u32[]{:S(2)}, u32[]{:S(2)}) collective-permute-start(bf16[512,384]{1,0:T(8,128)(2,1)S(1)} %collective-permute-done.4.rest_3_), channel_id=1, source_target_pairs={{0,4},{1,5},{4,8},{5,9},{6,2},{7,3},{8,12},{9,13},{10,6},{11,7},{1... | collective-permute-start | bytes 1179656 | tf_op jit(solution)/shard_map/ppermute | solution.py:24
  44.7 9.2 %collective-permute-start.15 = (s16[1216,128]{1,0:T(8,128)(2,1)S(1)}, s16[1216,128]{1,0:T(8,128)(2,1)S(1)}, u32[]{:S(2)}, u32[]{:S(2)}) collective-permute-start(s16[1216,128]{1,0:T(8,128)(2,1)S(1)} %get-tuple-element.102), channel_id=1, source_target_pairs={{0,2},{1,3},{2,0},{3,1},{4,6},{5,7},{6,4},{7,5},{8,10},{9,11},{10,... | collective-permute-start | bytes 933896 | tf_op jit(solution)/shard_map/ppermute | solution.py:24
  51.1 2.8 %collective-permute-start.14 = (bf16[256,384]{1,0:T(8,128)(2,1)S(1)}, bf16[256,384]{1,0:T(8,128)(2,1)S(1)}, u32[]{:S(2)}, u32[]{:S(2)}) collective-permute-start(bf16[256,384]{1,0:T(8,128)(2,1)S(1)} %get-tuple-element.116), channel_id=1, source_target_pairs={{0,1},{1,0},{2,3},{3,2},{4,5},{5,4},{6,7},{7,6},{8,9},{9,8},{10,11... | collective-permute-start | bytes 589832 | tf_op jit(solution)/shard_map/ppermute | solution.py:24
  51.2 2.7 %collective-permute-start.13 = (bf16[256,384]{1,0:T(8,128)(2,1)S(1)}, bf16[256,384]{1,0:T(8,128)(2,1)S(1)}, u32[]{:S(2)}, u32[]{:S(2)}) collective-permute-start(bf16[256,384]{1,0:T(8,128)(2,1)S(1)} %get-tuple-element.117), channel_id=1, source_target_pairs={{0,1},{1,0},{2,3},{3,2},{4,5},{5,4},{6,7},{7,6},{8,9},{9,8},{10,11... | collective-permute-start | bytes 589832 | tf_op jit(solution)/shard_map/ppermute | solution.py:24
  54.0 1.8 %collective-permute-start.16 = (bf16[512,384]{1,0:T(8,128)(2,1)S(1)}, bf16[512,384]{1,0:T(8,128)(2,1)S(1)}, u32[]{:S(2)}, u32[]{:S(2)}) collective-permute-start(bf16[512,384]{1,0:T(8,128)(2,1)S(1)} %broadcast_select_fusion), channel_id=1, source_target_pairs={{0,1},{1,0},{2,3},{3,2},{4,5},{5,4},{6,7},{7,6},{8,9},{9,8},{10,11... | collective-permute-start | bytes 1179656 | tf_op jit(solution)/shard_map/ppermute | solution.py:24
  62.5 2.1 %collective-permute-start.17 = (f32[1152,128]{1,0:T(8,128)S(1)}, f32[1152,128]{1,0:T(8,128)S(1)}, u32[]{:S(2)}, u32[]{:S(2)}) collective-permute-start(f32[1152,128]{1,0:T(8,128)S(1)} %get-tuple-element.109), channel_id=1, source_target_pairs={{0,1},{1,0},{2,3},{3,2},{4,5},{5,4},{6,7},{7,6},{8,9},{9,8},{10,11... | collective-permute-start | bytes 1769480 | tf_op jit(solution)/shard_map/ppermute | solution.py:24
  64.8 5.0 %collective-permute-start.18 = (s16[304,128]{1,0:T(8,128)(2,1)S(1)}, s16[304,128]{1,0:T(8,128)(2,1)S(1)}, u32[]{:S(2)}, u32[]{:S(2)}) collective-permute-start(s16[304,128]{1,0:T(8,128)(2,1)S(1)} %get-tuple-element.113), channel_id=1, source_target_pairs={{0,4},{1,5},{2,6},{3,7},{4,0},{5,1},{6,2},{7,3},{8,12},{9,13},{10,... | collective-permute-start | bytes 233480 | tf_op jit(solution)/shard_map/ppermute | solution.py:24
  66.9 9.3 %collective-permute-start.19 = (s16[304,128]{1,0:T(8,128)(2,1)S(1)}, s16[304,128]{1,0:T(8,128)(2,1)S(1)}, u32[]{:S(2)}, u32[]{:S(2)}) collective-permute-start(s16[304,128]{1,0:T(8,128)(2,1)S(1)} %get-tuple-element.114), channel_id=1, source_target_pairs={{0,8},{1,9},{2,10},{3,11},{4,12},{5,13},{6,14},{7,15},{8,0},{9,1},... | collective-permute-start | bytes 233480 | tf_op jit(solution)/shard_map/ppermute | solution.py:24
  69.8 6.5 %collective-permute-start.20 = (s16[304,128]{1,0:T(8,128)(2,1)S(1)}, s16[304,128]{1,0:T(8,128)(2,1)S(1)}, u32[]{:S(2)}, u32[]{:S(2)}) collective-permute-start(s16[304,128]{1,0:T(8,128)(2,1)S(1)} %get-tuple-element.115), channel_id=1, source_target_pairs={{0,12},{1,13},{2,14},{3,15},{4,8},{5,9},{6,10},{7,11},{8,4},{9,5},... | collective-permute-start | bytes 233480 | tf_op jit(solution)/shard_map/ppermute | solution.py:24
  76.4 7.1 %collective-permute-start.23 = (s16[304,128]{1,0:T(8,128)(2,1)S(1)}, s16[304,128]{1,0:T(8,128)(2,1)S(1)}, u32[]{:S(2)}, u32[]{:S(2)}) collective-permute-start(s16[304,128]{1,0:T(8,128)(2,1)S(1)} %sum_code.1), channel_id=1, source_target_pairs={{0,12},{1,13},{2,14},{3,15},{4,8},{5,9},{6,10},{7,11},{8,4},{9,5},... | collective-permute-start | bytes 233480 | tf_op jit(solution)/shard_map/ppermute | solution.py:24
  79.0 6.7 %collective-permute-start.22 = (s16[304,128]{1,0:T(8,128)(2,1)S(1)}, s16[304,128]{1,0:T(8,128)(2,1)S(1)}, u32[]{:S(2)}, u32[]{:S(2)}) collective-permute-start(s16[304,128]{1,0:T(8,128)(2,1)S(1)} %sum_code.1), channel_id=1, source_target_pairs={{0,8},{1,9},{2,10},{3,11},{4,12},{5,13},{6,14},{7,15},{8,0},{9,1},... | collective-permute-start | bytes 233480 | tf_op jit(solution)/shard_map/ppermute | solution.py:24
  79.4 6.8 %collective-permute-start.21 = (s16[304,128]{1,0:T(8,128)(2,1)S(1)}, s16[304,128]{1,0:T(8,128)(2,1)S(1)}, u32[]{:S(2)}, u32[]{:S(2)}) collective-permute-start(s16[304,128]{1,0:T(8,128)(2,1)S(1)} %sum_code.1), channel_id=1, source_target_pairs={{0,4},{1,5},{2,6},{3,7},{4,0},{5,1},{6,2},{7,3},{8,12},{9,13},{10,... | collective-permute-start | bytes 233480 | tf_op jit(solution)/shard_map/ppermute | solution.py:24
  80.8 7.1 %collective-permute-start.24 = (s16[304,128]{1,0:T(8,128)(2,1)S(1)}, s16[304,128]{1,0:T(8,128)(2,1)S(1)}, u32[]{:S(2)}, u32[]{:S(2)}) collective-permute-start(s16[304,128]{1,0:T(8,128)(2,1)S(1)} %sum_code.1), channel_id=1, source_target_pairs={{0,2},{1,3},{2,0},{3,1},{4,6},{5,7},{6,4},{7,5},{8,10},{9,11},{10,... | collective-permute-start | bytes 233480 | tf_op jit(solution)/shard_map/ppermute | solution.py:24
  83.4 5.2 %collective-permute-start.27 = (s16[304,128]{1,0:T(8,128)(2,1)S(1)}, s16[304,128]{1,0:T(8,128)(2,1)S(1)}, u32[]{:S(2)}, u32[]{:S(2)}) collective-permute-start(s16[304,128]{1,0:T(8,128)(2,1)S(1)} %collective-permute-done.23), channel_id=1, source_target_pairs={{0,2},{1,3},{2,0},{3,1},{4,6},{5,7},{6,4},{7,5},{8,10},{9,11},{10,... | collective-permute-start | bytes 233480 | tf_op jit(solution)/shard_map/ppermute | solution.py:24
  85.7 4.6 %collective-permute-start.26 = (s16[304,128]{1,0:T(8,128)(2,1)S(1)}, s16[304,128]{1,0:T(8,128)(2,1)S(1)}, u32[]{:S(2)}, u32[]{:S(2)}) collective-permute-start(s16[304,128]{1,0:T(8,128)(2,1)S(1)} %collective-permute-done.22), channel_id=1, source_target_pairs={{0,2},{1,3},{2,0},{3,1},{4,6},{5,7},{6,4},{7,5},{8,10},{9,11},{10,... | collective-permute-start | bytes 233480 | tf_op jit(solution)/shard_map/ppermute | solution.py:24
  86.3 4.9 %collective-permute-start.25 = (s16[304,128]{1,0:T(8,128)(2,1)S(1)}, s16[304,128]{1,0:T(8,128)(2,1)S(1)}, u32[]{:S(2)}, u32[]{:S(2)}) collective-permute-start(s16[304,128]{1,0:T(8,128)(2,1)S(1)} %collective-permute-done.21), channel_id=1, source_target_pairs={{0,2},{1,3},{2,0},{3,1},{4,6},{5,7},{6,4},{7,5},{8,10},{9,11},{10,... | collective-permute-start | bytes 233480 | tf_op jit(solution)/shard_map/ppermute | solution.py:24
  87.8 3.5 %collective-permute-start.28 = (s16[4,304,128]{2,1,0:T(8,128)(2,1)S(1)}, s16[4,304,128]{2,1,0:T(8,128)(2,1)S(1)}, u32[]{:S(2)}, u32[]{:S(2)}) collective-permute-start(s16[4,304,128]{2,1,0:T(8,128)(2,1)S(1)} %pad_add_fusion.a), channel_id=1, source_target_pairs={{0,1},{1,0},{2,3},{3,2},{4,5},{5,4},{6,7},{7,6},{8,9},{9,8},{10,11... | collective-permute-start | bytes 933896 | tf_op jit(solution)/shard_map/ppermute | solution.py:24
  91.2 1.7 %collective-permute-start.29 = (s16[4,304,128]{2,1,0:T(8,128)(2,1)S(1)}, s16[4,304,128]{2,1,0:T(8,128)(2,1)S(1)}, u32[]{:S(2)}, u32[]{:S(2)}) collective-permute-start(s16[4,304,128]{2,1,0:T(8,128)(2,1)S(1)} %pad_add_fusion.1.b), channel_id=1, source_target_pairs={{0,1},{1,0},{2,3},{3,2},{4,5},{5,4},{6,7},{7,6},{8,9},{9,8},{10,11... | collective-permute-start | bytes 933896 | tf_op jit(solution)/shard_map/ppermute | solution.py:24

commit v7 on v6

--- a/solution.py
+++ b/solution.py
@@ -12,7 +12,7 @@
 LANES = 128
 BLOCK = 256
 PAD = 16
-PER = 2
+PARTS = (416, 368, 432, 416, 416)
 GROUP = 32
 BITS = 14
 NT = (((1,), (1,)), ((), ()))
@@ -111,10 +111,10 @@
             halves[1][:, s] = (value - high.astype(F32)).astype(BF16)
 
 
-def split_kernel(places, me_ref, pairs, own, *rest):
+def split_kernel(cuts, me_ref, pairs, own, *rest):
     parts, sem = rest[:-1], rest[-1]
     copies = begin(
-        [(own.at[j, pl.ds(a, n)], part.at[pl.ds(0, n)]) for (j, a, n), part in zip(places, parts)], sem
+        [(own.at[pl.ds(a, b)], part.at[pl.ds(0, b)]) for a, b, part in zip(cuts, PARTS[1:], parts)], sem
     )
     rows, virt = parts[0].shape[0] - PAD, parts[0].shape[1]
     lane = lax.broadcasted_iota(I32, (PAD, virt), 1)
@@ -126,8 +126,8 @@
 
 
 def own_kernel(own, levels, weights, own_t, own_s, total, sem, amp):
-    virt = own.shape[2]
-    copies = begin([(own.at[j], own_s.at[:, pl.ds(j * virt, virt)]) for j in range(2)], sem)
+    aux, virt = own.shape[0] // 2, own.shape[1]
+    copies = begin([(own.at[pl.ds(j * aux, aux)], own_s.at[:, pl.ds(j * virt, virt)]) for j in range(2)], sem)
     level = levels[...].T
     finish(copies)
     own_t[...] = own_s[...].T
@@ -135,23 +135,23 @@
 
 
 def sib_kernel(own_t, total_in, sib, levels, weights, total, sem, other, amp):
-    virt = sib.shape[2]
-    copies = begin([(sib.at[j], other.at[:, pl.ds(j * virt, virt)]) for j in range(2)], sem)
+    aux, virt = sib.shape[0] // 2, sib.shape[1]
+    copies = begin([(sib.at[pl.ds(j * aux, aux)], other.at[:, pl.ds(j * virt, virt)]) for j in range(2)], sem)
     level = levels[...].T
     finish(copies)
     add_pair(own_t, other, amp, total, level, levels[1:2, :], weights[1:2, :], False)
 
 
-def fetch(plan, step, me, refs, other):
+def fetch(plan, step, me, refs, other, skip=0):
     counts = []
     for side, (rows, (name, at)) in enumerate(plan):
-        virt = other.shape[1] // 2
+        virt = other.shape[1] // len(plan)
         for source, first, n, to in rows:
             other[to:to + n, side * virt:(side + 1) * virt] = refs[source][first:first + n, :]
-        wanted = -offsets_of(me)[STEPS[step][side][0]]
+        wanted = -offsets_of(me)[STEPS[step][side + skip][0]]
         hits = jnp.where(refs[name][at:at + PAD, :].astype(F32)[0:1, :] == wanted.astype(F32), 1.0, 0.0)
         counts.append(jnp.broadcast_to(jnp.sum(hits, axis=1, keepdims=True), (1, virt)))
-    return jnp.concatenate(counts, axis=1)
+    return jnp.concatenate(counts, axis=1) if len(counts) > 1 else counts[0]
 
 
 def first_far_kernel(plan, names, step, me_ref, own_t, levels, weights, *rest):
@@ -206,6 +206,21 @@
             encode(x[t * piece:(t + 1) * piece, :], send, t * (piece + PAD))
 
 
+def half_kernel(plan, names, step, side, me_ref, own_t, levels, weights, total_in, *rest):
+    refs = dict(zip(names, rest))
+    total, other, amp = rest[len(names):]
+    add_half(plan, refs, step, side, me_ref[0], own_t, levels, weights, total, other, amp)
+
+
+def add_half(plan, refs, step, side, me, own_t, levels, weights, total, other, amp, halves=None, near=None):
+    virt = other.shape[1]
+    columns = slice(side * virt, (side + 1) * virt)
+    count = fetch([plan[side]], step, me, refs, other, side)
+    weight = weights[step:step + 1, columns] - count
+    level = levels[step:step + 1, columns]
+    add_pair(own_t, other, amp, total, levels[...].T, level, weight, False, halves, near)
+
+
 def last_kernel(plan, names, step, me_ref, own_t, levels, weights, total_in, own_s, near, *rest):
     refs = dict(zip(names, rest))
     total, residual, keep, send, sem, other, amp, high, low, packed = rest[len(names):]
@@ -213,8 +228,7 @@
     parity, core, _ = place_of(me)
     aux, wide = total.shape
     virt = wide // 2
-    weight = weights[step:step + 1, :] - fetch(plan, step, me, refs, other)
-    add_pair(own_t, other, amp, total, levels[...].T, levels[step:step + 1, :], weight, False, (high, low), near)
+    add_half(plan, refs, step, 1, me, own_t, levels, weights, total, other, amp, (high, low), near)
     copies = begin([(total.at[:, pl.ds(j * virt, virt)], residual.at[j]) for j in range(2)], sem)
     half, quarter = aux // 2, aux // 4
 
@@ -298,17 +312,25 @@
     encode((mine[...] + decode(a[...]) + decode(b[...]) + decode(c[...])) * scale, out, 0)
 
 
-def spread_kernel(me_ref, a, b, sib_a, sib_b, out, sem, packed, square):
+def unpack(src, which, side, z, packed):
+    rows = src.shape[1] - PAD
+    for t in range(4):
+        row = ((side * 2 + which) * 4 + (z ^ t)) * rows
+        packed[pl.ds(pl.multiple_of(row, 16), rows), :] = decode(src[t])
+
+
+def unpack_kernel(me_ref, a, b, sib_a, packed):
     parity, core, z = place_of(me_ref[0])
-    rows = a.shape[1] - PAD
+    for src, which, side in ((a, core, parity), (b, core, 1 - parity), (sib_a, 1 - core, parity)):
+        unpack(src, which, side, z, packed)
+
+
+def spread_kernel(me_ref, packed_in, sib_b, out, packed, sem, square):
+    parity, core, z = place_of(me_ref[0])
     aux = out.shape[1]
     half, quarter = aux // 2, aux // 4
     plane = packed.shape[0] // 2
-    sources = ((a, core, parity), (b, core, 1 - parity), (sib_a, 1 - core, parity), (sib_b, 1 - core, 1 - parity))
-    for src, which, side in sources:
-        for t in range(4):
-            row = ((side * 2 + which) * 4 + (z ^ t)) * rows
-            packed[pl.ds(pl.multiple_of(row, 16), rows), :] = decode(src[t])
+    unpack(sib_b, 1 - core, 1 - parity, z, packed)
     for side in range(2):
         at = side * plane + plane - half // LANES * quarter
         for c in range(half, aux, LANES):
@@ -370,18 +392,18 @@
     def plain(n):
         return jax.ShapeDtypeStruct((n, LANES), F32)
 
-    cuts = [[at * aux // PER + (PAD if at and at < PER and not j else 0) for at in range(PER + 1)] for j in range(orbitals)]
-    places = [(j, a, b - a) for j in range(orbitals) for a, b in zip(cuts[j], cuts[j][1:])]
-    count = len(places)
-    part = own[0, :places[0][2]]
+    flat = own.reshape(orbitals * aux, virt)
+    cuts = [sum(PARTS[:i]) for i in range(len(PARTS) + 1)]
+    count, early = len(PARTS), len(PARTS) - 2
+    part = flat[:PARTS[0]]
     y = [swapped(part, 2)]
     sib_pairs = swapped(pair_blocks, 1)
     gives_y = ((me[0] >> 1) ^ me[0]) & 1 == 0
-    later, part, gives_y = lax.optimization_barrier((own, part, gives_y))
+    later, part, gives_y = lax.optimization_barrier((flat, part, gives_y))
     sib = swapped(later, 1)
     parts = [None, *kernel(
-        functools.partial(split_kernel, places[1:]), "split", [smem, smem, hbm],
-        [jax.ShapeDtypeStruct((n + (0 if i else PAD), virt), BF16) for i, (_, _, n) in enumerate(places[1:])],
+        functools.partial(split_kernel, cuts[1:-1]), "split", [smem, smem, hbm],
+        [jax.ShapeDtypeStruct((n + (0 if i else PAD), virt), BF16) for i, n in enumerate(PARTS[1:])],
         [vmem] * (count - 1), [dma(count - 1)],
     )(me, pair_blocks, later)]
 
@@ -391,7 +413,7 @@
         functools.partial(prep_kernel, blocks), "prep", [smem] * 3 + [hbm] * 3, (small, small), (vmem, vmem),
         [dma(3), pltpu.VMEM((orbitals, blocks), F32), pltpu.VMEM(energy.shape, F32), pltpu.VMEM(domain_map.shape, I32)],
     )(me, pair_blocks, sib_pairs, occ_energy.T, energy, domain_map)
-    sib, near_own = lax.optimization_barrier((sib, own))
+    sib, near_own = lax.optimization_barrier((sib, flat))
     own_t, own_s, total = kernel(
         own_kernel, "own", [hbm, vmem, vmem],
         (jax.ShapeDtypeStruct((wide, aux), BF16), jax.ShapeDtypeStruct((aux, wide), BF16), total_t), (vmem,) * 3,
@@ -413,14 +435,13 @@
         y[i - 2], part, _ = lax.optimization_barrier((y[i - 2], parts[i], y[i - 3]))
         y.append(swapped(part, 2))
         z.append(forwarded(y[i - 2]))
-    y[-2], z[0] = lax.optimization_barrier((y[-2], z[0]))
-    z.append(forwarded(y[-2]))
-
-    y[-2], near = lax.optimization_barrier((y[-2], total))
+    y[-3], near = lax.optimization_barrier((y[-3], total))
     keep, away, *sends = kernel(
         near_metric_kernel, "near_metric", [smem, vmem, vmem], (plain(upper // 4),) * 2 + (coded(4 * (piece + PAD)),) * 2,
         (vmem,) * 4, [slab_s, slab_s, pltpu.VMEM((upper, LANES), F32)], LARGE_LIMIT, flops=int(1e10),
     )(me, near, own_s)
+    y[-2], z[0], keep = lax.optimization_barrier((y[-2], z[0], keep))
+    z.append(forwarded(y[-2]))
     got = [swapped(send, 1) for send in sends]
     y[-1], *got = lax.optimization_barrier((y[-1], *got))
     z.append(forwarded(y[-1]))
@@ -429,31 +450,38 @@
         chip_kernel, "chip", [vmem] * 4, (plain(upper // 4), coded(4 * (piece + PAD))), (vmem, vmem),
     )(keep, away, *got)
     across = swapped(send, 2)
-    (y[-1], own_t, keep), z[PER:-1] = lax.optimization_barrier(((y[-1], own_t, keep), z[PER:-1]))
+    (y[-1], own_t, keep), z[early:-1] = lax.optimization_barrier(((y[-1], own_t, keep), z[early:-1]))
 
     def given(rows_y, rows_z):
         return swapped(jnp.where(gives_y, jnp.concatenate(rows_y), jnp.concatenate(rows_z)), 1)
 
     arrays = {f"y{i}": part for i, part in enumerate(y)}
     arrays |= {f"z{i}": part for i, part in enumerate(z)}
-    arrays["x0"] = given(y[:PER], z[:PER])
+    arrays["x0"] = given(y[:early], z[:early])
 
     def half_of(which, j):
         name = "y" if which == Y else "z"
-        if which != X:
-            rows = [(f"{name}{i}", 0, n, to) for i, (k, to, n) in enumerate(places) if k == j]
-            return rows, (f"{name}1", places[1][2])
-        if j:
-            cut = places[-1][1]
-            rows = [("x1", 0, cut // 2, 0), ("x2", 0, cut // 2, cut // 2), ("x3", 0, aux - cut, cut)]
-        else:
-            cut = places[0][2] + places[1][2]
-            rows = [("x0", 0, cut, 0)] + ([("x0", cut + PAD, aux - cut, cut)] if cut < aux else [])
-        return rows, ("x0", places[0][2] + places[1][2])
-
-    def pair_step(body, name, step, before=(), outs=(), out_specs=(), scratch=(), flops=1):
+        rows = []
+        for i, (a, b) in enumerate(zip(cuts, cuts[1:])):
+            first, last = max(a, j * aux), min(b, (j + 1) * aux)
+            if first >= last:
+                continue
+            to = first - j * aux
+            if which != X:
+                rows.append((f"{name}{i}", first - a, last - first, to))
+            elif i < early:
+                rows.append(("x0", first + (PAD if i > 1 else 0), last - first, to))
+            elif i == early:
+                n = (b - a) // 2
+                rows += [("x1", 0, n, to), ("x2", 0, b - a - n, to + n)]
+            else:
+                rows.append(("x3", 0, b - a, to))
+        return rows, ("x0", cuts[2]) if which == X else (f"{name}1", PARTS[1])
+
+    def pair_step(body, name, step, before=(), outs=(), out_specs=(), scratch=(), flops=1, side=None):
         plan = [half_of(*half) for half in STEPS[step]]
-        names = list(dict.fromkeys(n for rows, (at, _) in plan for n in [r[0] for r in rows] + [at]))
+        used = plan if side is None else [plan[side]]
+        names = list(dict.fromkeys(n for rows, (at, _) in used for n in [r[0] for r in rows] + [at]))
         return kernel(
             functools.partial(body, plan, names, step), name,
             [smem] + [vmem] * (3 + len(before) + len(names)),
@@ -462,20 +490,23 @@
 
     (total,) = pair_step(first_far_kernel, "far2", 2, scratch=[slab_s, amp_s], flops=int(1e10))
     (total,) = pair_step(far_kernel, "far3", 3, (total,), scratch=[slab_s, amp_s], flops=1)
-    total, *late = lax.optimization_barrier((total, *y[PER:-1], *z[PER:-1]))
-    early = [jnp.where(gives_y, a, b) for a, b in zip(late[:PER - 1], late[PER - 1:])]
-    early = jnp.concatenate(early)
-    middle = early.shape[0] // 2
-    arrays["x1"], arrays["x2"] = swapped(early[:middle], 1), swapped(early[middle:], 1)
+    total, *late = lax.optimization_barrier((total, y[-2], z[-2]))
+    late = jnp.where(gives_y, *late)
+    middle = late.shape[0] // 2
+    arrays["x1"], arrays["x2"] = swapped(late[:middle], 1), swapped(late[middle:], 1)
     z[-1], total, arrays["x1"], arrays["x2"], across = lax.optimization_barrier(
         (z[-1], total, arrays["x1"], arrays["x2"], across)
     )
     arrays[f"z{count - 1}"] = z[-1]
     arrays["x3"] = given(y[-1:], z[-1:])
+    half_s = [pltpu.VMEM((aux, virt), BF16), pltpu.VMEM((wide, virt), BF16)]
+    (total,) = pair_step(
+        lambda *a: half_kernel(*a[:3], 0, *a[3:]), "half", 4, (total,), scratch=half_s, flops=int(1e9), side=0
+    )
     _, residual, mine, send = pair_step(
         last_kernel, "last", 4, (total, own_s, near),
         (jax.ShapeDtypeStruct(own.shape, F32), plain(upper // 4), plain(upper // 4)), (hbm, vmem, vmem),
-        [dma(2), slab_s, amp_s, slab_s, slab_s, pltpu.VMEM((upper // 2, LANES), F32)],
+        [dma(2), *half_s, slab_s, slab_s, pltpu.VMEM((upper // 2, LANES), F32)], side=1,
     )
 
     got = swapped(send, 1)
@@ -498,10 +529,12 @@
     column = [mine] + [swapped(mine, 4 * t) for t in (1, 2, 3)]
     across = [swapped(c, 2) for c in column]
     a, b = jnp.stack(column), jnp.stack(across)
-    gradient = kernel(
-        spread_kernel, "spread", [smem] + [vmem] * 4, jax.ShapeDtypeStruct((aux, aux), F32), hbm,
-        [dma(aux // LANES), pltpu.VMEM((upper, LANES), F32), pltpu.VMEM((aux, aux), F32)],
-    )(me, a, b, swapped(a, 1), swapped(b, 1))
+    sib_a, sib_b = swapped(a, 1), swapped(b, 1)
+    packed = kernel(unpack_kernel, "unpack", [smem] + [vmem] * 3, plain(upper), vmem, flops=int(1e9))(me, a, b, sib_a)
+    gradient, _ = kernel(
+        spread_kernel, "spread", [smem, vmem, vmem], (jax.ShapeDtypeStruct((aux, aux), F32), plain(upper)), (hbm, vmem),
+        [dma(aux // LANES), pltpu.VMEM((aux, aux), F32)], aliases={1: 1},
+    )(me, packed, sib_b)
     return residual[None], gradient
 
 

time: 96.1 us -> 95.2 us (level)
  waiting for transfers between devices: 28.5 us -> 25.2 us
  local copies, waits for them, and re-layouts: 3.17 us -> 4.53 us
    ppermute x30 -> x32, waiting for transfers between devices: 28.5 us -> 25.2 us  [move(): return lax.ppermute(x, 'dom', pairs)]
    unnamed x12, local copies, waits for them, and re-layouts: 2.08 us -> 3.48 us
    squeeze x1 -> x0, local copies, waits for them, and re-layouts: 1.05 us -> none  [shards(): part = own[0, :places[0][2]]]
    pallas_call x3 -> x4, Pallas kernels: 12 us -> 13 us  [pair_step(): kernel(functools.partial(body, plan, names, step), name, [smem] + [vmem]...]
    slice x1 -> x2, local copies, waits for them, and re-layouts: 0.04 us -> 1.05 us  [the longest x1 1.01 us: shards(): part = flat[:PARTS[0]]]
    pallas_call x2 -> x3, Pallas kernels: 3.94 us -> 3.75 us  [the longest x1 2.61 us: shards(): kernel(spread_kernel, 'spread', [smem, vmem, vmem], (jax.ShapeDtypeStruct...]
    ppermute x30 -> x32, starting transfers between devices: 36.1 us -> 36.1 us  [move(): return lax.ppermute(x, 'dom', pairs)]
  transfers between devices with their start and end apart: 30 -> 32, of which waited for: 15 -> 16; matrix products, arithmetic and copies ran while one was open for 0% -> 0% of each run, Pallas kernels for 17% -> 20%
where the time goes in v7:
time: 95.2 us; the launch traced here: 94.9 us
  starting transfers between devices  36.1 us (38%)
  Pallas kernels  27.5 us (29%)
  waiting for transfers between devices  25.2 us (26%)
  local copies, waits for them, and re-layouts  4.53 us (5%)
  between operations  1.18 us (1%)
    ppermute x32, starting transfers between devices, move(): return lax.ppermute(x, 'dom', pairs)  36.1 us
    ppermute x32, waiting for transfers between devices, move(): return lax.ppermute(x, 'dom', pairs)  25.2 us
    pallas_call x4, Pallas kernels, pair_step(): kernel(functools.partial(body, plan, names, step), name, [smem] + [vmem]...  13 us
    unnamed x12, local copies, waits for them, and re-layouts  3.48 us
    pallas_call x1, Pallas kernels, shards(): kernel(own_kernel, 'own', [hbm, vmem, vmem], (jax.ShapeDtypeStruct((wide,...  3.01 us
    pallas_call x1, Pallas kernels, shards(): kernel(sib_kernel, 'sib', [vmem, vmem, hbm, vmem, vmem], total_t, vmem, [...  2.98 us
    pallas_call x1, Pallas kernels, shards(): kernel(near_metric_kernel, 'near_metric', [smem, vmem, vmem], (plain(uppe...  2.72 us
    pallas_call x1, Pallas kernels, shards(): kernel(spread_kernel, 'spread', [smem, vmem, vmem], (jax.ShapeDtypeStruct...  2.61 us
  transfers between devices with their start and end apart: 32, of which 16 were waited for; matrix products, arithmetic and copies ran while one was open for 0% of the time, Pallas kernels for 20%

profile of v7, /device:TPU:0, one launch (start us, length us, event | category | flops | bytes accessed | tf_op | source)
XLA Modules:
  0.0 94.9 jit_solution(12134544405905234637)
XLA Ops:
  0.7 1.0 %slice.12 = bf16[416,384]{1,0:T(8,128)(2,1)S(1)} slice(bf16[2048,384]{1,0:T(8,128)(2,1)} %bitcast.13), slice={[0:416], [0:384]} | slice | bytes 638976 | tf_op jit(solution)/shard_map/slice | solution.py:398
  1.7 0.5 collective-permute-start.1
  2.2 2.6 %collective-permute-start = (bf16[416,384]{1,0:T(8,128)(2,1)S(1)}, bf16[416,384]{1,0:T(8,128)(2,1)S(1)}, u32[]{:S(2)}, u32[]{:S(2)}) collective-permute-start(bf16[416,384]{1,0:T(8,128)(2,1)S(1)} %slice.12), channel_id=1, source_target_pairs={{0,2},{1,3},{2,0},{3,1},{4,6},{5,7},{6,4},{7,5},{8,10},{9,11},{10,... | collective-permute-start | bytes 958472 | tf_op jit(solution)/shard_map/ppermute | solution.py:24
  4.8 0.2 collective-permute-start.2
  5.0 1.4 %copy-done = bf16[1,2,1024,384]{3,2,1,0:T(8,128)(2,1)S(1)} copy-done((bf16[1,2,1024,384]{3,2,1,0:T(8,128)(2,1)S(1)}, bf16[1,2,1024,384]{3,2,1,0:T(8,128)(2,1)}, u32[]{:S(2)}) %copy-start) | copy-done | bytes 1572888
  6.4 0.7 copy-done.4
  7.0 0.9 split.1
  8.0 1.3 %prep.1 = (f32[8,768]{1,0:T(8,128)S(1)}, f32[8,768]{1,0:T(8,128)S(1)}) custom-call(s32[1]{0:T(128)} %bitcast.me_ref.a_0_, s32[1,3]{1,0:T(1,128)S(1)} %copy-done.4, s32[1,3]{1,0:T(1,128)S(1)} %collective-permute-done.2.sib_pairs, f32[2,16]{1,0:T(2,128)S(1)} %bitcast.19, f32[64,128]{1,0:T(8,128)S(1)} %bitcast.18, s32[16,384]{1,0:T(8,128)S(1)} %copy-done.3), custom_call_target="tpu_custom_call" | custom-call | flops 1 | bytes 1 | tf_op jit(solution)/shard_map/prep/pallas_call | solution.py:412
  9.3 0.4 collective-permute-start.4
  9.7 1.4 %copy-done.1 = bf16[1,2,1024,384]{3,2,1,0:T(8,128)(2,1)S(1)} copy-done((bf16[1,2,1024,384]{3,2,1,0:T(8,128)(2,1)S(1)}, bf16[1,2,1024,384]{3,2,1,0:T(8,128)(2,1)}, u32[]{:S(2)}) %copy-start.1) | copy-done | bytes 1572888
  11.1 3.0 %own.1 = (bf16[768,1024]{1,0:T(8,128)(2,1)S(1)}, bf16[1024,768]{1,0:T(8,128)(2,1)S(1)}, f32[1024,768]{1,0:T(8,128)S(1)}) custom-call(bf16[2048,384]{1,0:T(8,128)(2,1)S(1)} %bitcast.16, f32[8,768]{1,0:T(8,128)S(1)} %get-tuple-element.66.levels.a_2_, f32[8,768]{1,0:T(8,128)S(1)} %get-tuple-element.67.weights.a_3_), custom_call_target="tpu_custom_call" | custom-call | flops 20000000000 | bytes 1 | tf_op jit(solution)/shard_map/own/pallas_call | solution.py:417
  14.1 3.7 %collective-permute-start.9 = (bf16[416,384]{1,0:T(8,128)(2,1)S(1)}, bf16[416,384]{1,0:T(8,128)(2,1)S(1)}, u32[]{:S(2)}, u32[]{:S(2)}) collective-permute-start(bf16[416,384]{1,0:T(8,128)(2,1)S(1)} %collective-permute-done.rest_0_), channel_id=1, source_target_pairs={{0,4},{1,5},{4,8},{5,9},{6,2},{7,3},{8,12},{9,13},{10,6},{11,7},{1... | collective-permute-start | bytes 958472 | tf_op jit(solution)/shard_map/ppermute | solution.py:24
  17.8 0.1 collective-permute-start.3
  17.9 3.0 %sib.1.total.near = f32[1024,768]{1,0:T(8,128)S(1)} custom-call(bf16[768,1024]{1,0:T(8,128)(2,1)S(1)} %get-tuple-element.102.own_t.a_1_, f32[1024,768]{1,0:T(8,128)S(1)} %get-tuple-element.78.total_in, bf16[2048,384]{1,0:T(8,128)(2,1)S(1)} %collective-permute-done.1.sib, f32[8,768]{1,0:T(8,128)S(1)} %get-tuple-element.66.levels.a_2_, ...), custom_call_target="tpu_custom_call", output_to_operand_aliasing={{}: (1, {})} | custom-call | flops 10000000000 | bytes 1 | tf_op jit(solution)/shard_map/sib/pallas_call | solution.py:427
  20.9 3.9 %collective-permute-start.12 = (bf16[384,384]{1,0:T(8,128)(2,1)S(1)}, bf16[384,384]{1,0:T(8,128)(2,1)S(1)}, u32[]{:S(2)}, u32[]{:S(2)}) collective-permute-start(bf16[384,384]{1,0:T(8,128)(2,1)S(1)} %collective-permute-done.4.rest_1_), channel_id=1, source_target_pairs={{0,4},{1,5},{4,8},{5,9},{6,2},{7,3},{8,12},{9,13},{10,6},{11,7},{1... | collective-permute-start | bytes 884744 | tf_op jit(solution)/shard_map/ppermute | solution.py:24
  24.7 0.1 collective-permute-start.8
  24.8 3.2 %collective-permute-done.3.rest_2_ = bf16[432,384]{1,0:T(8,128)(2,1)S(1)} collective-permute-done((bf16[432,384]{1,0:T(8,128)(2,1)S(1)}, bf16[432,384]{1,0:T(8,128)(2,1)S(1)}, u32[]{:S(2)}, u32[]{:S(2)}) %collective-permute-start.3) | collective-permute-done | bytes 331808 | tf_op jit(solution)/shard_map/ppermute | solution.py:24
  28.0 3.5 %collective-permute-start.13 = (bf16[432,384]{1,0:T(8,128)(2,1)S(1)}, bf16[432,384]{1,0:T(8,128)(2,1)S(1)}, u32[]{:S(2)}, u32[]{:S(2)}) collective-permute-start(bf16[432,384]{1,0:T(8,128)(2,1)S(1)} %collective-permute-done.3.rest_2_), channel_id=1, source_target_pairs={{0,4},{1,5},{4,8},{5,9},{6,2},{7,3},{8,12},{9,13},{10,6},{11,7},{1... | collective-permute-start | bytes 995336 | tf_op jit(solution)/shard_map/ppermute | solution.py:24
  31.5 0.1 collective-permute-start.5
  31.6 2.7 %near_metric.1 = (f32[1152,128]{1,0:T(8,128)S(1)}, f32[1152,128]{1,0:T(8,128)S(1)}, s16[1216,128]{1,0:T(8,128)(2,1)S(1)}, s16[1216,128]{1,0:T(8,128)(2,1)S(1)}) custom-call(s32[1]{0:T(128)} %bitcast.me_ref.a_0_, f32[1024,768]{1,0:T(8,128)S(1)} %sib.1.total.near, bf16[1024,768]{1,0:T(8,128)(2,1)S(1)} %get-tuple-element.86.own_s), custom_call_target="tpu_custom_call" | custom-call | flops 10000000000 | bytes 1 | tf_op jit(solution)/shard_map/near_metric/pallas_call | solution.py:439
  34.3 1.0 %collective-permute-done.8.rest_3_ = bf16[416,384]{1,0:T(8,128)(2,1)S(1)} collective-permute-done((bf16[416,384]{1,0:T(8,128)(2,1)S(1)}, bf16[416,384]{1,0:T(8,128)(2,1)S(1)}, u32[]{:S(2)}, u32[]{:S(2)}) %collective-permute-start.8) | collective-permute-done | bytes 319520 | tf_op jit(solution)/shard_map/ppermute | solution.py:24
  35.3 3.5 %collective-permute-start.10 = (bf16[416,384]{1,0:T(8,128)(2,1)S(1)}, bf16[416,384]{1,0:T(8,128)(2,1)S(1)}, u32[]{:S(2)}, u32[]{:S(2)}) collective-permute-start(bf16[416,384]{1,0:T(8,128)(2,1)S(1)} %collective-permute-done.8.rest_3_), channel_id=1, source_target_pairs={{0,4},{1,5},{4,8},{5,9},{6,2},{7,3},{8,12},{9,13},{10,6},{11,7},{1... | collective-permute-start | bytes 958472 | tf_op jit(solution)/shard_map/ppermute | solution.py:24
  38.8 0.5 collective-permute-start.7
  39.3 0.2 collective-permute-done.13.rest_2_.a_5_
  39.6 0.2 maximum_select_fusion
  39.8 0.1 collective-permute-start.14
  39.9 0.5 collective-permute-done.6.got_away
  40.4 0.4 collective-permute-done.7.got_keep
  40.9 0.2 collective-permute-done.5.rest_4_
  41.0 3.7 %collective-permute-start.11 = (bf16[416,384]{1,0:T(8,128)(2,1)S(1)}, bf16[416,384]{1,0:T(8,128)(2,1)S(1)}, u32[]{:S(2)}, u32[]{:S(2)}) collective-permute-start(bf16[416,384]{1,0:T(8,128)(2,1)S(1)} %collective-permute-done.5.rest_4_), channel_id=1, source_target_pairs={{0,4},{1,5},{4,8},{5,9},{6,2},{7,3},{8,12},{9,13},{10,6},{11,7},{1... | collective-permute-start | bytes 958472 | tf_op jit(solution)/shard_map/ppermute | solution.py:24
  44.7 0.3 chip.1
  45.0 0.1 collective-permute-start.17
  45.2 2.7 %far2.1.total_in = f32[1024,768]{1,0:T(8,128)S(1)} custom-call(s32[1]{0:T(128)} %bitcast.me_ref.a_0_, bf16[768,1024]{1,0:T(8,128)(2,1)S(1)} %get-tuple-element.102.own_t.a_1_, f32[8,768]{1,0:T(8,128)S(1)} %get-tuple-element.66.levels.a_2_, f32[8,768]{1,0:T(8,128)S(1)} %get-tuple-element.67.weights.a_3_, bf16[416,384]{1,0:T(8,128)(2,1)S(1)} %collective-permute-done.rest_0_, ...), custom_call_target="tpu_custom_call" | custom-call | flops 10000000000 | bytes 1 | tf_op jit(solution)/shard_map/far2/pallas_call | solution.py:485
  47.8 2.7 %far3.1.a_4_ = f32[1024,768]{1,0:T(8,128)S(1)} custom-call(s32[1]{0:T(128)} %bitcast.me_ref.a_0_, bf16[768,1024]{1,0:T(8,128)(2,1)S(1)} %get-tuple-element.102.own_t.a_1_, f32[8,768]{1,0:T(8,128)S(1)} %get-tuple-element.66.levels.a_2_, f32[8,768]{1,0:T(8,128)S(1)} %get-tuple-element.67.weights.a_3_, ...), custom_call_target="tpu_custom_call", output_to_operand_aliasing={{}: (4, {})} | custom-call | flops 1 | bytes 1 | tf_op jit(solution)/shard_map/far3/pallas_call | solution.py:485
  50.6 0.1 collective-permute-start.16
  50.7 0.5 collective-permute-start.15
  51.2 3.2 %collective-permute-done.17.across = s16[1216,128]{1,0:T(8,128)(2,1)S(1)} collective-permute-done((s16[1216,128]{1,0:T(8,128)(2,1)S(1)}, s16[1216,128]{1,0:T(8,128)(2,1)S(1)}, u32[]{:S(2)}, u32[]{:S(2)}) %collective-permute-start.17) | collective-permute-done | bytes 311328 | tf_op jit(solution)/shard_map/ppermute | solution.py:24
  54.5 0.1 collective-permute-start.18
  54.5 1.9 %half.1.total_in = f32[1024,768]{1,0:T(8,128)S(1)} custom-call(s32[1]{0:T(128)} %bitcast.me_ref.a_0_, bf16[768,1024]{1,0:T(8,128)(2,1)S(1)} %get-tuple-element.102.own_t.a_1_, f32[8,768]{1,0:T(8,128)S(1)} %get-tuple-element.66.levels.a_2_, f32[8,768]{1,0:T(8,128)S(1)} %get-tuple-element.67.weights.a_3_, ...), custom_call_target="tpu_custom_call", output_to_operand_aliasing={{}: (4, {})} | custom-call | flops 1000000000 | bytes 1 | tf_op jit(solution)/shard_map/half/pallas_call | solution.py:485
  56.4 5.8 %last.1 = (f32[1024,768]{1,0:T(8,128)S(1)}, f32[2,1024,384]{2,1,0:T(8,128)}, f32[1152,128]{1,0:T(8,128)S(1)}, f32[1152,128]{1,0:T(8,128)S(1)}) custom-call(s32[1]{0:T(128)} %bitcast.me_ref.a_0_, bf16[768,1024]{1,0:T(8,128)(2,1)S(1)} %get-tuple-element.102.own_t.a_1_, f32[8,768]{1,0:T(8,128)S(1)} %get-tuple-element.66.levels.a_2_, ...), custom_call_target="tpu_custom_call", output_to_operand_aliasing={{0}: (4, {})} | custom-call | flops 1 | bytes 1 | tf_op jit(solution)/shard_map/last/pallas_call | solution.py:485
  62.2 0.6 collective-permute-start.19
  62.8 1.6 %collective-permute-done.19.theirs = f32[1152,128]{1,0:T(8,128)S(1)} collective-permute-done((f32[1152,128]{1,0:T(8,128)S(1)}, f32[1152,128]{1,0:T(8,128)S(1)}, u32[]{:S(2)}, u32[]{:S(2)}) %collective-permute-start.19) | collective-permute-done | bytes 589856 | tf_op jit(solution)/shard_map/ppermute | solution.py:24
  64.4 0.3 column.1
  64.7 1.7 %collective-permute-start.20 = (s16[304,128]{1,0:T(8,128)(2,1)S(1)}, s16[304,128]{1,0:T(8,128)(2,1)S(1)}, u32[]{:S(2)}, u32[]{:S(2)}) collective-permute-start(s16[304,128]{1,0:T(8,128)(2,1)S(1)} %get-tuple-element.122), channel_id=1, source_target_pairs={{0,4},{1,5},{2,6},{3,7},{4,0},{5,1},{6,2},{7,3},{8,12},{9,13},{10,... | collective-permute-start | bytes 233480 | tf_op jit(solution)/shard_map/ppermute | solution.py:24
  66.4 1.8 %collective-permute-start.21 = (s16[304,128]{1,0:T(8,128)(2,1)S(1)}, s16[304,128]{1,0:T(8,128)(2,1)S(1)}, u32[]{:S(2)}, u32[]{:S(2)}) collective-permute-start(s16[304,128]{1,0:T(8,128)(2,1)S(1)} %get-tuple-element.123), channel_id=1, source_target_pairs={{0,8},{1,9},{2,10},{3,11},{4,12},{5,13},{6,14},{7,15},{8,0},{9,1},... | collective-permute-start | bytes 233480 | tf_op jit(solution)/shard_map/ppermute | solution.py:24
  68.2 1.0 %collective-permute-start.22 = (s16[304,128]{1,0:T(8,128)(2,1)S(1)}, s16[304,128]{1,0:T(8,128)(2,1)S(1)}, u32[]{:S(2)}, u32[]{:S(2)}) collective-permute-start(s16[304,128]{1,0:T(8,128)(2,1)S(1)} %get-tuple-element.124), channel_id=1, source_target_pairs={{0,12},{1,13},{2,14},{3,15},{4,8},{5,9},{6,10},{7,11},{8,4},{9,5},... | collective-permute-start | bytes 233480 | tf_op jit(solution)/shard_map/ppermute | solution.py:24
  69.2 0.2 collective-permute-done.20.a
  69.4 6.3 %collective-permute-done.21.b = s16[304,128]{1,0:T(8,128)(2,1)S(1)} collective-permute-done((s16[304,128]{1,0:T(8,128)(2,1)S(1)}, s16[304,128]{1,0:T(8,128)(2,1)S(1)}, u32[]{:S(2)}, u32[]{:S(2)}) %collective-permute-start.21) | collective-permute-done | bytes 77856 | tf_op jit(solution)/shard_map/ppermute | solution.py:24
  75.7 0.1 sum_code.1
  75.8 2.1 %collective-permute-start.25 = (s16[304,128]{1,0:T(8,128)(2,1)S(1)}, s16[304,128]{1,0:T(8,128)(2,1)S(1)}, u32[]{:S(2)}, u32[]{:S(2)}) collective-permute-start(s16[304,128]{1,0:T(8,128)(2,1)S(1)} %sum_code.1), channel_id=1, source_target_pairs={{0,12},{1,13},{2,14},{3,15},{4,8},{5,9},{6,10},{7,11},{8,4},{9,5},... | collective-permute-start | bytes 233480 | tf_op jit(solution)/shard_map/ppermute | solution.py:24
  77.9 0.9 collective-permute-start.24
  78.8 1.5 %collective-permute-start.23 = (s16[304,128]{1,0:T(8,128)(2,1)S(1)}, s16[304,128]{1,0:T(8,128)(2,1)S(1)}, u32[]{:S(2)}, u32[]{:S(2)}) collective-permute-start(s16[304,128]{1,0:T(8,128)(2,1)S(1)} %sum_code.1), channel_id=1, source_target_pairs={{0,4},{1,5},{2,6},{3,7},{4,0},{5,1},{6,2},{7,3},{8,12},{9,13},{10,... | collective-permute-start | bytes 233480 | tf_op jit(solution)/shard_map/ppermute | solution.py:24
  80.3 0.6 collective-permute-start.26
  80.8 2.1 %collective-permute-done.25 = s16[304,128]{1,0:T(8,128)(2,1)S(1)} collective-permute-done((s16[304,128]{1,0:T(8,128)(2,1)S(1)}, s16[304,128]{1,0:T(8,128)(2,1)S(1)}, u32[]{:S(2)}, u32[]{:S(2)}) %collective-permute-start.25) | collective-permute-done | bytes 77856 | tf_op jit(solution)/shard_map/ppermute | solution.py:24
  82.9 0.5 collective-permute-start.29
  83.4 1.7 %collective-permute-done.24 = s16[304,128]{1,0:T(8,128)(2,1)S(1)} collective-permute-done((s16[304,128]{1,0:T(8,128)(2,1)S(1)}, s16[304,128]{1,0:T(8,128)(2,1)S(1)}, u32[]{:S(2)}, u32[]{:S(2)}) %collective-permute-start.24) | collective-permute-done | bytes 77856 | tf_op jit(solution)/shard_map/ppermute | solution.py:24
  85.2 0.5 collective-permute-start.28
  85.7 1.5 %collective-permute-start.27 = (s16[304,128]{1,0:T(8,128)(2,1)S(1)}, s16[304,128]{1,0:T(8,128)(2,1)S(1)}, u32[]{:S(2)}, u32[]{:S(2)}) collective-permute-start(s16[304,128]{1,0:T(8,128)(2,1)S(1)} %collective-permute-done.23), channel_id=1, source_target_pairs={{0,2},{1,3},{2,0},{3,1},{4,6},{5,7},{6,4},{7,5},{8,10},{9,11},{10,... | collective-permute-start | bytes 233480 | tf_op jit(solution)/shard_map/ppermute | solution.py:24
  87.3 0.7 collective-permute-done.29
  88.0 1.5 %collective-permute-done.28 = s16[304,128]{1,0:T(8,128)(2,1)S(1)} collective-permute-done((s16[304,128]{1,0:T(8,128)(2,1)S(1)}, s16[304,128]{1,0:T(8,128)(2,1)S(1)}, u32[]{:S(2)}, u32[]{:S(2)}) %collective-permute-start.28) | collective-permute-done | bytes 77856 | tf_op jit(solution)/shard_map/ppermute | solution.py:24
  89.6 0.8 collective-permute-done.27
  90.5 0.2 unpack.1.packed_in
  90.7 1.4 %collective-permute-done.31.sib_b = s16[4,304,128]{2,1,0:T(8,128)(2,1)S(1)} collective-permute-done((s16[4,304,128]{2,1,0:T(8,128)(2,1)S(1)}, s16[4,304,128]{2,1,0:T(8,128)(2,1)S(1)}, u32[]{:S(2)}, u32[]{:S(2)}) %collective-permute-start.31) | collective-permute-done | bytes 311328 | tf_op jit(solution)/shard_map/ppermute | solution.py:24
  92.1 2.6 %spread.1 = (f32[1024,1024]{1,0:T(8,128)}, f32[4608,128]{1,0:T(8,128)S(1)}) custom-call(s32[1]{0:T(128)} %bitcast.me_ref.a_0_, f32[4608,128]{1,0:T(8,128)S(1)} %unpack.1.packed_in, s16[4,304,128]{2,1,0:T(8,128)(2,1)S(1)} %collective-permute-done.31.sib_b), custom_call_target="tpu_custom_call", output_to_operand_aliasing={{1}: (1, {})} | custom-call | flops 1 | bytes 1 | tf_op jit(solution)/shard_map/spread/pallas_call | solution.py:534
  (33 shorter events, 0.5 us)
Async XLA Ops:
  0.6 7.3 %copy-start.3 = (s32[16,384]{1,0:T(8,128)S(1)}, s32[16,384]{1,0:T(8,128)}, u32[]{:S(2)}) copy-start(s32[16,384]{1,0:T(8,128)} %maps_in.1) | copy-start | bytes 73732
  0.6 7.3 %copy-start.2 = (f32[8192]{0:T(1024)S(1)}, f32[8192]{0:T(1024)}, u32[]{:S(2)}) copy-start(f32[8192]{0:T(1024)} %param.8) | copy-start | bytes 98308
  0.7 7.3 %copy-start.5 = (f32[16,2]{0,1:T(2,128)S(1)}, f32[16,2]{0,1:T(2,128)}, u32[]{:S(2)}) copy-start(f32[16,2]{0,1:T(2,128)} %param.7) | copy-start | bytes 388
  1.7 7.6 %collective-permute-start.1 = (bf16[2048,384]{1,0:T(8,128)(2,1)}, bf16[2048,384]{1,0:T(8,128)(2,1)S(1)}, u32[]{:S(2)}, u32[]{:S(2)}) collective-permute-start(bf16[2048,384]{1,0:T(8,128)(2,1)} %bitcast.14), channel_id=1, source_target_pairs={{0,1},{1,0},{2,3},{3,2},{4,5},{5,4},{6,7},{7,6},{8,9},{9,8},{10,11... | collective-permute-start | bytes 4718600 | tf_op jit(solution)/shard_map/ppermute | solution.py:24
  2.2 11.9 %collective-permute-start = (bf16[416,384]{1,0:T(8,128)(2,1)S(1)}, bf16[416,384]{1,0:T(8,128)(2,1)S(1)}, u32[]{:S(2)}, u32[]{:S(2)}) collective-permute-start(bf16[416,384]{1,0:T(8,128)(2,1)S(1)} %slice.12), channel_id=1, source_target_pairs={{0,2},{1,3},{2,0},{3,1},{4,6},{5,7},{6,4},{7,5},{8,10},{9,11},{10,... | collective-permute-start | bytes 958472 | tf_op jit(solution)/shard_map/ppermute | solution.py:24
  4.8 3.2 %collective-permute-start.2 = (s32[1,3]{1,0:T(1,128)}, s32[1,3]{1,0:T(1,128)S(1)}, u32[]{:S(2)}, u32[]{:S(2)}) collective-permute-start(s32[1,3]{1,0:T(1,128)} %pairs.3), channel_id=1, source_target_pairs={{0,1},{1,0},{2,3},{3,2},{4,5},{5,4},{6,7},{7,6},{8,9},{9,8},{10,11... | collective-permute-start | bytes 44 | tf_op jit(solution)/shard_map/ppermute | solution.py:24
  5.0 1.4 %copy-start = (bf16[1,2,1024,384]{3,2,1,0:T(8,128)(2,1)S(1)}, bf16[1,2,1024,384]{3,2,1,0:T(8,128)(2,1)}, u32[]{:S(2)}) copy-start(bf16[1,2,1024,384]{3,2,1,0:T(8,128)(2,1)} %param.5) | copy-start | bytes 4718596
  6.4 0.7 copy-start.4
  9.3 11.6 %collective-permute-start.4 = (bf16[384,384]{1,0:T(8,128)(2,1)S(1)}, bf16[384,384]{1,0:T(8,128)(2,1)S(1)}, u32[]{:S(2)}, u32[]{:S(2)}) collective-permute-start(bf16[384,384]{1,0:T(8,128)(2,1)S(1)} %get-tuple-element.76), channel_id=1, source_target_pairs={{0,2},{1,3},{2,0},{3,1},{4,6},{5,7},{6,4},{7,5},{8,10},{9,11},{10,... | collective-permute-start | bytes 884744 | tf_op jit(solution)/shard_map/ppermute | solution.py:24
  9.7 1.4 %copy-start.1 = (bf16[1,2,1024,384]{3,2,1,0:T(8,128)(2,1)S(1)}, bf16[1,2,1024,384]{3,2,1,0:T(8,128)(2,1)}, u32[]{:S(2)}) copy-start(bf16[1,2,1024,384]{3,2,1,0:T(8,128)(2,1)} %param.5) | copy-start | bytes 4718596
  14.1 20.2 %collective-permute-start.9 = (bf16[416,384]{1,0:T(8,128)(2,1)S(1)}, bf16[416,384]{1,0:T(8,128)(2,1)S(1)}, u32[]{:S(2)}, u32[]{:S(2)}) collective-permute-start(bf16[416,384]{1,0:T(8,128)(2,1)S(1)} %collective-permute-done.rest_0_), channel_id=1, source_target_pairs={{0,4},{1,5},{4,8},{5,9},{6,2},{7,3},{8,12},{9,13},{10,6},{11,7},{1... | collective-permute-start | bytes 958472 | tf_op jit(solution)/shard_map/ppermute | solution.py:24
  17.8 10.2 %collective-permute-start.3 = (bf16[432,384]{1,0:T(8,128)(2,1)S(1)}, bf16[432,384]{1,0:T(8,128)(2,1)S(1)}, u32[]{:S(2)}, u32[]{:S(2)}) collective-permute-start(bf16[432,384]{1,0:T(8,128)(2,1)S(1)} %get-tuple-element.74), channel_id=1, source_target_pairs={{0,2},{1,3},{2,0},{3,1},{4,6},{5,7},{6,4},{7,5},{8,10},{9,11},{10,... | collective-permute-start | bytes 995336 | tf_op jit(solution)/shard_map/ppermute | solution.py:24
  20.9 18.0 %collective-permute-start.12 = (bf16[384,384]{1,0:T(8,128)(2,1)S(1)}, bf16[384,384]{1,0:T(8,128)(2,1)S(1)}, u32[]{:S(2)}, u32[]{:S(2)}) collective-permute-start(bf16[384,384]{1,0:T(8,128)(2,1)S(1)} %collective-permute-done.4.rest_1_), channel_id=1, source_target_pairs={{0,4},{1,5},{4,8},{5,9},{6,2},{7,3},{8,12},{9,13},{10,6},{11,7},{1... | collective-permute-start | bytes 884744 | tf_op jit(solution)/shard_map/ppermute | solution.py:24
  24.7 10.5 %collective-permute-start.8 = (bf16[416,384]{1,0:T(8,128)(2,1)S(1)}, bf16[416,384]{1,0:T(8,128)(2,1)S(1)}, u32[]{:S(2)}, u32[]{:S(2)}) collective-permute-start(bf16[416,384]{1,0:T(8,128)(2,1)S(1)} %get-tuple-element.90), channel_id=1, source_target_pairs={{0,2},{1,3},{2,0},{3,1},{4,6},{5,7},{6,4},{7,5},{8,10},{9,11},{10,... | collective-permute-start | bytes 958472 | tf_op jit(solution)/shard_map/ppermute | solution.py:24
  28.0 11.6 %collective-permute-start.13 = (bf16[432,384]{1,0:T(8,128)(2,1)S(1)}, bf16[432,384]{1,0:T(8,128)(2,1)S(1)}, u32[]{:S(2)}, u32[]{:S(2)}) collective-permute-start(bf16[432,384]{1,0:T(8,128)(2,1)S(1)} %collective-permute-done.3.rest_2_), channel_id=1, source_target_pairs={{0,4},{1,5},{4,8},{5,9},{6,2},{7,3},{8,12},{9,13},{10,6},{11,7},{1... | collective-permute-start | bytes 995336 | tf_op jit(solution)/shard_map/ppermute | solution.py:24
  31.5 9.5 %collective-permute-start.5 = (bf16[416,384]{1,0:T(8,128)(2,1)S(1)}, bf16[416,384]{1,0:T(8,128)(2,1)S(1)}, u32[]{:S(2)}, u32[]{:S(2)}) collective-permute-start(bf16[416,384]{1,0:T(8,128)(2,1)S(1)} %get-tuple-element.82), channel_id=1, source_target_pairs={{0,2},{1,3},{2,0},{3,1},{4,6},{5,7},{6,4},{7,5},{8,10},{9,11},{10,... | collective-permute-start | bytes 958472 | tf_op jit(solution)/shard_map/ppermute | solution.py:24
  35.3 9.9 %collective-permute-start.10 = (bf16[416,384]{1,0:T(8,128)(2,1)S(1)}, bf16[416,384]{1,0:T(8,128)(2,1)S(1)}, u32[]{:S(2)}, u32[]{:S(2)}) collective-permute-start(bf16[416,384]{1,0:T(8,128)(2,1)S(1)} %collective-permute-done.8.rest_3_), channel_id=1, source_target_pairs={{0,4},{1,5},{4,8},{5,9},{6,2},{7,3},{8,12},{9,13},{10,6},{11,7},{1... | collective-permute-start | bytes 958472 | tf_op jit(solution)/shard_map/ppermute | solution.py:24
  38.8 1.7 %collective-permute-start.6 = (s16[1216,128]{1,0:T(8,128)(2,1)S(1)}, s16[1216,128]{1,0:T(8,128)(2,1)S(1)}, u32[]{:S(2)}, u32[]{:S(2)}) collective-permute-start(s16[1216,128]{1,0:T(8,128)(2,1)S(1)} %get-tuple-element.87), channel_id=1, source_target_pairs={{0,1},{1,0},{2,3},{3,2},{4,5},{5,4},{6,7},{7,6},{8,9},{9,8},{10,11... | collective-permute-start | bytes 933896 | tf_op jit(solution)/shard_map/ppermute | solution.py:24
  38.8 2.0 %collective-permute-start.7 = (s16[1216,128]{1,0:T(8,128)(2,1)S(1)}, s16[1216,128]{1,0:T(8,128)(2,1)S(1)}, u32[]{:S(2)}, u32[]{:S(2)}) collective-permute-start(s16[1216,128]{1,0:T(8,128)(2,1)S(1)} %get-tuple-element.88), channel_id=1, source_target_pairs={{0,1},{1,0},{2,3},{3,2},{4,5},{5,4},{6,7},{7,6},{8,9},{9,8},{10,11... | collective-permute-start | bytes 933896 | tf_op jit(solution)/shard_map/ppermute | solution.py:24
  39.8 8.0 %collective-permute-start.14 = (bf16[1232,384]{1,0:T(8,128)(2,1)S(1)}, bf16[1232,384]{1,0:T(8,128)(2,1)S(1)}, u32[]{:S(2)}, u32[]{:S(2)}) collective-permute-start(bf16[1232,384]{1,0:T(8,128)(2,1)S(1)} %maximum_select_fusion), channel_id=1, source_target_pairs={{0,1},{1,0},{2,3},{3,2},{4,5},{5,4},{6,7},{7,6},{8,9},{9,8},{10,11... | collective-permute-start | bytes 2838536 | tf_op jit(solution)/shard_map/ppermute | solution.py:24
  41.0 13.3 %collective-permute-start.11 = (bf16[416,384]{1,0:T(8,128)(2,1)S(1)}, bf16[416,384]{1,0:T(8,128)(2,1)S(1)}, u32[]{:S(2)}, u32[]{:S(2)}) collective-permute-start(bf16[416,384]{1,0:T(8,128)(2,1)S(1)} %collective-permute-done.5.rest_4_), channel_id=1, source_target_pairs={{0,4},{1,5},{4,8},{5,9},{6,2},{7,3},{8,12},{9,13},{10,6},{11,7},{1... | collective-permute-start | bytes 958472 | tf_op jit(solution)/shard_map/ppermute | solution.py:24
  45.0 9.3 %collective-permute-start.17 = (s16[1216,128]{1,0:T(8,128)(2,1)S(1)}, s16[1216,128]{1,0:T(8,128)(2,1)S(1)}, u32[]{:S(2)}, u32[]{:S(2)}) collective-permute-start(s16[1216,128]{1,0:T(8,128)(2,1)S(1)} %get-tuple-element.111), channel_id=1, source_target_pairs={{0,2},{1,3},{2,0},{3,1},{4,6},{5,7},{6,4},{7,5},{8,10},{9,11},{10,... | collective-permute-start | bytes 933896 | tf_op jit(solution)/shard_map/ppermute | solution.py:24
  50.6 3.8 %collective-permute-start.16 = (bf16[208,384]{1,0:T(8,128)(2,1)S(1)}, bf16[208,384]{1,0:T(8,128)(2,1)S(1)}, u32[]{:S(2)}, u32[]{:S(2)}) collective-permute-start(bf16[208,384]{1,0:T(8,128)(2,1)S(1)} %get-tuple-element.126), channel_id=1, source_target_pairs={{0,1},{1,0},{2,3},{3,2},{4,5},{5,4},{6,7},{7,6},{8,9},{9,8},{10,11... | collective-permute-start | bytes 479240 | tf_op jit(solution)/shard_map/ppermute | solution.py:24
  50.7 3.7 %collective-permute-start.15 = (bf16[208,384]{1,0:T(8,128)(2,1)S(1)}, bf16[208,384]{1,0:T(8,128)(2,1)S(1)}, u32[]{:S(2)}, u32[]{:S(2)}) collective-permute-start(bf16[208,384]{1,0:T(8,128)(2,1)S(1)} %get-tuple-element.127), channel_id=1, source_target_pairs={{0,1},{1,0},{2,3},{3,2},{4,5},{5,4},{6,7},{7,6},{8,9},{9,8},{10,11... | collective-permute-start | bytes 479240 | tf_op jit(solution)/shard_map/ppermute | solution.py:24
  54.5 2.0 %collective-permute-start.18 = (bf16[416,384]{1,0:T(8,128)(2,1)S(1)}, bf16[416,384]{1,0:T(8,128)(2,1)S(1)}, u32[]{:S(2)}, u32[]{:S(2)}) collective-permute-start(bf16[416,384]{1,0:T(8,128)(2,1)S(1)} %broadcast_select_fusion), channel_id=1, source_target_pairs={{0,1},{1,0},{2,3},{3,2},{4,5},{5,4},{6,7},{7,6},{8,9},{9,8},{10,11... | collective-permute-start | bytes 958472 | tf_op jit(solution)/shard_map/ppermute | solution.py:24
  62.2 2.2 %collective-permute-start.19 = (f32[1152,128]{1,0:T(8,128)S(1)}, f32[1152,128]{1,0:T(8,128)S(1)}, u32[]{:S(2)}, u32[]{:S(2)}) collective-permute-start(f32[1152,128]{1,0:T(8,128)S(1)} %get-tuple-element.118), channel_id=1, source_target_pairs={{0,1},{1,0},{2,3},{3,2},{4,5},{5,4},{6,7},{7,6},{8,9},{9,8},{10,11... | collective-permute-start | bytes 1769480 | tf_op jit(solution)/shard_map/ppermute | solution.py:24
  64.7 4.7 %collective-permute-start.20 = (s16[304,128]{1,0:T(8,128)(2,1)S(1)}, s16[304,128]{1,0:T(8,128)(2,1)S(1)}, u32[]{:S(2)}, u32[]{:S(2)}) collective-permute-start(s16[304,128]{1,0:T(8,128)(2,1)S(1)} %get-tuple-element.122), channel_id=1, source_target_pairs={{0,4},{1,5},{2,6},{3,7},{4,0},{5,1},{6,2},{7,3},{8,12},{9,13},{10,... | collective-permute-start | bytes 233480 | tf_op jit(solution)/shard_map/ppermute | solution.py:24
  66.4 9.3 %collective-permute-start.21 = (s16[304,128]{1,0:T(8,128)(2,1)S(1)}, s16[304,128]{1,0:T(8,128)(2,1)S(1)}, u32[]{:S(2)}, u32[]{:S(2)}) collective-permute-start(s16[304,128]{1,0:T(8,128)(2,1)S(1)} %get-tuple-element.123), channel_id=1, source_target_pairs={{0,8},{1,9},{2,10},{3,11},{4,12},{5,13},{6,14},{7,15},{8,0},{9,1},... | collective-permute-start | bytes 233480 | tf_op jit(solution)/shard_map/ppermute | solution.py:24
  68.2 7.5 %collective-permute-start.22 = (s16[304,128]{1,0:T(8,128)(2,1)S(1)}, s16[304,128]{1,0:T(8,128)(2,1)S(1)}, u32[]{:S(2)}, u32[]{:S(2)}) collective-permute-start(s16[304,128]{1,0:T(8,128)(2,1)S(1)} %get-tuple-element.124), channel_id=1, source_target_pairs={{0,12},{1,13},{2,14},{3,15},{4,8},{5,9},{6,10},{7,11},{8,4},{9,5},... | collective-permute-start | bytes 233480 | tf_op jit(solution)/shard_map/ppermute | solution.py:24
  75.8 7.1 %collective-permute-start.25 = (s16[304,128]{1,0:T(8,128)(2,1)S(1)}, s16[304,128]{1,0:T(8,128)(2,1)S(1)}, u32[]{:S(2)}, u32[]{:S(2)}) collective-permute-start(s16[304,128]{1,0:T(8,128)(2,1)S(1)} %sum_code.1), channel_id=1, source_target_pairs={{0,12},{1,13},{2,14},{3,15},{4,8},{5,9},{6,10},{7,11},{8,4},{9,5},... | collective-permute-start | bytes 233480 | tf_op jit(solution)/shard_map/ppermute | solution.py:24
  77.9 7.2 %collective-permute-start.24 = (s16[304,128]{1,0:T(8,128)(2,1)S(1)}, s16[304,128]{1,0:T(8,128)(2,1)S(1)}, u32[]{:S(2)}, u32[]{:S(2)}) collective-permute-start(s16[304,128]{1,0:T(8,128)(2,1)S(1)} %sum_code.1), channel_id=1, source_target_pairs={{0,8},{1,9},{2,10},{3,11},{4,12},{5,13},{6,14},{7,15},{8,0},{9,1},... | collective-permute-start | bytes 233480 | tf_op jit(solution)/shard_map/ppermute | solution.py:24
  78.8 6.8 %collective-permute-start.23 = (s16[304,128]{1,0:T(8,128)(2,1)S(1)}, s16[304,128]{1,0:T(8,128)(2,1)S(1)}, u32[]{:S(2)}, u32[]{:S(2)}) collective-permute-start(s16[304,128]{1,0:T(8,128)(2,1)S(1)} %sum_code.1), channel_id=1, source_target_pairs={{0,4},{1,5},{2,6},{3,7},{4,0},{5,1},{6,2},{7,3},{8,12},{9,13},{10,... | collective-permute-start | bytes 233480 | tf_op jit(solution)/shard_map/ppermute | solution.py:24
  80.3 7.0 %collective-permute-start.26 = (s16[304,128]{1,0:T(8,128)(2,1)S(1)}, s16[304,128]{1,0:T(8,128)(2,1)S(1)}, u32[]{:S(2)}, u32[]{:S(2)}) collective-permute-start(s16[304,128]{1,0:T(8,128)(2,1)S(1)} %sum_code.1), channel_id=1, source_target_pairs={{0,2},{1,3},{2,0},{3,1},{4,6},{5,7},{6,4},{7,5},{8,10},{9,11},{10,... | collective-permute-start | bytes 233480 | tf_op jit(solution)/shard_map/ppermute | solution.py:24
  82.9 5.2 %collective-permute-start.29 = (s16[304,128]{1,0:T(8,128)(2,1)S(1)}, s16[304,128]{1,0:T(8,128)(2,1)S(1)}, u32[]{:S(2)}, u32[]{:S(2)}) collective-permute-start(s16[304,128]{1,0:T(8,128)(2,1)S(1)} %collective-permute-done.25), channel_id=1, source_target_pairs={{0,2},{1,3},{2,0},{3,1},{4,6},{5,7},{6,4},{7,5},{8,10},{9,11},{10,... | collective-permute-start | bytes 233480 | tf_op jit(solution)/shard_map/ppermute | solution.py:24
  85.2 4.4 %collective-permute-start.28 = (s16[304,128]{1,0:T(8,128)(2,1)S(1)}, s16[304,128]{1,0:T(8,128)(2,1)S(1)}, u32[]{:S(2)}, u32[]{:S(2)}) collective-permute-start(s16[304,128]{1,0:T(8,128)(2,1)S(1)} %collective-permute-done.24), channel_id=1, source_target_pairs={{0,2},{1,3},{2,0},{3,1},{4,6},{5,7},{6,4},{7,5},{8,10},{9,11},{10,... | collective-permute-start | bytes 233480 | tf_op jit(solution)/shard_map/ppermute | solution.py:24
  85.7 4.7 %collective-permute-start.27 = (s16[304,128]{1,0:T(8,128)(2,1)S(1)}, s16[304,128]{1,0:T(8,128)(2,1)S(1)}, u32[]{:S(2)}, u32[]{:S(2)}) collective-permute-start(s16[304,128]{1,0:T(8,128)(2,1)S(1)} %collective-permute-done.23), channel_id=1, source_target_pairs={{0,2},{1,3},{2,0},{3,1},{4,6},{5,7},{6,4},{7,5},{8,10},{9,11},{10,... | collective-permute-start | bytes 233480 | tf_op jit(solution)/shard_map/ppermute | solution.py:24
  87.2 3.3 %collective-permute-start.30 = (s16[4,304,128]{2,1,0:T(8,128)(2,1)S(1)}, s16[4,304,128]{2,1,0:T(8,128)(2,1)S(1)}, u32[]{:S(2)}, u32[]{:S(2)}) collective-permute-start(s16[4,304,128]{2,1,0:T(8,128)(2,1)S(1)} %pad_add_fusion.a), channel_id=1, source_target_pairs={{0,1},{1,0},{2,3},{3,2},{4,5},{5,4},{6,7},{7,6},{8,9},{9,8},{10,11... | collective-permute-start | bytes 933896 | tf_op jit(solution)/shard_map/ppermute | solution.py:24
  90.4 1.7 %collective-permute-start.31 = (s16[4,304,128]{2,1,0:T(8,128)(2,1)S(1)}, s16[4,304,128]{2,1,0:T(8,128)(2,1)S(1)}, u32[]{:S(2)}, u32[]{:S(2)}) collective-permute-start(s16[4,304,128]{2,1,0:T(8,128)(2,1)S(1)} %pad_add_fusion.1.b), channel_id=1, source_target_pairs={{0,1},{1,0},{2,3},{3,2},{4,5},{5,4},{6,7},{7,6},{8,9},{9,8},{10,11... | collective-permute-start | bytes 933896 | tf_op jit(solution)/shard_map/ppermute | solution.py:24

commit v8 on v7

--- a/solution.py
+++ b/solution.py
@@ -168,6 +168,17 @@
     add_pair(own_t, other, amp, total, levels[...].T, levels[step:step + 1, :], weight, False)
 
 
+def segments(plane, which):
+    side = plane // 18
+    return (which * side * 5, side * 5), (side * 10 + which * side * 4, side * 4)
+
+
+def rows_of(packed, base, plane, which):
+    return jnp.concatenate(
+        [packed[pl.ds(pl.multiple_of(base + a, 16), n), :] for a, n in segments(plane, which)]
+    )
+
+
 def near_metric_kernel(me_ref, total, own_s, keep, away, *rest):
     *sends, high, low, packed = rest
     parity, core, _ = place_of(me_ref[0])
@@ -195,7 +206,7 @@
     size = plane // 2
 
     def part(side, which):
-        return packed[pl.ds(pl.multiple_of((2 * side + which) * size, 16), size), :]
+        return rows_of(packed, side * plane, plane, which)
 
     keep[...] = part(parity, core)
     away[...] = part(1 - parity, core)
@@ -221,23 +232,25 @@
     add_pair(own_t, other, amp, total, levels[...].T, level, weight, False, halves, near)
 
 
+def mirrored(high, low, own_s, first, n, q):
+    rows, columns = pl.ds(pl.multiple_of(first, 16), n), pl.ds(pl.multiple_of(q, 16), BLOCK)
+    pairs = ((high, own_s), (low, own_s), (own_s, high), (own_s, low))
+    return sum(lax.dot_general(a[rows, :], b[columns, :], NT, preferred_element_type=F32) for a, b in pairs)
+
+
 def last_kernel(plan, names, step, me_ref, own_t, levels, weights, total_in, own_s, near, *rest):
     refs = dict(zip(names, rest))
-    total, residual, keep, send, sem, other, amp, high, low, packed = rest[len(names):]
+    total, residual, keep, send, high, low, sem, other, amp, packed = rest[len(names):]
     me = me_ref[0]
     parity, core, _ = place_of(me)
     aux, wide = total.shape
     virt = wide // 2
     add_half(plan, refs, step, 1, me, own_t, levels, weights, total, other, amp, (high, low), near)
     copies = begin([(total.at[:, pl.ds(j * virt, virt)], residual.at[j]) for j in range(2)], sem)
-    half, quarter = aux // 2, aux // 4
+    half = aux // 2
 
     def both(first, n, q):
-        rows, columns = pl.ds(pl.multiple_of(first, 16), n), pl.ds(pl.multiple_of(q, 16), BLOCK)
-        pairs = ((high, own_s), (low, own_s), (own_s, high), (own_s, low))
-        return sum(
-            lax.dot_general(a[rows, :], b[columns, :], NT, preferred_element_type=F32) for a, b in pairs
-        )
+        return mirrored(high, low, own_s, first, n, q)
 
     at = 0
     for q in range(0, half, BLOCK):
@@ -246,15 +259,27 @@
             upper = q + c + LANES
             packed[at:at + upper, :] = block[:upper, c:c + LANES]
             at += upper
+    share(packed, core, keep, send)
+    finish(copies)
+
+
+def share(packed, core, keep, send):
+    size = keep.shape[0]
+    keep[...] = packed[pl.ds(pl.multiple_of(core * size, 16), size), :]
+    send[...] = packed[pl.ds(pl.multiple_of((1 - core) * size, 16), size), :]
+
+
+def corner_kernel(me_ref, high, low, own_s, keep, send, packed):
+    parity, core, _ = place_of(me_ref[0])
+    aux = own_s.shape[0]
+    half, quarter = aux // 2, aux // 4
+    at = 0
     for q in range(half, aux, BLOCK):
-        block = both(parity * quarter, quarter, q)
+        block = mirrored(high, low, own_s, parity * quarter, quarter, q)
         for c in range(0, BLOCK, LANES):
             packed[at:at + quarter, :] = block[:, c:c + LANES]
             at += quarter
-    size = keep.shape[0]
-    keep[...] = packed[pl.ds(pl.multiple_of(core * size, 16), size), :]
-    send[...] = packed[pl.ds(pl.multiple_of((1 - core) * size, 16), size), :]
-    finish(copies)
+    share(packed, core, keep, send)
 
 
 def encode(x, out, row):
@@ -287,36 +312,50 @@
         keep[at, :] = keep_in[at, :] + decode(got_keep[coded, :])
 
 
-def column_kernel(me_ref, mine, theirs, near, across, keep, *sends):
+def column_kernel(first, me_ref, mine, theirs, near, across, keep, *sends):
     _, _, z = place_of(me_ref[0])
     piece = keep.shape[0]
-    for t in range(4):
-        at = pl.ds(pl.multiple_of((z ^ t) * piece, 16), piece)
-        coded = across[pl.ds(pl.multiple_of((z ^ t) * (piece + PAD), 16), piece + PAD), :]
-        value = (mine[at, :] + theirs[at, :]) + (near[at, :] + decode(coded))
-        if t:
-            encode(value, sends[t - 1], 0)
-        else:
+    away = across.shape[0] // 4
+    far = jnp.concatenate([decode(across[i * away:(i + 1) * away, :]) for i in range(4)])
+    for i in range(4):
+        at = slice(i * piece, (i + 1) * piece)
+        inner = slice(first + i * piece, first + (i + 1) * piece)
+        value = (mine[at, :] + theirs[at, :]) + (near[inner, :] + far[inner, :])
+
+        @pl.when(z == i)
+        def _():
             keep[...] = value
 
-
-def sum_kernel(mine, a, b, c, out):
-    out[...] = mine[...] + decode(a[...]) + decode(b[...]) + decode(c[...])
+        for t in (1, 2, 3):
+            pl.when((z ^ t) == i)(functools.partial(encode, value, sends[t - 1], 0))
+
+
+def sum_of(parts):
+    return jnp.concatenate([sum((decode(x[...]) for x in others), mine[...]) for mine, *others in (parts[:4], parts[4:])])
+
+
+def sum_kernel(*rest):
+    rest[-1][...] = sum_of(rest[:-1])
 
 
 def code_kernel(scale, x, out):
     encode(x[...] * scale, out, 0)
 
 
-def sum_code_kernel(scale, mine, a, b, c, out):
-    encode((mine[...] + decode(a[...]) + decode(b[...]) + decode(c[...])) * scale, out, 0)
+def sum_code_kernel(scale, *rest):
+    encode(sum_of(rest[:-1]) * scale, rest[-1], 0)
 
 
 def unpack(src, which, side, z, packed):
-    rows = src.shape[1] - PAD
+    plane = packed.shape[0] // 2
     for t in range(4):
-        row = ((side * 2 + which) * 4 + (z ^ t)) * rows
-        packed[pl.ds(pl.multiple_of(row, 16), rows), :] = decode(src[t])
+        value = decode(src[t])
+        used = 0
+        for first, n in ((which * (plane // 18) * 5, plane // 18 * 5), (plane // 18 * (10 + which * 4), plane // 18 * 4)):
+            piece = n // 4
+            row = side * plane + first + (z ^ t) * piece
+            packed[pl.ds(pl.multiple_of(row, 16), piece), :] = value[used:used + piece, :]
+            used += piece
 
 
 def unpack_kernel(me_ref, a, b, sib_a, packed):
@@ -503,23 +542,39 @@
     (total,) = pair_step(
         lambda *a: half_kernel(*a[:3], 0, *a[3:]), "half", 4, (total,), scratch=half_s, flops=int(1e9), side=0
     )
-    _, residual, mine, send = pair_step(
+    plane = upper // 2
+    (_, square), (_, corner) = segments(plane, 0)
+    slab_t = jax.ShapeDtypeStruct((aux, wide), BF16)
+    _, residual, mine, send, high, low = pair_step(
         last_kernel, "last", 4, (total, own_s, near),
-        (jax.ShapeDtypeStruct(own.shape, F32), plain(upper // 4), plain(upper // 4)), (hbm, vmem, vmem),
-        [dma(2), *half_s, slab_s, slab_s, pltpu.VMEM((upper // 2, LANES), F32)], side=1,
+        (jax.ShapeDtypeStruct(own.shape, F32), plain(square), plain(square), slab_t, slab_t), (hbm,) + (vmem,) * 4,
+        [dma(2), *half_s, pltpu.VMEM((2 * square, LANES), F32)], side=1,
     )
 
+    def column(first, size, mine, got):
+        n = size // 4
+        return kernel(
+            functools.partial(column_kernel, first), "column", [smem] + [vmem] * 4, (plain(n),) + (coded(n + PAD),) * 3,
+            (vmem,) * 4,
+        )(me, mine, got, keep, across)
+
     got = swapped(send, 1)
-    keep, *sends = kernel(
-        column_kernel, "column", [smem] + [vmem] * 4, (plain(piece),) + (coded(piece + PAD),) * 3, (vmem,) * 4,
-    )(me, mine, got, keep, across)
-    got = [swapped(send, 4 * t) for t, send in zip((1, 2, 3), sends)]
+    mine_b, send_b = kernel(
+        corner_kernel, "corner", [smem] + [vmem] * 3, (plain(corner), plain(corner)), (vmem, vmem),
+        [pltpu.VMEM((2 * corner, LANES), F32)], LARGE_LIMIT, flops=int(2e9),
+    )(me, high, low, own_s)
+    got, send_b = lax.optimization_barrier((got, send_b))
+    got_b = swapped(send_b, 1)
+    keep_a, *sends_a = column(0, square, mine, got)
+    summed = [keep_a] + [swapped(sends_a[t - 1], 4 * t) for t in (3, 2, 1)]
+    keep_b, *sends_b = column(square, corner, mine_b, got_b)
+    summed += [keep_b] + [swapped(sends_b[t - 1], 4 * t) for t in (3, 2, 1)]
     if blocks == 16:
         mine = kernel(
-            functools.partial(sum_code_kernel, 1.0 / blocks), "sum_code", [vmem] * 4, coded(piece + PAD), vmem,
-        )(keep, *got)
+            functools.partial(sum_code_kernel, 1.0 / blocks), "sum_code", [vmem] * 8, coded(piece + PAD), vmem,
+        )(*summed)
     else:
-        value = kernel(sum_kernel, "sum", [vmem] * 4, plain(piece), vmem)(keep, *got)
+        value = kernel(sum_kernel, "sum", [vmem] * 8, plain(piece), vmem)(*summed)
         bit = 16
         while bit < blocks:
             value = value + swapped(value, bit)

time: 95.2 us -> 94.4 us (level)
  waiting for transfers between devices: 25.2 us -> 19.3 us
  starting transfers between devices: 36.1 us -> 41.8 us
    ppermute x32 -> x36, waiting for transfers between devices: 25.2 us -> 19.3 us  [move(): return lax.ppermute(x, 'dom', pairs)]
    ppermute x32 -> x36, starting transfers between devices: 36.1 us -> 41.8 us  [move(): return lax.ppermute(x, 'dom', pairs)]
    pallas_call x4, Pallas kernels: 13 us -> 11.2 us  [pair_step(): kernel(functools.partial(body, plan, names, step), name, [smem] + [vmem]...]
    pallas_call x1 -> x3, Pallas kernels: 0.28 us -> 1.55 us  [the longest x1 1.09 us: shards(): kernel(corner_kernel, 'corner', [smem] + [vmem] * 3, (plain(corner), plai...]
  transfers between devices with their start and end apart: 32 -> 36, of which waited for: 16 -> 16; matrix products, arithmetic and copies ran while one was open for 0% -> 0% of each run, Pallas kernels for 20% -> 21%
where the time goes in v8:
time: 94.4 us; the launch traced here: 94.1 us
  starting transfers between devices  41.8 us (44%)
  Pallas kernels  26.9 us (28%)
  waiting for transfers between devices  19.3 us (20%)
  local copies, waits for them, and re-layouts  4.53 us (5%)
  between operations  1.21 us (1%)
    ppermute x36, starting transfers between devices, move(): return lax.ppermute(x, 'dom', pairs)  41.8 us
    ppermute x36, waiting for transfers between devices, move(): return lax.ppermute(x, 'dom', pairs)  19.3 us
    pallas_call x4, Pallas kernels, pair_step(): kernel(functools.partial(body, plan, names, step), name, [smem] + [vmem]...  11.2 us
    unnamed x12, local copies, waits for them, and re-layouts  3.48 us
    pallas_call x1, Pallas kernels, shards(): kernel(own_kernel, 'own', [hbm, vmem, vmem], (jax.ShapeDtypeStruct((wide,...  3.01 us
    pallas_call x1, Pallas kernels, shards(): kernel(sib_kernel, 'sib', [vmem, vmem, hbm, vmem, vmem], total_t, vmem, [...  2.98 us
    pallas_call x1, Pallas kernels, shards(): kernel(near_metric_kernel, 'near_metric', [smem, vmem, vmem], (plain(uppe...  2.71 us
    pallas_call x1, Pallas kernels, shards(): kernel(spread_kernel, 'spread', [smem, vmem, vmem], (jax.ShapeDtypeStruct...  2.61 us
  transfers between devices with their start and end apart: 36, of which 16 were waited for; matrix products, arithmetic and copies ran while one was open for 0% of the time, Pallas kernels for 21%

profile of v8, /device:TPU:0, one launch (start us, length us, event | category | flops | bytes accessed | tf_op | source)
XLA Modules:
  0.0 94.1 jit_solution(7887785069259029721)
XLA Ops:
  0.7 1.0 %slice.12 = bf16[416,384]{1,0:T(8,128)(2,1)S(1)} slice(bf16[2048,384]{1,0:T(8,128)(2,1)} %bitcast.13), slice={[0:416], [0:384]} | slice | bytes 638976 | tf_op jit(solution)/shard_map/slice | solution.py:437
  1.7 0.5 collective-permute-start.1
  2.2 2.6 %collective-permute-start = (bf16[416,384]{1,0:T(8,128)(2,1)S(1)}, bf16[416,384]{1,0:T(8,128)(2,1)S(1)}, u32[]{:S(2)}, u32[]{:S(2)}) collective-permute-start(bf16[416,384]{1,0:T(8,128)(2,1)S(1)} %slice.12), channel_id=1, source_target_pairs={{0,2},{1,3},{2,0},{3,1},{4,6},{5,7},{6,4},{7,5},{8,10},{9,11},{10,... | collective-permute-start | bytes 958472 | tf_op jit(solution)/shard_map/ppermute | solution.py:24
  4.8 0.2 collective-permute-start.2
  5.0 1.4 %copy-done = bf16[1,2,1024,384]{3,2,1,0:T(8,128)(2,1)S(1)} copy-done((bf16[1,2,1024,384]{3,2,1,0:T(8,128)(2,1)S(1)}, bf16[1,2,1024,384]{3,2,1,0:T(8,128)(2,1)}, u32[]{:S(2)}) %copy-start) | copy-done | bytes 1572888
  6.4 0.7 copy-done.4
  7.0 0.9 split.1
  8.0 1.3 %prep.1 = (f32[8,768]{1,0:T(8,128)S(1)}, f32[8,768]{1,0:T(8,128)S(1)}) custom-call(s32[1]{0:T(128)} %bitcast.me_ref.a_0_, s32[1,3]{1,0:T(1,128)S(1)} %copy-done.4, s32[1,3]{1,0:T(1,128)S(1)} %collective-permute-done.2.sib_pairs, f32[2,16]{1,0:T(2,128)S(1)} %bitcast.19, f32[64,128]{1,0:T(8,128)S(1)} %bitcast.18, s32[16,384]{1,0:T(8,128)S(1)} %copy-done.3), custom_call_target="tpu_custom_call" | custom-call | flops 1 | bytes 1 | tf_op jit(solution)/shard_map/prep/pallas_call | solution.py:451
  9.3 0.4 collective-permute-start.4
  9.7 1.4 %copy-done.1 = bf16[1,2,1024,384]{3,2,1,0:T(8,128)(2,1)S(1)} copy-done((bf16[1,2,1024,384]{3,2,1,0:T(8,128)(2,1)S(1)}, bf16[1,2,1024,384]{3,2,1,0:T(8,128)(2,1)}, u32[]{:S(2)}) %copy-start.1) | copy-done | bytes 1572888
  11.1 3.0 %own.1 = (bf16[768,1024]{1,0:T(8,128)(2,1)S(1)}, bf16[1024,768]{1,0:T(8,128)(2,1)S(1)}, f32[1024,768]{1,0:T(8,128)S(1)}) custom-call(bf16[2048,384]{1,0:T(8,128)(2,1)S(1)} %bitcast.16, f32[8,768]{1,0:T(8,128)S(1)} %get-tuple-element.76.levels.a_2_, f32[8,768]{1,0:T(8,128)S(1)} %get-tuple-element.77.weights.a_3_), custom_call_target="tpu_custom_call" | custom-call | flops 20000000000 | bytes 1 | tf_op jit(solution)/shard_map/own/pallas_call | solution.py:456
  14.1 3.7 %collective-permute-start.9 = (bf16[416,384]{1,0:T(8,128)(2,1)S(1)}, bf16[416,384]{1,0:T(8,128)(2,1)S(1)}, u32[]{:S(2)}, u32[]{:S(2)}) collective-permute-start(bf16[416,384]{1,0:T(8,128)(2,1)S(1)} %collective-permute-done.rest_0_), channel_id=1, source_target_pairs={{0,4},{1,5},{4,8},{5,9},{6,2},{7,3},{8,12},{9,13},{10,6},{11,7},{1... | collective-permute-start | bytes 958472 | tf_op jit(solution)/shard_map/ppermute | solution.py:24
  17.9 3.0 %sib.1.total.near = f32[1024,768]{1,0:T(8,128)S(1)} custom-call(bf16[768,1024]{1,0:T(8,128)(2,1)S(1)} %get-tuple-element.112.own_t.a_1_, f32[1024,768]{1,0:T(8,128)S(1)} %get-tuple-element.88.total_in, bf16[2048,384]{1,0:T(8,128)(2,1)S(1)} %collective-permute-done.1.sib, f32[8,768]{1,0:T(8,128)S(1)} %get-tuple-element.76.levels.a_2_, ...), custom_call_target="tpu_custom_call", output_to_operand_aliasing={{}: (1, {})} | custom-call | flops 10000000000 | bytes 1 | tf_op jit(solution)/shard_map/sib/pallas_call | solution.py:466
  20.9 3.9 %collective-permute-start.12 = (bf16[384,384]{1,0:T(8,128)(2,1)S(1)}, bf16[384,384]{1,0:T(8,128)(2,1)S(1)}, u32[]{:S(2)}, u32[]{:S(2)}) collective-permute-start(bf16[384,384]{1,0:T(8,128)(2,1)S(1)} %collective-permute-done.4.rest_1_), channel_id=1, source_target_pairs={{0,4},{1,5},{4,8},{5,9},{6,2},{7,3},{8,12},{9,13},{10,6},{11,7},{1... | collective-permute-start | bytes 884744 | tf_op jit(solution)/shard_map/ppermute | solution.py:24
  24.8 3.2 %collective-permute-done.3.rest_2_ = bf16[432,384]{1,0:T(8,128)(2,1)S(1)} collective-permute-done((bf16[432,384]{1,0:T(8,128)(2,1)S(1)}, bf16[432,384]{1,0:T(8,128)(2,1)S(1)}, u32[]{:S(2)}, u32[]{:S(2)}) %collective-permute-start.3) | collective-permute-done | bytes 331808 | tf_op jit(solution)/shard_map/ppermute | solution.py:24
  28.0 3.5 %collective-permute-start.13 = (bf16[432,384]{1,0:T(8,128)(2,1)S(1)}, bf16[432,384]{1,0:T(8,128)(2,1)S(1)}, u32[]{:S(2)}, u32[]{:S(2)}) collective-permute-start(bf16[432,384]{1,0:T(8,128)(2,1)S(1)} %collective-permute-done.3.rest_2_), channel_id=1, source_target_pairs={{0,4},{1,5},{4,8},{5,9},{6,2},{7,3},{8,12},{9,13},{10,6},{11,7},{1... | collective-permute-start | bytes 995336 | tf_op jit(solution)/shard_map/ppermute | solution.py:24
  31.6 2.7 %near_metric.1 = (f32[1152,128]{1,0:T(8,128)S(1)}, f32[1152,128]{1,0:T(8,128)S(1)}, s16[1216,128]{1,0:T(8,128)(2,1)S(1)}, s16[1216,128]{1,0:T(8,128)(2,1)S(1)}) custom-call(s32[1]{0:T(128)} %bitcast.me_ref.a_0_, f32[1024,768]{1,0:T(8,128)S(1)} %sib.1.total.near, bf16[1024,768]{1,0:T(8,128)(2,1)S(1)} %get-tuple-element.96.own_s), custom_call_target="tpu_custom_call" | custom-call | flops 10000000000 | bytes 1 | tf_op jit(solution)/shard_map/near_metric/pallas_call | solution.py:478
  34.3 1.0 %collective-permute-done.8.rest_3_ = bf16[416,384]{1,0:T(8,128)(2,1)S(1)} collective-permute-done((bf16[416,384]{1,0:T(8,128)(2,1)S(1)}, bf16[416,384]{1,0:T(8,128)(2,1)S(1)}, u32[]{:S(2)}, u32[]{:S(2)}) %collective-permute-start.8) | collective-permute-done | bytes 319520 | tf_op jit(solution)/shard_map/ppermute | solution.py:24
  35.3 3.5 %collective-permute-start.10 = (bf16[416,384]{1,0:T(8,128)(2,1)S(1)}, bf16[416,384]{1,0:T(8,128)(2,1)S(1)}, u32[]{:S(2)}, u32[]{:S(2)}) collective-permute-start(bf16[416,384]{1,0:T(8,128)(2,1)S(1)} %collective-permute-done.8.rest_3_), channel_id=1, source_target_pairs={{0,4},{1,5},{4,8},{5,9},{6,2},{7,3},{8,12},{9,13},{10,6},{11,7},{1... | collective-permute-start | bytes 958472 | tf_op jit(solution)/shard_map/ppermute | solution.py:24
  38.8 0.1 collective-permute-start.6
  38.8 0.5 collective-permute-start.7
  39.3 0.2 collective-permute-done.13.rest_2_.a_5_
  39.6 0.2 maximum_select_fusion
  39.9 0.5 collective-permute-done.6.got_away
  40.4 0.4 collective-permute-done.7.got_keep
  40.9 0.2 collective-permute-done.5.rest_4_
  41.0 3.7 %collective-permute-start.11 = (bf16[416,384]{1,0:T(8,128)(2,1)S(1)}, bf16[416,384]{1,0:T(8,128)(2,1)S(1)}, u32[]{:S(2)}, u32[]{:S(2)}) collective-permute-start(bf16[416,384]{1,0:T(8,128)(2,1)S(1)} %collective-permute-done.5.rest_4_), channel_id=1, source_target_pairs={{0,4},{1,5},{4,8},{5,9},{6,2},{7,3},{8,12},{9,13},{10,6},{11,7},{1... | collective-permute-start | bytes 958472 | tf_op jit(solution)/shard_map/ppermute | solution.py:24
  44.7 0.3 chip.1
  45.1 0.1 collective-permute-start.17
  45.2 2.7 %far2.1.total_in = f32[1024,768]{1,0:T(8,128)S(1)} custom-call(s32[1]{0:T(128)} %bitcast.me_ref.a_0_, bf16[768,1024]{1,0:T(8,128)(2,1)S(1)} %get-tuple-element.112.own_t.a_1_, f32[8,768]{1,0:T(8,128)S(1)} %get-tuple-element.76.levels.a_2_, f32[8,768]{1,0:T(8,128)S(1)} %get-tuple-element.77.weights.a_3_, bf16[416,384]{1,0:T(8,128)(2,1)S(1)} %collective-permute-done.rest_0_, ...), custom_call_target="tpu_custom_call" | custom-call | flops 10000000000 | bytes 1 | tf_op jit(solution)/shard_map/far2/pallas_call | solution.py:524
  47.8 2.7 %far3.1.a_4_ = f32[1024,768]{1,0:T(8,128)S(1)} custom-call(s32[1]{0:T(128)} %bitcast.me_ref.a_0_, bf16[768,1024]{1,0:T(8,128)(2,1)S(1)} %get-tuple-element.112.own_t.a_1_, f32[8,768]{1,0:T(8,128)S(1)} %get-tuple-element.76.levels.a_2_, f32[8,768]{1,0:T(8,128)S(1)} %get-tuple-element.77.weights.a_3_, ...), custom_call_target="tpu_custom_call", output_to_operand_aliasing={{}: (4, {})} | custom-call | flops 1 | bytes 1 | tf_op jit(solution)/shard_map/far3/pallas_call | solution.py:524
  50.7 0.5 collective-permute-start.15
  51.2 3.2 %collective-permute-done.17.across = s16[1216,128]{1,0:T(8,128)(2,1)S(1)} collective-permute-done((s16[1216,128]{1,0:T(8,128)(2,1)S(1)}, s16[1216,128]{1,0:T(8,128)(2,1)S(1)}, u32[]{:S(2)}, u32[]{:S(2)}) %collective-permute-start.17) | collective-permute-done | bytes 311328 | tf_op jit(solution)/shard_map/ppermute | solution.py:24
  54.5 1.9 %half.1.total_in = f32[1024,768]{1,0:T(8,128)S(1)} custom-call(s32[1]{0:T(128)} %bitcast.me_ref.a_0_, bf16[768,1024]{1,0:T(8,128)(2,1)S(1)} %get-tuple-element.112.own_t.a_1_, f32[8,768]{1,0:T(8,128)S(1)} %get-tuple-element.76.levels.a_2_, f32[8,768]{1,0:T(8,128)S(1)} %get-tuple-element.77.weights.a_3_, ...), custom_call_target="tpu_custom_call", output_to_operand_aliasing={{}: (4, {})} | custom-call | flops 1000000000 | bytes 1 | tf_op jit(solution)/shard_map/half/pallas_call | solution.py:524
  56.4 4.0 %last.1 = (f32[1024,768]{1,0:T(8,128)S(1)}, f32[2,1024,384]{2,1,0:T(8,128)}, f32[640,128]{1,0:T(8,128)S(1)}, f32[640,128]{1,0:T(8,128)S(1)}, bf16[1024,768]{1,0:...) custom-call(s32[1]{0:T(128)} %bitcast.me_ref.a_0_, ...), custom_call_target="tpu_custom_call", output_to_operand_aliasing={{0}: (4, {})} | custom-call | flops 1 | bytes 1 | tf_op jit(solution)/shard_map/last/pallas_call | solution.py:524
  60.4 0.6 collective-permute-start.19
  61.0 1.1 %corner.1 = (f32[512,128]{1,0:T(8,128)S(1)}, f32[512,128]{1,0:T(8,128)S(1)}) custom-call(s32[1]{0:T(128)} %bitcast.me_ref.a_0_, bf16[1024,768]{1,0:T(8,128)(2,1)S(1)} %get-tuple-element.129.high, bf16[1024,768]{1,0:T(8,128)(2,1)S(1)} %get-tuple-element.130.low, bf16[1024,768]{1,0:T(8,128)(2,1)S(1)} %get-tuple-element.96.own_s), custom_call_target="tpu_custom_call" | custom-call | flops 2000000000 | bytes 1 | tf_op jit(solution)/shard_map/corner/pallas_call | solution.py:562
  62.1 0.2 collective-permute-done.19.theirs
  62.2 0.4 collective-permute-start.23
  62.6 0.2 column.2
  62.9 2.8 %collective-permute-start.20 = (s16[176,128]{1,0:T(8,128)(2,1)S(1)}, s16[176,128]{1,0:T(8,128)(2,1)S(1)}, u32[]{:S(2)}, u32[]{:S(2)}) collective-permute-start(s16[176,128]{1,0:T(8,128)(2,1)S(1)} %get-tuple-element.136), channel_id=1, source_target_pairs={{0,12},{1,13},{2,14},{3,15},{4,8},{5,9},{6,10},{7,11},{8,4},{9,5},... | collective-permute-start | bytes 135176 | tf_op jit(solution)/shard_map/ppermute | solution.py:24
  65.6 0.3 collective-permute-start.21
  66.0 1.4 %collective-permute-start.22 = (s16[176,128]{1,0:T(8,128)(2,1)S(1)}, s16[176,128]{1,0:T(8,128)(2,1)S(1)}, u32[]{:S(2)}, u32[]{:S(2)}) collective-permute-start(s16[176,128]{1,0:T(8,128)(2,1)S(1)} %get-tuple-element.138), channel_id=1, source_target_pairs={{0,4},{1,5},{2,6},{3,7},{4,0},{5,1},{6,2},{7,3},{8,12},{9,13},{10,... | collective-permute-start | bytes 135176 | tf_op jit(solution)/shard_map/ppermute | solution.py:24
  67.3 0.2 column.3
  67.5 2.8 %collective-permute-start.24 = (s16[144,128]{1,0:T(8,128)(2,1)S(1)}, s16[144,128]{1,0:T(8,128)(2,1)S(1)}, u32[]{:S(2)}, u32[]{:S(2)}) collective-permute-start(s16[144,128]{1,0:T(8,128)(2,1)S(1)} %get-tuple-element.142), channel_id=1, source_target_pairs={{0,12},{1,13},{2,14},{3,15},{4,8},{5,9},{6,10},{7,11},{8,4},{9,5},... | collective-permute-start | bytes 110600 | tf_op jit(solution)/shard_map/ppermute | solution.py:24
  70.3 1.7 %collective-permute-start.26 = (s16[144,128]{1,0:T(8,128)(2,1)S(1)}, s16[144,128]{1,0:T(8,128)(2,1)S(1)}, u32[]{:S(2)}, u32[]{:S(2)}) collective-permute-start(s16[144,128]{1,0:T(8,128)(2,1)S(1)} %get-tuple-element.144), channel_id=1, source_target_pairs={{0,4},{1,5},{2,6},{3,7},{4,0},{5,1},{6,2},{7,3},{8,12},{9,13},{10,... | collective-permute-start | bytes 110600 | tf_op jit(solution)/shard_map/ppermute | solution.py:24
  72.0 1.4 %collective-permute-done.24.rest_5_ = s16[144,128]{1,0:T(8,128)(2,1)S(1)} collective-permute-done((s16[144,128]{1,0:T(8,128)(2,1)S(1)}, s16[144,128]{1,0:T(8,128)(2,1)S(1)}, u32[]{:S(2)}, u32[]{:S(2)}) %collective-permute-start.24) | collective-permute-done | bytes 36896 | tf_op jit(solution)/shard_map/ppermute | solution.py:24
  73.4 1.8 %collective-permute-done.25.rest_6_ = s16[144,128]{1,0:T(8,128)(2,1)S(1)} collective-permute-done((s16[144,128]{1,0:T(8,128)(2,1)S(1)}, s16[144,128]{1,0:T(8,128)(2,1)S(1)}, u32[]{:S(2)}, u32[]{:S(2)}) %collective-permute-start.25) | collective-permute-done | bytes 36896 | tf_op jit(solution)/shard_map/ppermute | solution.py:24
  75.2 0.1 sum_code.1
  75.3 1.9 %collective-permute-start.29 = (s16[304,128]{1,0:T(8,128)(2,1)S(1)}, s16[304,128]{1,0:T(8,128)(2,1)S(1)}, u32[]{:S(2)}, u32[]{:S(2)}) collective-permute-start(s16[304,128]{1,0:T(8,128)(2,1)S(1)} %sum_code.1), channel_id=1, source_target_pairs={{0,12},{1,13},{2,14},{3,15},{4,8},{5,9},{6,10},{7,11},{8,4},{9,5},... | collective-permute-start | bytes 233480 | tf_op jit(solution)/shard_map/ppermute | solution.py:24
  77.2 0.4 collective-permute-start.28
  77.6 2.1 %collective-permute-start.27 = (s16[304,128]{1,0:T(8,128)(2,1)S(1)}, s16[304,128]{1,0:T(8,128)(2,1)S(1)}, u32[]{:S(2)}, u32[]{:S(2)}) collective-permute-start(s16[304,128]{1,0:T(8,128)(2,1)S(1)} %sum_code.1), channel_id=1, source_target_pairs={{0,4},{1,5},{2,6},{3,7},{4,0},{5,1},{6,2},{7,3},{8,12},{9,13},{10,... | collective-permute-start | bytes 233480 | tf_op jit(solution)/shard_map/ppermute | solution.py:24
  79.7 1.1 %collective-permute-start.30 = (s16[304,128]{1,0:T(8,128)(2,1)S(1)}, s16[304,128]{1,0:T(8,128)(2,1)S(1)}, u32[]{:S(2)}, u32[]{:S(2)}) collective-permute-start(s16[304,128]{1,0:T(8,128)(2,1)S(1)} %sum_code.1), channel_id=1, source_target_pairs={{0,2},{1,3},{2,0},{3,1},{4,6},{5,7},{6,4},{7,5},{8,10},{9,11},{10,... | collective-permute-start | bytes 233480 | tf_op jit(solution)/shard_map/ppermute | solution.py:24
  80.9 1.1 %collective-permute-done.29 = s16[304,128]{1,0:T(8,128)(2,1)S(1)} collective-permute-done((s16[304,128]{1,0:T(8,128)(2,1)S(1)}, s16[304,128]{1,0:T(8,128)(2,1)S(1)}, u32[]{:S(2)}, u32[]{:S(2)}) %collective-permute-start.29) | collective-permute-done | bytes 77856 | tf_op jit(solution)/shard_map/ppermute | solution.py:24
  82.0 0.8 collective-permute-start.33
  82.8 1.4 %collective-permute-done.28 = s16[304,128]{1,0:T(8,128)(2,1)S(1)} collective-permute-done((s16[304,128]{1,0:T(8,128)(2,1)S(1)}, s16[304,128]{1,0:T(8,128)(2,1)S(1)}, u32[]{:S(2)}, u32[]{:S(2)}) %collective-permute-start.28) | collective-permute-done | bytes 77856 | tf_op jit(solution)/shard_map/ppermute | solution.py:24
  84.2 0.4 collective-permute-start.32
  84.6 1.6 %collective-permute-start.31 = (s16[304,128]{1,0:T(8,128)(2,1)S(1)}, s16[304,128]{1,0:T(8,128)(2,1)S(1)}, u32[]{:S(2)}, u32[]{:S(2)}) collective-permute-start(s16[304,128]{1,0:T(8,128)(2,1)S(1)} %collective-permute-done.27), channel_id=1, source_target_pairs={{0,2},{1,3},{2,0},{3,1},{4,6},{5,7},{6,4},{7,5},{8,10},{9,11},{10,... | collective-permute-start | bytes 233480 | tf_op jit(solution)/shard_map/ppermute | solution.py:24
  86.3 0.9 collective-permute-done.33
  87.2 1.5 %collective-permute-done.32 = s16[304,128]{1,0:T(8,128)(2,1)S(1)} collective-permute-done((s16[304,128]{1,0:T(8,128)(2,1)S(1)}, s16[304,128]{1,0:T(8,128)(2,1)S(1)}, u32[]{:S(2)}, u32[]{:S(2)}) %collective-permute-start.32) | collective-permute-done | bytes 77856 | tf_op jit(solution)/shard_map/ppermute | solution.py:24
  88.8 0.8 collective-permute-done.31
  89.7 0.2 unpack.1.packed_in
  90.0 1.4 %collective-permute-done.35.sib_b = s16[4,304,128]{2,1,0:T(8,128)(2,1)S(1)} collective-permute-done((s16[4,304,128]{2,1,0:T(8,128)(2,1)S(1)}, s16[4,304,128]{2,1,0:T(8,128)(2,1)S(1)}, u32[]{:S(2)}, u32[]{:S(2)}) %collective-permute-start.35) | collective-permute-done | bytes 311328 | tf_op jit(solution)/shard_map/ppermute | solution.py:24
  91.3 2.6 %spread.1 = (f32[1024,1024]{1,0:T(8,128)}, f32[4608,128]{1,0:T(8,128)S(1)}) custom-call(s32[1]{0:T(128)} %bitcast.me_ref.a_0_, f32[4608,128]{1,0:T(8,128)S(1)} %unpack.1.packed_in, s16[4,304,128]{2,1,0:T(8,128)(2,1)S(1)} %collective-permute-done.35.sib_b), custom_call_target="tpu_custom_call", output_to_operand_aliasing={{1}: (1, {})} | custom-call | flops 1 | bytes 1 | tf_op jit(solution)/shard_map/spread/pallas_call | solution.py:589
  (43 shorter events, 0.8 us)
Async XLA Ops:
  0.6 7.3 %copy-start.3 = (s32[16,384]{1,0:T(8,128)S(1)}, s32[16,384]{1,0:T(8,128)}, u32[]{:S(2)}) copy-start(s32[16,384]{1,0:T(8,128)} %maps_in.1) | copy-start | bytes 73732
  0.6 7.3 %copy-start.2 = (f32[8192]{0:T(1024)S(1)}, f32[8192]{0:T(1024)}, u32[]{:S(2)}) copy-start(f32[8192]{0:T(1024)} %param.8) | copy-start | bytes 98308
  0.7 7.3 %copy-start.5 = (f32[16,2]{0,1:T(2,128)S(1)}, f32[16,2]{0,1:T(2,128)}, u32[]{:S(2)}) copy-start(f32[16,2]{0,1:T(2,128)} %param.7) | copy-start | bytes 388
  1.7 7.6 %collective-permute-start.1 = (bf16[2048,384]{1,0:T(8,128)(2,1)}, bf16[2048,384]{1,0:T(8,128)(2,1)S(1)}, u32[]{:S(2)}, u32[]{:S(2)}) collective-permute-start(bf16[2048,384]{1,0:T(8,128)(2,1)} %bitcast.14), channel_id=1, source_target_pairs={{0,1},{1,0},{2,3},{3,2},{4,5},{5,4},{6,7},{7,6},{8,9},{9,8},{10,11... | collective-permute-start | bytes 4718600 | tf_op jit(solution)/shard_map/ppermute | solution.py:24
  2.2 11.9 %collective-permute-start = (bf16[416,384]{1,0:T(8,128)(2,1)S(1)}, bf16[416,384]{1,0:T(8,128)(2,1)S(1)}, u32[]{:S(2)}, u32[]{:S(2)}) collective-permute-start(bf16[416,384]{1,0:T(8,128)(2,1)S(1)} %slice.12), channel_id=1, source_target_pairs={{0,2},{1,3},{2,0},{3,1},{4,6},{5,7},{6,4},{7,5},{8,10},{9,11},{10,... | collective-permute-start | bytes 958472 | tf_op jit(solution)/shard_map/ppermute | solution.py:24
  4.8 3.2 %collective-permute-start.2 = (s32[1,3]{1,0:T(1,128)}, s32[1,3]{1,0:T(1,128)S(1)}, u32[]{:S(2)}, u32[]{:S(2)}) collective-permute-start(s32[1,3]{1,0:T(1,128)} %pairs.3), channel_id=1, source_target_pairs={{0,1},{1,0},{2,3},{3,2},{4,5},{5,4},{6,7},{7,6},{8,9},{9,8},{10,11... | collective-permute-start | bytes 44 | tf_op jit(solution)/shard_map/ppermute | solution.py:24
  5.0 1.4 %copy-start = (bf16[1,2,1024,384]{3,2,1,0:T(8,128)(2,1)S(1)}, bf16[1,2,1024,384]{3,2,1,0:T(8,128)(2,1)}, u32[]{:S(2)}) copy-start(bf16[1,2,1024,384]{3,2,1,0:T(8,128)(2,1)} %param.5) | copy-start | bytes 4718596
  6.4 0.7 copy-start.4
  9.3 11.6 %collective-permute-start.4 = (bf16[384,384]{1,0:T(8,128)(2,1)S(1)}, bf16[384,384]{1,0:T(8,128)(2,1)S(1)}, u32[]{:S(2)}, u32[]{:S(2)}) collective-permute-start(bf16[384,384]{1,0:T(8,128)(2,1)S(1)} %get-tuple-element.86), channel_id=1, source_target_pairs={{0,2},{1,3},{2,0},{3,1},{4,6},{5,7},{6,4},{7,5},{8,10},{9,11},{10,... | collective-permute-start | bytes 884744 | tf_op jit(solution)/shard_map/ppermute | solution.py:24
  9.7 1.4 %copy-start.1 = (bf16[1,2,1024,384]{3,2,1,0:T(8,128)(2,1)S(1)}, bf16[1,2,1024,384]{3,2,1,0:T(8,128)(2,1)}, u32[]{:S(2)}) copy-start(bf16[1,2,1024,384]{3,2,1,0:T(8,128)(2,1)} %param.5) | copy-start | bytes 4718596
  14.1 20.2 %collective-permute-start.9 = (bf16[416,384]{1,0:T(8,128)(2,1)S(1)}, bf16[416,384]{1,0:T(8,128)(2,1)S(1)}, u32[]{:S(2)}, u32[]{:S(2)}) collective-permute-start(bf16[416,384]{1,0:T(8,128)(2,1)S(1)} %collective-permute-done.rest_0_), channel_id=1, source_target_pairs={{0,4},{1,5},{4,8},{5,9},{6,2},{7,3},{8,12},{9,13},{10,6},{11,7},{1... | collective-permute-start | bytes 958472 | tf_op jit(solution)/shard_map/ppermute | solution.py:24
  17.8 10.2 %collective-permute-start.3 = (bf16[432,384]{1,0:T(8,128)(2,1)S(1)}, bf16[432,384]{1,0:T(8,128)(2,1)S(1)}, u32[]{:S(2)}, u32[]{:S(2)}) collective-permute-start(bf16[432,384]{1,0:T(8,128)(2,1)S(1)} %get-tuple-element.84), channel_id=1, source_target_pairs={{0,2},{1,3},{2,0},{3,1},{4,6},{5,7},{6,4},{7,5},{8,10},{9,11},{10,... | collective-permute-start | bytes 995336 | tf_op jit(solution)/shard_map/ppermute | solution.py:24
  20.9 18.0 %collective-permute-start.12 = (bf16[384,384]{1,0:T(8,128)(2,1)S(1)}, bf16[384,384]{1,0:T(8,128)(2,1)S(1)}, u32[]{:S(2)}, u32[]{:S(2)}) collective-permute-start(bf16[384,384]{1,0:T(8,128)(2,1)S(1)} %collective-permute-done.4.rest_1_), channel_id=1, source_target_pairs={{0,4},{1,5},{4,8},{5,9},{6,2},{7,3},{8,12},{9,13},{10,6},{11,7},{1... | collective-permute-start | bytes 884744 | tf_op jit(solution)/shard_map/ppermute | solution.py:24
  24.7 10.5 %collective-permute-start.8 = (bf16[416,384]{1,0:T(8,128)(2,1)S(1)}, bf16[416,384]{1,0:T(8,128)(2,1)S(1)}, u32[]{:S(2)}, u32[]{:S(2)}) collective-permute-start(bf16[416,384]{1,0:T(8,128)(2,1)S(1)} %get-tuple-element.100), channel_id=1, source_target_pairs={{0,2},{1,3},{2,0},{3,1},{4,6},{5,7},{6,4},{7,5},{8,10},{9,11},{10,... | collective-permute-start | bytes 958472 | tf_op jit(solution)/shard_map/ppermute | solution.py:24
  28.0 11.6 %collective-permute-start.13 = (bf16[432,384]{1,0:T(8,128)(2,1)S(1)}, bf16[432,384]{1,0:T(8,128)(2,1)S(1)}, u32[]{:S(2)}, u32[]{:S(2)}) collective-permute-start(bf16[432,384]{1,0:T(8,128)(2,1)S(1)} %collective-permute-done.3.rest_2_), channel_id=1, source_target_pairs={{0,4},{1,5},{4,8},{5,9},{6,2},{7,3},{8,12},{9,13},{10,6},{11,7},{1... | collective-permute-start | bytes 995336 | tf_op jit(solution)/shard_map/ppermute | solution.py:24
  31.5 9.5 %collective-permute-start.5 = (bf16[416,384]{1,0:T(8,128)(2,1)S(1)}, bf16[416,384]{1,0:T(8,128)(2,1)S(1)}, u32[]{:S(2)}, u32[]{:S(2)}) collective-permute-start(bf16[416,384]{1,0:T(8,128)(2,1)S(1)} %get-tuple-element.92), channel_id=1, source_target_pairs={{0,2},{1,3},{2,0},{3,1},{4,6},{5,7},{6,4},{7,5},{8,10},{9,11},{10,... | collective-permute-start | bytes 958472 | tf_op jit(solution)/shard_map/ppermute | solution.py:24
  35.3 9.9 %collective-permute-start.10 = (bf16[416,384]{1,0:T(8,128)(2,1)S(1)}, bf16[416,384]{1,0:T(8,128)(2,1)S(1)}, u32[]{:S(2)}, u32[]{:S(2)}) collective-permute-start(bf16[416,384]{1,0:T(8,128)(2,1)S(1)} %collective-permute-done.8.rest_3_), channel_id=1, source_target_pairs={{0,4},{1,5},{4,8},{5,9},{6,2},{7,3},{8,12},{9,13},{10,6},{11,7},{1... | collective-permute-start | bytes 958472 | tf_op jit(solution)/shard_map/ppermute | solution.py:24
  38.8 1.7 %collective-permute-start.6 = (s16[1216,128]{1,0:T(8,128)(2,1)S(1)}, s16[1216,128]{1,0:T(8,128)(2,1)S(1)}, u32[]{:S(2)}, u32[]{:S(2)}) collective-permute-start(s16[1216,128]{1,0:T(8,128)(2,1)S(1)} %get-tuple-element.97), channel_id=1, source_target_pairs={{0,1},{1,0},{2,3},{3,2},{4,5},{5,4},{6,7},{7,6},{8,9},{9,8},{10,11... | collective-permute-start | bytes 933896 | tf_op jit(solution)/shard_map/ppermute | solution.py:24
  38.8 2.0 %collective-permute-start.7 = (s16[1216,128]{1,0:T(8,128)(2,1)S(1)}, s16[1216,128]{1,0:T(8,128)(2,1)S(1)}, u32[]{:S(2)}, u32[]{:S(2)}) collective-permute-start(s16[1216,128]{1,0:T(8,128)(2,1)S(1)} %get-tuple-element.98), channel_id=1, source_target_pairs={{0,1},{1,0},{2,3},{3,2},{4,5},{5,4},{6,7},{7,6},{8,9},{9,8},{10,11... | collective-permute-start | bytes 933896 | tf_op jit(solution)/shard_map/ppermute | solution.py:24
  39.8 8.0 %collective-permute-start.14 = (bf16[1232,384]{1,0:T(8,128)(2,1)S(1)}, bf16[1232,384]{1,0:T(8,128)(2,1)S(1)}, u32[]{:S(2)}, u32[]{:S(2)}) collective-permute-start(bf16[1232,384]{1,0:T(8,128)(2,1)S(1)} %maximum_select_fusion), channel_id=1, source_target_pairs={{0,1},{1,0},{2,3},{3,2},{4,5},{5,4},{6,7},{7,6},{8,9},{9,8},{10,11... | collective-permute-start | bytes 2838536 | tf_op jit(solution)/shard_map/ppermute | solution.py:24
  41.0 13.4 %collective-permute-start.11 = (bf16[416,384]{1,0:T(8,128)(2,1)S(1)}, bf16[416,384]{1,0:T(8,128)(2,1)S(1)}, u32[]{:S(2)}, u32[]{:S(2)}) collective-permute-start(bf16[416,384]{1,0:T(8,128)(2,1)S(1)} %collective-permute-done.5.rest_4_), channel_id=1, source_target_pairs={{0,4},{1,5},{4,8},{5,9},{6,2},{7,3},{8,12},{9,13},{10,6},{11,7},{1... | collective-permute-start | bytes 958472 | tf_op jit(solution)/shard_map/ppermute | solution.py:24
  45.1 9.3 %collective-permute-start.17 = (s16[1216,128]{1,0:T(8,128)(2,1)S(1)}, s16[1216,128]{1,0:T(8,128)(2,1)S(1)}, u32[]{:S(2)}, u32[]{:S(2)}) collective-permute-start(s16[1216,128]{1,0:T(8,128)(2,1)S(1)} %get-tuple-element.121), channel_id=1, source_target_pairs={{0,2},{1,3},{2,0},{3,1},{4,6},{5,7},{6,4},{7,5},{8,10},{9,11},{10,... | collective-permute-start | bytes 933896 | tf_op jit(solution)/shard_map/ppermute | solution.py:24
  50.6 3.8 %collective-permute-start.16 = (bf16[208,384]{1,0:T(8,128)(2,1)S(1)}, bf16[208,384]{1,0:T(8,128)(2,1)S(1)}, u32[]{:S(2)}, u32[]{:S(2)}) collective-permute-start(bf16[208,384]{1,0:T(8,128)(2,1)S(1)} %get-tuple-element.146), channel_id=1, source_target_pairs={{0,1},{1,0},{2,3},{3,2},{4,5},{5,4},{6,7},{7,6},{8,9},{9,8},{10,11... | collective-permute-start | bytes 479240 | tf_op jit(solution)/shard_map/ppermute | solution.py:24
  50.7 3.7 %collective-permute-start.15 = (bf16[208,384]{1,0:T(8,128)(2,1)S(1)}, bf16[208,384]{1,0:T(8,128)(2,1)S(1)}, u32[]{:S(2)}, u32[]{:S(2)}) collective-permute-start(bf16[208,384]{1,0:T(8,128)(2,1)S(1)} %get-tuple-element.147), channel_id=1, source_target_pairs={{0,1},{1,0},{2,3},{3,2},{4,5},{5,4},{6,7},{7,6},{8,9},{9,8},{10,11... | collective-permute-start | bytes 479240 | tf_op jit(solution)/shard_map/ppermute | solution.py:24
  54.5 2.0 %collective-permute-start.18 = (bf16[416,384]{1,0:T(8,128)(2,1)S(1)}, bf16[416,384]{1,0:T(8,128)(2,1)S(1)}, u32[]{:S(2)}, u32[]{:S(2)}) collective-permute-start(bf16[416,384]{1,0:T(8,128)(2,1)S(1)} %broadcast_select_fusion), channel_id=1, source_target_pairs={{0,1},{1,0},{2,3},{3,2},{4,5},{5,4},{6,7},{7,6},{8,9},{9,8},{10,11... | collective-permute-start | bytes 958472 | tf_op jit(solution)/shard_map/ppermute | solution.py:24
  60.4 1.8 %collective-permute-start.19 = (f32[640,128]{1,0:T(8,128)S(1)}, f32[640,128]{1,0:T(8,128)S(1)}, u32[]{:S(2)}, u32[]{:S(2)}) collective-permute-start(f32[640,128]{1,0:T(8,128)S(1)} %get-tuple-element.128), channel_id=1, source_target_pairs={{0,1},{1,0},{2,3},{3,2},{4,5},{5,4},{6,7},{7,6},{8,9},{9,8},{10,11... | collective-permute-start | bytes 983048 | tf_op jit(solution)/shard_map/ppermute | solution.py:24
  62.2 5.1 %collective-permute-start.23 = (f32[512,128]{1,0:T(8,128)S(1)}, f32[512,128]{1,0:T(8,128)S(1)}, u32[]{:S(2)}, u32[]{:S(2)}) collective-permute-start(f32[512,128]{1,0:T(8,128)S(1)} %get-tuple-element.140), channel_id=1, source_target_pairs={{0,1},{1,0},{2,3},{3,2},{4,5},{5,4},{6,7},{7,6},{8,9},{9,8},{10,11... | collective-permute-start | bytes 786440 | tf_op jit(solution)/shard_map/ppermute | solution.py:24
  62.9 7.4 %collective-permute-start.20 = (s16[176,128]{1,0:T(8,128)(2,1)S(1)}, s16[176,128]{1,0:T(8,128)(2,1)S(1)}, u32[]{:S(2)}, u32[]{:S(2)}) collective-permute-start(s16[176,128]{1,0:T(8,128)(2,1)S(1)} %get-tuple-element.136), channel_id=1, source_target_pairs={{0,12},{1,13},{2,14},{3,15},{4,8},{5,9},{6,10},{7,11},{8,4},{9,5},... | collective-permute-start | bytes 135176 | tf_op jit(solution)/shard_map/ppermute | solution.py:24
  65.6 6.4 %collective-permute-start.21 = (s16[176,128]{1,0:T(8,128)(2,1)S(1)}, s16[176,128]{1,0:T(8,128)(2,1)S(1)}, u32[]{:S(2)}, u32[]{:S(2)}) collective-permute-start(s16[176,128]{1,0:T(8,128)(2,1)S(1)} %get-tuple-element.137), channel_id=1, source_target_pairs={{0,8},{1,9},{2,10},{3,11},{4,12},{5,13},{6,14},{7,15},{8,0},{9,1},... | collective-permute-start | bytes 135176 | tf_op jit(solution)/shard_map/ppermute | solution.py:24
  66.0 6.0 %collective-permute-start.22 = (s16[176,128]{1,0:T(8,128)(2,1)S(1)}, s16[176,128]{1,0:T(8,128)(2,1)S(1)}, u32[]{:S(2)}, u32[]{:S(2)}) collective-permute-start(s16[176,128]{1,0:T(8,128)(2,1)S(1)} %get-tuple-element.138), channel_id=1, source_target_pairs={{0,4},{1,5},{2,6},{3,7},{4,0},{5,1},{6,2},{7,3},{8,12},{9,13},{10,... | collective-permute-start | bytes 135176 | tf_op jit(solution)/shard_map/ppermute | solution.py:24
  67.5 5.8 %collective-permute-start.24 = (s16[144,128]{1,0:T(8,128)(2,1)S(1)}, s16[144,128]{1,0:T(8,128)(2,1)S(1)}, u32[]{:S(2)}, u32[]{:S(2)}) collective-permute-start(s16[144,128]{1,0:T(8,128)(2,1)S(1)} %get-tuple-element.142), channel_id=1, source_target_pairs={{0,12},{1,13},{2,14},{3,15},{4,8},{5,9},{6,10},{7,11},{8,4},{9,5},... | collective-permute-start | bytes 110600 | tf_op jit(solution)/shard_map/ppermute | solution.py:24
  70.3 4.9 %collective-permute-start.25 = (s16[144,128]{1,0:T(8,128)(2,1)S(1)}, s16[144,128]{1,0:T(8,128)(2,1)S(1)}, u32[]{:S(2)}, u32[]{:S(2)}) collective-permute-start(s16[144,128]{1,0:T(8,128)(2,1)S(1)} %get-tuple-element.143), channel_id=1, source_target_pairs={{0,8},{1,9},{2,10},{3,11},{4,12},{5,13},{6,14},{7,15},{8,0},{9,1},... | collective-permute-start | bytes 110600 | tf_op jit(solution)/shard_map/ppermute | solution.py:24
  70.3 4.9 %collective-permute-start.26 = (s16[144,128]{1,0:T(8,128)(2,1)S(1)}, s16[144,128]{1,0:T(8,128)(2,1)S(1)}, u32[]{:S(2)}, u32[]{:S(2)}) collective-permute-start(s16[144,128]{1,0:T(8,128)(2,1)S(1)} %get-tuple-element.144), channel_id=1, source_target_pairs={{0,4},{1,5},{2,6},{3,7},{4,0},{5,1},{6,2},{7,3},{8,12},{9,13},{10,... | collective-permute-start | bytes 110600 | tf_op jit(solution)/shard_map/ppermute | solution.py:24
  75.3 6.7 %collective-permute-start.29 = (s16[304,128]{1,0:T(8,128)(2,1)S(1)}, s16[304,128]{1,0:T(8,128)(2,1)S(1)}, u32[]{:S(2)}, u32[]{:S(2)}) collective-permute-start(s16[304,128]{1,0:T(8,128)(2,1)S(1)} %sum_code.1), channel_id=1, source_target_pairs={{0,12},{1,13},{2,14},{3,15},{4,8},{5,9},{6,10},{7,11},{8,4},{9,5},... | collective-permute-start | bytes 233480 | tf_op jit(solution)/shard_map/ppermute | solution.py:24
  77.2 7.0 %collective-permute-start.28 = (s16[304,128]{1,0:T(8,128)(2,1)S(1)}, s16[304,128]{1,0:T(8,128)(2,1)S(1)}, u32[]{:S(2)}, u32[]{:S(2)}) collective-permute-start(s16[304,128]{1,0:T(8,128)(2,1)S(1)} %sum_code.1), channel_id=1, source_target_pairs={{0,8},{1,9},{2,10},{3,11},{4,12},{5,13},{6,14},{7,15},{8,0},{9,1},... | collective-permute-start | bytes 233480 | tf_op jit(solution)/shard_map/ppermute | solution.py:24
  77.6 7.0 %collective-permute-start.27 = (s16[304,128]{1,0:T(8,128)(2,1)S(1)}, s16[304,128]{1,0:T(8,128)(2,1)S(1)}, u32[]{:S(2)}, u32[]{:S(2)}) collective-permute-start(s16[304,128]{1,0:T(8,128)(2,1)S(1)} %sum_code.1), channel_id=1, source_target_pairs={{0,4},{1,5},{2,6},{3,7},{4,0},{5,1},{6,2},{7,3},{8,12},{9,13},{10,... | collective-permute-start | bytes 233480 | tf_op jit(solution)/shard_map/ppermute | solution.py:24
  79.7 6.6 %collective-permute-start.30 = (s16[304,128]{1,0:T(8,128)(2,1)S(1)}, s16[304,128]{1,0:T(8,128)(2,1)S(1)}, u32[]{:S(2)}, u32[]{:S(2)}) collective-permute-start(s16[304,128]{1,0:T(8,128)(2,1)S(1)} %sum_code.1), channel_id=1, source_target_pairs={{0,2},{1,3},{2,0},{3,1},{4,6},{5,7},{6,4},{7,5},{8,10},{9,11},{10,... | collective-permute-start | bytes 233480 | tf_op jit(solution)/shard_map/ppermute | solution.py:24
  82.0 5.2 %collective-permute-start.33 = (s16[304,128]{1,0:T(8,128)(2,1)S(1)}, s16[304,128]{1,0:T(8,128)(2,1)S(1)}, u32[]{:S(2)}, u32[]{:S(2)}) collective-permute-start(s16[304,128]{1,0:T(8,128)(2,1)S(1)} %collective-permute-done.29), channel_id=1, source_target_pairs={{0,2},{1,3},{2,0},{3,1},{4,6},{5,7},{6,4},{7,5},{8,10},{9,11},{10,... | collective-permute-start | bytes 233480 | tf_op jit(solution)/shard_map/ppermute | solution.py:24
  84.2 4.6 %collective-permute-start.32 = (s16[304,128]{1,0:T(8,128)(2,1)S(1)}, s16[304,128]{1,0:T(8,128)(2,1)S(1)}, u32[]{:S(2)}, u32[]{:S(2)}) collective-permute-start(s16[304,128]{1,0:T(8,128)(2,1)S(1)} %collective-permute-done.28), channel_id=1, source_target_pairs={{0,2},{1,3},{2,0},{3,1},{4,6},{5,7},{6,4},{7,5},{8,10},{9,11},{10,... | collective-permute-start | bytes 233480 | tf_op jit(solution)/shard_map/ppermute | solution.py:24
  84.6 5.0 %collective-permute-start.31 = (s16[304,128]{1,0:T(8,128)(2,1)S(1)}, s16[304,128]{1,0:T(8,128)(2,1)S(1)}, u32[]{:S(2)}, u32[]{:S(2)}) collective-permute-start(s16[304,128]{1,0:T(8,128)(2,1)S(1)} %collective-permute-done.27), channel_id=1, source_target_pairs={{0,2},{1,3},{2,0},{3,1},{4,6},{5,7},{6,4},{7,5},{8,10},{9,11},{10,... | collective-permute-start | bytes 233480 | tf_op jit(solution)/shard_map/ppermute | solution.py:24
  86.2 3.5 %collective-permute-start.34 = (s16[4,304,128]{2,1,0:T(8,128)(2,1)S(1)}, s16[4,304,128]{2,1,0:T(8,128)(2,1)S(1)}, u32[]{:S(2)}, u32[]{:S(2)}) collective-permute-start(s16[4,304,128]{2,1,0:T(8,128)(2,1)S(1)} %pad_add_fusion.a), channel_id=1, source_target_pairs={{0,1},{1,0},{2,3},{3,2},{4,5},{5,4},{6,7},{7,6},{8,9},{9,8},{10,11... | collective-permute-start | bytes 933896 | tf_op jit(solution)/shard_map/ppermute | solution.py:24
  89.6 1.7 %collective-permute-start.35 = (s16[4,304,128]{2,1,0:T(8,128)(2,1)S(1)}, s16[4,304,128]{2,1,0:T(8,128)(2,1)S(1)}, u32[]{:S(2)}, u32[]{:S(2)}) collective-permute-start(s16[4,304,128]{2,1,0:T(8,128)(2,1)S(1)} %pad_add_fusion.1.b), channel_id=1, source_target_pairs={{0,1},{1,0},{2,3},{3,2},{4,5},{5,4},{6,7},{7,6},{8,9},{9,8},{10,11... | collective-permute-start | bytes 933896 | tf_op jit(solution)/shard_map/ppermute | solution.py:24

commit v9 on v8

--- a/solution.py
+++ b/solution.py
@@ -358,39 +358,65 @@
             used += piece
 
 
-def unpack_kernel(me_ref, a, b, sib_a, packed):
+def lay_corner(side, packed, square):
+    aux = square.shape[0]
+    half, quarter = aux // 2, aux // 4
+    at = (side + 1) * (packed.shape[0] // 2) - half // LANES * quarter
+    first = side * quarter
+    for c in range(half, aux, LANES):
+        square[first:first + quarter, c:c + LANES] = packed[at:at + quarter, :]
+        for r in range(0, quarter, LANES):
+            square[c:c + LANES, first + r:first + r + LANES] = packed[at + r:at + r + LANES, :].T
+        at += quarter
+
+
+def lay_triangle(side, packed, square, after=None):
+    aux = square.shape[0]
+    half, quarter = aux // 2, aux // 4
+    at = (side + 1) * (packed.shape[0] // 2) - half // LANES * quarter
+    base = side * half
+    for c in range(half - LANES, -1, -LANES):
+        at -= c + LANES
+        columns = slice(base + c, base + c + LANES)
+        square[base:base + c + LANES, columns] = packed[at:at + c + LANES, :]
+        for r in range(0, c, LANES):
+            square[columns, base + r:base + r + LANES] = packed[at + r:at + r + LANES, :].T
+        if after is not None:
+            after(base + c)
+
+
+def write_plane(side, packed, square, out, sem):
+    aux = square.shape[0]
+    half, quarter = aux // 2, aux // 4
+    first, base = side * quarter, side * half
+
+    def copy(at, row, rows, column, columns):
+        where = (pl.ds(row, rows), pl.ds(column, columns))
+        started = pltpu.make_async_copy(square.at[where], out.at[where], sem.at[at])
+        started.start()
+        return started
+
+    lay_corner(side, packed, square)
+    copies = [copy(0, first, quarter, half, half), copy(1, half, half, first, quarter)]
+    lay_triangle(
+        side, packed, square, lambda row: copies.append(copy(2 + (row - base) // LANES, row, LANES, base, half))
+    )
+    finish(copies)
+
+
+def unpack_kernel(me_ref, a, b, sib_a, out, packed, sem, square):
     parity, core, z = place_of(me_ref[0])
     for src, which, side in ((a, core, parity), (b, core, 1 - parity), (sib_a, 1 - core, parity)):
         unpack(src, which, side, z, packed)
-
-
-def spread_kernel(me_ref, packed_in, sib_b, out, packed, sem, square):
+    for side in range(2):
+        pl.when(parity == side)(functools.partial(write_plane, side, packed, square, out, sem))
+
+
+def spread_kernel(me_ref, out_in, packed_in, sib_b, out, packed, sem, square):
     parity, core, z = place_of(me_ref[0])
-    aux = out.shape[1]
-    half, quarter = aux // 2, aux // 4
-    plane = packed.shape[0] // 2
     unpack(sib_b, 1 - core, 1 - parity, z, packed)
     for side in range(2):
-        at = side * plane + plane - half // LANES * quarter
-        for c in range(half, aux, LANES):
-            first = side * quarter
-            square[first:first + quarter, c:c + LANES] = packed[at:at + quarter, :]
-            for r in range(0, quarter, LANES):
-                square[c:c + LANES, first + r:first + r + LANES] = packed[at + r:at + r + LANES, :].T
-            at += quarter
-    copies = []
-    for side in range(2):
-        at = side * plane + plane - half // LANES * quarter
-        base = side * half
-        for c in range(half - LANES, -1, -LANES):
-            at -= c + LANES
-            columns = slice(base + c, base + c + LANES)
-            square[base:base + c + LANES, columns] = packed[at:at + c + LANES, :]
-            for r in range(0, c, LANES):
-                square[columns, base + r:base + r + LANES] = packed[at + r:at + r + LANES, :].T
-            done = pl.ds(base + c, LANES)
-            copies += begin([(square.at[done], out.at[done])], sem, len(copies))
-    finish(copies)
+        pl.when(parity != side)(functools.partial(write_plane, side, packed, square, out, sem))
 
 
 def shards(slabs, pair_blocks, occ_energy, virt_energy, domain_map):
@@ -585,11 +611,15 @@
     across = [swapped(c, 2) for c in column]
     a, b = jnp.stack(column), jnp.stack(across)
     sib_a, sib_b = swapped(a, 1), swapped(b, 1)
-    packed = kernel(unpack_kernel, "unpack", [smem] + [vmem] * 3, plain(upper), vmem, flops=int(1e9))(me, a, b, sib_a)
+    whole = jax.ShapeDtypeStruct((aux, aux), F32)
+    scratch = [dma(2 + aux // 2 // LANES), pltpu.VMEM((aux, aux), F32)]
+    gradient, packed = kernel(
+        unpack_kernel, "unpack", [smem] + [vmem] * 3, (whole, plain(upper)), (hbm, vmem), scratch, flops=int(1e9),
+    )(me, a, b, sib_a)
     gradient, _ = kernel(
-        spread_kernel, "spread", [smem, vmem, vmem], (jax.ShapeDtypeStruct((aux, aux), F32), plain(upper)), (hbm, vmem),
-        [dma(aux // LANES), pltpu.VMEM((aux, aux), F32)], aliases={1: 1},
-    )(me, packed, sib_b)
+        spread_kernel, "spread", [smem, hbm, vmem, vmem], (whole, plain(upper)), (hbm, vmem), scratch,
+        aliases={1: 0, 2: 1},
+    )(me, gradient, packed, sib_b)
     return residual[None], gradient
 
 

time: 94.4 us -> 93.9 us (level)
  waiting for transfers between devices: 19.3 us -> 17.9 us
    ppermute x36, waiting for transfers between devices: 19.3 us -> 17.9 us  [move(): return lax.ppermute(x, 'dom', pairs)]
  transfers between devices with their start and end apart: 36 -> 36, of which waited for: 16 -> 15; matrix products, arithmetic and copies ran while one was open for 0% -> 0% of each run, Pallas kernels for 21% -> 23%
where the time goes in v9:
time: 93.9 us; the launch traced here: 93.6 us
  starting transfers between devices  41.8 us (45%)
  Pallas kernels  27.7 us (29%)
  waiting for transfers between devices  17.9 us (19%)
  local copies, waits for them, and re-layouts  4.53 us (5%)
  between operations  1.24 us (1%)
    ppermute x36, starting transfers between devices, move(): return lax.ppermute(x, 'dom', pairs)  41.8 us
    ppermute x36, waiting for transfers between devices, move(): return lax.ppermute(x, 'dom', pairs)  17.9 us
    pallas_call x4, Pallas kernels, pair_step(): kernel(functools.partial(body, plan, names, step), name, [smem] + [vmem]...  11.2 us
    unnamed x12, local copies, waits for them, and re-layouts  3.48 us
    pallas_call x1, Pallas kernels, shards(): kernel(own_kernel, 'own', [hbm, vmem, vmem], (jax.ShapeDtypeStruct((wide,...  3.01 us
    pallas_call x1, Pallas kernels, shards(): kernel(sib_kernel, 'sib', [vmem, vmem, hbm, vmem, vmem], total_t, vmem, [...  2.98 us
    pallas_call x1, Pallas kernels, shards(): kernel(near_metric_kernel, 'near_metric', [smem, vmem, vmem], (plain(uppe...  2.71 us
  transfers between devices with their start and end apart: 36, of which 15 were waited for; matrix products, arithmetic and copies ran while one was open for 0% of the time, Pallas kernels for 23%

profile of v9, /device:TPU:0, one launch (start us, length us, event | category | flops | bytes accessed | tf_op | source)
XLA Modules:
  0.0 93.6 jit_solution(3896782431045610959)
XLA Ops:
  0.7 1.0 %slice.12 = bf16[416,384]{1,0:T(8,128)(2,1)S(1)} slice(bf16[2048,384]{1,0:T(8,128)(2,1)} %bitcast.13), slice={[0:416], [0:384]} | slice | bytes 638976 | tf_op jit(solution)/shard_map/slice | solution.py:463
  1.7 0.5 collective-permute-start.1
  2.2 2.6 %collective-permute-start = (bf16[416,384]{1,0:T(8,128)(2,1)S(1)}, bf16[416,384]{1,0:T(8,128)(2,1)S(1)}, u32[]{:S(2)}, u32[]{:S(2)}) collective-permute-start(bf16[416,384]{1,0:T(8,128)(2,1)S(1)} %slice.12), channel_id=1, source_target_pairs={{0,2},{1,3},{2,0},{3,1},{4,6},{5,7},{6,4},{7,5},{8,10},{9,11},{10,... | collective-permute-start | bytes 958472 | tf_op jit(solution)/shard_map/ppermute | solution.py:24
  4.8 0.2 collective-permute-start.2
  5.0 1.4 %copy-done = bf16[1,2,1024,384]{3,2,1,0:T(8,128)(2,1)S(1)} copy-done((bf16[1,2,1024,384]{3,2,1,0:T(8,128)(2,1)S(1)}, bf16[1,2,1024,384]{3,2,1,0:T(8,128)(2,1)}, u32[]{:S(2)}) %copy-start) | copy-done | bytes 1572888
  6.4 0.7 copy-done.4
  7.0 0.9 split.1
  8.0 1.3 %prep.1 = (f32[8,768]{1,0:T(8,128)S(1)}, f32[8,768]{1,0:T(8,128)S(1)}) custom-call(s32[1]{0:T(128)} %bitcast.me_ref.a_0_, s32[1,3]{1,0:T(1,128)S(1)} %copy-done.4, s32[1,3]{1,0:T(1,128)S(1)} %collective-permute-done.2.sib_pairs, f32[2,16]{1,0:T(2,128)S(1)} %bitcast.19, f32[64,128]{1,0:T(8,128)S(1)} %bitcast.18, s32[16,384]{1,0:T(8,128)S(1)} %copy-done.3), custom_call_target="tpu_custom_call" | custom-call | flops 1 | bytes 1 | tf_op jit(solution)/shard_map/prep/pallas_call | solution.py:477
  9.3 0.4 collective-permute-start.4
  9.7 1.4 %copy-done.1 = bf16[1,2,1024,384]{3,2,1,0:T(8,128)(2,1)S(1)} copy-done((bf16[1,2,1024,384]{3,2,1,0:T(8,128)(2,1)S(1)}, bf16[1,2,1024,384]{3,2,1,0:T(8,128)(2,1)}, u32[]{:S(2)}) %copy-start.1) | copy-done | bytes 1572888
  11.1 3.0 %own.1 = (bf16[768,1024]{1,0:T(8,128)(2,1)S(1)}, bf16[1024,768]{1,0:T(8,128)(2,1)S(1)}, f32[1024,768]{1,0:T(8,128)S(1)}) custom-call(bf16[2048,384]{1,0:T(8,128)(2,1)S(1)} %bitcast.16, f32[8,768]{1,0:T(8,128)S(1)} %get-tuple-element.78.levels.a_2_, f32[8,768]{1,0:T(8,128)S(1)} %get-tuple-element.79.weights.a_3_), custom_call_target="tpu_custom_call" | custom-call | flops 20000000000 | bytes 1 | tf_op jit(solution)/shard_map/own/pallas_call | solution.py:482
  14.1 3.7 %collective-permute-start.9 = (bf16[416,384]{1,0:T(8,128)(2,1)S(1)}, bf16[416,384]{1,0:T(8,128)(2,1)S(1)}, u32[]{:S(2)}, u32[]{:S(2)}) collective-permute-start(bf16[416,384]{1,0:T(8,128)(2,1)S(1)} %collective-permute-done.rest_0_), channel_id=1, source_target_pairs={{0,4},{1,5},{4,8},{5,9},{6,2},{7,3},{8,12},{9,13},{10,6},{11,7},{1... | collective-permute-start | bytes 958472 | tf_op jit(solution)/shard_map/ppermute | solution.py:24
  17.8 0.1 collective-permute-start.3
  17.9 3.0 %sib.1.total.near = f32[1024,768]{1,0:T(8,128)S(1)} custom-call(bf16[768,1024]{1,0:T(8,128)(2,1)S(1)} %get-tuple-element.114.own_t.a_1_, f32[1024,768]{1,0:T(8,128)S(1)} %get-tuple-element.90.total_in, bf16[2048,384]{1,0:T(8,128)(2,1)S(1)} %collective-permute-done.1.sib, f32[8,768]{1,0:T(8,128)S(1)} %get-tuple-element.78.levels.a_2_, ...), custom_call_target="tpu_custom_call", output_to_operand_aliasing={{}: (1, {})} | custom-call | flops 10000000000 | bytes 1 | tf_op jit(solution)/shard_map/sib/pallas_call | solution.py:492
  20.9 3.9 %collective-permute-start.12 = (bf16[384,384]{1,0:T(8,128)(2,1)S(1)}, bf16[384,384]{1,0:T(8,128)(2,1)S(1)}, u32[]{:S(2)}, u32[]{:S(2)}) collective-permute-start(bf16[384,384]{1,0:T(8,128)(2,1)S(1)} %collective-permute-done.4.rest_1_), channel_id=1, source_target_pairs={{0,4},{1,5},{4,8},{5,9},{6,2},{7,3},{8,12},{9,13},{10,6},{11,7},{1... | collective-permute-start | bytes 884744 | tf_op jit(solution)/shard_map/ppermute | solution.py:24
  24.7 0.1 collective-permute-start.8
  24.8 3.2 %collective-permute-done.3.rest_2_ = bf16[432,384]{1,0:T(8,128)(2,1)S(1)} collective-permute-done((bf16[432,384]{1,0:T(8,128)(2,1)S(1)}, bf16[432,384]{1,0:T(8,128)(2,1)S(1)}, u32[]{:S(2)}, u32[]{:S(2)}) %collective-permute-start.3) | collective-permute-done | bytes 331808 | tf_op jit(solution)/shard_map/ppermute | solution.py:24
  28.0 3.5 %collective-permute-start.13 = (bf16[432,384]{1,0:T(8,128)(2,1)S(1)}, bf16[432,384]{1,0:T(8,128)(2,1)S(1)}, u32[]{:S(2)}, u32[]{:S(2)}) collective-permute-start(bf16[432,384]{1,0:T(8,128)(2,1)S(1)} %collective-permute-done.3.rest_2_), channel_id=1, source_target_pairs={{0,4},{1,5},{4,8},{5,9},{6,2},{7,3},{8,12},{9,13},{10,6},{11,7},{1... | collective-permute-start | bytes 995336 | tf_op jit(solution)/shard_map/ppermute | solution.py:24
  31.5 0.1 collective-permute-start.5
  31.6 2.7 %near_metric.1 = (f32[1152,128]{1,0:T(8,128)S(1)}, f32[1152,128]{1,0:T(8,128)S(1)}, s16[1216,128]{1,0:T(8,128)(2,1)S(1)}, s16[1216,128]{1,0:T(8,128)(2,1)S(1)}) custom-call(s32[1]{0:T(128)} %bitcast.me_ref.a_0_, f32[1024,768]{1,0:T(8,128)S(1)} %sib.1.total.near, bf16[1024,768]{1,0:T(8,128)(2,1)S(1)} %get-tuple-element.98.own_s), custom_call_target="tpu_custom_call" | custom-call | flops 10000000000 | bytes 1 | tf_op jit(solution)/shard_map/near_metric/pallas_call | solution.py:504
  34.3 1.0 %collective-permute-done.8.rest_3_ = bf16[416,384]{1,0:T(8,128)(2,1)S(1)} collective-permute-done((bf16[416,384]{1,0:T(8,128)(2,1)S(1)}, bf16[416,384]{1,0:T(8,128)(2,1)S(1)}, u32[]{:S(2)}, u32[]{:S(2)}) %collective-permute-start.8) | collective-permute-done | bytes 319520 | tf_op jit(solution)/shard_map/ppermute | solution.py:24
  35.3 3.5 %collective-permute-start.10 = (bf16[416,384]{1,0:T(8,128)(2,1)S(1)}, bf16[416,384]{1,0:T(8,128)(2,1)S(1)}, u32[]{:S(2)}, u32[]{:S(2)}) collective-permute-start(bf16[416,384]{1,0:T(8,128)(2,1)S(1)} %collective-permute-done.8.rest_3_), channel_id=1, source_target_pairs={{0,4},{1,5},{4,8},{5,9},{6,2},{7,3},{8,12},{9,13},{10,6},{11,7},{1... | collective-permute-start | bytes 958472 | tf_op jit(solution)/shard_map/ppermute | solution.py:24
  38.8 0.5 collective-permute-start.7
  39.3 0.2 collective-permute-done.13.rest_2_.a_5_
  39.6 0.2 maximum_select_fusion
  39.9 0.5 collective-permute-done.6.got_away
  40.4 0.4 collective-permute-done.7.got_keep
  40.9 0.2 collective-permute-done.5.rest_4_
  41.0 3.7 %collective-permute-start.11 = (bf16[416,384]{1,0:T(8,128)(2,1)S(1)}, bf16[416,384]{1,0:T(8,128)(2,1)S(1)}, u32[]{:S(2)}, u32[]{:S(2)}) collective-permute-start(bf16[416,384]{1,0:T(8,128)(2,1)S(1)} %collective-permute-done.5.rest_4_), channel_id=1, source_target_pairs={{0,4},{1,5},{4,8},{5,9},{6,2},{7,3},{8,12},{9,13},{10,6},{11,7},{1... | collective-permute-start | bytes 958472 | tf_op jit(solution)/shard_map/ppermute | solution.py:24
  44.7 0.3 chip.1
  45.2 2.7 %far2.1.total_in = f32[1024,768]{1,0:T(8,128)S(1)} custom-call(s32[1]{0:T(128)} %bitcast.me_ref.a_0_, bf16[768,1024]{1,0:T(8,128)(2,1)S(1)} %get-tuple-element.114.own_t.a_1_, f32[8,768]{1,0:T(8,128)S(1)} %get-tuple-element.78.levels.a_2_, f32[8,768]{1,0:T(8,128)S(1)} %get-tuple-element.79.weights.a_3_, bf16[416,384]{1,0:T(8,128)(2,1)S(1)} %collective-permute-done.rest_0_, ...), custom_call_target="tpu_custom_call" | custom-call | flops 10000000000 | bytes 1 | tf_op jit(solution)/shard_map/far2/pallas_call | solution.py:550
  47.8 2.7 %far3.1.a_4_ = f32[1024,768]{1,0:T(8,128)S(1)} custom-call(s32[1]{0:T(128)} %bitcast.me_ref.a_0_, bf16[768,1024]{1,0:T(8,128)(2,1)S(1)} %get-tuple-element.114.own_t.a_1_, f32[8,768]{1,0:T(8,128)S(1)} %get-tuple-element.78.levels.a_2_, f32[8,768]{1,0:T(8,128)S(1)} %get-tuple-element.79.weights.a_3_, ...), custom_call_target="tpu_custom_call", output_to_operand_aliasing={{}: (4, {})} | custom-call | flops 1 | bytes 1 | tf_op jit(solution)/shard_map/far3/pallas_call | solution.py:550
  50.7 0.5 collective-permute-start.15
  51.2 3.2 %collective-permute-done.17.across = s16[1216,128]{1,0:T(8,128)(2,1)S(1)} collective-permute-done((s16[1216,128]{1,0:T(8,128)(2,1)S(1)}, s16[1216,128]{1,0:T(8,128)(2,1)S(1)}, u32[]{:S(2)}, u32[]{:S(2)}) %collective-permute-start.17) | collective-permute-done | bytes 311328 | tf_op jit(solution)/shard_map/ppermute | solution.py:24
  54.5 1.9 %half.1.total_in = f32[1024,768]{1,0:T(8,128)S(1)} custom-call(s32[1]{0:T(128)} %bitcast.me_ref.a_0_, bf16[768,1024]{1,0:T(8,128)(2,1)S(1)} %get-tuple-element.114.own_t.a_1_, f32[8,768]{1,0:T(8,128)S(1)} %get-tuple-element.78.levels.a_2_, f32[8,768]{1,0:T(8,128)S(1)} %get-tuple-element.79.weights.a_3_, ...), custom_call_target="tpu_custom_call", output_to_operand_aliasing={{}: (4, {})} | custom-call | flops 1000000000 | bytes 1 | tf_op jit(solution)/shard_map/half/pallas_call | solution.py:550
  56.4 4.0 %last.1 = (f32[1024,768]{1,0:T(8,128)S(1)}, f32[2,1024,384]{2,1,0:T(8,128)}, f32[640,128]{1,0:T(8,128)S(1)}, f32[640,128]{1,0:T(8,128)S(1)}, bf16[1024,768]{1,0:...) custom-call(s32[1]{0:T(128)} %bitcast.me_ref.a_0_, ...), custom_call_target="tpu_custom_call", output_to_operand_aliasing={{0}: (4, {})} | custom-call | flops 1 | bytes 1 | tf_op jit(solution)/shard_map/last/pallas_call | solution.py:550
  60.4 0.6 collective-permute-start.19
  61.0 1.1 %corner.1 = (f32[512,128]{1,0:T(8,128)S(1)}, f32[512,128]{1,0:T(8,128)S(1)}) custom-call(s32[1]{0:T(128)} %bitcast.me_ref.a_0_, bf16[1024,768]{1,0:T(8,128)(2,1)S(1)} %get-tuple-element.131.high, bf16[1024,768]{1,0:T(8,128)(2,1)S(1)} %get-tuple-element.132.low, bf16[1024,768]{1,0:T(8,128)(2,1)S(1)} %get-tuple-element.98.own_s), custom_call_target="tpu_custom_call" | custom-call | flops 2000000000 | bytes 1 | tf_op jit(solution)/shard_map/corner/pallas_call | solution.py:588
  62.1 0.2 collective-permute-done.19.theirs
  62.2 0.4 collective-permute-start.23
  62.6 0.2 column.2
  62.9 2.8 %collective-permute-start.20 = (s16[176,128]{1,0:T(8,128)(2,1)S(1)}, s16[176,128]{1,0:T(8,128)(2,1)S(1)}, u32[]{:S(2)}, u32[]{:S(2)}) collective-permute-start(s16[176,128]{1,0:T(8,128)(2,1)S(1)} %get-tuple-element.138), channel_id=1, source_target_pairs={{0,12},{1,13},{2,14},{3,15},{4,8},{5,9},{6,10},{7,11},{8,4},{9,5},... | collective-permute-start | bytes 135176 | tf_op jit(solution)/shard_map/ppermute | solution.py:24
  65.6 0.3 collective-permute-start.21
  66.0 1.4 %collective-permute-start.22 = (s16[176,128]{1,0:T(8,128)(2,1)S(1)}, s16[176,128]{1,0:T(8,128)(2,1)S(1)}, u32[]{:S(2)}, u32[]{:S(2)}) collective-permute-start(s16[176,128]{1,0:T(8,128)(2,1)S(1)} %get-tuple-element.140), channel_id=1, source_target_pairs={{0,4},{1,5},{2,6},{3,7},{4,0},{5,1},{6,2},{7,3},{8,12},{9,13},{10,... | collective-permute-start | bytes 135176 | tf_op jit(solution)/shard_map/ppermute | solution.py:24
  67.3 0.4 column.3
  67.8 2.8 %collective-permute-start.24 = (s16[144,128]{1,0:T(8,128)(2,1)S(1)}, s16[144,128]{1,0:T(8,128)(2,1)S(1)}, u32[]{:S(2)}, u32[]{:S(2)}) collective-permute-start(s16[144,128]{1,0:T(8,128)(2,1)S(1)} %get-tuple-element.144), channel_id=1, source_target_pairs={{0,12},{1,13},{2,14},{3,15},{4,8},{5,9},{6,10},{7,11},{8,4},{9,5},... | collective-permute-start | bytes 110600 | tf_op jit(solution)/shard_map/ppermute | solution.py:24
  70.5 1.7 %collective-permute-start.26 = (s16[144,128]{1,0:T(8,128)(2,1)S(1)}, s16[144,128]{1,0:T(8,128)(2,1)S(1)}, u32[]{:S(2)}, u32[]{:S(2)}) collective-permute-start(s16[144,128]{1,0:T(8,128)(2,1)S(1)} %get-tuple-element.146), channel_id=1, source_target_pairs={{0,4},{1,5},{2,6},{3,7},{4,0},{5,1},{6,2},{7,3},{8,12},{9,13},{10,... | collective-permute-start | bytes 110600 | tf_op jit(solution)/shard_map/ppermute | solution.py:24
  72.2 1.4 %collective-permute-done.24.rest_5_ = s16[144,128]{1,0:T(8,128)(2,1)S(1)} collective-permute-done((s16[144,128]{1,0:T(8,128)(2,1)S(1)}, s16[144,128]{1,0:T(8,128)(2,1)S(1)}, u32[]{:S(2)}, u32[]{:S(2)}) %collective-permute-start.24) | collective-permute-done | bytes 36896 | tf_op jit(solution)/shard_map/ppermute | solution.py:24
  73.6 1.8 %collective-permute-done.25.rest_6_ = s16[144,128]{1,0:T(8,128)(2,1)S(1)} collective-permute-done((s16[144,128]{1,0:T(8,128)(2,1)S(1)}, s16[144,128]{1,0:T(8,128)(2,1)S(1)}, u32[]{:S(2)}, u32[]{:S(2)}) %collective-permute-start.25) | collective-permute-done | bytes 36896 | tf_op jit(solution)/shard_map/ppermute | solution.py:24
  75.4 0.1 sum_code.1
  75.5 1.9 %collective-permute-start.29 = (s16[304,128]{1,0:T(8,128)(2,1)S(1)}, s16[304,128]{1,0:T(8,128)(2,1)S(1)}, u32[]{:S(2)}, u32[]{:S(2)}) collective-permute-start(s16[304,128]{1,0:T(8,128)(2,1)S(1)} %sum_code.1), channel_id=1, source_target_pairs={{0,12},{1,13},{2,14},{3,15},{4,8},{5,9},{6,10},{7,11},{8,4},{9,5},... | collective-permute-start | bytes 233480 | tf_op jit(solution)/shard_map/ppermute | solution.py:24
  77.4 0.4 collective-permute-start.28
  77.8 2.1 %collective-permute-start.27 = (s16[304,128]{1,0:T(8,128)(2,1)S(1)}, s16[304,128]{1,0:T(8,128)(2,1)S(1)}, u32[]{:S(2)}, u32[]{:S(2)}) collective-permute-start(s16[304,128]{1,0:T(8,128)(2,1)S(1)} %sum_code.1), channel_id=1, source_target_pairs={{0,4},{1,5},{2,6},{3,7},{4,0},{5,1},{6,2},{7,3},{8,12},{9,13},{10,... | collective-permute-start | bytes 233480 | tf_op jit(solution)/shard_map/ppermute | solution.py:24
  80.0 1.1 %collective-permute-start.30 = (s16[304,128]{1,0:T(8,128)(2,1)S(1)}, s16[304,128]{1,0:T(8,128)(2,1)S(1)}, u32[]{:S(2)}, u32[]{:S(2)}) collective-permute-start(s16[304,128]{1,0:T(8,128)(2,1)S(1)} %sum_code.1), channel_id=1, source_target_pairs={{0,2},{1,3},{2,0},{3,1},{4,6},{5,7},{6,4},{7,5},{8,10},{9,11},{10,... | collective-permute-start | bytes 233480 | tf_op jit(solution)/shard_map/ppermute | solution.py:24
  81.1 1.1 %collective-permute-done.29 = s16[304,128]{1,0:T(8,128)(2,1)S(1)} collective-permute-done((s16[304,128]{1,0:T(8,128)(2,1)S(1)}, s16[304,128]{1,0:T(8,128)(2,1)S(1)}, u32[]{:S(2)}, u32[]{:S(2)}) %collective-permute-start.29) | collective-permute-done | bytes 77856 | tf_op jit(solution)/shard_map/ppermute | solution.py:24
  82.2 0.8 collective-permute-start.33
  83.0 1.4 %collective-permute-done.28 = s16[304,128]{1,0:T(8,128)(2,1)S(1)} collective-permute-done((s16[304,128]{1,0:T(8,128)(2,1)S(1)}, s16[304,128]{1,0:T(8,128)(2,1)S(1)}, u32[]{:S(2)}, u32[]{:S(2)}) %collective-permute-start.28) | collective-permute-done | bytes 77856 | tf_op jit(solution)/shard_map/ppermute | solution.py:24
  84.4 0.4 collective-permute-start.32
  84.8 1.6 %collective-permute-start.31 = (s16[304,128]{1,0:T(8,128)(2,1)S(1)}, s16[304,128]{1,0:T(8,128)(2,1)S(1)}, u32[]{:S(2)}, u32[]{:S(2)}) collective-permute-start(s16[304,128]{1,0:T(8,128)(2,1)S(1)} %collective-permute-done.27), channel_id=1, source_target_pairs={{0,2},{1,3},{2,0},{3,1},{4,6},{5,7},{6,4},{7,5},{8,10},{9,11},{10,... | collective-permute-start | bytes 233480 | tf_op jit(solution)/shard_map/ppermute | solution.py:24
  86.6 0.9 collective-permute-done.33
  87.5 1.5 %collective-permute-done.32 = s16[304,128]{1,0:T(8,128)(2,1)S(1)} collective-permute-done((s16[304,128]{1,0:T(8,128)(2,1)S(1)}, s16[304,128]{1,0:T(8,128)(2,1)S(1)}, u32[]{:S(2)}, u32[]{:S(2)}) %collective-permute-start.32) | collective-permute-done | bytes 77856 | tf_op jit(solution)/shard_map/ppermute | solution.py:24
  89.0 0.8 collective-permute-done.31
  90.0 1.8 %unpack.1 = (f32[1024,1024]{1,0:T(8,128)}, f32[4608,128]{1,0:T(8,128)S(1)}) custom-call(s32[1]{0:T(128)} %bitcast.me_ref.a_0_, s16[4,304,128]{2,1,0:T(8,128)(2,1)S(1)} %pad_add_fusion.a, s16[4,304,128]{2,1,0:T(8,128)(2,1)S(1)} %pad_add_fusion.1.b, s16[4,304,128]{2,1,0:T(8,128)(2,1)S(1)} %collective-permute-done.34.sib_a), custom_call_target="tpu_custom_call" | custom-call | flops 1000000000 | bytes 1 | tf_op jit(solution)/shard_map/unpack/pallas_call | solution.py:616
  91.8 1.6 %spread.1 = (f32[1024,1024]{1,0:T(8,128)}, f32[4608,128]{1,0:T(8,128)S(1)}) custom-call(s32[1]{0:T(128)} %bitcast.me_ref.a_0_, f32[1024,1024]{1,0:T(8,128)} %get-tuple-element.147.out_in, f32[4608,128]{1,0:T(8,128)S(1)} %get-tuple-element.148.packed_in, ...), custom_call_target="tpu_custom_call", output_to_operand_aliasing={{0}: (1, {}), {1}: (2, {})} | custom-call | flops 1 | bytes 1 | tf_op jit(solution)/shard_map/spread/pallas_call | solution.py:619
  (43 shorter events, 0.8 us)
Async XLA Ops:
  0.6 7.3 %copy-start.3 = (s32[16,384]{1,0:T(8,128)S(1)}, s32[16,384]{1,0:T(8,128)}, u32[]{:S(2)}) copy-start(s32[16,384]{1,0:T(8,128)} %maps_in.1) | copy-start | bytes 73732
  0.6 7.3 %copy-start.2 = (f32[8192]{0:T(1024)S(1)}, f32[8192]{0:T(1024)}, u32[]{:S(2)}) copy-start(f32[8192]{0:T(1024)} %param.8) | copy-start | bytes 98308
  0.7 7.3 %copy-start.5 = (f32[16,2]{0,1:T(2,128)S(1)}, f32[16,2]{0,1:T(2,128)}, u32[]{:S(2)}) copy-start(f32[16,2]{0,1:T(2,128)} %param.7) | copy-start | bytes 388
  1.7 7.6 %collective-permute-start.1 = (bf16[2048,384]{1,0:T(8,128)(2,1)}, bf16[2048,384]{1,0:T(8,128)(2,1)S(1)}, u32[]{:S(2)}, u32[]{:S(2)}) collective-permute-start(bf16[2048,384]{1,0:T(8,128)(2,1)} %bitcast.14), channel_id=1, source_target_pairs={{0,1},{1,0},{2,3},{3,2},{4,5},{5,4},{6,7},{7,6},{8,9},{9,8},{10,11... | collective-permute-start | bytes 4718600 | tf_op jit(solution)/shard_map/ppermute | solution.py:24
  2.2 11.9 %collective-permute-start = (bf16[416,384]{1,0:T(8,128)(2,1)S(1)}, bf16[416,384]{1,0:T(8,128)(2,1)S(1)}, u32[]{:S(2)}, u32[]{:S(2)}) collective-permute-start(bf16[416,384]{1,0:T(8,128)(2,1)S(1)} %slice.12), channel_id=1, source_target_pairs={{0,2},{1,3},{2,0},{3,1},{4,6},{5,7},{6,4},{7,5},{8,10},{9,11},{10,... | collective-permute-start | bytes 958472 | tf_op jit(solution)/shard_map/ppermute | solution.py:24
  4.8 3.2 %collective-permute-start.2 = (s32[1,3]{1,0:T(1,128)}, s32[1,3]{1,0:T(1,128)S(1)}, u32[]{:S(2)}, u32[]{:S(2)}) collective-permute-start(s32[1,3]{1,0:T(1,128)} %pairs.3), channel_id=1, source_target_pairs={{0,1},{1,0},{2,3},{3,2},{4,5},{5,4},{6,7},{7,6},{8,9},{9,8},{10,11... | collective-permute-start | bytes 44 | tf_op jit(solution)/shard_map/ppermute | solution.py:24
  5.0 1.4 %copy-start = (bf16[1,2,1024,384]{3,2,1,0:T(8,128)(2,1)S(1)}, bf16[1,2,1024,384]{3,2,1,0:T(8,128)(2,1)}, u32[]{:S(2)}) copy-start(bf16[1,2,1024,384]{3,2,1,0:T(8,128)(2,1)} %param.5) | copy-start | bytes 4718596
  6.4 0.7 copy-start.4
  9.3 11.6 %collective-permute-start.4 = (bf16[384,384]{1,0:T(8,128)(2,1)S(1)}, bf16[384,384]{1,0:T(8,128)(2,1)S(1)}, u32[]{:S(2)}, u32[]{:S(2)}) collective-permute-start(bf16[384,384]{1,0:T(8,128)(2,1)S(1)} %get-tuple-element.88), channel_id=1, source_target_pairs={{0,2},{1,3},{2,0},{3,1},{4,6},{5,7},{6,4},{7,5},{8,10},{9,11},{10,... | collective-permute-start | bytes 884744 | tf_op jit(solution)/shard_map/ppermute | solution.py:24
  9.7 1.4 %copy-start.1 = (bf16[1,2,1024,384]{3,2,1,0:T(8,128)(2,1)S(1)}, bf16[1,2,1024,384]{3,2,1,0:T(8,128)(2,1)}, u32[]{:S(2)}) copy-start(bf16[1,2,1024,384]{3,2,1,0:T(8,128)(2,1)} %param.5) | copy-start | bytes 4718596
  14.1 20.2 %collective-permute-start.9 = (bf16[416,384]{1,0:T(8,128)(2,1)S(1)}, bf16[416,384]{1,0:T(8,128)(2,1)S(1)}, u32[]{:S(2)}, u32[]{:S(2)}) collective-permute-start(bf16[416,384]{1,0:T(8,128)(2,1)S(1)} %collective-permute-done.rest_0_), channel_id=1, source_target_pairs={{0,4},{1,5},{4,8},{5,9},{6,2},{7,3},{8,12},{9,13},{10,6},{11,7},{1... | collective-permute-start | bytes 958472 | tf_op jit(solution)/shard_map/ppermute | solution.py:24
  17.8 10.2 %collective-permute-start.3 = (bf16[432,384]{1,0:T(8,128)(2,1)S(1)}, bf16[432,384]{1,0:T(8,128)(2,1)S(1)}, u32[]{:S(2)}, u32[]{:S(2)}) collective-permute-start(bf16[432,384]{1,0:T(8,128)(2,1)S(1)} %get-tuple-element.86), channel_id=1, source_target_pairs={{0,2},{1,3},{2,0},{3,1},{4,6},{5,7},{6,4},{7,5},{8,10},{9,11},{10,... | collective-permute-start | bytes 995336 | tf_op jit(solution)/shard_map/ppermute | solution.py:24
  20.9 18.0 %collective-permute-start.12 = (bf16[384,384]{1,0:T(8,128)(2,1)S(1)}, bf16[384,384]{1,0:T(8,128)(2,1)S(1)}, u32[]{:S(2)}, u32[]{:S(2)}) collective-permute-start(bf16[384,384]{1,0:T(8,128)(2,1)S(1)} %collective-permute-done.4.rest_1_), channel_id=1, source_target_pairs={{0,4},{1,5},{4,8},{5,9},{6,2},{7,3},{8,12},{9,13},{10,6},{11,7},{1... | collective-permute-start | bytes 884744 | tf_op jit(solution)/shard_map/ppermute | solution.py:24
  24.7 10.5 %collective-permute-start.8 = (bf16[416,384]{1,0:T(8,128)(2,1)S(1)}, bf16[416,384]{1,0:T(8,128)(2,1)S(1)}, u32[]{:S(2)}, u32[]{:S(2)}) collective-permute-start(bf16[416,384]{1,0:T(8,128)(2,1)S(1)} %get-tuple-element.102), channel_id=1, source_target_pairs={{0,2},{1,3},{2,0},{3,1},{4,6},{5,7},{6,4},{7,5},{8,10},{9,11},{10,... | collective-permute-start | bytes 958472 | tf_op jit(solution)/shard_map/ppermute | solution.py:24
  28.0 11.6 %collective-permute-start.13 = (bf16[432,384]{1,0:T(8,128)(2,1)S(1)}, bf16[432,384]{1,0:T(8,128)(2,1)S(1)}, u32[]{:S(2)}, u32[]{:S(2)}) collective-permute-start(bf16[432,384]{1,0:T(8,128)(2,1)S(1)} %collective-permute-done.3.rest_2_), channel_id=1, source_target_pairs={{0,4},{1,5},{4,8},{5,9},{6,2},{7,3},{8,12},{9,13},{10,6},{11,7},{1... | collective-permute-start | bytes 995336 | tf_op jit(solution)/shard_map/ppermute | solution.py:24
  31.5 9.5 %collective-permute-start.5 = (bf16[416,384]{1,0:T(8,128)(2,1)S(1)}, bf16[416,384]{1,0:T(8,128)(2,1)S(1)}, u32[]{:S(2)}, u32[]{:S(2)}) collective-permute-start(bf16[416,384]{1,0:T(8,128)(2,1)S(1)} %get-tuple-element.94), channel_id=1, source_target_pairs={{0,2},{1,3},{2,0},{3,1},{4,6},{5,7},{6,4},{7,5},{8,10},{9,11},{10,... | collective-permute-start | bytes 958472 | tf_op jit(solution)/shard_map/ppermute | solution.py:24
  35.3 9.9 %collective-permute-start.10 = (bf16[416,384]{1,0:T(8,128)(2,1)S(1)}, bf16[416,384]{1,0:T(8,128)(2,1)S(1)}, u32[]{:S(2)}, u32[]{:S(2)}) collective-permute-start(bf16[416,384]{1,0:T(8,128)(2,1)S(1)} %collective-permute-done.8.rest_3_), channel_id=1, source_target_pairs={{0,4},{1,5},{4,8},{5,9},{6,2},{7,3},{8,12},{9,13},{10,6},{11,7},{1... | collective-permute-start | bytes 958472 | tf_op jit(solution)/shard_map/ppermute | solution.py:24
  38.8 1.7 %collective-permute-start.6 = (s16[1216,128]{1,0:T(8,128)(2,1)S(1)}, s16[1216,128]{1,0:T(8,128)(2,1)S(1)}, u32[]{:S(2)}, u32[]{:S(2)}) collective-permute-start(s16[1216,128]{1,0:T(8,128)(2,1)S(1)} %get-tuple-element.99), channel_id=1, source_target_pairs={{0,1},{1,0},{2,3},{3,2},{4,5},{5,4},{6,7},{7,6},{8,9},{9,8},{10,11... | collective-permute-start | bytes 933896 | tf_op jit(solution)/shard_map/ppermute | solution.py:24
  38.8 2.0 %collective-permute-start.7 = (s16[1216,128]{1,0:T(8,128)(2,1)S(1)}, s16[1216,128]{1,0:T(8,128)(2,1)S(1)}, u32[]{:S(2)}, u32[]{:S(2)}) collective-permute-start(s16[1216,128]{1,0:T(8,128)(2,1)S(1)} %get-tuple-element.100), channel_id=1, source_target_pairs={{0,1},{1,0},{2,3},{3,2},{4,5},{5,4},{6,7},{7,6},{8,9},{9,8},{10,11... | collective-permute-start | bytes 933896 | tf_op jit(solution)/shard_map/ppermute | solution.py:24
  39.8 8.0 %collective-permute-start.14 = (bf16[1232,384]{1,0:T(8,128)(2,1)S(1)}, bf16[1232,384]{1,0:T(8,128)(2,1)S(1)}, u32[]{:S(2)}, u32[]{:S(2)}) collective-permute-start(bf16[1232,384]{1,0:T(8,128)(2,1)S(1)} %maximum_select_fusion), channel_id=1, source_target_pairs={{0,1},{1,0},{2,3},{3,2},{4,5},{5,4},{6,7},{7,6},{8,9},{9,8},{10,11... | collective-permute-start | bytes 2838536 | tf_op jit(solution)/shard_map/ppermute | solution.py:24
  41.0 13.4 %collective-permute-start.11 = (bf16[416,384]{1,0:T(8,128)(2,1)S(1)}, bf16[416,384]{1,0:T(8,128)(2,1)S(1)}, u32[]{:S(2)}, u32[]{:S(2)}) collective-permute-start(bf16[416,384]{1,0:T(8,128)(2,1)S(1)} %collective-permute-done.5.rest_4_), channel_id=1, source_target_pairs={{0,4},{1,5},{4,8},{5,9},{6,2},{7,3},{8,12},{9,13},{10,6},{11,7},{1... | collective-permute-start | bytes 958472 | tf_op jit(solution)/shard_map/ppermute | solution.py:24
  45.1 9.3 %collective-permute-start.17 = (s16[1216,128]{1,0:T(8,128)(2,1)S(1)}, s16[1216,128]{1,0:T(8,128)(2,1)S(1)}, u32[]{:S(2)}, u32[]{:S(2)}) collective-permute-start(s16[1216,128]{1,0:T(8,128)(2,1)S(1)} %get-tuple-element.123), channel_id=1, source_target_pairs={{0,2},{1,3},{2,0},{3,1},{4,6},{5,7},{6,4},{7,5},{8,10},{9,11},{10,... | collective-permute-start | bytes 933896 | tf_op jit(solution)/shard_map/ppermute | solution.py:24
  50.6 3.8 %collective-permute-start.16 = (bf16[208,384]{1,0:T(8,128)(2,1)S(1)}, bf16[208,384]{1,0:T(8,128)(2,1)S(1)}, u32[]{:S(2)}, u32[]{:S(2)}) collective-permute-start(bf16[208,384]{1,0:T(8,128)(2,1)S(1)} %get-tuple-element.150), channel_id=1, source_target_pairs={{0,1},{1,0},{2,3},{3,2},{4,5},{5,4},{6,7},{7,6},{8,9},{9,8},{10,11... | collective-permute-start | bytes 479240 | tf_op jit(solution)/shard_map/ppermute | solution.py:24
  50.7 3.7 %collective-permute-start.15 = (bf16[208,384]{1,0:T(8,128)(2,1)S(1)}, bf16[208,384]{1,0:T(8,128)(2,1)S(1)}, u32[]{:S(2)}, u32[]{:S(2)}) collective-permute-start(bf16[208,384]{1,0:T(8,128)(2,1)S(1)} %get-tuple-element.151), channel_id=1, source_target_pairs={{0,1},{1,0},{2,3},{3,2},{4,5},{5,4},{6,7},{7,6},{8,9},{9,8},{10,11... | collective-permute-start | bytes 479240 | tf_op jit(solution)/shard_map/ppermute | solution.py:24
  54.5 2.0 %collective-permute-start.18 = (bf16[416,384]{1,0:T(8,128)(2,1)S(1)}, bf16[416,384]{1,0:T(8,128)(2,1)S(1)}, u32[]{:S(2)}, u32[]{:S(2)}) collective-permute-start(bf16[416,384]{1,0:T(8,128)(2,1)S(1)} %broadcast_select_fusion), channel_id=1, source_target_pairs={{0,1},{1,0},{2,3},{3,2},{4,5},{5,4},{6,7},{7,6},{8,9},{9,8},{10,11... | collective-permute-start | bytes 958472 | tf_op jit(solution)/shard_map/ppermute | solution.py:24
  60.4 1.8 %collective-permute-start.19 = (f32[640,128]{1,0:T(8,128)S(1)}, f32[640,128]{1,0:T(8,128)S(1)}, u32[]{:S(2)}, u32[]{:S(2)}) collective-permute-start(f32[640,128]{1,0:T(8,128)S(1)} %get-tuple-element.130), channel_id=1, source_target_pairs={{0,1},{1,0},{2,3},{3,2},{4,5},{5,4},{6,7},{7,6},{8,9},{9,8},{10,11... | collective-permute-start | bytes 983048 | tf_op jit(solution)/shard_map/ppermute | solution.py:24
  62.2 5.1 %collective-permute-start.23 = (f32[512,128]{1,0:T(8,128)S(1)}, f32[512,128]{1,0:T(8,128)S(1)}, u32[]{:S(2)}, u32[]{:S(2)}) collective-permute-start(f32[512,128]{1,0:T(8,128)S(1)} %get-tuple-element.142), channel_id=1, source_target_pairs={{0,1},{1,0},{2,3},{3,2},{4,5},{5,4},{6,7},{7,6},{8,9},{9,8},{10,11... | collective-permute-start | bytes 786440 | tf_op jit(solution)/shard_map/ppermute | solution.py:24
  62.9 7.7 %collective-permute-start.20 = (s16[176,128]{1,0:T(8,128)(2,1)S(1)}, s16[176,128]{1,0:T(8,128)(2,1)S(1)}, u32[]{:S(2)}, u32[]{:S(2)}) collective-permute-start(s16[176,128]{1,0:T(8,128)(2,1)S(1)} %get-tuple-element.138), channel_id=1, source_target_pairs={{0,12},{1,13},{2,14},{3,15},{4,8},{5,9},{6,10},{7,11},{8,4},{9,5},... | collective-permute-start | bytes 135176 | tf_op jit(solution)/shard_map/ppermute | solution.py:24
  65.6 6.6 %collective-permute-start.21 = (s16[176,128]{1,0:T(8,128)(2,1)S(1)}, s16[176,128]{1,0:T(8,128)(2,1)S(1)}, u32[]{:S(2)}, u32[]{:S(2)}) collective-permute-start(s16[176,128]{1,0:T(8,128)(2,1)S(1)} %get-tuple-element.139), channel_id=1, source_target_pairs={{0,8},{1,9},{2,10},{3,11},{4,12},{5,13},{6,14},{7,15},{8,0},{9,1},... | collective-permute-start | bytes 135176 | tf_op jit(solution)/shard_map/ppermute | solution.py:24
  66.0 6.3 %collective-permute-start.22 = (s16[176,128]{1,0:T(8,128)(2,1)S(1)}, s16[176,128]{1,0:T(8,128)(2,1)S(1)}, u32[]{:S(2)}, u32[]{:S(2)}) collective-permute-start(s16[176,128]{1,0:T(8,128)(2,1)S(1)} %get-tuple-element.140), channel_id=1, source_target_pairs={{0,4},{1,5},{2,6},{3,7},{4,0},{5,1},{6,2},{7,3},{8,12},{9,13},{10,... | collective-permute-start | bytes 135176 | tf_op jit(solution)/shard_map/ppermute | solution.py:24
  67.8 5.8 %collective-permute-start.24 = (s16[144,128]{1,0:T(8,128)(2,1)S(1)}, s16[144,128]{1,0:T(8,128)(2,1)S(1)}, u32[]{:S(2)}, u32[]{:S(2)}) collective-permute-start(s16[144,128]{1,0:T(8,128)(2,1)S(1)} %get-tuple-element.144), channel_id=1, source_target_pairs={{0,12},{1,13},{2,14},{3,15},{4,8},{5,9},{6,10},{7,11},{8,4},{9,5},... | collective-permute-start | bytes 110600 | tf_op jit(solution)/shard_map/ppermute | solution.py:24
  70.5 4.9 %collective-permute-start.25 = (s16[144,128]{1,0:T(8,128)(2,1)S(1)}, s16[144,128]{1,0:T(8,128)(2,1)S(1)}, u32[]{:S(2)}, u32[]{:S(2)}) collective-permute-start(s16[144,128]{1,0:T(8,128)(2,1)S(1)} %get-tuple-element.145), channel_id=1, source_target_pairs={{0,8},{1,9},{2,10},{3,11},{4,12},{5,13},{6,14},{7,15},{8,0},{9,1},... | collective-permute-start | bytes 110600 | tf_op jit(solution)/shard_map/ppermute | solution.py:24
  70.5 4.9 %collective-permute-start.26 = (s16[144,128]{1,0:T(8,128)(2,1)S(1)}, s16[144,128]{1,0:T(8,128)(2,1)S(1)}, u32[]{:S(2)}, u32[]{:S(2)}) collective-permute-start(s16[144,128]{1,0:T(8,128)(2,1)S(1)} %get-tuple-element.146), channel_id=1, source_target_pairs={{0,4},{1,5},{2,6},{3,7},{4,0},{5,1},{6,2},{7,3},{8,12},{9,13},{10,... | collective-permute-start | bytes 110600 | tf_op jit(solution)/shard_map/ppermute | solution.py:24
  75.5 6.7 %collective-permute-start.29 = (s16[304,128]{1,0:T(8,128)(2,1)S(1)}, s16[304,128]{1,0:T(8,128)(2,1)S(1)}, u32[]{:S(2)}, u32[]{:S(2)}) collective-permute-start(s16[304,128]{1,0:T(8,128)(2,1)S(1)} %sum_code.1), channel_id=1, source_target_pairs={{0,12},{1,13},{2,14},{3,15},{4,8},{5,9},{6,10},{7,11},{8,4},{9,5},... | collective-permute-start | bytes 233480 | tf_op jit(solution)/shard_map/ppermute | solution.py:24
  77.4 7.0 %collective-permute-start.28 = (s16[304,128]{1,0:T(8,128)(2,1)S(1)}, s16[304,128]{1,0:T(8,128)(2,1)S(1)}, u32[]{:S(2)}, u32[]{:S(2)}) collective-permute-start(s16[304,128]{1,0:T(8,128)(2,1)S(1)} %sum_code.1), channel_id=1, source_target_pairs={{0,8},{1,9},{2,10},{3,11},{4,12},{5,13},{6,14},{7,15},{8,0},{9,1},... | collective-permute-start | bytes 233480 | tf_op jit(solution)/shard_map/ppermute | solution.py:24
  77.8 7.0 %collective-permute-start.27 = (s16[304,128]{1,0:T(8,128)(2,1)S(1)}, s16[304,128]{1,0:T(8,128)(2,1)S(1)}, u32[]{:S(2)}, u32[]{:S(2)}) collective-permute-start(s16[304,128]{1,0:T(8,128)(2,1)S(1)} %sum_code.1), channel_id=1, source_target_pairs={{0,4},{1,5},{2,6},{3,7},{4,0},{5,1},{6,2},{7,3},{8,12},{9,13},{10,... | collective-permute-start | bytes 233480 | tf_op jit(solution)/shard_map/ppermute | solution.py:24
  80.0 6.6 %collective-permute-start.30 = (s16[304,128]{1,0:T(8,128)(2,1)S(1)}, s16[304,128]{1,0:T(8,128)(2,1)S(1)}, u32[]{:S(2)}, u32[]{:S(2)}) collective-permute-start(s16[304,128]{1,0:T(8,128)(2,1)S(1)} %sum_code.1), channel_id=1, source_target_pairs={{0,2},{1,3},{2,0},{3,1},{4,6},{5,7},{6,4},{7,5},{8,10},{9,11},{10,... | collective-permute-start | bytes 233480 | tf_op jit(solution)/shard_map/ppermute | solution.py:24
  82.2 5.2 %collective-permute-start.33 = (s16[304,128]{1,0:T(8,128)(2,1)S(1)}, s16[304,128]{1,0:T(8,128)(2,1)S(1)}, u32[]{:S(2)}, u32[]{:S(2)}) collective-permute-start(s16[304,128]{1,0:T(8,128)(2,1)S(1)} %collective-permute-done.29), channel_id=1, source_target_pairs={{0,2},{1,3},{2,0},{3,1},{4,6},{5,7},{6,4},{7,5},{8,10},{9,11},{10,... | collective-permute-start | bytes 233480 | tf_op jit(solution)/shard_map/ppermute | solution.py:24
  84.4 4.6 %collective-permute-start.32 = (s16[304,128]{1,0:T(8,128)(2,1)S(1)}, s16[304,128]{1,0:T(8,128)(2,1)S(1)}, u32[]{:S(2)}, u32[]{:S(2)}) collective-permute-start(s16[304,128]{1,0:T(8,128)(2,1)S(1)} %collective-permute-done.28), channel_id=1, source_target_pairs={{0,2},{1,3},{2,0},{3,1},{4,6},{5,7},{6,4},{7,5},{8,10},{9,11},{10,... | collective-permute-start | bytes 233480 | tf_op jit(solution)/shard_map/ppermute | solution.py:24
  84.8 5.0 %collective-permute-start.31 = (s16[304,128]{1,0:T(8,128)(2,1)S(1)}, s16[304,128]{1,0:T(8,128)(2,1)S(1)}, u32[]{:S(2)}, u32[]{:S(2)}) collective-permute-start(s16[304,128]{1,0:T(8,128)(2,1)S(1)} %collective-permute-done.27), channel_id=1, source_target_pairs={{0,2},{1,3},{2,0},{3,1},{4,6},{5,7},{6,4},{7,5},{8,10},{9,11},{10,... | collective-permute-start | bytes 233480 | tf_op jit(solution)/shard_map/ppermute | solution.py:24
  86.5 3.5 %collective-permute-start.34 = (s16[4,304,128]{2,1,0:T(8,128)(2,1)S(1)}, s16[4,304,128]{2,1,0:T(8,128)(2,1)S(1)}, u32[]{:S(2)}, u32[]{:S(2)}) collective-permute-start(s16[4,304,128]{2,1,0:T(8,128)(2,1)S(1)} %pad_add_fusion.a), channel_id=1, source_target_pairs={{0,1},{1,0},{2,3},{3,2},{4,5},{5,4},{6,7},{7,6},{8,9},{9,8},{10,11... | collective-permute-start | bytes 933896 | tf_op jit(solution)/shard_map/ppermute | solution.py:24
  89.9 1.9 %collective-permute-start.35 = (s16[4,304,128]{2,1,0:T(8,128)(2,1)S(1)}, s16[4,304,128]{2,1,0:T(8,128)(2,1)S(1)}, u32[]{:S(2)}, u32[]{:S(2)}) collective-permute-start(s16[4,304,128]{2,1,0:T(8,128)(2,1)S(1)} %pad_add_fusion.1.b), channel_id=1, source_target_pairs={{0,1},{1,0},{2,3},{3,2},{4,5},{5,4},{6,7},{7,6},{8,9},{9,8},{10,11... | collective-permute-start | bytes 933896 | tf_op jit(solution)/shard_map/ppermute | solution.py:24

commit v10 on v9

--- a/solution.py
+++ b/solution.py
@@ -282,14 +282,19 @@
     share(packed, core, keep, send)
 
 
+def powers(exponent):
+    first = jnp.clip(exponent, -100.0, 100.0)
+    return jnp.exp2(first), jnp.exp2(exponent - first)
+
+
 def encode(x, out, row):
     rows = x.shape[0]
     groups = x.reshape(rows // GROUP, GROUP, LANES)
     largest = jnp.max(jnp.abs(groups), axis=1)
-    power = jnp.floor(jnp.log2(jnp.maximum(largest, 1e-30))) + 1.0
-    unit = jnp.exp2(BITS - power)
+    power = jnp.floor(jnp.log2(jnp.maximum(largest, 1e-37))) + 1.0
+    a, b = powers(BITS - power)
     for g in range(rows // GROUP):
-        whole = jnp.round(groups[g] * unit[g:g + 1, :]).astype(I32)
+        whole = jnp.round(groups[g] * a[g:g + 1, :] * b[g:g + 1, :]).astype(I32)
         out[pl.ds(row + g * GROUP, GROUP), :] = whole.astype(I16)
     pad = jnp.zeros((PAD - rows // GROUP, LANES), F32)
     out[pl.ds(row + rows, PAD), :] = jnp.concatenate([power, pad]).astype(I32).astype(I16)
@@ -298,9 +303,9 @@
 def decode(coded):
     rows = coded.shape[0] - PAD
     wide = coded.astype(I32).astype(F32)
-    unit = jnp.exp2(wide[rows:] - BITS)
+    a, b = powers(wide[rows:] - BITS)
     return jnp.concatenate(
-        [wide[g * GROUP:(g + 1) * GROUP] * unit[g:g + 1, :] for g in range(rows // GROUP)]
+        [wide[g * GROUP:(g + 1) * GROUP] * a[g:g + 1, :] * b[g:g + 1, :] for g in range(rows // GROUP)]
     )
 
 

time: 93.9 us -> 94.2 us (level)
  transfers between devices with their start and end apart: 36 -> 36, of which waited for: 15 -> 15; matrix products, arithmetic and copies ran while one was open for 0% -> 0% of each run, Pallas kernels for 23% -> 24%
where the time goes in v10:
time: 94.2 us; the launch traced here: 93.9 us
  starting transfers between devices  41.9 us (44%)
  Pallas kernels  28.1 us (30%)
  waiting for transfers between devices  17.8 us (19%)
  local copies, waits for them, and re-layouts  4.53 us (5%)
  between operations  1.25 us (1%)
    ppermute x36, starting transfers between devices, move(): return lax.ppermute(x, 'dom', pairs)  41.9 us
    ppermute x36, waiting for transfers between devices, move(): return lax.ppermute(x, 'dom', pairs)  17.8 us
    pallas_call x4, Pallas kernels, pair_step(): kernel(functools.partial(body, plan, names, step), name, [smem] + [vmem]...  11.2 us
    unnamed x12, local copies, waits for them, and re-layouts  3.48 us
    pallas_call x1, Pallas kernels, shards(): kernel(own_kernel, 'own', [hbm, vmem, vmem], (jax.ShapeDtypeStruct((wide,...  3.01 us
    pallas_call x1, Pallas kernels, shards(): kernel(sib_kernel, 'sib', [vmem, vmem, hbm, vmem, vmem], total_t, vmem, [...  2.98 us
    pallas_call x1, Pallas kernels, shards(): kernel(near_metric_kernel, 'near_metric', [smem, vmem, vmem], (plain(uppe...  2.76 us
  transfers between devices with their start and end apart: 36, of which 15 were waited for; matrix products, arithmetic and copies ran while one was open for 0% of the time, Pallas kernels for 24%

profile of v10, /device:TPU:0, one launch (start us, length us, event | category | flops | bytes accessed | tf_op | source)
XLA Modules:
  0.0 93.9 jit_solution(16152184297183022211)
XLA Ops:
  0.7 1.0 %slice.12 = bf16[416,384]{1,0:T(8,128)(2,1)S(1)} slice(bf16[2048,384]{1,0:T(8,128)(2,1)} %bitcast.13), slice={[0:416], [0:384]} | slice | bytes 638976 | tf_op jit(solution)/shard_map/slice | solution.py:468
  1.7 0.5 collective-permute-start.1
  2.2 2.6 %collective-permute-start = (bf16[416,384]{1,0:T(8,128)(2,1)S(1)}, bf16[416,384]{1,0:T(8,128)(2,1)S(1)}, u32[]{:S(2)}, u32[]{:S(2)}) collective-permute-start(bf16[416,384]{1,0:T(8,128)(2,1)S(1)} %slice.12), channel_id=1, source_target_pairs={{0,2},{1,3},{2,0},{3,1},{4,6},{5,7},{6,4},{7,5},{8,10},{9,11},{10,... | collective-permute-start | bytes 958472 | tf_op jit(solution)/shard_map/ppermute | solution.py:24
  4.8 0.2 collective-permute-start.2
  5.0 1.4 %copy-done = bf16[1,2,1024,384]{3,2,1,0:T(8,128)(2,1)S(1)} copy-done((bf16[1,2,1024,384]{3,2,1,0:T(8,128)(2,1)S(1)}, bf16[1,2,1024,384]{3,2,1,0:T(8,128)(2,1)}, u32[]{:S(2)}) %copy-start) | copy-done | bytes 1572888
  6.4 0.7 copy-done.4
  7.0 0.9 split.1
  8.0 1.3 %prep.1 = (f32[8,768]{1,0:T(8,128)S(1)}, f32[8,768]{1,0:T(8,128)S(1)}) custom-call(s32[1]{0:T(128)} %bitcast.me_ref.a_0_, s32[1,3]{1,0:T(1,128)S(1)} %copy-done.4, s32[1,3]{1,0:T(1,128)S(1)} %collective-permute-done.2.sib_pairs, f32[2,16]{1,0:T(2,128)S(1)} %bitcast.19, f32[64,128]{1,0:T(8,128)S(1)} %bitcast.18, s32[16,384]{1,0:T(8,128)S(1)} %copy-done.3), custom_call_target="tpu_custom_call" | custom-call | flops 1 | bytes 1 | tf_op jit(solution)/shard_map/prep/pallas_call | solution.py:482
  9.3 0.4 collective-permute-start.4
  9.7 1.4 %copy-done.1 = bf16[1,2,1024,384]{3,2,1,0:T(8,128)(2,1)S(1)} copy-done((bf16[1,2,1024,384]{3,2,1,0:T(8,128)(2,1)S(1)}, bf16[1,2,1024,384]{3,2,1,0:T(8,128)(2,1)}, u32[]{:S(2)}) %copy-start.1) | copy-done | bytes 1572888
  11.1 3.0 %own.1 = (bf16[768,1024]{1,0:T(8,128)(2,1)S(1)}, bf16[1024,768]{1,0:T(8,128)(2,1)S(1)}, f32[1024,768]{1,0:T(8,128)S(1)}) custom-call(bf16[2048,384]{1,0:T(8,128)(2,1)S(1)} %bitcast.16, f32[8,768]{1,0:T(8,128)S(1)} %get-tuple-element.78.levels.a_2_, f32[8,768]{1,0:T(8,128)S(1)} %get-tuple-element.79.weights.a_3_), custom_call_target="tpu_custom_call" | custom-call | flops 20000000000 | bytes 1 | tf_op jit(solution)/shard_map/own/pallas_call | solution.py:487
  14.1 3.7 %collective-permute-start.9 = (bf16[416,384]{1,0:T(8,128)(2,1)S(1)}, bf16[416,384]{1,0:T(8,128)(2,1)S(1)}, u32[]{:S(2)}, u32[]{:S(2)}) collective-permute-start(bf16[416,384]{1,0:T(8,128)(2,1)S(1)} %collective-permute-done.rest_0_), channel_id=1, source_target_pairs={{0,4},{1,5},{4,8},{5,9},{6,2},{7,3},{8,12},{9,13},{10,6},{11,7},{1... | collective-permute-start | bytes 958472 | tf_op jit(solution)/shard_map/ppermute | solution.py:24
  17.9 3.0 %sib.1.total.near = f32[1024,768]{1,0:T(8,128)S(1)} custom-call(bf16[768,1024]{1,0:T(8,128)(2,1)S(1)} %get-tuple-element.114.own_t.a_1_, f32[1024,768]{1,0:T(8,128)S(1)} %get-tuple-element.90.total_in, bf16[2048,384]{1,0:T(8,128)(2,1)S(1)} %collective-permute-done.1.sib, f32[8,768]{1,0:T(8,128)S(1)} %get-tuple-element.78.levels.a_2_, ...), custom_call_target="tpu_custom_call", output_to_operand_aliasing={{}: (1, {})} | custom-call | flops 10000000000 | bytes 1 | tf_op jit(solution)/shard_map/sib/pallas_call | solution.py:497
  20.9 3.9 %collective-permute-start.12 = (bf16[384,384]{1,0:T(8,128)(2,1)S(1)}, bf16[384,384]{1,0:T(8,128)(2,1)S(1)}, u32[]{:S(2)}, u32[]{:S(2)}) collective-permute-start(bf16[384,384]{1,0:T(8,128)(2,1)S(1)} %collective-permute-done.4.rest_1_), channel_id=1, source_target_pairs={{0,4},{1,5},{4,8},{5,9},{6,2},{7,3},{8,12},{9,13},{10,6},{11,7},{1... | collective-permute-start | bytes 884744 | tf_op jit(solution)/shard_map/ppermute | solution.py:24
  24.8 3.2 %collective-permute-done.3.rest_2_ = bf16[432,384]{1,0:T(8,128)(2,1)S(1)} collective-permute-done((bf16[432,384]{1,0:T(8,128)(2,1)S(1)}, bf16[432,384]{1,0:T(8,128)(2,1)S(1)}, u32[]{:S(2)}, u32[]{:S(2)}) %collective-permute-start.3) | collective-permute-done | bytes 331808 | tf_op jit(solution)/shard_map/ppermute | solution.py:24
  28.0 3.5 %collective-permute-start.13 = (bf16[432,384]{1,0:T(8,128)(2,1)S(1)}, bf16[432,384]{1,0:T(8,128)(2,1)S(1)}, u32[]{:S(2)}, u32[]{:S(2)}) collective-permute-start(bf16[432,384]{1,0:T(8,128)(2,1)S(1)} %collective-permute-done.3.rest_2_), channel_id=1, source_target_pairs={{0,4},{1,5},{4,8},{5,9},{6,2},{7,3},{8,12},{9,13},{10,6},{11,7},{1... | collective-permute-start | bytes 995336 | tf_op jit(solution)/shard_map/ppermute | solution.py:24
  31.5 0.1 collective-permute-start.5
  31.6 2.8 %near_metric.1 = (f32[1152,128]{1,0:T(8,128)S(1)}, f32[1152,128]{1,0:T(8,128)S(1)}, s16[1216,128]{1,0:T(8,128)(2,1)S(1)}, s16[1216,128]{1,0:T(8,128)(2,1)S(1)}) custom-call(s32[1]{0:T(128)} %bitcast.me_ref.a_0_, f32[1024,768]{1,0:T(8,128)S(1)} %sib.1.total.near, bf16[1024,768]{1,0:T(8,128)(2,1)S(1)} %get-tuple-element.98.own_s), custom_call_target="tpu_custom_call" | custom-call | flops 10000000000 | bytes 1 | tf_op jit(solution)/shard_map/near_metric/pallas_call | solution.py:509
  34.4 0.9 collective-permute-done.8.rest_3_
  35.3 3.5 %collective-permute-start.10 = (bf16[416,384]{1,0:T(8,128)(2,1)S(1)}, bf16[416,384]{1,0:T(8,128)(2,1)S(1)}, u32[]{:S(2)}, u32[]{:S(2)}) collective-permute-start(bf16[416,384]{1,0:T(8,128)(2,1)S(1)} %collective-permute-done.8.rest_3_), channel_id=1, source_target_pairs={{0,4},{1,5},{4,8},{5,9},{6,2},{7,3},{8,12},{9,13},{10,6},{11,7},{1... | collective-permute-start | bytes 958472 | tf_op jit(solution)/shard_map/ppermute | solution.py:24
  38.8 0.1 collective-permute-start.6
  38.8 0.5 collective-permute-start.7
  39.3 0.2 collective-permute-done.13.rest_2_.a_5_
  39.6 0.2 maximum_select_fusion
  39.9 0.5 collective-permute-done.6.got_away
  40.4 0.4 collective-permute-done.7.got_keep
  40.9 0.2 collective-permute-done.5.rest_4_
  41.0 3.7 %collective-permute-start.11 = (bf16[416,384]{1,0:T(8,128)(2,1)S(1)}, bf16[416,384]{1,0:T(8,128)(2,1)S(1)}, u32[]{:S(2)}, u32[]{:S(2)}) collective-permute-start(bf16[416,384]{1,0:T(8,128)(2,1)S(1)} %collective-permute-done.5.rest_4_), channel_id=1, source_target_pairs={{0,4},{1,5},{4,8},{5,9},{6,2},{7,3},{8,12},{9,13},{10,6},{11,7},{1... | collective-permute-start | bytes 958472 | tf_op jit(solution)/shard_map/ppermute | solution.py:24
  44.7 0.4 chip.1
  45.1 0.1 collective-permute-start.17
  45.2 2.7 %far2.1.total_in = f32[1024,768]{1,0:T(8,128)S(1)} custom-call(s32[1]{0:T(128)} %bitcast.me_ref.a_0_, bf16[768,1024]{1,0:T(8,128)(2,1)S(1)} %get-tuple-element.114.own_t.a_1_, f32[8,768]{1,0:T(8,128)S(1)} %get-tuple-element.78.levels.a_2_, f32[8,768]{1,0:T(8,128)S(1)} %get-tuple-element.79.weights.a_3_, bf16[416,384]{1,0:T(8,128)(2,1)S(1)} %collective-permute-done.rest_0_, ...), custom_call_target="tpu_custom_call" | custom-call | flops 10000000000 | bytes 1 | tf_op jit(solution)/shard_map/far2/pallas_call | solution.py:555
  47.9 2.7 %far3.1.a_4_ = f32[1024,768]{1,0:T(8,128)S(1)} custom-call(s32[1]{0:T(128)} %bitcast.me_ref.a_0_, bf16[768,1024]{1,0:T(8,128)(2,1)S(1)} %get-tuple-element.114.own_t.a_1_, f32[8,768]{1,0:T(8,128)S(1)} %get-tuple-element.78.levels.a_2_, f32[8,768]{1,0:T(8,128)S(1)} %get-tuple-element.79.weights.a_3_, ...), custom_call_target="tpu_custom_call", output_to_operand_aliasing={{}: (4, {})} | custom-call | flops 1 | bytes 1 | tf_op jit(solution)/shard_map/far3/pallas_call | solution.py:555
  50.8 0.5 collective-permute-start.15
  51.3 3.2 %collective-permute-done.17.across = s16[1216,128]{1,0:T(8,128)(2,1)S(1)} collective-permute-done((s16[1216,128]{1,0:T(8,128)(2,1)S(1)}, s16[1216,128]{1,0:T(8,128)(2,1)S(1)}, u32[]{:S(2)}, u32[]{:S(2)}) %collective-permute-start.17) | collective-permute-done | bytes 311328 | tf_op jit(solution)/shard_map/ppermute | solution.py:24
  54.6 1.9 %half.1.total_in = f32[1024,768]{1,0:T(8,128)S(1)} custom-call(s32[1]{0:T(128)} %bitcast.me_ref.a_0_, bf16[768,1024]{1,0:T(8,128)(2,1)S(1)} %get-tuple-element.114.own_t.a_1_, f32[8,768]{1,0:T(8,128)S(1)} %get-tuple-element.78.levels.a_2_, f32[8,768]{1,0:T(8,128)S(1)} %get-tuple-element.79.weights.a_3_, ...), custom_call_target="tpu_custom_call", output_to_operand_aliasing={{}: (4, {})} | custom-call | flops 1000000000 | bytes 1 | tf_op jit(solution)/shard_map/half/pallas_call | solution.py:555
  56.5 4.0 %last.1 = (f32[1024,768]{1,0:T(8,128)S(1)}, f32[2,1024,384]{2,1,0:T(8,128)}, f32[640,128]{1,0:T(8,128)S(1)}, f32[640,128]{1,0:T(8,128)S(1)}, bf16[1024,768]{1,0:...) custom-call(s32[1]{0:T(128)} %bitcast.me_ref.a_0_, ...), custom_call_target="tpu_custom_call", output_to_operand_aliasing={{0}: (4, {})} | custom-call | flops 1 | bytes 1 | tf_op jit(solution)/shard_map/last/pallas_call | solution.py:555
  60.5 0.6 collective-permute-start.19
  61.1 1.1 %corner.1 = (f32[512,128]{1,0:T(8,128)S(1)}, f32[512,128]{1,0:T(8,128)S(1)}) custom-call(s32[1]{0:T(128)} %bitcast.me_ref.a_0_, bf16[1024,768]{1,0:T(8,128)(2,1)S(1)} %get-tuple-element.131.high, bf16[1024,768]{1,0:T(8,128)(2,1)S(1)} %get-tuple-element.132.low, bf16[1024,768]{1,0:T(8,128)(2,1)S(1)} %get-tuple-element.98.own_s), custom_call_target="tpu_custom_call" | custom-call | flops 2000000000 | bytes 1 | tf_op jit(solution)/shard_map/corner/pallas_call | solution.py:593
  62.2 0.2 collective-permute-done.19.theirs
  62.3 0.4 collective-permute-start.23
  62.7 0.3 column.2
  63.0 2.7 %collective-permute-start.20 = (s16[176,128]{1,0:T(8,128)(2,1)S(1)}, s16[176,128]{1,0:T(8,128)(2,1)S(1)}, u32[]{:S(2)}, u32[]{:S(2)}) collective-permute-start(s16[176,128]{1,0:T(8,128)(2,1)S(1)} %get-tuple-element.138), channel_id=1, source_target_pairs={{0,12},{1,13},{2,14},{3,15},{4,8},{5,9},{6,10},{7,11},{8,4},{9,5},... | collective-permute-start | bytes 135176 | tf_op jit(solution)/shard_map/ppermute | solution.py:24
  65.6 0.4 collective-permute-start.21
  66.1 1.4 %collective-permute-start.22 = (s16[176,128]{1,0:T(8,128)(2,1)S(1)}, s16[176,128]{1,0:T(8,128)(2,1)S(1)}, u32[]{:S(2)}, u32[]{:S(2)}) collective-permute-start(s16[176,128]{1,0:T(8,128)(2,1)S(1)} %get-tuple-element.140), channel_id=1, source_target_pairs={{0,4},{1,5},{2,6},{3,7},{4,0},{5,1},{6,2},{7,3},{8,12},{9,13},{10,... | collective-permute-start | bytes 135176 | tf_op jit(solution)/shard_map/ppermute | solution.py:24
  67.4 0.5 column.3
  67.9 2.7 %collective-permute-start.24 = (s16[144,128]{1,0:T(8,128)(2,1)S(1)}, s16[144,128]{1,0:T(8,128)(2,1)S(1)}, u32[]{:S(2)}, u32[]{:S(2)}) collective-permute-start(s16[144,128]{1,0:T(8,128)(2,1)S(1)} %get-tuple-element.144), channel_id=1, source_target_pairs={{0,12},{1,13},{2,14},{3,15},{4,8},{5,9},{6,10},{7,11},{8,4},{9,5},... | collective-permute-start | bytes 110600 | tf_op jit(solution)/shard_map/ppermute | solution.py:24
  70.6 1.8 %collective-permute-start.26 = (s16[144,128]{1,0:T(8,128)(2,1)S(1)}, s16[144,128]{1,0:T(8,128)(2,1)S(1)}, u32[]{:S(2)}, u32[]{:S(2)}) collective-permute-start(s16[144,128]{1,0:T(8,128)(2,1)S(1)} %get-tuple-element.146), channel_id=1, source_target_pairs={{0,4},{1,5},{2,6},{3,7},{4,0},{5,1},{6,2},{7,3},{8,12},{9,13},{10,... | collective-permute-start | bytes 110600 | tf_op jit(solution)/shard_map/ppermute | solution.py:24
  72.4 1.5 %collective-permute-done.24.rest_5_ = s16[144,128]{1,0:T(8,128)(2,1)S(1)} collective-permute-done((s16[144,128]{1,0:T(8,128)(2,1)S(1)}, s16[144,128]{1,0:T(8,128)(2,1)S(1)}, u32[]{:S(2)}, u32[]{:S(2)}) %collective-permute-start.24) | collective-permute-done | bytes 36896 | tf_op jit(solution)/shard_map/ppermute | solution.py:24
  73.8 1.6 %collective-permute-done.25.rest_6_ = s16[144,128]{1,0:T(8,128)(2,1)S(1)} collective-permute-done((s16[144,128]{1,0:T(8,128)(2,1)S(1)}, s16[144,128]{1,0:T(8,128)(2,1)S(1)}, u32[]{:S(2)}, u32[]{:S(2)}) %collective-permute-start.25) | collective-permute-done | bytes 36896 | tf_op jit(solution)/shard_map/ppermute | solution.py:24
  75.4 0.2 sum_code.1
  75.6 1.9 %collective-permute-start.29 = (s16[304,128]{1,0:T(8,128)(2,1)S(1)}, s16[304,128]{1,0:T(8,128)(2,1)S(1)}, u32[]{:S(2)}, u32[]{:S(2)}) collective-permute-start(s16[304,128]{1,0:T(8,128)(2,1)S(1)} %sum_code.1), channel_id=1, source_target_pairs={{0,12},{1,13},{2,14},{3,15},{4,8},{5,9},{6,10},{7,11},{8,4},{9,5},... | collective-permute-start | bytes 233480 | tf_op jit(solution)/shard_map/ppermute | solution.py:24
  77.5 0.5 collective-permute-start.28
  78.0 2.0 %collective-permute-start.27 = (s16[304,128]{1,0:T(8,128)(2,1)S(1)}, s16[304,128]{1,0:T(8,128)(2,1)S(1)}, u32[]{:S(2)}, u32[]{:S(2)}) collective-permute-start(s16[304,128]{1,0:T(8,128)(2,1)S(1)} %sum_code.1), channel_id=1, source_target_pairs={{0,4},{1,5},{2,6},{3,7},{4,0},{5,1},{6,2},{7,3},{8,12},{9,13},{10,... | collective-permute-start | bytes 233480 | tf_op jit(solution)/shard_map/ppermute | solution.py:24
  80.0 1.2 %collective-permute-start.30 = (s16[304,128]{1,0:T(8,128)(2,1)S(1)}, s16[304,128]{1,0:T(8,128)(2,1)S(1)}, u32[]{:S(2)}, u32[]{:S(2)}) collective-permute-start(s16[304,128]{1,0:T(8,128)(2,1)S(1)} %sum_code.1), channel_id=1, source_target_pairs={{0,2},{1,3},{2,0},{3,1},{4,6},{5,7},{6,4},{7,5},{8,10},{9,11},{10,... | collective-permute-start | bytes 233480 | tf_op jit(solution)/shard_map/ppermute | solution.py:24
  81.2 1.1 %collective-permute-done.29 = s16[304,128]{1,0:T(8,128)(2,1)S(1)} collective-permute-done((s16[304,128]{1,0:T(8,128)(2,1)S(1)}, s16[304,128]{1,0:T(8,128)(2,1)S(1)}, u32[]{:S(2)}, u32[]{:S(2)}) %collective-permute-start.29) | collective-permute-done | bytes 77856 | tf_op jit(solution)/shard_map/ppermute | solution.py:24
  82.4 0.8 collective-permute-start.33
  83.2 1.4 %collective-permute-done.28 = s16[304,128]{1,0:T(8,128)(2,1)S(1)} collective-permute-done((s16[304,128]{1,0:T(8,128)(2,1)S(1)}, s16[304,128]{1,0:T(8,128)(2,1)S(1)}, u32[]{:S(2)}, u32[]{:S(2)}) %collective-permute-start.28) | collective-permute-done | bytes 77856 | tf_op jit(solution)/shard_map/ppermute | solution.py:24
  84.6 0.4 collective-permute-start.32
  85.0 1.6 %collective-permute-start.31 = (s16[304,128]{1,0:T(8,128)(2,1)S(1)}, s16[304,128]{1,0:T(8,128)(2,1)S(1)}, u32[]{:S(2)}, u32[]{:S(2)}) collective-permute-start(s16[304,128]{1,0:T(8,128)(2,1)S(1)} %collective-permute-done.27), channel_id=1, source_target_pairs={{0,2},{1,3},{2,0},{3,1},{4,6},{5,7},{6,4},{7,5},{8,10},{9,11},{10,... | collective-permute-start | bytes 233480 | tf_op jit(solution)/shard_map/ppermute | solution.py:24
  86.7 0.9 collective-permute-done.33
  87.6 1.6 %collective-permute-done.32 = s16[304,128]{1,0:T(8,128)(2,1)S(1)} collective-permute-done((s16[304,128]{1,0:T(8,128)(2,1)S(1)}, s16[304,128]{1,0:T(8,128)(2,1)S(1)}, u32[]{:S(2)}, u32[]{:S(2)}) %collective-permute-start.32) | collective-permute-done | bytes 77856 | tf_op jit(solution)/shard_map/ppermute | solution.py:24
  89.2 0.8 collective-permute-done.31
  90.1 1.9 %unpack.1 = (f32[1024,1024]{1,0:T(8,128)}, f32[4608,128]{1,0:T(8,128)S(1)}) custom-call(s32[1]{0:T(128)} %bitcast.me_ref.a_0_, s16[4,304,128]{2,1,0:T(8,128)(2,1)S(1)} %pad_add_fusion.a, s16[4,304,128]{2,1,0:T(8,128)(2,1)S(1)} %pad_add_fusion.1.b, s16[4,304,128]{2,1,0:T(8,128)(2,1)S(1)} %collective-permute-done.34.sib_a), custom_call_target="tpu_custom_call" | custom-call | flops 1000000000 | bytes 1 | tf_op jit(solution)/shard_map/unpack/pallas_call | solution.py:621
  92.0 1.7 %spread.1 = (f32[1024,1024]{1,0:T(8,128)}, f32[4608,128]{1,0:T(8,128)S(1)}) custom-call(s32[1]{0:T(128)} %bitcast.me_ref.a_0_, f32[1024,1024]{1,0:T(8,128)} %get-tuple-element.147.out_in, f32[4608,128]{1,0:T(8,128)S(1)} %get-tuple-element.148.packed_in, ...), custom_call_target="tpu_custom_call", output_to_operand_aliasing={{0}: (1, {}), {1}: (2, {})} | custom-call | flops 1 | bytes 1 | tf_op jit(solution)/shard_map/spread/pallas_call | solution.py:624
  (43 shorter events, 0.8 us)
Async XLA Ops:
  0.6 7.3 %copy-start.3 = (s32[16,384]{1,0:T(8,128)S(1)}, s32[16,384]{1,0:T(8,128)}, u32[]{:S(2)}) copy-start(s32[16,384]{1,0:T(8,128)} %maps_in.1) | copy-start | bytes 73732
  0.6 7.3 %copy-start.2 = (f32[8192]{0:T(1024)S(1)}, f32[8192]{0:T(1024)}, u32[]{:S(2)}) copy-start(f32[8192]{0:T(1024)} %param.8) | copy-start | bytes 98308
  0.7 7.3 %copy-start.5 = (f32[16,2]{0,1:T(2,128)S(1)}, f32[16,2]{0,1:T(2,128)}, u32[]{:S(2)}) copy-start(f32[16,2]{0,1:T(2,128)} %param.7) | copy-start | bytes 388
  1.7 7.6 %collective-permute-start.1 = (bf16[2048,384]{1,0:T(8,128)(2,1)}, bf16[2048,384]{1,0:T(8,128)(2,1)S(1)}, u32[]{:S(2)}, u32[]{:S(2)}) collective-permute-start(bf16[2048,384]{1,0:T(8,128)(2,1)} %bitcast.14), channel_id=1, source_target_pairs={{0,1},{1,0},{2,3},{3,2},{4,5},{5,4},{6,7},{7,6},{8,9},{9,8},{10,11... | collective-permute-start | bytes 4718600 | tf_op jit(solution)/shard_map/ppermute | solution.py:24
  2.2 11.9 %collective-permute-start = (bf16[416,384]{1,0:T(8,128)(2,1)S(1)}, bf16[416,384]{1,0:T(8,128)(2,1)S(1)}, u32[]{:S(2)}, u32[]{:S(2)}) collective-permute-start(bf16[416,384]{1,0:T(8,128)(2,1)S(1)} %slice.12), channel_id=1, source_target_pairs={{0,2},{1,3},{2,0},{3,1},{4,6},{5,7},{6,4},{7,5},{8,10},{9,11},{10,... | collective-permute-start | bytes 958472 | tf_op jit(solution)/shard_map/ppermute | solution.py:24
  4.8 3.2 %collective-permute-start.2 = (s32[1,3]{1,0:T(1,128)}, s32[1,3]{1,0:T(1,128)S(1)}, u32[]{:S(2)}, u32[]{:S(2)}) collective-permute-start(s32[1,3]{1,0:T(1,128)} %pairs.3), channel_id=1, source_target_pairs={{0,1},{1,0},{2,3},{3,2},{4,5},{5,4},{6,7},{7,6},{8,9},{9,8},{10,11... | collective-permute-start | bytes 44 | tf_op jit(solution)/shard_map/ppermute | solution.py:24
  5.0 1.4 %copy-start = (bf16[1,2,1024,384]{3,2,1,0:T(8,128)(2,1)S(1)}, bf16[1,2,1024,384]{3,2,1,0:T(8,128)(2,1)}, u32[]{:S(2)}) copy-start(bf16[1,2,1024,384]{3,2,1,0:T(8,128)(2,1)} %param.5) | copy-start | bytes 4718596
  6.4 0.7 copy-start.4
  9.3 11.6 %collective-permute-start.4 = (bf16[384,384]{1,0:T(8,128)(2,1)S(1)}, bf16[384,384]{1,0:T(8,128)(2,1)S(1)}, u32[]{:S(2)}, u32[]{:S(2)}) collective-permute-start(bf16[384,384]{1,0:T(8,128)(2,1)S(1)} %get-tuple-element.88), channel_id=1, source_target_pairs={{0,2},{1,3},{2,0},{3,1},{4,6},{5,7},{6,4},{7,5},{8,10},{9,11},{10,... | collective-permute-start | bytes 884744 | tf_op jit(solution)/shard_map/ppermute | solution.py:24
  9.7 1.4 %copy-start.1 = (bf16[1,2,1024,384]{3,2,1,0:T(8,128)(2,1)S(1)}, bf16[1,2,1024,384]{3,2,1,0:T(8,128)(2,1)}, u32[]{:S(2)}) copy-start(bf16[1,2,1024,384]{3,2,1,0:T(8,128)(2,1)} %param.5) | copy-start | bytes 4718596
  14.1 20.2 %collective-permute-start.9 = (bf16[416,384]{1,0:T(8,128)(2,1)S(1)}, bf16[416,384]{1,0:T(8,128)(2,1)S(1)}, u32[]{:S(2)}, u32[]{:S(2)}) collective-permute-start(bf16[416,384]{1,0:T(8,128)(2,1)S(1)} %collective-permute-done.rest_0_), channel_id=1, source_target_pairs={{0,4},{1,5},{4,8},{5,9},{6,2},{7,3},{8,12},{9,13},{10,6},{11,7},{1... | collective-permute-start | bytes 958472 | tf_op jit(solution)/shard_map/ppermute | solution.py:24
  17.8 10.2 %collective-permute-start.3 = (bf16[432,384]{1,0:T(8,128)(2,1)S(1)}, bf16[432,384]{1,0:T(8,128)(2,1)S(1)}, u32[]{:S(2)}, u32[]{:S(2)}) collective-permute-start(bf16[432,384]{1,0:T(8,128)(2,1)S(1)} %get-tuple-element.86), channel_id=1, source_target_pairs={{0,2},{1,3},{2,0},{3,1},{4,6},{5,7},{6,4},{7,5},{8,10},{9,11},{10,... | collective-permute-start | bytes 995336 | tf_op jit(solution)/shard_map/ppermute | solution.py:24
  20.9 18.0 %collective-permute-start.12 = (bf16[384,384]{1,0:T(8,128)(2,1)S(1)}, bf16[384,384]{1,0:T(8,128)(2,1)S(1)}, u32[]{:S(2)}, u32[]{:S(2)}) collective-permute-start(bf16[384,384]{1,0:T(8,128)(2,1)S(1)} %collective-permute-done.4.rest_1_), channel_id=1, source_target_pairs={{0,4},{1,5},{4,8},{5,9},{6,2},{7,3},{8,12},{9,13},{10,6},{11,7},{1... | collective-permute-start | bytes 884744 | tf_op jit(solution)/shard_map/ppermute | solution.py:24
  24.7 10.5 %collective-permute-start.8 = (bf16[416,384]{1,0:T(8,128)(2,1)S(1)}, bf16[416,384]{1,0:T(8,128)(2,1)S(1)}, u32[]{:S(2)}, u32[]{:S(2)}) collective-permute-start(bf16[416,384]{1,0:T(8,128)(2,1)S(1)} %get-tuple-element.102), channel_id=1, source_target_pairs={{0,2},{1,3},{2,0},{3,1},{4,6},{5,7},{6,4},{7,5},{8,10},{9,11},{10,... | collective-permute-start | bytes 958472 | tf_op jit(solution)/shard_map/ppermute | solution.py:24
  28.0 11.6 %collective-permute-start.13 = (bf16[432,384]{1,0:T(8,128)(2,1)S(1)}, bf16[432,384]{1,0:T(8,128)(2,1)S(1)}, u32[]{:S(2)}, u32[]{:S(2)}) collective-permute-start(bf16[432,384]{1,0:T(8,128)(2,1)S(1)} %collective-permute-done.3.rest_2_), channel_id=1, source_target_pairs={{0,4},{1,5},{4,8},{5,9},{6,2},{7,3},{8,12},{9,13},{10,6},{11,7},{1... | collective-permute-start | bytes 995336 | tf_op jit(solution)/shard_map/ppermute | solution.py:24
  31.5 9.5 %collective-permute-start.5 = (bf16[416,384]{1,0:T(8,128)(2,1)S(1)}, bf16[416,384]{1,0:T(8,128)(2,1)S(1)}, u32[]{:S(2)}, u32[]{:S(2)}) collective-permute-start(bf16[416,384]{1,0:T(8,128)(2,1)S(1)} %get-tuple-element.94), channel_id=1, source_target_pairs={{0,2},{1,3},{2,0},{3,1},{4,6},{5,7},{6,4},{7,5},{8,10},{9,11},{10,... | collective-permute-start | bytes 958472 | tf_op jit(solution)/shard_map/ppermute | solution.py:24
  35.3 9.9 %collective-permute-start.10 = (bf16[416,384]{1,0:T(8,128)(2,1)S(1)}, bf16[416,384]{1,0:T(8,128)(2,1)S(1)}, u32[]{:S(2)}, u32[]{:S(2)}) collective-permute-start(bf16[416,384]{1,0:T(8,128)(2,1)S(1)} %collective-permute-done.8.rest_3_), channel_id=1, source_target_pairs={{0,4},{1,5},{4,8},{5,9},{6,2},{7,3},{8,12},{9,13},{10,6},{11,7},{1... | collective-permute-start | bytes 958472 | tf_op jit(solution)/shard_map/ppermute | solution.py:24
  38.8 1.7 %collective-permute-start.6 = (s16[1216,128]{1,0:T(8,128)(2,1)S(1)}, s16[1216,128]{1,0:T(8,128)(2,1)S(1)}, u32[]{:S(2)}, u32[]{:S(2)}) collective-permute-start(s16[1216,128]{1,0:T(8,128)(2,1)S(1)} %get-tuple-element.99), channel_id=1, source_target_pairs={{0,1},{1,0},{2,3},{3,2},{4,5},{5,4},{6,7},{7,6},{8,9},{9,8},{10,11... | collective-permute-start | bytes 933896 | tf_op jit(solution)/shard_map/ppermute | solution.py:24
  38.8 2.0 %collective-permute-start.7 = (s16[1216,128]{1,0:T(8,128)(2,1)S(1)}, s16[1216,128]{1,0:T(8,128)(2,1)S(1)}, u32[]{:S(2)}, u32[]{:S(2)}) collective-permute-start(s16[1216,128]{1,0:T(8,128)(2,1)S(1)} %get-tuple-element.100), channel_id=1, source_target_pairs={{0,1},{1,0},{2,3},{3,2},{4,5},{5,4},{6,7},{7,6},{8,9},{9,8},{10,11... | collective-permute-start | bytes 933896 | tf_op jit(solution)/shard_map/ppermute | solution.py:24
  39.8 8.1 %collective-permute-start.14 = (bf16[1232,384]{1,0:T(8,128)(2,1)S(1)}, bf16[1232,384]{1,0:T(8,128)(2,1)S(1)}, u32[]{:S(2)}, u32[]{:S(2)}) collective-permute-start(bf16[1232,384]{1,0:T(8,128)(2,1)S(1)} %maximum_select_fusion), channel_id=1, source_target_pairs={{0,1},{1,0},{2,3},{3,2},{4,5},{5,4},{6,7},{7,6},{8,9},{9,8},{10,11... | collective-permute-start | bytes 2838536 | tf_op jit(solution)/shard_map/ppermute | solution.py:24
  41.0 13.4 %collective-permute-start.11 = (bf16[416,384]{1,0:T(8,128)(2,1)S(1)}, bf16[416,384]{1,0:T(8,128)(2,1)S(1)}, u32[]{:S(2)}, u32[]{:S(2)}) collective-permute-start(bf16[416,384]{1,0:T(8,128)(2,1)S(1)} %collective-permute-done.5.rest_4_), channel_id=1, source_target_pairs={{0,4},{1,5},{4,8},{5,9},{6,2},{7,3},{8,12},{9,13},{10,6},{11,7},{1... | collective-permute-start | bytes 958472 | tf_op jit(solution)/shard_map/ppermute | solution.py:24
  45.1 9.3 %collective-permute-start.17 = (s16[1216,128]{1,0:T(8,128)(2,1)S(1)}, s16[1216,128]{1,0:T(8,128)(2,1)S(1)}, u32[]{:S(2)}, u32[]{:S(2)}) collective-permute-start(s16[1216,128]{1,0:T(8,128)(2,1)S(1)} %get-tuple-element.123), channel_id=1, source_target_pairs={{0,2},{1,3},{2,0},{3,1},{4,6},{5,7},{6,4},{7,5},{8,10},{9,11},{10,... | collective-permute-start | bytes 933896 | tf_op jit(solution)/shard_map/ppermute | solution.py:24
  50.7 3.8 %collective-permute-start.16 = (bf16[208,384]{1,0:T(8,128)(2,1)S(1)}, bf16[208,384]{1,0:T(8,128)(2,1)S(1)}, u32[]{:S(2)}, u32[]{:S(2)}) collective-permute-start(bf16[208,384]{1,0:T(8,128)(2,1)S(1)} %get-tuple-element.150), channel_id=1, source_target_pairs={{0,1},{1,0},{2,3},{3,2},{4,5},{5,4},{6,7},{7,6},{8,9},{9,8},{10,11... | collective-permute-start | bytes 479240 | tf_op jit(solution)/shard_map/ppermute | solution.py:24
  50.8 3.7 %collective-permute-start.15 = (bf16[208,384]{1,0:T(8,128)(2,1)S(1)}, bf16[208,384]{1,0:T(8,128)(2,1)S(1)}, u32[]{:S(2)}, u32[]{:S(2)}) collective-permute-start(bf16[208,384]{1,0:T(8,128)(2,1)S(1)} %get-tuple-element.151), channel_id=1, source_target_pairs={{0,1},{1,0},{2,3},{3,2},{4,5},{5,4},{6,7},{7,6},{8,9},{9,8},{10,11... | collective-permute-start | bytes 479240 | tf_op jit(solution)/shard_map/ppermute | solution.py:24
  54.5 2.0 %collective-permute-start.18 = (bf16[416,384]{1,0:T(8,128)(2,1)S(1)}, bf16[416,384]{1,0:T(8,128)(2,1)S(1)}, u32[]{:S(2)}, u32[]{:S(2)}) collective-permute-start(bf16[416,384]{1,0:T(8,128)(2,1)S(1)} %broadcast_select_fusion), channel_id=1, source_target_pairs={{0,1},{1,0},{2,3},{3,2},{4,5},{5,4},{6,7},{7,6},{8,9},{9,8},{10,11... | collective-permute-start | bytes 958472 | tf_op jit(solution)/shard_map/ppermute | solution.py:24
  60.5 1.8 %collective-permute-start.19 = (f32[640,128]{1,0:T(8,128)S(1)}, f32[640,128]{1,0:T(8,128)S(1)}, u32[]{:S(2)}, u32[]{:S(2)}) collective-permute-start(f32[640,128]{1,0:T(8,128)S(1)} %get-tuple-element.130), channel_id=1, source_target_pairs={{0,1},{1,0},{2,3},{3,2},{4,5},{5,4},{6,7},{7,6},{8,9},{9,8},{10,11... | collective-permute-start | bytes 983048 | tf_op jit(solution)/shard_map/ppermute | solution.py:24
  62.3 5.1 %collective-permute-start.23 = (f32[512,128]{1,0:T(8,128)S(1)}, f32[512,128]{1,0:T(8,128)S(1)}, u32[]{:S(2)}, u32[]{:S(2)}) collective-permute-start(f32[512,128]{1,0:T(8,128)S(1)} %get-tuple-element.142), channel_id=1, source_target_pairs={{0,1},{1,0},{2,3},{3,2},{4,5},{5,4},{6,7},{7,6},{8,9},{9,8},{10,11... | collective-permute-start | bytes 786440 | tf_op jit(solution)/shard_map/ppermute | solution.py:24
  63.0 7.6 %collective-permute-start.20 = (s16[176,128]{1,0:T(8,128)(2,1)S(1)}, s16[176,128]{1,0:T(8,128)(2,1)S(1)}, u32[]{:S(2)}, u32[]{:S(2)}) collective-permute-start(s16[176,128]{1,0:T(8,128)(2,1)S(1)} %get-tuple-element.138), channel_id=1, source_target_pairs={{0,12},{1,13},{2,14},{3,15},{4,8},{5,9},{6,10},{7,11},{8,4},{9,5},... | collective-permute-start | bytes 135176 | tf_op jit(solution)/shard_map/ppermute | solution.py:24
  65.6 6.7 %collective-permute-start.21 = (s16[176,128]{1,0:T(8,128)(2,1)S(1)}, s16[176,128]{1,0:T(8,128)(2,1)S(1)}, u32[]{:S(2)}, u32[]{:S(2)}) collective-permute-start(s16[176,128]{1,0:T(8,128)(2,1)S(1)} %get-tuple-element.139), channel_id=1, source_target_pairs={{0,8},{1,9},{2,10},{3,11},{4,12},{5,13},{6,14},{7,15},{8,0},{9,1},... | collective-permute-start | bytes 135176 | tf_op jit(solution)/shard_map/ppermute | solution.py:24
  66.1 6.3 %collective-permute-start.22 = (s16[176,128]{1,0:T(8,128)(2,1)S(1)}, s16[176,128]{1,0:T(8,128)(2,1)S(1)}, u32[]{:S(2)}, u32[]{:S(2)}) collective-permute-start(s16[176,128]{1,0:T(8,128)(2,1)S(1)} %get-tuple-element.140), channel_id=1, source_target_pairs={{0,4},{1,5},{2,6},{3,7},{4,0},{5,1},{6,2},{7,3},{8,12},{9,13},{10,... | collective-permute-start | bytes 135176 | tf_op jit(solution)/shard_map/ppermute | solution.py:24
  67.9 5.9 %collective-permute-start.24 = (s16[144,128]{1,0:T(8,128)(2,1)S(1)}, s16[144,128]{1,0:T(8,128)(2,1)S(1)}, u32[]{:S(2)}, u32[]{:S(2)}) collective-permute-start(s16[144,128]{1,0:T(8,128)(2,1)S(1)} %get-tuple-element.144), channel_id=1, source_target_pairs={{0,12},{1,13},{2,14},{3,15},{4,8},{5,9},{6,10},{7,11},{8,4},{9,5},... | collective-permute-start | bytes 110600 | tf_op jit(solution)/shard_map/ppermute | solution.py:24
  70.6 4.9 %collective-permute-start.25 = (s16[144,128]{1,0:T(8,128)(2,1)S(1)}, s16[144,128]{1,0:T(8,128)(2,1)S(1)}, u32[]{:S(2)}, u32[]{:S(2)}) collective-permute-start(s16[144,128]{1,0:T(8,128)(2,1)S(1)} %get-tuple-element.145), channel_id=1, source_target_pairs={{0,8},{1,9},{2,10},{3,11},{4,12},{5,13},{6,14},{7,15},{8,0},{9,1},... | collective-permute-start | bytes 110600 | tf_op jit(solution)/shard_map/ppermute | solution.py:24
  70.6 4.9 %collective-permute-start.26 = (s16[144,128]{1,0:T(8,128)(2,1)S(1)}, s16[144,128]{1,0:T(8,128)(2,1)S(1)}, u32[]{:S(2)}, u32[]{:S(2)}) collective-permute-start(s16[144,128]{1,0:T(8,128)(2,1)S(1)} %get-tuple-element.146), channel_id=1, source_target_pairs={{0,4},{1,5},{2,6},{3,7},{4,0},{5,1},{6,2},{7,3},{8,12},{9,13},{10,... | collective-permute-start | bytes 110600 | tf_op jit(solution)/shard_map/ppermute | solution.py:24
  75.6 6.8 %collective-permute-start.29 = (s16[304,128]{1,0:T(8,128)(2,1)S(1)}, s16[304,128]{1,0:T(8,128)(2,1)S(1)}, u32[]{:S(2)}, u32[]{:S(2)}) collective-permute-start(s16[304,128]{1,0:T(8,128)(2,1)S(1)} %sum_code.1), channel_id=1, source_target_pairs={{0,12},{1,13},{2,14},{3,15},{4,8},{5,9},{6,10},{7,11},{8,4},{9,5},... | collective-permute-start | bytes 233480 | tf_op jit(solution)/shard_map/ppermute | solution.py:24
  77.5 7.1 %collective-permute-start.28 = (s16[304,128]{1,0:T(8,128)(2,1)S(1)}, s16[304,128]{1,0:T(8,128)(2,1)S(1)}, u32[]{:S(2)}, u32[]{:S(2)}) collective-permute-start(s16[304,128]{1,0:T(8,128)(2,1)S(1)} %sum_code.1), channel_id=1, source_target_pairs={{0,8},{1,9},{2,10},{3,11},{4,12},{5,13},{6,14},{7,15},{8,0},{9,1},... | collective-permute-start | bytes 233480 | tf_op jit(solution)/shard_map/ppermute | solution.py:24
  78.0 7.0 %collective-permute-start.27 = (s16[304,128]{1,0:T(8,128)(2,1)S(1)}, s16[304,128]{1,0:T(8,128)(2,1)S(1)}, u32[]{:S(2)}, u32[]{:S(2)}) collective-permute-start(s16[304,128]{1,0:T(8,128)(2,1)S(1)} %sum_code.1), channel_id=1, source_target_pairs={{0,4},{1,5},{2,6},{3,7},{4,0},{5,1},{6,2},{7,3},{8,12},{9,13},{10,... | collective-permute-start | bytes 233480 | tf_op jit(solution)/shard_map/ppermute | solution.py:24
  80.0 6.7 %collective-permute-start.30 = (s16[304,128]{1,0:T(8,128)(2,1)S(1)}, s16[304,128]{1,0:T(8,128)(2,1)S(1)}, u32[]{:S(2)}, u32[]{:S(2)}) collective-permute-start(s16[304,128]{1,0:T(8,128)(2,1)S(1)} %sum_code.1), channel_id=1, source_target_pairs={{0,2},{1,3},{2,0},{3,1},{4,6},{5,7},{6,4},{7,5},{8,10},{9,11},{10,... | collective-permute-start | bytes 233480 | tf_op jit(solution)/shard_map/ppermute | solution.py:24
  82.4 5.2 %collective-permute-start.33 = (s16[304,128]{1,0:T(8,128)(2,1)S(1)}, s16[304,128]{1,0:T(8,128)(2,1)S(1)}, u32[]{:S(2)}, u32[]{:S(2)}) collective-permute-start(s16[304,128]{1,0:T(8,128)(2,1)S(1)} %collective-permute-done.29), channel_id=1, source_target_pairs={{0,2},{1,3},{2,0},{3,1},{4,6},{5,7},{6,4},{7,5},{8,10},{9,11},{10,... | collective-permute-start | bytes 233480 | tf_op jit(solution)/shard_map/ppermute | solution.py:24
  84.6 4.6 %collective-permute-start.32 = (s16[304,128]{1,0:T(8,128)(2,1)S(1)}, s16[304,128]{1,0:T(8,128)(2,1)S(1)}, u32[]{:S(2)}, u32[]{:S(2)}) collective-permute-start(s16[304,128]{1,0:T(8,128)(2,1)S(1)} %collective-permute-done.28), channel_id=1, source_target_pairs={{0,2},{1,3},{2,0},{3,1},{4,6},{5,7},{6,4},{7,5},{8,10},{9,11},{10,... | collective-permute-start | bytes 233480 | tf_op jit(solution)/shard_map/ppermute | solution.py:24
  85.0 5.0 %collective-permute-start.31 = (s16[304,128]{1,0:T(8,128)(2,1)S(1)}, s16[304,128]{1,0:T(8,128)(2,1)S(1)}, u32[]{:S(2)}, u32[]{:S(2)}) collective-permute-start(s16[304,128]{1,0:T(8,128)(2,1)S(1)} %collective-permute-done.27), channel_id=1, source_target_pairs={{0,2},{1,3},{2,0},{3,1},{4,6},{5,7},{6,4},{7,5},{8,10},{9,11},{10,... | collective-permute-start | bytes 233480 | tf_op jit(solution)/shard_map/ppermute | solution.py:24
  86.6 3.5 %collective-permute-start.34 = (s16[4,304,128]{2,1,0:T(8,128)(2,1)S(1)}, s16[4,304,128]{2,1,0:T(8,128)(2,1)S(1)}, u32[]{:S(2)}, u32[]{:S(2)}) collective-permute-start(s16[4,304,128]{2,1,0:T(8,128)(2,1)S(1)} %pad_add_fusion.a), channel_id=1, source_target_pairs={{0,1},{1,0},{2,3},{3,2},{4,5},{5,4},{6,7},{7,6},{8,9},{9,8},{10,11... | collective-permute-start | bytes 933896 | tf_op jit(solution)/shard_map/ppermute | solution.py:24
  90.0 2.0 %collective-permute-start.35 = (s16[4,304,128]{2,1,0:T(8,128)(2,1)S(1)}, s16[4,304,128]{2,1,0:T(8,128)(2,1)S(1)}, u32[]{:S(2)}, u32[]{:S(2)}) collective-permute-start(s16[4,304,128]{2,1,0:T(8,128)(2,1)S(1)} %pad_add_fusion.1.b), channel_id=1, source_target_pairs={{0,1},{1,0},{2,3},{3,2},{4,5},{5,4},{6,7},{7,6},{8,9},{9,8},{10,11... | collective-permute-start | bytes 933896 | tf_op jit(solution)/shard_map/ppermute | solution.py:24

commit v11 on v10

--- a/solution.py
+++ b/solution.py
@@ -287,7 +287,7 @@
     return jnp.exp2(first), jnp.exp2(exponent - first)
 
 
-def encode(x, out, row):
+def quantize(x, out, row):
     rows = x.shape[0]
     groups = x.reshape(rows // GROUP, GROUP, LANES)
     largest = jnp.max(jnp.abs(groups), axis=1)
@@ -296,17 +296,29 @@
     for g in range(rows // GROUP):
         whole = jnp.round(groups[g] * a[g:g + 1, :] * b[g:g + 1, :]).astype(I32)
         out[pl.ds(row + g * GROUP, GROUP), :] = whole.astype(I16)
-    pad = jnp.zeros((PAD - rows // GROUP, LANES), F32)
-    out[pl.ds(row + rows, PAD), :] = jnp.concatenate([power, pad]).astype(I32).astype(I16)
+    return power
+
+
+def padded(power):
+    return jnp.concatenate([power, jnp.zeros((PAD - power.shape[0], LANES), F32)])
+
+
+def encode(x, out, row):
+    power = quantize(x, out, row)
+    out[pl.ds(row + x.shape[0], PAD), :] = padded(power).astype(I32).astype(I16)
+
+
+def restore(coded, power):
+    wide = coded.astype(I32).astype(F32)
+    a, b = powers(power - BITS)
+    return jnp.concatenate([
+        wide[g * GROUP:(g + 1) * GROUP] * a[g:g + 1, :] * b[g:g + 1, :] for g in range(wide.shape[0] // GROUP)
+    ])
 
 
 def decode(coded):
     rows = coded.shape[0] - PAD
-    wide = coded.astype(I32).astype(F32)
-    a, b = powers(wide[rows:] - BITS)
-    return jnp.concatenate(
-        [wide[g * GROUP:(g + 1) * GROUP] * a[g:g + 1, :] * b[g:g + 1, :] for g in range(rows // GROUP)]
-    )
+    return restore(coded[:rows], coded[rows:].astype(I32).astype(F32))
 
 
 def chip_kernel(keep_in, away, got_away, got_keep, keep, send):
@@ -317,8 +329,22 @@
         keep[at, :] = keep_in[at, :] + decode(got_keep[coded, :])
 
 
-def column_kernel(first, me_ref, mine, theirs, near, across, keep, *sends):
+def column_kernel(first, me_ref, mine, theirs, near, across, *rest):
+    *given, keep, s1, s2, s3 = rest[:5] if first else rest[:4]
+    sends = (s1, s2, s3)
+    apart = None if first else rest[4]
     _, _, z = place_of(me_ref[0])
+
+    def send(value, t):
+        out = sends[t - 1]
+        power = quantize(value, out, 0)
+        if apart is not None:
+            apart[t - 1] = padded(power)
+        else:
+            early = given[0][t - 1][:first // 4 // GROUP, :]
+            both = padded(jnp.concatenate([early, power]))
+            out[value.shape[0]:, :] = both.astype(I32).astype(I16)
+
     piece = keep.shape[0]
     away = across.shape[0] // 4
     far = jnp.concatenate([decode(across[i * away:(i + 1) * away, :]) for i in range(4)])
@@ -332,11 +358,19 @@
             keep[...] = value
 
         for t in (1, 2, 3):
-            pl.when((z ^ t) == i)(functools.partial(encode, value, sends[t - 1], 0))
+            pl.when((z ^ t) == i)(functools.partial(send, value, t))
 
 
 def sum_of(parts):
-    return jnp.concatenate([sum((decode(x[...]) for x in others), mine[...]) for mine, *others in (parts[:4], parts[4:])])
+    (keep_a, *early), (keep_b, *late) = parts[:4], parts[4:]
+    rows_a, rows_b = keep_a.shape[0], keep_b.shape[0]
+    cut = rows_a // GROUP
+    total_a, total_b = keep_a[...], keep_b[...]
+    for a, b in zip(early, late):
+        power = b[rows_b:, :].astype(I32).astype(F32)
+        total_a += restore(a[...], power)
+        total_b += restore(b[:rows_b, :], power[cut:, :])
+    return jnp.concatenate([total_a, total_b])
 
 
 def sum_kernel(*rest):
@@ -582,12 +616,14 @@
         [dma(2), *half_s, pltpu.VMEM((2 * square, LANES), F32)], side=1,
     )
 
-    def column(first, size, mine, got):
+    def column(first, size, mine, got, *given):
         n = size // 4
+        apart = () if given else (jax.ShapeDtypeStruct((3, PAD, LANES), F32),)
+        outs = (plain(n),) + (coded(n + (PAD if given else 0)),) * 3 + apart
         return kernel(
-            functools.partial(column_kernel, first), "column", [smem] + [vmem] * 4, (plain(n),) + (coded(n + PAD),) * 3,
-            (vmem,) * 4,
-        )(me, mine, got, keep, across)
+            functools.partial(column_kernel, first), "column", [smem] + [vmem] * (4 + len(given)), outs,
+            (vmem,) * len(outs),
+        )(me, mine, got, keep, across, *given)
 
     got = swapped(send, 1)
     mine_b, send_b = kernel(
@@ -596,9 +632,9 @@
     )(me, high, low, own_s)
     got, send_b = lax.optimization_barrier((got, send_b))
     got_b = swapped(send_b, 1)
-    keep_a, *sends_a = column(0, square, mine, got)
+    keep_a, *sends_a, apart = column(0, square, mine, got)
     summed = [keep_a] + [swapped(sends_a[t - 1], 4 * t) for t in (3, 2, 1)]
-    keep_b, *sends_b = column(square, corner, mine_b, got_b)
+    keep_b, *sends_b = column(square, corner, mine_b, got_b, apart)
     summed += [keep_b] + [swapped(sends_b[t - 1], 4 * t) for t in (3, 2, 1)]
     if blocks == 16:
         mine = kernel(

time: 94.2 us -> 94.2 us (level)
  no operation moved by 1% of the time
where the time goes in v11:
time: 94.2 us; the launch traced here: 93.9 us
  starting transfers between devices  41.8 us (44%)
  Pallas kernels  28.1 us (30%)
  waiting for transfers between devices  17.8 us (19%)
  local copies, waits for them, and re-layouts  4.53 us (5%)
  between operations  1.25 us (1%)
    ppermute x36, starting transfers between devices, move(): return lax.ppermute(x, 'dom', pairs)  41.8 us
    ppermute x36, waiting for transfers between devices, move(): return lax.ppermute(x, 'dom', pairs)  17.8 us
    pallas_call x4, Pallas kernels, pair_step(): kernel(functools.partial(body, plan, names, step), name, [smem] + [vmem]...  11.2 us
    unnamed x12, local copies, waits for them, and re-layouts  3.48 us
    pallas_call x1, Pallas kernels, shards(): kernel(own_kernel, 'own', [hbm, vmem, vmem], (jax.ShapeDtypeStruct((wide,...  3.01 us
    pallas_call x1, Pallas kernels, shards(): kernel(sib_kernel, 'sib', [vmem, vmem, hbm, vmem, vmem], total_t, vmem, [...  2.98 us
    pallas_call x1, Pallas kernels, shards(): kernel(near_metric_kernel, 'near_metric', [smem, vmem, vmem], (plain(uppe...  2.76 us
  transfers between devices with their start and end apart: 36, of which 15 were waited for; matrix products, arithmetic and copies ran while one was open for 0% of the time, Pallas kernels for 24%

profile of v11, /device:TPU:0, one launch (start us, length us, event | category | flops | bytes accessed | tf_op | source)
XLA Modules:
  0.0 93.9 jit_solution(6537798187294699802)
XLA Ops:
  0.7 1.0 %slice.12 = bf16[416,384]{1,0:T(8,128)(2,1)S(1)} slice(bf16[2048,384]{1,0:T(8,128)(2,1)} %bitcast.13), slice={[0:416], [0:384]} | slice | bytes 638976 | tf_op jit(solution)/shard_map/slice | solution.py:502
  1.7 0.5 collective-permute-start.1
  2.2 2.6 %collective-permute-start = (bf16[416,384]{1,0:T(8,128)(2,1)S(1)}, bf16[416,384]{1,0:T(8,128)(2,1)S(1)}, u32[]{:S(2)}, u32[]{:S(2)}) collective-permute-start(bf16[416,384]{1,0:T(8,128)(2,1)S(1)} %slice.12), channel_id=1, source_target_pairs={{0,2},{1,3},{2,0},{3,1},{4,6},{5,7},{6,4},{7,5},{8,10},{9,11},{10,... | collective-permute-start | bytes 958472 | tf_op jit(solution)/shard_map/ppermute | solution.py:24
  4.8 0.2 collective-permute-start.2
  5.0 1.4 %copy-done = bf16[1,2,1024,384]{3,2,1,0:T(8,128)(2,1)S(1)} copy-done((bf16[1,2,1024,384]{3,2,1,0:T(8,128)(2,1)S(1)}, bf16[1,2,1024,384]{3,2,1,0:T(8,128)(2,1)}, u32[]{:S(2)}) %copy-start) | copy-done | bytes 1572888
  6.4 0.7 copy-done.4
  7.0 0.9 split.1
  8.0 1.3 %prep.1 = (f32[8,768]{1,0:T(8,128)S(1)}, f32[8,768]{1,0:T(8,128)S(1)}) custom-call(s32[1]{0:T(128)} %bitcast.me_ref.a_0_, s32[1,3]{1,0:T(1,128)S(1)} %copy-done.4, s32[1,3]{1,0:T(1,128)S(1)} %collective-permute-done.2.sib_pairs, f32[2,16]{1,0:T(2,128)S(1)} %bitcast.19, f32[64,128]{1,0:T(8,128)S(1)} %bitcast.18, s32[16,384]{1,0:T(8,128)S(1)} %copy-done.3), custom_call_target="tpu_custom_call" | custom-call | flops 1 | bytes 1 | tf_op jit(solution)/shard_map/prep/pallas_call | solution.py:516
  9.3 0.4 collective-permute-start.4
  9.7 1.4 %copy-done.1 = bf16[1,2,1024,384]{3,2,1,0:T(8,128)(2,1)S(1)} copy-done((bf16[1,2,1024,384]{3,2,1,0:T(8,128)(2,1)S(1)}, bf16[1,2,1024,384]{3,2,1,0:T(8,128)(2,1)}, u32[]{:S(2)}) %copy-start.1) | copy-done | bytes 1572888
  11.1 3.0 %own.1 = (bf16[768,1024]{1,0:T(8,128)(2,1)S(1)}, bf16[1024,768]{1,0:T(8,128)(2,1)S(1)}, f32[1024,768]{1,0:T(8,128)S(1)}) custom-call(bf16[2048,384]{1,0:T(8,128)(2,1)S(1)} %bitcast.16, f32[8,768]{1,0:T(8,128)S(1)} %get-tuple-element.79.levels.a_2_, f32[8,768]{1,0:T(8,128)S(1)} %get-tuple-element.80.weights.a_3_), custom_call_target="tpu_custom_call" | custom-call | flops 20000000000 | bytes 1 | tf_op jit(solution)/shard_map/own/pallas_call | solution.py:521
  14.1 3.7 %collective-permute-start.9 = (bf16[416,384]{1,0:T(8,128)(2,1)S(1)}, bf16[416,384]{1,0:T(8,128)(2,1)S(1)}, u32[]{:S(2)}, u32[]{:S(2)}) collective-permute-start(bf16[416,384]{1,0:T(8,128)(2,1)S(1)} %collective-permute-done.rest_0_), channel_id=1, source_target_pairs={{0,4},{1,5},{4,8},{5,9},{6,2},{7,3},{8,12},{9,13},{10,6},{11,7},{1... | collective-permute-start | bytes 958472 | tf_op jit(solution)/shard_map/ppermute | solution.py:24
  17.9 3.0 %sib.1.total.near = f32[1024,768]{1,0:T(8,128)S(1)} custom-call(bf16[768,1024]{1,0:T(8,128)(2,1)S(1)} %get-tuple-element.115.own_t.a_1_, f32[1024,768]{1,0:T(8,128)S(1)} %get-tuple-element.91.total_in, bf16[2048,384]{1,0:T(8,128)(2,1)S(1)} %collective-permute-done.1.sib, f32[8,768]{1,0:T(8,128)S(1)} %get-tuple-element.79.levels.a_2_, ...), custom_call_target="tpu_custom_call", output_to_operand_aliasing={{}: (1, {})} | custom-call | flops 10000000000 | bytes 1 | tf_op jit(solution)/shard_map/sib/pallas_call | solution.py:531
  20.9 3.9 %collective-permute-start.12 = (bf16[384,384]{1,0:T(8,128)(2,1)S(1)}, bf16[384,384]{1,0:T(8,128)(2,1)S(1)}, u32[]{:S(2)}, u32[]{:S(2)}) collective-permute-start(bf16[384,384]{1,0:T(8,128)(2,1)S(1)} %collective-permute-done.4.rest_1_), channel_id=1, source_target_pairs={{0,4},{1,5},{4,8},{5,9},{6,2},{7,3},{8,12},{9,13},{10,6},{11,7},{1... | collective-permute-start | bytes 884744 | tf_op jit(solution)/shard_map/ppermute | solution.py:24
  24.8 3.2 %collective-permute-done.3.rest_2_ = bf16[432,384]{1,0:T(8,128)(2,1)S(1)} collective-permute-done((bf16[432,384]{1,0:T(8,128)(2,1)S(1)}, bf16[432,384]{1,0:T(8,128)(2,1)S(1)}, u32[]{:S(2)}, u32[]{:S(2)}) %collective-permute-start.3) | collective-permute-done | bytes 331808 | tf_op jit(solution)/shard_map/ppermute | solution.py:24
  28.0 3.5 %collective-permute-start.13 = (bf16[432,384]{1,0:T(8,128)(2,1)S(1)}, bf16[432,384]{1,0:T(8,128)(2,1)S(1)}, u32[]{:S(2)}, u32[]{:S(2)}) collective-permute-start(bf16[432,384]{1,0:T(8,128)(2,1)S(1)} %collective-permute-done.3.rest_2_), channel_id=1, source_target_pairs={{0,4},{1,5},{4,8},{5,9},{6,2},{7,3},{8,12},{9,13},{10,6},{11,7},{1... | collective-permute-start | bytes 995336 | tf_op jit(solution)/shard_map/ppermute | solution.py:24
  31.5 0.1 collective-permute-start.5
  31.6 2.8 %near_metric.1 = (f32[1152,128]{1,0:T(8,128)S(1)}, f32[1152,128]{1,0:T(8,128)S(1)}, s16[1216,128]{1,0:T(8,128)(2,1)S(1)}, s16[1216,128]{1,0:T(8,128)(2,1)S(1)}) custom-call(s32[1]{0:T(128)} %bitcast.me_ref.a_0_, f32[1024,768]{1,0:T(8,128)S(1)} %sib.1.total.near, bf16[1024,768]{1,0:T(8,128)(2,1)S(1)} %get-tuple-element.99.own_s), custom_call_target="tpu_custom_call" | custom-call | flops 10000000000 | bytes 1 | tf_op jit(solution)/shard_map/near_metric/pallas_call | solution.py:543
  34.4 0.9 collective-permute-done.8.rest_3_
  35.3 3.5 %collective-permute-start.10 = (bf16[416,384]{1,0:T(8,128)(2,1)S(1)}, bf16[416,384]{1,0:T(8,128)(2,1)S(1)}, u32[]{:S(2)}, u32[]{:S(2)}) collective-permute-start(bf16[416,384]{1,0:T(8,128)(2,1)S(1)} %collective-permute-done.8.rest_3_), channel_id=1, source_target_pairs={{0,4},{1,5},{4,8},{5,9},{6,2},{7,3},{8,12},{9,13},{10,6},{11,7},{1... | collective-permute-start | bytes 958472 | tf_op jit(solution)/shard_map/ppermute | solution.py:24
  38.8 0.1 collective-permute-start.6
  38.8 0.5 collective-permute-start.7
  39.3 0.2 collective-permute-done.13.rest_2_.a_5_
  39.6 0.2 maximum_select_fusion
  39.9 0.5 collective-permute-done.6.got_away
  40.4 0.4 collective-permute-done.7.got_keep
  40.9 0.2 collective-permute-done.5.rest_4_
  41.0 3.7 %collective-permute-start.11 = (bf16[416,384]{1,0:T(8,128)(2,1)S(1)}, bf16[416,384]{1,0:T(8,128)(2,1)S(1)}, u32[]{:S(2)}, u32[]{:S(2)}) collective-permute-start(bf16[416,384]{1,0:T(8,128)(2,1)S(1)} %collective-permute-done.5.rest_4_), channel_id=1, source_target_pairs={{0,4},{1,5},{4,8},{5,9},{6,2},{7,3},{8,12},{9,13},{10,6},{11,7},{1... | collective-permute-start | bytes 958472 | tf_op jit(solution)/shard_map/ppermute | solution.py:24
  44.7 0.4 chip.1
  45.2 2.7 %far2.1.total_in = f32[1024,768]{1,0:T(8,128)S(1)} custom-call(s32[1]{0:T(128)} %bitcast.me_ref.a_0_, bf16[768,1024]{1,0:T(8,128)(2,1)S(1)} %get-tuple-element.115.own_t.a_1_, f32[8,768]{1,0:T(8,128)S(1)} %get-tuple-element.79.levels.a_2_, f32[8,768]{1,0:T(8,128)S(1)} %get-tuple-element.80.weights.a_3_, bf16[416,384]{1,0:T(8,128)(2,1)S(1)} %collective-permute-done.rest_0_, ...), custom_call_target="tpu_custom_call" | custom-call | flops 10000000000 | bytes 1 | tf_op jit(solution)/shard_map/far2/pallas_call | solution.py:589
  47.9 2.7 %far3.1.a_4_ = f32[1024,768]{1,0:T(8,128)S(1)} custom-call(s32[1]{0:T(128)} %bitcast.me_ref.a_0_, bf16[768,1024]{1,0:T(8,128)(2,1)S(1)} %get-tuple-element.115.own_t.a_1_, f32[8,768]{1,0:T(8,128)S(1)} %get-tuple-element.79.levels.a_2_, f32[8,768]{1,0:T(8,128)S(1)} %get-tuple-element.80.weights.a_3_, ...), custom_call_target="tpu_custom_call", output_to_operand_aliasing={{}: (4, {})} | custom-call | flops 1 | bytes 1 | tf_op jit(solution)/shard_map/far3/pallas_call | solution.py:589
  50.7 0.1 collective-permute-start.16
  50.8 0.5 collective-permute-start.15
  51.3 3.2 %collective-permute-done.17.across = s16[1216,128]{1,0:T(8,128)(2,1)S(1)} collective-permute-done((s16[1216,128]{1,0:T(8,128)(2,1)S(1)}, s16[1216,128]{1,0:T(8,128)(2,1)S(1)}, u32[]{:S(2)}, u32[]{:S(2)}) %collective-permute-start.17) | collective-permute-done | bytes 311328 | tf_op jit(solution)/shard_map/ppermute | solution.py:24
  54.6 1.9 %half.1.total_in = f32[1024,768]{1,0:T(8,128)S(1)} custom-call(s32[1]{0:T(128)} %bitcast.me_ref.a_0_, bf16[768,1024]{1,0:T(8,128)(2,1)S(1)} %get-tuple-element.115.own_t.a_1_, f32[8,768]{1,0:T(8,128)S(1)} %get-tuple-element.79.levels.a_2_, f32[8,768]{1,0:T(8,128)S(1)} %get-tuple-element.80.weights.a_3_, ...), custom_call_target="tpu_custom_call", output_to_operand_aliasing={{}: (4, {})} | custom-call | flops 1000000000 | bytes 1 | tf_op jit(solution)/shard_map/half/pallas_call | solution.py:589
  56.5 4.0 %last.1 = (f32[1024,768]{1,0:T(8,128)S(1)}, f32[2,1024,384]{2,1,0:T(8,128)}, f32[640,128]{1,0:T(8,128)S(1)}, f32[640,128]{1,0:T(8,128)S(1)}, bf16[1024,768]{1,0:...) custom-call(s32[1]{0:T(128)} %bitcast.me_ref.a_0_, ...), custom_call_target="tpu_custom_call", output_to_operand_aliasing={{0}: (4, {})} | custom-call | flops 1 | bytes 1 | tf_op jit(solution)/shard_map/last/pallas_call | solution.py:589
  60.5 0.6 collective-permute-start.19
  61.1 1.1 %corner.1 = (f32[512,128]{1,0:T(8,128)S(1)}, f32[512,128]{1,0:T(8,128)S(1)}) custom-call(s32[1]{0:T(128)} %bitcast.me_ref.a_0_, bf16[1024,768]{1,0:T(8,128)(2,1)S(1)} %get-tuple-element.132.high, bf16[1024,768]{1,0:T(8,128)(2,1)S(1)} %get-tuple-element.133.low, bf16[1024,768]{1,0:T(8,128)(2,1)S(1)} %get-tuple-element.99.own_s), custom_call_target="tpu_custom_call" | custom-call | flops 2000000000 | bytes 1 | tf_op jit(solution)/shard_map/corner/pallas_call | solution.py:629
  62.2 0.2 collective-permute-done.19.theirs
  62.3 0.4 collective-permute-start.23
  62.7 0.3 column.2
  63.0 2.7 %collective-permute-start.20 = (s16[160,128]{1,0:T(8,128)(2,1)S(1)}, s16[160,128]{1,0:T(8,128)(2,1)S(1)}, u32[]{:S(2)}, u32[]{:S(2)}) collective-permute-start(s16[160,128]{1,0:T(8,128)(2,1)S(1)} %get-tuple-element.139), channel_id=1, source_target_pairs={{0,12},{1,13},{2,14},{3,15},{4,8},{5,9},{6,10},{7,11},{8,4},{9,5},... | collective-permute-start | bytes 122888 | tf_op jit(solution)/shard_map/ppermute | solution.py:24
  65.6 0.4 collective-permute-start.21
  66.1 1.4 %collective-permute-start.22 = (s16[160,128]{1,0:T(8,128)(2,1)S(1)}, s16[160,128]{1,0:T(8,128)(2,1)S(1)}, u32[]{:S(2)}, u32[]{:S(2)}) collective-permute-start(s16[160,128]{1,0:T(8,128)(2,1)S(1)} %get-tuple-element.141), channel_id=1, source_target_pairs={{0,4},{1,5},{2,6},{3,7},{4,0},{5,1},{6,2},{7,3},{8,12},{9,13},{10,... | collective-permute-start | bytes 122888 | tf_op jit(solution)/shard_map/ppermute | solution.py:24
  67.4 0.5 column.3
  67.9 2.7 %collective-permute-start.24 = (s16[144,128]{1,0:T(8,128)(2,1)S(1)}, s16[144,128]{1,0:T(8,128)(2,1)S(1)}, u32[]{:S(2)}, u32[]{:S(2)}) collective-permute-start(s16[144,128]{1,0:T(8,128)(2,1)S(1)} %get-tuple-element.146), channel_id=1, source_target_pairs={{0,12},{1,13},{2,14},{3,15},{4,8},{5,9},{6,10},{7,11},{8,4},{9,5},... | collective-permute-start | bytes 110600 | tf_op jit(solution)/shard_map/ppermute | solution.py:24
  70.6 1.8 %collective-permute-start.26 = (s16[144,128]{1,0:T(8,128)(2,1)S(1)}, s16[144,128]{1,0:T(8,128)(2,1)S(1)}, u32[]{:S(2)}, u32[]{:S(2)}) collective-permute-start(s16[144,128]{1,0:T(8,128)(2,1)S(1)} %get-tuple-element.148), channel_id=1, source_target_pairs={{0,4},{1,5},{2,6},{3,7},{4,0},{5,1},{6,2},{7,3},{8,12},{9,13},{10,... | collective-permute-start | bytes 110600 | tf_op jit(solution)/shard_map/ppermute | solution.py:24
  72.4 1.5 %collective-permute-done.24.rest_5_ = s16[144,128]{1,0:T(8,128)(2,1)S(1)} collective-permute-done((s16[144,128]{1,0:T(8,128)(2,1)S(1)}, s16[144,128]{1,0:T(8,128)(2,1)S(1)}, u32[]{:S(2)}, u32[]{:S(2)}) %collective-permute-start.24) | collective-permute-done | bytes 36896 | tf_op jit(solution)/shard_map/ppermute | solution.py:24
  73.8 1.6 %collective-permute-done.25.rest_6_ = s16[144,128]{1,0:T(8,128)(2,1)S(1)} collective-permute-done((s16[144,128]{1,0:T(8,128)(2,1)S(1)}, s16[144,128]{1,0:T(8,128)(2,1)S(1)}, u32[]{:S(2)}, u32[]{:S(2)}) %collective-permute-start.25) | collective-permute-done | bytes 36896 | tf_op jit(solution)/shard_map/ppermute | solution.py:24
  75.4 0.2 sum_code.1
  75.6 1.9 %collective-permute-start.29 = (s16[304,128]{1,0:T(8,128)(2,1)S(1)}, s16[304,128]{1,0:T(8,128)(2,1)S(1)}, u32[]{:S(2)}, u32[]{:S(2)}) collective-permute-start(s16[304,128]{1,0:T(8,128)(2,1)S(1)} %sum_code.1), channel_id=1, source_target_pairs={{0,12},{1,13},{2,14},{3,15},{4,8},{5,9},{6,10},{7,11},{8,4},{9,5},... | collective-permute-start | bytes 233480 | tf_op jit(solution)/shard_map/ppermute | solution.py:24
  77.5 0.5 collective-permute-start.28
  78.0 2.1 %collective-permute-start.27 = (s16[304,128]{1,0:T(8,128)(2,1)S(1)}, s16[304,128]{1,0:T(8,128)(2,1)S(1)}, u32[]{:S(2)}, u32[]{:S(2)}) collective-permute-start(s16[304,128]{1,0:T(8,128)(2,1)S(1)} %sum_code.1), channel_id=1, source_target_pairs={{0,4},{1,5},{2,6},{3,7},{4,0},{5,1},{6,2},{7,3},{8,12},{9,13},{10,... | collective-permute-start | bytes 233480 | tf_op jit(solution)/shard_map/ppermute | solution.py:24
  80.0 1.2 %collective-permute-start.30 = (s16[304,128]{1,0:T(8,128)(2,1)S(1)}, s16[304,128]{1,0:T(8,128)(2,1)S(1)}, u32[]{:S(2)}, u32[]{:S(2)}) collective-permute-start(s16[304,128]{1,0:T(8,128)(2,1)S(1)} %sum_code.1), channel_id=1, source_target_pairs={{0,2},{1,3},{2,0},{3,1},{4,6},{5,7},{6,4},{7,5},{8,10},{9,11},{10,... | collective-permute-start | bytes 233480 | tf_op jit(solution)/shard_map/ppermute | solution.py:24
  81.2 1.1 %collective-permute-done.29 = s16[304,128]{1,0:T(8,128)(2,1)S(1)} collective-permute-done((s16[304,128]{1,0:T(8,128)(2,1)S(1)}, s16[304,128]{1,0:T(8,128)(2,1)S(1)}, u32[]{:S(2)}, u32[]{:S(2)}) %collective-permute-start.29) | collective-permute-done | bytes 77856 | tf_op jit(solution)/shard_map/ppermute | solution.py:24
  82.4 0.8 collective-permute-start.33
  83.2 1.4 %collective-permute-done.28 = s16[304,128]{1,0:T(8,128)(2,1)S(1)} collective-permute-done((s16[304,128]{1,0:T(8,128)(2,1)S(1)}, s16[304,128]{1,0:T(8,128)(2,1)S(1)}, u32[]{:S(2)}, u32[]{:S(2)}) %collective-permute-start.28) | collective-permute-done | bytes 77856 | tf_op jit(solution)/shard_map/ppermute | solution.py:24
  84.6 0.4 collective-permute-start.32
  85.0 1.6 %collective-permute-start.31 = (s16[304,128]{1,0:T(8,128)(2,1)S(1)}, s16[304,128]{1,0:T(8,128)(2,1)S(1)}, u32[]{:S(2)}, u32[]{:S(2)}) collective-permute-start(s16[304,128]{1,0:T(8,128)(2,1)S(1)} %collective-permute-done.27), channel_id=1, source_target_pairs={{0,2},{1,3},{2,0},{3,1},{4,6},{5,7},{6,4},{7,5},{8,10},{9,11},{10,... | collective-permute-start | bytes 233480 | tf_op jit(solution)/shard_map/ppermute | solution.py:24
  86.7 0.9 collective-permute-done.33
  87.6 1.5 %collective-permute-done.32 = s16[304,128]{1,0:T(8,128)(2,1)S(1)} collective-permute-done((s16[304,128]{1,0:T(8,128)(2,1)S(1)}, s16[304,128]{1,0:T(8,128)(2,1)S(1)}, u32[]{:S(2)}, u32[]{:S(2)}) %collective-permute-start.32) | collective-permute-done | bytes 77856 | tf_op jit(solution)/shard_map/ppermute | solution.py:24
  89.2 0.8 collective-permute-done.31
  90.1 1.9 %unpack.1 = (f32[1024,1024]{1,0:T(8,128)}, f32[4608,128]{1,0:T(8,128)S(1)}) custom-call(s32[1]{0:T(128)} %bitcast.me_ref.a_0_, s16[4,304,128]{2,1,0:T(8,128)(2,1)S(1)} %pad_add_fusion.a, s16[4,304,128]{2,1,0:T(8,128)(2,1)S(1)} %pad_add_fusion.1.b, s16[4,304,128]{2,1,0:T(8,128)(2,1)S(1)} %collective-permute-done.34.sib_a), custom_call_target="tpu_custom_call" | custom-call | flops 1000000000 | bytes 1 | tf_op jit(solution)/shard_map/unpack/pallas_call | solution.py:657
  92.0 1.7 %spread.1 = (f32[1024,1024]{1,0:T(8,128)}, f32[4608,128]{1,0:T(8,128)S(1)}) custom-call(s32[1]{0:T(128)} %bitcast.me_ref.a_0_, f32[1024,1024]{1,0:T(8,128)} %get-tuple-element.149.out_in, f32[4608,128]{1,0:T(8,128)S(1)} %get-tuple-element.150.packed_in, ...), custom_call_target="tpu_custom_call", output_to_operand_aliasing={{0}: (1, {}), {1}: (2, {})} | custom-call | flops 1 | bytes 1 | tf_op jit(solution)/shard_map/spread/pallas_call | solution.py:660
  (43 shorter events, 0.8 us)
Async XLA Ops:
  0.6 7.3 %copy-start.3 = (s32[16,384]{1,0:T(8,128)S(1)}, s32[16,384]{1,0:T(8,128)}, u32[]{:S(2)}) copy-start(s32[16,384]{1,0:T(8,128)} %maps_in.1) | copy-start | bytes 73732
  0.6 7.3 %copy-start.2 = (f32[8192]{0:T(1024)S(1)}, f32[8192]{0:T(1024)}, u32[]{:S(2)}) copy-start(f32[8192]{0:T(1024)} %param.8) | copy-start | bytes 98308
  0.7 7.3 %copy-start.5 = (f32[16,2]{0,1:T(2,128)S(1)}, f32[16,2]{0,1:T(2,128)}, u32[]{:S(2)}) copy-start(f32[16,2]{0,1:T(2,128)} %param.7) | copy-start | bytes 388
  1.7 7.6 %collective-permute-start.1 = (bf16[2048,384]{1,0:T(8,128)(2,1)}, bf16[2048,384]{1,0:T(8,128)(2,1)S(1)}, u32[]{:S(2)}, u32[]{:S(2)}) collective-permute-start(bf16[2048,384]{1,0:T(8,128)(2,1)} %bitcast.14), channel_id=1, source_target_pairs={{0,1},{1,0},{2,3},{3,2},{4,5},{5,4},{6,7},{7,6},{8,9},{9,8},{10,11... | collective-permute-start | bytes 4718600 | tf_op jit(solution)/shard_map/ppermute | solution.py:24
  2.2 11.9 %collective-permute-start = (bf16[416,384]{1,0:T(8,128)(2,1)S(1)}, bf16[416,384]{1,0:T(8,128)(2,1)S(1)}, u32[]{:S(2)}, u32[]{:S(2)}) collective-permute-start(bf16[416,384]{1,0:T(8,128)(2,1)S(1)} %slice.12), channel_id=1, source_target_pairs={{0,2},{1,3},{2,0},{3,1},{4,6},{5,7},{6,4},{7,5},{8,10},{9,11},{10,... | collective-permute-start | bytes 958472 | tf_op jit(solution)/shard_map/ppermute | solution.py:24
  4.8 3.2 %collective-permute-start.2 = (s32[1,3]{1,0:T(1,128)}, s32[1,3]{1,0:T(1,128)S(1)}, u32[]{:S(2)}, u32[]{:S(2)}) collective-permute-start(s32[1,3]{1,0:T(1,128)} %pairs.3), channel_id=1, source_target_pairs={{0,1},{1,0},{2,3},{3,2},{4,5},{5,4},{6,7},{7,6},{8,9},{9,8},{10,11... | collective-permute-start | bytes 44 | tf_op jit(solution)/shard_map/ppermute | solution.py:24
  5.0 1.4 %copy-start = (bf16[1,2,1024,384]{3,2,1,0:T(8,128)(2,1)S(1)}, bf16[1,2,1024,384]{3,2,1,0:T(8,128)(2,1)}, u32[]{:S(2)}) copy-start(bf16[1,2,1024,384]{3,2,1,0:T(8,128)(2,1)} %param.5) | copy-start | bytes 4718596
  6.4 0.7 copy-start.4
  9.3 11.6 %collective-permute-start.4 = (bf16[384,384]{1,0:T(8,128)(2,1)S(1)}, bf16[384,384]{1,0:T(8,128)(2,1)S(1)}, u32[]{:S(2)}, u32[]{:S(2)}) collective-permute-start(bf16[384,384]{1,0:T(8,128)(2,1)S(1)} %get-tuple-element.89), channel_id=1, source_target_pairs={{0,2},{1,3},{2,0},{3,1},{4,6},{5,7},{6,4},{7,5},{8,10},{9,11},{10,... | collective-permute-start | bytes 884744 | tf_op jit(solution)/shard_map/ppermute | solution.py:24
  9.7 1.4 %copy-start.1 = (bf16[1,2,1024,384]{3,2,1,0:T(8,128)(2,1)S(1)}, bf16[1,2,1024,384]{3,2,1,0:T(8,128)(2,1)}, u32[]{:S(2)}) copy-start(bf16[1,2,1024,384]{3,2,1,0:T(8,128)(2,1)} %param.5) | copy-start | bytes 4718596
  14.1 20.2 %collective-permute-start.9 = (bf16[416,384]{1,0:T(8,128)(2,1)S(1)}, bf16[416,384]{1,0:T(8,128)(2,1)S(1)}, u32[]{:S(2)}, u32[]{:S(2)}) collective-permute-start(bf16[416,384]{1,0:T(8,128)(2,1)S(1)} %collective-permute-done.rest_0_), channel_id=1, source_target_pairs={{0,4},{1,5},{4,8},{5,9},{6,2},{7,3},{8,12},{9,13},{10,6},{11,7},{1... | collective-permute-start | bytes 958472 | tf_op jit(solution)/shard_map/ppermute | solution.py:24
  17.8 10.2 %collective-permute-start.3 = (bf16[432,384]{1,0:T(8,128)(2,1)S(1)}, bf16[432,384]{1,0:T(8,128)(2,1)S(1)}, u32[]{:S(2)}, u32[]{:S(2)}) collective-permute-start(bf16[432,384]{1,0:T(8,128)(2,1)S(1)} %get-tuple-element.87), channel_id=1, source_target_pairs={{0,2},{1,3},{2,0},{3,1},{4,6},{5,7},{6,4},{7,5},{8,10},{9,11},{10,... | collective-permute-start | bytes 995336 | tf_op jit(solution)/shard_map/ppermute | solution.py:24
  20.9 18.0 %collective-permute-start.12 = (bf16[384,384]{1,0:T(8,128)(2,1)S(1)}, bf16[384,384]{1,0:T(8,128)(2,1)S(1)}, u32[]{:S(2)}, u32[]{:S(2)}) collective-permute-start(bf16[384,384]{1,0:T(8,128)(2,1)S(1)} %collective-permute-done.4.rest_1_), channel_id=1, source_target_pairs={{0,4},{1,5},{4,8},{5,9},{6,2},{7,3},{8,12},{9,13},{10,6},{11,7},{1... | collective-permute-start | bytes 884744 | tf_op jit(solution)/shard_map/ppermute | solution.py:24
  24.7 10.5 %collective-permute-start.8 = (bf16[416,384]{1,0:T(8,128)(2,1)S(1)}, bf16[416,384]{1,0:T(8,128)(2,1)S(1)}, u32[]{:S(2)}, u32[]{:S(2)}) collective-permute-start(bf16[416,384]{1,0:T(8,128)(2,1)S(1)} %get-tuple-element.103), channel_id=1, source_target_pairs={{0,2},{1,3},{2,0},{3,1},{4,6},{5,7},{6,4},{7,5},{8,10},{9,11},{10,... | collective-permute-start | bytes 958472 | tf_op jit(solution)/shard_map/ppermute | solution.py:24
  28.0 11.6 %collective-permute-start.13 = (bf16[432,384]{1,0:T(8,128)(2,1)S(1)}, bf16[432,384]{1,0:T(8,128)(2,1)S(1)}, u32[]{:S(2)}, u32[]{:S(2)}) collective-permute-start(bf16[432,384]{1,0:T(8,128)(2,1)S(1)} %collective-permute-done.3.rest_2_), channel_id=1, source_target_pairs={{0,4},{1,5},{4,8},{5,9},{6,2},{7,3},{8,12},{9,13},{10,6},{11,7},{1... | collective-permute-start | bytes 995336 | tf_op jit(solution)/shard_map/ppermute | solution.py:24
  31.5 9.5 %collective-permute-start.5 = (bf16[416,384]{1,0:T(8,128)(2,1)S(1)}, bf16[416,384]{1,0:T(8,128)(2,1)S(1)}, u32[]{:S(2)}, u32[]{:S(2)}) collective-permute-start(bf16[416,384]{1,0:T(8,128)(2,1)S(1)} %get-tuple-element.95), channel_id=1, source_target_pairs={{0,2},{1,3},{2,0},{3,1},{4,6},{5,7},{6,4},{7,5},{8,10},{9,11},{10,... | collective-permute-start | bytes 958472 | tf_op jit(solution)/shard_map/ppermute | solution.py:24
  35.3 9.9 %collective-permute-start.10 = (bf16[416,384]{1,0:T(8,128)(2,1)S(1)}, bf16[416,384]{1,0:T(8,128)(2,1)S(1)}, u32[]{:S(2)}, u32[]{:S(2)}) collective-permute-start(bf16[416,384]{1,0:T(8,128)(2,1)S(1)} %collective-permute-done.8.rest_3_), channel_id=1, source_target_pairs={{0,4},{1,5},{4,8},{5,9},{6,2},{7,3},{8,12},{9,13},{10,6},{11,7},{1... | collective-permute-start | bytes 958472 | tf_op jit(solution)/shard_map/ppermute | solution.py:24
  38.8 1.7 %collective-permute-start.6 = (s16[1216,128]{1,0:T(8,128)(2,1)S(1)}, s16[1216,128]{1,0:T(8,128)(2,1)S(1)}, u32[]{:S(2)}, u32[]{:S(2)}) collective-permute-start(s16[1216,128]{1,0:T(8,128)(2,1)S(1)} %get-tuple-element.100), channel_id=1, source_target_pairs={{0,1},{1,0},{2,3},{3,2},{4,5},{5,4},{6,7},{7,6},{8,9},{9,8},{10,11... | collective-permute-start | bytes 933896 | tf_op jit(solution)/shard_map/ppermute | solution.py:24
  38.8 2.0 %collective-permute-start.7 = (s16[1216,128]{1,0:T(8,128)(2,1)S(1)}, s16[1216,128]{1,0:T(8,128)(2,1)S(1)}, u32[]{:S(2)}, u32[]{:S(2)}) collective-permute-start(s16[1216,128]{1,0:T(8,128)(2,1)S(1)} %get-tuple-element.101), channel_id=1, source_target_pairs={{0,1},{1,0},{2,3},{3,2},{4,5},{5,4},{6,7},{7,6},{8,9},{9,8},{10,11... | collective-permute-start | bytes 933896 | tf_op jit(solution)/shard_map/ppermute | solution.py:24
  39.8 8.1 %collective-permute-start.14 = (bf16[1232,384]{1,0:T(8,128)(2,1)S(1)}, bf16[1232,384]{1,0:T(8,128)(2,1)S(1)}, u32[]{:S(2)}, u32[]{:S(2)}) collective-permute-start(bf16[1232,384]{1,0:T(8,128)(2,1)S(1)} %maximum_select_fusion), channel_id=1, source_target_pairs={{0,1},{1,0},{2,3},{3,2},{4,5},{5,4},{6,7},{7,6},{8,9},{9,8},{10,11... | collective-permute-start | bytes 2838536 | tf_op jit(solution)/shard_map/ppermute | solution.py:24
  41.0 13.4 %collective-permute-start.11 = (bf16[416,384]{1,0:T(8,128)(2,1)S(1)}, bf16[416,384]{1,0:T(8,128)(2,1)S(1)}, u32[]{:S(2)}, u32[]{:S(2)}) collective-permute-start(bf16[416,384]{1,0:T(8,128)(2,1)S(1)} %collective-permute-done.5.rest_4_), channel_id=1, source_target_pairs={{0,4},{1,5},{4,8},{5,9},{6,2},{7,3},{8,12},{9,13},{10,6},{11,7},{1... | collective-permute-start | bytes 958472 | tf_op jit(solution)/shard_map/ppermute | solution.py:24
  45.1 9.3 %collective-permute-start.17 = (s16[1216,128]{1,0:T(8,128)(2,1)S(1)}, s16[1216,128]{1,0:T(8,128)(2,1)S(1)}, u32[]{:S(2)}, u32[]{:S(2)}) collective-permute-start(s16[1216,128]{1,0:T(8,128)(2,1)S(1)} %get-tuple-element.124), channel_id=1, source_target_pairs={{0,2},{1,3},{2,0},{3,1},{4,6},{5,7},{6,4},{7,5},{8,10},{9,11},{10,... | collective-permute-start | bytes 933896 | tf_op jit(solution)/shard_map/ppermute | solution.py:24
  50.7 3.8 %collective-permute-start.16 = (bf16[208,384]{1,0:T(8,128)(2,1)S(1)}, bf16[208,384]{1,0:T(8,128)(2,1)S(1)}, u32[]{:S(2)}, u32[]{:S(2)}) collective-permute-start(bf16[208,384]{1,0:T(8,128)(2,1)S(1)} %get-tuple-element.152), channel_id=1, source_target_pairs={{0,1},{1,0},{2,3},{3,2},{4,5},{5,4},{6,7},{7,6},{8,9},{9,8},{10,11... | collective-permute-start | bytes 479240 | tf_op jit(solution)/shard_map/ppermute | solution.py:24
  50.8 3.7 %collective-permute-start.15 = (bf16[208,384]{1,0:T(8,128)(2,1)S(1)}, bf16[208,384]{1,0:T(8,128)(2,1)S(1)}, u32[]{:S(2)}, u32[]{:S(2)}) collective-permute-start(bf16[208,384]{1,0:T(8,128)(2,1)S(1)} %get-tuple-element.153), channel_id=1, source_target_pairs={{0,1},{1,0},{2,3},{3,2},{4,5},{5,4},{6,7},{7,6},{8,9},{9,8},{10,11... | collective-permute-start | bytes 479240 | tf_op jit(solution)/shard_map/ppermute | solution.py:24
  54.5 2.0 %collective-permute-start.18 = (bf16[416,384]{1,0:T(8,128)(2,1)S(1)}, bf16[416,384]{1,0:T(8,128)(2,1)S(1)}, u32[]{:S(2)}, u32[]{:S(2)}) collective-permute-start(bf16[416,384]{1,0:T(8,128)(2,1)S(1)} %broadcast_select_fusion), channel_id=1, source_target_pairs={{0,1},{1,0},{2,3},{3,2},{4,5},{5,4},{6,7},{7,6},{8,9},{9,8},{10,11... | collective-permute-start | bytes 958472 | tf_op jit(solution)/shard_map/ppermute | solution.py:24
  60.5 1.8 %collective-permute-start.19 = (f32[640,128]{1,0:T(8,128)S(1)}, f32[640,128]{1,0:T(8,128)S(1)}, u32[]{:S(2)}, u32[]{:S(2)}) collective-permute-start(f32[640,128]{1,0:T(8,128)S(1)} %get-tuple-element.131), channel_id=1, source_target_pairs={{0,1},{1,0},{2,3},{3,2},{4,5},{5,4},{6,7},{7,6},{8,9},{9,8},{10,11... | collective-permute-start | bytes 983048 | tf_op jit(solution)/shard_map/ppermute | solution.py:24
  62.3 5.1 %collective-permute-start.23 = (f32[512,128]{1,0:T(8,128)S(1)}, f32[512,128]{1,0:T(8,128)S(1)}, u32[]{:S(2)}, u32[]{:S(2)}) collective-permute-start(f32[512,128]{1,0:T(8,128)S(1)} %get-tuple-element.143), channel_id=1, source_target_pairs={{0,1},{1,0},{2,3},{3,2},{4,5},{5,4},{6,7},{7,6},{8,9},{9,8},{10,11... | collective-permute-start | bytes 786440 | tf_op jit(solution)/shard_map/ppermute | solution.py:24
  63.0 7.6 %collective-permute-start.20 = (s16[160,128]{1,0:T(8,128)(2,1)S(1)}, s16[160,128]{1,0:T(8,128)(2,1)S(1)}, u32[]{:S(2)}, u32[]{:S(2)}) collective-permute-start(s16[160,128]{1,0:T(8,128)(2,1)S(1)} %get-tuple-element.139), channel_id=1, source_target_pairs={{0,12},{1,13},{2,14},{3,15},{4,8},{5,9},{6,10},{7,11},{8,4},{9,5},... | collective-permute-start | bytes 122888 | tf_op jit(solution)/shard_map/ppermute | solution.py:24
  65.6 6.7 %collective-permute-start.21 = (s16[160,128]{1,0:T(8,128)(2,1)S(1)}, s16[160,128]{1,0:T(8,128)(2,1)S(1)}, u32[]{:S(2)}, u32[]{:S(2)}) collective-permute-start(s16[160,128]{1,0:T(8,128)(2,1)S(1)} %get-tuple-element.140), channel_id=1, source_target_pairs={{0,8},{1,9},{2,10},{3,11},{4,12},{5,13},{6,14},{7,15},{8,0},{9,1},... | collective-permute-start | bytes 122888 | tf_op jit(solution)/shard_map/ppermute | solution.py:24
  66.1 6.3 %collective-permute-start.22 = (s16[160,128]{1,0:T(8,128)(2,1)S(1)}, s16[160,128]{1,0:T(8,128)(2,1)S(1)}, u32[]{:S(2)}, u32[]{:S(2)}) collective-permute-start(s16[160,128]{1,0:T(8,128)(2,1)S(1)} %get-tuple-element.141), channel_id=1, source_target_pairs={{0,4},{1,5},{2,6},{3,7},{4,0},{5,1},{6,2},{7,3},{8,12},{9,13},{10,... | collective-permute-start | bytes 122888 | tf_op jit(solution)/shard_map/ppermute | solution.py:24
  67.9 5.9 %collective-permute-start.24 = (s16[144,128]{1,0:T(8,128)(2,1)S(1)}, s16[144,128]{1,0:T(8,128)(2,1)S(1)}, u32[]{:S(2)}, u32[]{:S(2)}) collective-permute-start(s16[144,128]{1,0:T(8,128)(2,1)S(1)} %get-tuple-element.146), channel_id=1, source_target_pairs={{0,12},{1,13},{2,14},{3,15},{4,8},{5,9},{6,10},{7,11},{8,4},{9,5},... | collective-permute-start | bytes 110600 | tf_op jit(solution)/shard_map/ppermute | solution.py:24
  70.6 4.9 %collective-permute-start.25 = (s16[144,128]{1,0:T(8,128)(2,1)S(1)}, s16[144,128]{1,0:T(8,128)(2,1)S(1)}, u32[]{:S(2)}, u32[]{:S(2)}) collective-permute-start(s16[144,128]{1,0:T(8,128)(2,1)S(1)} %get-tuple-element.147), channel_id=1, source_target_pairs={{0,8},{1,9},{2,10},{3,11},{4,12},{5,13},{6,14},{7,15},{8,0},{9,1},... | collective-permute-start | bytes 110600 | tf_op jit(solution)/shard_map/ppermute | solution.py:24
  70.6 4.9 %collective-permute-start.26 = (s16[144,128]{1,0:T(8,128)(2,1)S(1)}, s16[144,128]{1,0:T(8,128)(2,1)S(1)}, u32[]{:S(2)}, u32[]{:S(2)}) collective-permute-start(s16[144,128]{1,0:T(8,128)(2,1)S(1)} %get-tuple-element.148), channel_id=1, source_target_pairs={{0,4},{1,5},{2,6},{3,7},{4,0},{5,1},{6,2},{7,3},{8,12},{9,13},{10,... | collective-permute-start | bytes 110600 | tf_op jit(solution)/shard_map/ppermute | solution.py:24
  75.6 6.8 %collective-permute-start.29 = (s16[304,128]{1,0:T(8,128)(2,1)S(1)}, s16[304,128]{1,0:T(8,128)(2,1)S(1)}, u32[]{:S(2)}, u32[]{:S(2)}) collective-permute-start(s16[304,128]{1,0:T(8,128)(2,1)S(1)} %sum_code.1), channel_id=1, source_target_pairs={{0,12},{1,13},{2,14},{3,15},{4,8},{5,9},{6,10},{7,11},{8,4},{9,5},... | collective-permute-start | bytes 233480 | tf_op jit(solution)/shard_map/ppermute | solution.py:24
  77.5 7.1 %collective-permute-start.28 = (s16[304,128]{1,0:T(8,128)(2,1)S(1)}, s16[304,128]{1,0:T(8,128)(2,1)S(1)}, u32[]{:S(2)}, u32[]{:S(2)}) collective-permute-start(s16[304,128]{1,0:T(8,128)(2,1)S(1)} %sum_code.1), channel_id=1, source_target_pairs={{0,8},{1,9},{2,10},{3,11},{4,12},{5,13},{6,14},{7,15},{8,0},{9,1},... | collective-permute-start | bytes 233480 | tf_op jit(solution)/shard_map/ppermute | solution.py:24
  78.0 7.0 %collective-permute-start.27 = (s16[304,128]{1,0:T(8,128)(2,1)S(1)}, s16[304,128]{1,0:T(8,128)(2,1)S(1)}, u32[]{:S(2)}, u32[]{:S(2)}) collective-permute-start(s16[304,128]{1,0:T(8,128)(2,1)S(1)} %sum_code.1), channel_id=1, source_target_pairs={{0,4},{1,5},{2,6},{3,7},{4,0},{5,1},{6,2},{7,3},{8,12},{9,13},{10,... | collective-permute-start | bytes 233480 | tf_op jit(solution)/shard_map/ppermute | solution.py:24
  80.0 6.7 %collective-permute-start.30 = (s16[304,128]{1,0:T(8,128)(2,1)S(1)}, s16[304,128]{1,0:T(8,128)(2,1)S(1)}, u32[]{:S(2)}, u32[]{:S(2)}) collective-permute-start(s16[304,128]{1,0:T(8,128)(2,1)S(1)} %sum_code.1), channel_id=1, source_target_pairs={{0,2},{1,3},{2,0},{3,1},{4,6},{5,7},{6,4},{7,5},{8,10},{9,11},{10,... | collective-permute-start | bytes 233480 | tf_op jit(solution)/shard_map/ppermute | solution.py:24
  82.4 5.2 %collective-permute-start.33 = (s16[304,128]{1,0:T(8,128)(2,1)S(1)}, s16[304,128]{1,0:T(8,128)(2,1)S(1)}, u32[]{:S(2)}, u32[]{:S(2)}) collective-permute-start(s16[304,128]{1,0:T(8,128)(2,1)S(1)} %collective-permute-done.29), channel_id=1, source_target_pairs={{0,2},{1,3},{2,0},{3,1},{4,6},{5,7},{6,4},{7,5},{8,10},{9,11},{10,... | collective-permute-start | bytes 233480 | tf_op jit(solution)/shard_map/ppermute | solution.py:24
  84.6 4.6 %collective-permute-start.32 = (s16[304,128]{1,0:T(8,128)(2,1)S(1)}, s16[304,128]{1,0:T(8,128)(2,1)S(1)}, u32[]{:S(2)}, u32[]{:S(2)}) collective-permute-start(s16[304,128]{1,0:T(8,128)(2,1)S(1)} %collective-permute-done.28), channel_id=1, source_target_pairs={{0,2},{1,3},{2,0},{3,1},{4,6},{5,7},{6,4},{7,5},{8,10},{9,11},{10,... | collective-permute-start | bytes 233480 | tf_op jit(solution)/shard_map/ppermute | solution.py:24
  85.0 5.0 %collective-permute-start.31 = (s16[304,128]{1,0:T(8,128)(2,1)S(1)}, s16[304,128]{1,0:T(8,128)(2,1)S(1)}, u32[]{:S(2)}, u32[]{:S(2)}) collective-permute-start(s16[304,128]{1,0:T(8,128)(2,1)S(1)} %collective-permute-done.27), channel_id=1, source_target_pairs={{0,2},{1,3},{2,0},{3,1},{4,6},{5,7},{6,4},{7,5},{8,10},{9,11},{10,... | collective-permute-start | bytes 233480 | tf_op jit(solution)/shard_map/ppermute | solution.py:24
  86.6 3.5 %collective-permute-start.34 = (s16[4,304,128]{2,1,0:T(8,128)(2,1)S(1)}, s16[4,304,128]{2,1,0:T(8,128)(2,1)S(1)}, u32[]{:S(2)}, u32[]{:S(2)}) collective-permute-start(s16[4,304,128]{2,1,0:T(8,128)(2,1)S(1)} %pad_add_fusion.a), channel_id=1, source_target_pairs={{0,1},{1,0},{2,3},{3,2},{4,5},{5,4},{6,7},{7,6},{8,9},{9,8},{10,11... | collective-permute-start | bytes 933896 | tf_op jit(solution)/shard_map/ppermute | solution.py:24
  90.0 2.0 %collective-permute-start.35 = (s16[4,304,128]{2,1,0:T(8,128)(2,1)S(1)}, s16[4,304,128]{2,1,0:T(8,128)(2,1)S(1)}, u32[]{:S(2)}, u32[]{:S(2)}) collective-permute-start(s16[4,304,128]{2,1,0:T(8,128)(2,1)S(1)} %pad_add_fusion.1.b), channel_id=1, source_target_pairs={{0,1},{1,0},{2,3},{3,2},{4,5},{5,4},{6,7},{7,6},{8,9},{9,8},{10,11... | collective-permute-start | bytes 933896 | tf_op jit(solution)/shard_map/ppermute | solution.py:24

commit v12 on v10

--- a/solution.py
+++ b/solution.py
@@ -354,7 +354,7 @@
 def unpack(src, which, side, z, packed):
     plane = packed.shape[0] // 2
     for t in range(4):
-        value = decode(src[t])
+        value = decode(src[3 - t])
         used = 0
         for first, n in ((which * (plane // 18) * 5, plane // 18 * 5), (plane // 18 * (10 + which * 4), plane // 18 * 4)):
             piece = n // 4
@@ -614,7 +614,7 @@
 
     column = [mine] + [swapped(mine, 4 * t) for t in (1, 2, 3)]
     across = [swapped(c, 2) for c in column]
-    a, b = jnp.stack(column), jnp.stack(across)
+    a, b = jnp.stack(column[::-1]), jnp.stack(across[::-1])
     sib_a, sib_b = swapped(a, 1), swapped(b, 1)
     whole = jax.ShapeDtypeStruct((aux, aux), F32)
     scratch = [dma(2 + aux // 2 // LANES), pltpu.VMEM((aux, aux), F32)]

time: 94.2 us -> 92.9 us (0.986)
  waiting for transfers between devices: 17.8 us -> 16.6 us
    ppermute x36, waiting for transfers between devices: 17.8 us -> 16.6 us  [move(): return lax.ppermute(x, 'dom', pairs)]
where the time goes in v12:
time: 92.9 us; the launch traced here: 92.6 us
  starting transfers between devices  41.8 us (45%)
  Pallas kernels  28.1 us (30%)
  waiting for transfers between devices  16.6 us (18%)
  local copies, waits for them, and re-layouts  4.53 us (5%)
  between operations  1.25 us (1%)
    ppermute x36, starting transfers between devices, move(): return lax.ppermute(x, 'dom', pairs)  41.8 us
    ppermute x36, waiting for transfers between devices, move(): return lax.ppermute(x, 'dom', pairs)  16.6 us
    pallas_call x4, Pallas kernels, pair_step(): kernel(functools.partial(body, plan, names, step), name, [smem] + [vmem]...  11.2 us
    unnamed x12, local copies, waits for them, and re-layouts  3.48 us
    pallas_call x1, Pallas kernels, shards(): kernel(own_kernel, 'own', [hbm, vmem, vmem], (jax.ShapeDtypeStruct((wide,...  3.01 us
    pallas_call x1, Pallas kernels, shards(): kernel(sib_kernel, 'sib', [vmem, vmem, hbm, vmem, vmem], total_t, vmem, [...  2.98 us
    pallas_call x1, Pallas kernels, shards(): kernel(near_metric_kernel, 'near_metric', [smem, vmem, vmem], (plain(uppe...  2.76 us
    pallas_call x1, Pallas kernels, shards(): kernel(unpack_kernel, 'unpack', [smem] + [vmem] * 3, (whole, plain(upper)...  1.86 us
  transfers between devices with their start and end apart: 36, of which 15 were waited for; matrix products, arithmetic and copies ran while one was open for 0% of the time, Pallas kernels for 24%

profile of v12, /device:TPU:0, one launch (start us, length us, event | category | flops | bytes accessed | tf_op | source)
XLA Modules:
  0.0 92.6 jit_solution(4405045128325558944)
XLA Ops:
  0.7 1.0 %slice.12 = bf16[416,384]{1,0:T(8,128)(2,1)S(1)} slice(bf16[2048,384]{1,0:T(8,128)(2,1)} %bitcast.13), slice={[0:416], [0:384]} | slice | bytes 638976 | tf_op jit(solution)/shard_map/slice | solution.py:468
  1.7 0.5 collective-permute-start.1
  2.2 2.6 %collective-permute-start = (bf16[416,384]{1,0:T(8,128)(2,1)S(1)}, bf16[416,384]{1,0:T(8,128)(2,1)S(1)}, u32[]{:S(2)}, u32[]{:S(2)}) collective-permute-start(bf16[416,384]{1,0:T(8,128)(2,1)S(1)} %slice.12), channel_id=1, source_target_pairs={{0,2},{1,3},{2,0},{3,1},{4,6},{5,7},{6,4},{7,5},{8,10},{9,11},{10,... | collective-permute-start | bytes 958472 | tf_op jit(solution)/shard_map/ppermute | solution.py:24
  4.8 0.2 collective-permute-start.2
  5.0 1.4 %copy-done = bf16[1,2,1024,384]{3,2,1,0:T(8,128)(2,1)S(1)} copy-done((bf16[1,2,1024,384]{3,2,1,0:T(8,128)(2,1)S(1)}, bf16[1,2,1024,384]{3,2,1,0:T(8,128)(2,1)}, u32[]{:S(2)}) %copy-start) | copy-done | bytes 1572888
  6.4 0.7 copy-done.4
  7.0 0.9 %split.1 = (bf16[384,384]{1,0:T(8,128)(2,1)S(1)}, bf16[432,384]{1,0:T(8,128)(2,1)S(1)}, bf16[416,384]{1,0:T(8,128)(2,1)S(1)}, bf16[416,384]{1,0:T(8,128)(2,1)S(1)}) custom-call(s32[1]{0:T(128)} %bitcast.me_ref.a_0_, s32[1,3]{1,0:T(1,128)S(1)} %copy-done.4, bf16[2048,384]{1,0:T(8,128)(2,1)S(1)} %bitcast.15), custom_call_target="tpu_custom_call" | custom-call | flops 1 | bytes 1 | tf_op jit(solution)/shard_map/split/pallas_call | solution.py:474
  8.0 1.3 %prep.1 = (f32[8,768]{1,0:T(8,128)S(1)}, f32[8,768]{1,0:T(8,128)S(1)}) custom-call(s32[1]{0:T(128)} %bitcast.me_ref.a_0_, s32[1,3]{1,0:T(1,128)S(1)} %copy-done.4, s32[1,3]{1,0:T(1,128)S(1)} %collective-permute-done.2.sib_pairs, f32[2,16]{1,0:T(2,128)S(1)} %bitcast.19, f32[64,128]{1,0:T(8,128)S(1)} %bitcast.18, s32[16,384]{1,0:T(8,128)S(1)} %copy-done.3), custom_call_target="tpu_custom_call" | custom-call | flops 1 | bytes 1 | tf_op jit(solution)/shard_map/prep/pallas_call | solution.py:482
  9.3 0.4 collective-permute-start.4
  9.7 1.4 %copy-done.1 = bf16[1,2,1024,384]{3,2,1,0:T(8,128)(2,1)S(1)} copy-done((bf16[1,2,1024,384]{3,2,1,0:T(8,128)(2,1)S(1)}, bf16[1,2,1024,384]{3,2,1,0:T(8,128)(2,1)}, u32[]{:S(2)}) %copy-start.1) | copy-done | bytes 1572888
  11.1 3.0 %own.1 = (bf16[768,1024]{1,0:T(8,128)(2,1)S(1)}, bf16[1024,768]{1,0:T(8,128)(2,1)S(1)}, f32[1024,768]{1,0:T(8,128)S(1)}) custom-call(bf16[2048,384]{1,0:T(8,128)(2,1)S(1)} %bitcast.16, f32[8,768]{1,0:T(8,128)S(1)} %get-tuple-element.78.levels.a_2_, f32[8,768]{1,0:T(8,128)S(1)} %get-tuple-element.79.weights.a_3_), custom_call_target="tpu_custom_call" | custom-call | flops 20000000000 | bytes 1 | tf_op jit(solution)/shard_map/own/pallas_call | solution.py:487
  14.1 3.7 %collective-permute-start.9 = (bf16[416,384]{1,0:T(8,128)(2,1)S(1)}, bf16[416,384]{1,0:T(8,128)(2,1)S(1)}, u32[]{:S(2)}, u32[]{:S(2)}) collective-permute-start(bf16[416,384]{1,0:T(8,128)(2,1)S(1)} %collective-permute-done.rest_0_), channel_id=1, source_target_pairs={{0,4},{1,5},{4,8},{5,9},{6,2},{7,3},{8,12},{9,13},{10,6},{11,7},{1... | collective-permute-start | bytes 958472 | tf_op jit(solution)/shard_map/ppermute | solution.py:24
  17.8 0.1 collective-permute-start.3
  17.9 3.0 %sib.1.total.near = f32[1024,768]{1,0:T(8,128)S(1)} custom-call(bf16[768,1024]{1,0:T(8,128)(2,1)S(1)} %get-tuple-element.114.own_t.a_1_, f32[1024,768]{1,0:T(8,128)S(1)} %get-tuple-element.90.total_in, bf16[2048,384]{1,0:T(8,128)(2,1)S(1)} %collective-permute-done.1.sib, f32[8,768]{1,0:T(8,128)S(1)} %get-tuple-element.78.levels.a_2_, ...), custom_call_target="tpu_custom_call", output_to_operand_aliasing={{}: (1, {})} | custom-call | flops 10000000000 | bytes 1 | tf_op jit(solution)/shard_map/sib/pallas_call | solution.py:497
  20.9 3.9 %collective-permute-start.12 = (bf16[384,384]{1,0:T(8,128)(2,1)S(1)}, bf16[384,384]{1,0:T(8,128)(2,1)S(1)}, u32[]{:S(2)}, u32[]{:S(2)}) collective-permute-start(bf16[384,384]{1,0:T(8,128)(2,1)S(1)} %collective-permute-done.4.rest_1_), channel_id=1, source_target_pairs={{0,4},{1,5},{4,8},{5,9},{6,2},{7,3},{8,12},{9,13},{10,6},{11,7},{1... | collective-permute-start | bytes 884744 | tf_op jit(solution)/shard_map/ppermute | solution.py:24
  24.8 3.2 %collective-permute-done.3.rest_2_ = bf16[432,384]{1,0:T(8,128)(2,1)S(1)} collective-permute-done((bf16[432,384]{1,0:T(8,128)(2,1)S(1)}, bf16[432,384]{1,0:T(8,128)(2,1)S(1)}, u32[]{:S(2)}, u32[]{:S(2)}) %collective-permute-start.3) | collective-permute-done | bytes 331808 | tf_op jit(solution)/shard_map/ppermute | solution.py:24
  28.0 3.5 %collective-permute-start.13 = (bf16[432,384]{1,0:T(8,128)(2,1)S(1)}, bf16[432,384]{1,0:T(8,128)(2,1)S(1)}, u32[]{:S(2)}, u32[]{:S(2)}) collective-permute-start(bf16[432,384]{1,0:T(8,128)(2,1)S(1)} %collective-permute-done.3.rest_2_), channel_id=1, source_target_pairs={{0,4},{1,5},{4,8},{5,9},{6,2},{7,3},{8,12},{9,13},{10,6},{11,7},{1... | collective-permute-start | bytes 995336 | tf_op jit(solution)/shard_map/ppermute | solution.py:24
  31.5 0.1 collective-permute-start.5
  31.6 2.8 %near_metric.1 = (f32[1152,128]{1,0:T(8,128)S(1)}, f32[1152,128]{1,0:T(8,128)S(1)}, s16[1216,128]{1,0:T(8,128)(2,1)S(1)}, s16[1216,128]{1,0:T(8,128)(2,1)S(1)}) custom-call(s32[1]{0:T(128)} %bitcast.me_ref.a_0_, f32[1024,768]{1,0:T(8,128)S(1)} %sib.1.total.near, bf16[1024,768]{1,0:T(8,128)(2,1)S(1)} %get-tuple-element.98.own_s), custom_call_target="tpu_custom_call" | custom-call | flops 10000000000 | bytes 1 | tf_op jit(solution)/shard_map/near_metric/pallas_call | solution.py:509
  34.4 0.9 collective-permute-done.8.rest_3_
  35.3 3.5 %collective-permute-start.10 = (bf16[416,384]{1,0:T(8,128)(2,1)S(1)}, bf16[416,384]{1,0:T(8,128)(2,1)S(1)}, u32[]{:S(2)}, u32[]{:S(2)}) collective-permute-start(bf16[416,384]{1,0:T(8,128)(2,1)S(1)} %collective-permute-done.8.rest_3_), channel_id=1, source_target_pairs={{0,4},{1,5},{4,8},{5,9},{6,2},{7,3},{8,12},{9,13},{10,6},{11,7},{1... | collective-permute-start | bytes 958472 | tf_op jit(solution)/shard_map/ppermute | solution.py:24
  38.8 0.1 collective-permute-start.6
  38.8 0.5 collective-permute-start.7
  39.3 0.2 collective-permute-done.13.rest_2_.a_5_
  39.6 0.2 maximum_select_fusion
  39.9 0.5 collective-permute-done.6.got_away
  40.4 0.4 collective-permute-done.7.got_keep
  40.9 0.2 collective-permute-done.5.rest_4_
  41.0 3.7 %collective-permute-start.11 = (bf16[416,384]{1,0:T(8,128)(2,1)S(1)}, bf16[416,384]{1,0:T(8,128)(2,1)S(1)}, u32[]{:S(2)}, u32[]{:S(2)}) collective-permute-start(bf16[416,384]{1,0:T(8,128)(2,1)S(1)} %collective-permute-done.5.rest_4_), channel_id=1, source_target_pairs={{0,4},{1,5},{4,8},{5,9},{6,2},{7,3},{8,12},{9,13},{10,6},{11,7},{1... | collective-permute-start | bytes 958472 | tf_op jit(solution)/shard_map/ppermute | solution.py:24
  44.7 0.4 chip.1
  45.2 2.7 %far2.1.total_in = f32[1024,768]{1,0:T(8,128)S(1)} custom-call(s32[1]{0:T(128)} %bitcast.me_ref.a_0_, bf16[768,1024]{1,0:T(8,128)(2,1)S(1)} %get-tuple-element.114.own_t.a_1_, f32[8,768]{1,0:T(8,128)S(1)} %get-tuple-element.78.levels.a_2_, f32[8,768]{1,0:T(8,128)S(1)} %get-tuple-element.79.weights.a_3_, bf16[416,384]{1,0:T(8,128)(2,1)S(1)} %collective-permute-done.rest_0_, ...), custom_call_target="tpu_custom_call" | custom-call | flops 10000000000 | bytes 1 | tf_op jit(solution)/shard_map/far2/pallas_call | solution.py:555
  47.9 2.7 %far3.1.a_4_ = f32[1024,768]{1,0:T(8,128)S(1)} custom-call(s32[1]{0:T(128)} %bitcast.me_ref.a_0_, bf16[768,1024]{1,0:T(8,128)(2,1)S(1)} %get-tuple-element.114.own_t.a_1_, f32[8,768]{1,0:T(8,128)S(1)} %get-tuple-element.78.levels.a_2_, f32[8,768]{1,0:T(8,128)S(1)} %get-tuple-element.79.weights.a_3_, ...), custom_call_target="tpu_custom_call", output_to_operand_aliasing={{}: (4, {})} | custom-call | flops 1 | bytes 1 | tf_op jit(solution)/shard_map/far3/pallas_call | solution.py:555
  50.8 0.5 collective-permute-start.15
  51.3 3.2 %collective-permute-done.17.across = s16[1216,128]{1,0:T(8,128)(2,1)S(1)} collective-permute-done((s16[1216,128]{1,0:T(8,128)(2,1)S(1)}, s16[1216,128]{1,0:T(8,128)(2,1)S(1)}, u32[]{:S(2)}, u32[]{:S(2)}) %collective-permute-start.17) | collective-permute-done | bytes 311328 | tf_op jit(solution)/shard_map/ppermute | solution.py:24
  54.6 1.9 %half.1.total_in = f32[1024,768]{1,0:T(8,128)S(1)} custom-call(s32[1]{0:T(128)} %bitcast.me_ref.a_0_, bf16[768,1024]{1,0:T(8,128)(2,1)S(1)} %get-tuple-element.114.own_t.a_1_, f32[8,768]{1,0:T(8,128)S(1)} %get-tuple-element.78.levels.a_2_, f32[8,768]{1,0:T(8,128)S(1)} %get-tuple-element.79.weights.a_3_, ...), custom_call_target="tpu_custom_call", output_to_operand_aliasing={{}: (4, {})} | custom-call | flops 1000000000 | bytes 1 | tf_op jit(solution)/shard_map/half/pallas_call | solution.py:555
  56.5 4.0 %last.1 = (f32[1024,768]{1,0:T(8,128)S(1)}, f32[2,1024,384]{2,1,0:T(8,128)}, f32[640,128]{1,0:T(8,128)S(1)}, f32[640,128]{1,0:T(8,128)S(1)}, bf16[1024,768]{1,0:...) custom-call(s32[1]{0:T(128)} %bitcast.me_ref.a_0_, ...), custom_call_target="tpu_custom_call", output_to_operand_aliasing={{0}: (4, {})} | custom-call | flops 1 | bytes 1 | tf_op jit(solution)/shard_map/last/pallas_call | solution.py:555
  60.5 0.6 collective-permute-start.19
  61.1 1.1 %corner.1 = (f32[512,128]{1,0:T(8,128)S(1)}, f32[512,128]{1,0:T(8,128)S(1)}) custom-call(s32[1]{0:T(128)} %bitcast.me_ref.a_0_, bf16[1024,768]{1,0:T(8,128)(2,1)S(1)} %get-tuple-element.131.high, bf16[1024,768]{1,0:T(8,128)(2,1)S(1)} %get-tuple-element.132.low, bf16[1024,768]{1,0:T(8,128)(2,1)S(1)} %get-tuple-element.98.own_s), custom_call_target="tpu_custom_call" | custom-call | flops 2000000000 | bytes 1 | tf_op jit(solution)/shard_map/corner/pallas_call | solution.py:593
  62.2 0.2 collective-permute-done.19.theirs
  62.3 0.4 collective-permute-start.23
  62.7 0.3 column.2
  63.0 2.7 %collective-permute-start.20 = (s16[176,128]{1,0:T(8,128)(2,1)S(1)}, s16[176,128]{1,0:T(8,128)(2,1)S(1)}, u32[]{:S(2)}, u32[]{:S(2)}) collective-permute-start(s16[176,128]{1,0:T(8,128)(2,1)S(1)} %get-tuple-element.138), channel_id=1, source_target_pairs={{0,12},{1,13},{2,14},{3,15},{4,8},{5,9},{6,10},{7,11},{8,4},{9,5},... | collective-permute-start | bytes 135176 | tf_op jit(solution)/shard_map/ppermute | solution.py:24
  65.6 0.4 collective-permute-start.21
  66.1 1.4 %collective-permute-start.22 = (s16[176,128]{1,0:T(8,128)(2,1)S(1)}, s16[176,128]{1,0:T(8,128)(2,1)S(1)}, u32[]{:S(2)}, u32[]{:S(2)}) collective-permute-start(s16[176,128]{1,0:T(8,128)(2,1)S(1)} %get-tuple-element.140), channel_id=1, source_target_pairs={{0,4},{1,5},{2,6},{3,7},{4,0},{5,1},{6,2},{7,3},{8,12},{9,13},{10,... | collective-permute-start | bytes 135176 | tf_op jit(solution)/shard_map/ppermute | solution.py:24
  67.4 0.5 column.3
  67.9 2.7 %collective-permute-start.24 = (s16[144,128]{1,0:T(8,128)(2,1)S(1)}, s16[144,128]{1,0:T(8,128)(2,1)S(1)}, u32[]{:S(2)}, u32[]{:S(2)}) collective-permute-start(s16[144,128]{1,0:T(8,128)(2,1)S(1)} %get-tuple-element.144), channel_id=1, source_target_pairs={{0,12},{1,13},{2,14},{3,15},{4,8},{5,9},{6,10},{7,11},{8,4},{9,5},... | collective-permute-start | bytes 110600 | tf_op jit(solution)/shard_map/ppermute | solution.py:24
  70.6 1.8 %collective-permute-start.26 = (s16[144,128]{1,0:T(8,128)(2,1)S(1)}, s16[144,128]{1,0:T(8,128)(2,1)S(1)}, u32[]{:S(2)}, u32[]{:S(2)}) collective-permute-start(s16[144,128]{1,0:T(8,128)(2,1)S(1)} %get-tuple-element.146), channel_id=1, source_target_pairs={{0,4},{1,5},{2,6},{3,7},{4,0},{5,1},{6,2},{7,3},{8,12},{9,13},{10,... | collective-permute-start | bytes 110600 | tf_op jit(solution)/shard_map/ppermute | solution.py:24
  72.4 1.5 %collective-permute-done.24.rest_5_ = s16[144,128]{1,0:T(8,128)(2,1)S(1)} collective-permute-done((s16[144,128]{1,0:T(8,128)(2,1)S(1)}, s16[144,128]{1,0:T(8,128)(2,1)S(1)}, u32[]{:S(2)}, u32[]{:S(2)}) %collective-permute-start.24) | collective-permute-done | bytes 36896 | tf_op jit(solution)/shard_map/ppermute | solution.py:24
  73.8 1.6 %collective-permute-done.25.rest_6_ = s16[144,128]{1,0:T(8,128)(2,1)S(1)} collective-permute-done((s16[144,128]{1,0:T(8,128)(2,1)S(1)}, s16[144,128]{1,0:T(8,128)(2,1)S(1)}, u32[]{:S(2)}, u32[]{:S(2)}) %collective-permute-start.25) | collective-permute-done | bytes 36896 | tf_op jit(solution)/shard_map/ppermute | solution.py:24
  75.4 0.2 sum_code.1
  75.6 0.9 %collective-permute-start.29 = (s16[304,128]{1,0:T(8,128)(2,1)S(1)}, s16[304,128]{1,0:T(8,128)(2,1)S(1)}, u32[]{:S(2)}, u32[]{:S(2)}) collective-permute-start(s16[304,128]{1,0:T(8,128)(2,1)S(1)} %sum_code.1), channel_id=1, source_target_pairs={{0,4},{1,5},{2,6},{3,7},{4,0},{5,1},{6,2},{7,3},{8,12},{9,13},{10,... | collective-permute-start | bytes 233480 | tf_op jit(solution)/shard_map/ppermute | solution.py:24
  76.5 1.5 %collective-permute-start.28 = (s16[304,128]{1,0:T(8,128)(2,1)S(1)}, s16[304,128]{1,0:T(8,128)(2,1)S(1)}, u32[]{:S(2)}, u32[]{:S(2)}) collective-permute-start(s16[304,128]{1,0:T(8,128)(2,1)S(1)} %sum_code.1), channel_id=1, source_target_pairs={{0,8},{1,9},{2,10},{3,11},{4,12},{5,13},{6,14},{7,15},{8,0},{9,1},... | collective-permute-start | bytes 233480 | tf_op jit(solution)/shard_map/ppermute | solution.py:24
  78.0 2.0 %collective-permute-start.27 = (s16[304,128]{1,0:T(8,128)(2,1)S(1)}, s16[304,128]{1,0:T(8,128)(2,1)S(1)}, u32[]{:S(2)}, u32[]{:S(2)}) collective-permute-start(s16[304,128]{1,0:T(8,128)(2,1)S(1)} %sum_code.1), channel_id=1, source_target_pairs={{0,12},{1,13},{2,14},{3,15},{4,8},{5,9},{6,10},{7,11},{8,4},{9,5},... | collective-permute-start | bytes 233480 | tf_op jit(solution)/shard_map/ppermute | solution.py:24
  80.0 1.2 %collective-permute-start.33 = (s16[304,128]{1,0:T(8,128)(2,1)S(1)}, s16[304,128]{1,0:T(8,128)(2,1)S(1)}, u32[]{:S(2)}, u32[]{:S(2)}) collective-permute-start(s16[304,128]{1,0:T(8,128)(2,1)S(1)} %sum_code.1), channel_id=1, source_target_pairs={{0,2},{1,3},{2,0},{3,1},{4,6},{5,7},{6,4},{7,5},{8,10},{9,11},{10,... | collective-permute-start | bytes 233480 | tf_op jit(solution)/shard_map/ppermute | solution.py:24
  81.3 1.7 %collective-permute-start.32 = (s16[304,128]{1,0:T(8,128)(2,1)S(1)}, s16[304,128]{1,0:T(8,128)(2,1)S(1)}, u32[]{:S(2)}, u32[]{:S(2)}) collective-permute-start(s16[304,128]{1,0:T(8,128)(2,1)S(1)} %collective-permute-done.29), channel_id=1, source_target_pairs={{0,2},{1,3},{2,0},{3,1},{4,6},{5,7},{6,4},{7,5},{8,10},{9,11},{10,... | collective-permute-start | bytes 233480 | tf_op jit(solution)/shard_map/ppermute | solution.py:24
  82.9 0.2 collective-permute-done.28
  83.1 0.2 collective-permute-start.31
  83.3 1.1 %collective-permute-done.27 = s16[304,128]{1,0:T(8,128)(2,1)S(1)} collective-permute-done((s16[304,128]{1,0:T(8,128)(2,1)S(1)}, s16[304,128]{1,0:T(8,128)(2,1)S(1)}, u32[]{:S(2)}, u32[]{:S(2)}) %collective-permute-start.27) | collective-permute-done | bytes 77856 | tf_op jit(solution)/shard_map/ppermute | solution.py:24
  84.4 0.9 collective-permute-start.30
  85.4 0.7 collective-permute-done.32
  86.1 1.5 %collective-permute-done.31 = s16[304,128]{1,0:T(8,128)(2,1)S(1)} collective-permute-done((s16[304,128]{1,0:T(8,128)(2,1)S(1)}, s16[304,128]{1,0:T(8,128)(2,1)S(1)}, u32[]{:S(2)}, u32[]{:S(2)}) %collective-permute-start.31) | collective-permute-done | bytes 77856 | tf_op jit(solution)/shard_map/ppermute | solution.py:24
  87.5 1.2 %collective-permute-done.30 = s16[304,128]{1,0:T(8,128)(2,1)S(1)} collective-permute-done((s16[304,128]{1,0:T(8,128)(2,1)S(1)}, s16[304,128]{1,0:T(8,128)(2,1)S(1)}, u32[]{:S(2)}, u32[]{:S(2)}) %collective-permute-start.30) | collective-permute-done | bytes 77856 | tf_op jit(solution)/shard_map/ppermute | solution.py:24
  88.9 1.9 %unpack.1 = (f32[1024,1024]{1,0:T(8,128)}, f32[4608,128]{1,0:T(8,128)S(1)}) custom-call(s32[1]{0:T(128)} %bitcast.me_ref.a_0_, s16[4,304,128]{2,1,0:T(8,128)(2,1)S(1)} %pad_add_fusion.a, s16[4,304,128]{2,1,0:T(8,128)(2,1)S(1)} %pad_add_fusion.1.b, s16[4,304,128]{2,1,0:T(8,128)(2,1)S(1)} %collective-permute-done.34.sib_a), custom_call_target="tpu_custom_call" | custom-call | flops 1000000000 | bytes 1 | tf_op jit(solution)/shard_map/unpack/pallas_call | solution.py:621
  90.8 1.7 %spread.1 = (f32[1024,1024]{1,0:T(8,128)}, f32[4608,128]{1,0:T(8,128)S(1)}) custom-call(s32[1]{0:T(128)} %bitcast.me_ref.a_0_, f32[1024,1024]{1,0:T(8,128)} %get-tuple-element.147.out_in, f32[4608,128]{1,0:T(8,128)S(1)} %get-tuple-element.148.packed_in, ...), custom_call_target="tpu_custom_call", output_to_operand_aliasing={{0}: (1, {}), {1}: (2, {})} | custom-call | flops 1 | bytes 1 | tf_op jit(solution)/shard_map/spread/pallas_call | solution.py:624
  (43 shorter events, 0.8 us)
Async XLA Ops:
  0.6 7.3 %copy-start.3 = (s32[16,384]{1,0:T(8,128)S(1)}, s32[16,384]{1,0:T(8,128)}, u32[]{:S(2)}) copy-start(s32[16,384]{1,0:T(8,128)} %maps_in.1) | copy-start | bytes 73732
  0.6 7.3 %copy-start.2 = (f32[8192]{0:T(1024)S(1)}, f32[8192]{0:T(1024)}, u32[]{:S(2)}) copy-start(f32[8192]{0:T(1024)} %param.8) | copy-start | bytes 98308
  0.7 7.3 %copy-start.5 = (f32[16,2]{0,1:T(2,128)S(1)}, f32[16,2]{0,1:T(2,128)}, u32[]{:S(2)}) copy-start(f32[16,2]{0,1:T(2,128)} %param.7) | copy-start | bytes 388
  1.7 7.6 %collective-permute-start.1 = (bf16[2048,384]{1,0:T(8,128)(2,1)}, bf16[2048,384]{1,0:T(8,128)(2,1)S(1)}, u32[]{:S(2)}, u32[]{:S(2)}) collective-permute-start(bf16[2048,384]{1,0:T(8,128)(2,1)} %bitcast.14), channel_id=1, source_target_pairs={{0,1},{1,0},{2,3},{3,2},{4,5},{5,4},{6,7},{7,6},{8,9},{9,8},{10,11... | collective-permute-start | bytes 4718600 | tf_op jit(solution)/shard_map/ppermute | solution.py:24
  2.2 11.9 %collective-permute-start = (bf16[416,384]{1,0:T(8,128)(2,1)S(1)}, bf16[416,384]{1,0:T(8,128)(2,1)S(1)}, u32[]{:S(2)}, u32[]{:S(2)}) collective-permute-start(bf16[416,384]{1,0:T(8,128)(2,1)S(1)} %slice.12), channel_id=1, source_target_pairs={{0,2},{1,3},{2,0},{3,1},{4,6},{5,7},{6,4},{7,5},{8,10},{9,11},{10,... | collective-permute-start | bytes 958472 | tf_op jit(solution)/shard_map/ppermute | solution.py:24
  4.8 3.2 %collective-permute-start.2 = (s32[1,3]{1,0:T(1,128)}, s32[1,3]{1,0:T(1,128)S(1)}, u32[]{:S(2)}, u32[]{:S(2)}) collective-permute-start(s32[1,3]{1,0:T(1,128)} %pairs.3), channel_id=1, source_target_pairs={{0,1},{1,0},{2,3},{3,2},{4,5},{5,4},{6,7},{7,6},{8,9},{9,8},{10,11... | collective-permute-start | bytes 44 | tf_op jit(solution)/shard_map/ppermute | solution.py:24
  5.0 1.4 %copy-start = (bf16[1,2,1024,384]{3,2,1,0:T(8,128)(2,1)S(1)}, bf16[1,2,1024,384]{3,2,1,0:T(8,128)(2,1)}, u32[]{:S(2)}) copy-start(bf16[1,2,1024,384]{3,2,1,0:T(8,128)(2,1)} %param.5) | copy-start | bytes 4718596
  6.4 0.7 copy-start.4
  9.3 11.6 %collective-permute-start.4 = (bf16[384,384]{1,0:T(8,128)(2,1)S(1)}, bf16[384,384]{1,0:T(8,128)(2,1)S(1)}, u32[]{:S(2)}, u32[]{:S(2)}) collective-permute-start(bf16[384,384]{1,0:T(8,128)(2,1)S(1)} %get-tuple-element.88), channel_id=1, source_target_pairs={{0,2},{1,3},{2,0},{3,1},{4,6},{5,7},{6,4},{7,5},{8,10},{9,11},{10,... | collective-permute-start | bytes 884744 | tf_op jit(solution)/shard_map/ppermute | solution.py:24
  9.7 1.4 %copy-start.1 = (bf16[1,2,1024,384]{3,2,1,0:T(8,128)(2,1)S(1)}, bf16[1,2,1024,384]{3,2,1,0:T(8,128)(2,1)}, u32[]{:S(2)}) copy-start(bf16[1,2,1024,384]{3,2,1,0:T(8,128)(2,1)} %param.5) | copy-start | bytes 4718596
  14.1 20.2 %collective-permute-start.9 = (bf16[416,384]{1,0:T(8,128)(2,1)S(1)}, bf16[416,384]{1,0:T(8,128)(2,1)S(1)}, u32[]{:S(2)}, u32[]{:S(2)}) collective-permute-start(bf16[416,384]{1,0:T(8,128)(2,1)S(1)} %collective-permute-done.rest_0_), channel_id=1, source_target_pairs={{0,4},{1,5},{4,8},{5,9},{6,2},{7,3},{8,12},{9,13},{10,6},{11,7},{1... | collective-permute-start | bytes 958472 | tf_op jit(solution)/shard_map/ppermute | solution.py:24
  17.8 10.2 %collective-permute-start.3 = (bf16[432,384]{1,0:T(8,128)(2,1)S(1)}, bf16[432,384]{1,0:T(8,128)(2,1)S(1)}, u32[]{:S(2)}, u32[]{:S(2)}) collective-permute-start(bf16[432,384]{1,0:T(8,128)(2,1)S(1)} %get-tuple-element.86), channel_id=1, source_target_pairs={{0,2},{1,3},{2,0},{3,1},{4,6},{5,7},{6,4},{7,5},{8,10},{9,11},{10,... | collective-permute-start | bytes 995336 | tf_op jit(solution)/shard_map/ppermute | solution.py:24
  20.9 18.0 %collective-permute-start.12 = (bf16[384,384]{1,0:T(8,128)(2,1)S(1)}, bf16[384,384]{1,0:T(8,128)(2,1)S(1)}, u32[]{:S(2)}, u32[]{:S(2)}) collective-permute-start(bf16[384,384]{1,0:T(8,128)(2,1)S(1)} %collective-permute-done.4.rest_1_), channel_id=1, source_target_pairs={{0,4},{1,5},{4,8},{5,9},{6,2},{7,3},{8,12},{9,13},{10,6},{11,7},{1... | collective-permute-start | bytes 884744 | tf_op jit(solution)/shard_map/ppermute | solution.py:24
  24.7 10.5 %collective-permute-start.8 = (bf16[416,384]{1,0:T(8,128)(2,1)S(1)}, bf16[416,384]{1,0:T(8,128)(2,1)S(1)}, u32[]{:S(2)}, u32[]{:S(2)}) collective-permute-start(bf16[416,384]{1,0:T(8,128)(2,1)S(1)} %get-tuple-element.102), channel_id=1, source_target_pairs={{0,2},{1,3},{2,0},{3,1},{4,6},{5,7},{6,4},{7,5},{8,10},{9,11},{10,... | collective-permute-start | bytes 958472 | tf_op jit(solution)/shard_map/ppermute | solution.py:24
  28.0 11.6 %collective-permute-start.13 = (bf16[432,384]{1,0:T(8,128)(2,1)S(1)}, bf16[432,384]{1,0:T(8,128)(2,1)S(1)}, u32[]{:S(2)}, u32[]{:S(2)}) collective-permute-start(bf16[432,384]{1,0:T(8,128)(2,1)S(1)} %collective-permute-done.3.rest_2_), channel_id=1, source_target_pairs={{0,4},{1,5},{4,8},{5,9},{6,2},{7,3},{8,12},{9,13},{10,6},{11,7},{1... | collective-permute-start | bytes 995336 | tf_op jit(solution)/shard_map/ppermute | solution.py:24
  31.5 9.5 %collective-permute-start.5 = (bf16[416,384]{1,0:T(8,128)(2,1)S(1)}, bf16[416,384]{1,0:T(8,128)(2,1)S(1)}, u32[]{:S(2)}, u32[]{:S(2)}) collective-permute-start(bf16[416,384]{1,0:T(8,128)(2,1)S(1)} %get-tuple-element.94), channel_id=1, source_target_pairs={{0,2},{1,3},{2,0},{3,1},{4,6},{5,7},{6,4},{7,5},{8,10},{9,11},{10,... | collective-permute-start | bytes 958472 | tf_op jit(solution)/shard_map/ppermute | solution.py:24
  35.3 9.9 %collective-permute-start.10 = (bf16[416,384]{1,0:T(8,128)(2,1)S(1)}, bf16[416,384]{1,0:T(8,128)(2,1)S(1)}, u32[]{:S(2)}, u32[]{:S(2)}) collective-permute-start(bf16[416,384]{1,0:T(8,128)(2,1)S(1)} %collective-permute-done.8.rest_3_), channel_id=1, source_target_pairs={{0,4},{1,5},{4,8},{5,9},{6,2},{7,3},{8,12},{9,13},{10,6},{11,7},{1... | collective-permute-start | bytes 958472 | tf_op jit(solution)/shard_map/ppermute | solution.py:24
  38.8 1.7 %collective-permute-start.6 = (s16[1216,128]{1,0:T(8,128)(2,1)S(1)}, s16[1216,128]{1,0:T(8,128)(2,1)S(1)}, u32[]{:S(2)}, u32[]{:S(2)}) collective-permute-start(s16[1216,128]{1,0:T(8,128)(2,1)S(1)} %get-tuple-element.99), channel_id=1, source_target_pairs={{0,1},{1,0},{2,3},{3,2},{4,5},{5,4},{6,7},{7,6},{8,9},{9,8},{10,11... | collective-permute-start | bytes 933896 | tf_op jit(solution)/shard_map/ppermute | solution.py:24
  38.8 2.0 %collective-permute-start.7 = (s16[1216,128]{1,0:T(8,128)(2,1)S(1)}, s16[1216,128]{1,0:T(8,128)(2,1)S(1)}, u32[]{:S(2)}, u32[]{:S(2)}) collective-permute-start(s16[1216,128]{1,0:T(8,128)(2,1)S(1)} %get-tuple-element.100), channel_id=1, source_target_pairs={{0,1},{1,0},{2,3},{3,2},{4,5},{5,4},{6,7},{7,6},{8,9},{9,8},{10,11... | collective-permute-start | bytes 933896 | tf_op jit(solution)/shard_map/ppermute | solution.py:24
  39.8 8.1 %collective-permute-start.14 = (bf16[1232,384]{1,0:T(8,128)(2,1)S(1)}, bf16[1232,384]{1,0:T(8,128)(2,1)S(1)}, u32[]{:S(2)}, u32[]{:S(2)}) collective-permute-start(bf16[1232,384]{1,0:T(8,128)(2,1)S(1)} %maximum_select_fusion), channel_id=1, source_target_pairs={{0,1},{1,0},{2,3},{3,2},{4,5},{5,4},{6,7},{7,6},{8,9},{9,8},{10,11... | collective-permute-start | bytes 2838536 | tf_op jit(solution)/shard_map/ppermute | solution.py:24
  41.0 13.4 %collective-permute-start.11 = (bf16[416,384]{1,0:T(8,128)(2,1)S(1)}, bf16[416,384]{1,0:T(8,128)(2,1)S(1)}, u32[]{:S(2)}, u32[]{:S(2)}) collective-permute-start(bf16[416,384]{1,0:T(8,128)(2,1)S(1)} %collective-permute-done.5.rest_4_), channel_id=1, source_target_pairs={{0,4},{1,5},{4,8},{5,9},{6,2},{7,3},{8,12},{9,13},{10,6},{11,7},{1... | collective-permute-start | bytes 958472 | tf_op jit(solution)/shard_map/ppermute | solution.py:24
  45.1 9.3 %collective-permute-start.17 = (s16[1216,128]{1,0:T(8,128)(2,1)S(1)}, s16[1216,128]{1,0:T(8,128)(2,1)S(1)}, u32[]{:S(2)}, u32[]{:S(2)}) collective-permute-start(s16[1216,128]{1,0:T(8,128)(2,1)S(1)} %get-tuple-element.123), channel_id=1, source_target_pairs={{0,2},{1,3},{2,0},{3,1},{4,6},{5,7},{6,4},{7,5},{8,10},{9,11},{10,... | collective-permute-start | bytes 933896 | tf_op jit(solution)/shard_map/ppermute | solution.py:24
  50.7 3.8 %collective-permute-start.16 = (bf16[208,384]{1,0:T(8,128)(2,1)S(1)}, bf16[208,384]{1,0:T(8,128)(2,1)S(1)}, u32[]{:S(2)}, u32[]{:S(2)}) collective-permute-start(bf16[208,384]{1,0:T(8,128)(2,1)S(1)} %get-tuple-element.150), channel_id=1, source_target_pairs={{0,1},{1,0},{2,3},{3,2},{4,5},{5,4},{6,7},{7,6},{8,9},{9,8},{10,11... | collective-permute-start | bytes 479240 | tf_op jit(solution)/shard_map/ppermute | solution.py:24
  50.8 3.7 %collective-permute-start.15 = (bf16[208,384]{1,0:T(8,128)(2,1)S(1)}, bf16[208,384]{1,0:T(8,128)(2,1)S(1)}, u32[]{:S(2)}, u32[]{:S(2)}) collective-permute-start(bf16[208,384]{1,0:T(8,128)(2,1)S(1)} %get-tuple-element.151), channel_id=1, source_target_pairs={{0,1},{1,0},{2,3},{3,2},{4,5},{5,4},{6,7},{7,6},{8,9},{9,8},{10,11... | collective-permute-start | bytes 479240 | tf_op jit(solution)/shard_map/ppermute | solution.py:24
  54.5 2.0 %collective-permute-start.18 = (bf16[416,384]{1,0:T(8,128)(2,1)S(1)}, bf16[416,384]{1,0:T(8,128)(2,1)S(1)}, u32[]{:S(2)}, u32[]{:S(2)}) collective-permute-start(bf16[416,384]{1,0:T(8,128)(2,1)S(1)} %broadcast_select_fusion), channel_id=1, source_target_pairs={{0,1},{1,0},{2,3},{3,2},{4,5},{5,4},{6,7},{7,6},{8,9},{9,8},{10,11... | collective-permute-start | bytes 958472 | tf_op jit(solution)/shard_map/ppermute | solution.py:24
  60.5 1.8 %collective-permute-start.19 = (f32[640,128]{1,0:T(8,128)S(1)}, f32[640,128]{1,0:T(8,128)S(1)}, u32[]{:S(2)}, u32[]{:S(2)}) collective-permute-start(f32[640,128]{1,0:T(8,128)S(1)} %get-tuple-element.130), channel_id=1, source_target_pairs={{0,1},{1,0},{2,3},{3,2},{4,5},{5,4},{6,7},{7,6},{8,9},{9,8},{10,11... | collective-permute-start | bytes 983048 | tf_op jit(solution)/shard_map/ppermute | solution.py:24
  62.3 5.1 %collective-permute-start.23 = (f32[512,128]{1,0:T(8,128)S(1)}, f32[512,128]{1,0:T(8,128)S(1)}, u32[]{:S(2)}, u32[]{:S(2)}) collective-permute-start(f32[512,128]{1,0:T(8,128)S(1)} %get-tuple-element.142), channel_id=1, source_target_pairs={{0,1},{1,0},{2,3},{3,2},{4,5},{5,4},{6,7},{7,6},{8,9},{9,8},{10,11... | collective-permute-start | bytes 786440 | tf_op jit(solution)/shard_map/ppermute | solution.py:24
  63.0 7.6 %collective-permute-start.20 = (s16[176,128]{1,0:T(8,128)(2,1)S(1)}, s16[176,128]{1,0:T(8,128)(2,1)S(1)}, u32[]{:S(2)}, u32[]{:S(2)}) collective-permute-start(s16[176,128]{1,0:T(8,128)(2,1)S(1)} %get-tuple-element.138), channel_id=1, source_target_pairs={{0,12},{1,13},{2,14},{3,15},{4,8},{5,9},{6,10},{7,11},{8,4},{9,5},... | collective-permute-start | bytes 135176 | tf_op jit(solution)/shard_map/ppermute | solution.py:24
  65.6 6.7 %collective-permute-start.21 = (s16[176,128]{1,0:T(8,128)(2,1)S(1)}, s16[176,128]{1,0:T(8,128)(2,1)S(1)}, u32[]{:S(2)}, u32[]{:S(2)}) collective-permute-start(s16[176,128]{1,0:T(8,128)(2,1)S(1)} %get-tuple-element.139), channel_id=1, source_target_pairs={{0,8},{1,9},{2,10},{3,11},{4,12},{5,13},{6,14},{7,15},{8,0},{9,1},... | collective-permute-start | bytes 135176 | tf_op jit(solution)/shard_map/ppermute | solution.py:24
  66.1 6.3 %collective-permute-start.22 = (s16[176,128]{1,0:T(8,128)(2,1)S(1)}, s16[176,128]{1,0:T(8,128)(2,1)S(1)}, u32[]{:S(2)}, u32[]{:S(2)}) collective-permute-start(s16[176,128]{1,0:T(8,128)(2,1)S(1)} %get-tuple-element.140), channel_id=1, source_target_pairs={{0,4},{1,5},{2,6},{3,7},{4,0},{5,1},{6,2},{7,3},{8,12},{9,13},{10,... | collective-permute-start | bytes 135176 | tf_op jit(solution)/shard_map/ppermute | solution.py:24
  67.9 5.9 %collective-permute-start.24 = (s16[144,128]{1,0:T(8,128)(2,1)S(1)}, s16[144,128]{1,0:T(8,128)(2,1)S(1)}, u32[]{:S(2)}, u32[]{:S(2)}) collective-permute-start(s16[144,128]{1,0:T(8,128)(2,1)S(1)} %get-tuple-element.144), channel_id=1, source_target_pairs={{0,12},{1,13},{2,14},{3,15},{4,8},{5,9},{6,10},{7,11},{8,4},{9,5},... | collective-permute-start | bytes 110600 | tf_op jit(solution)/shard_map/ppermute | solution.py:24
  70.6 4.9 %collective-permute-start.25 = (s16[144,128]{1,0:T(8,128)(2,1)S(1)}, s16[144,128]{1,0:T(8,128)(2,1)S(1)}, u32[]{:S(2)}, u32[]{:S(2)}) collective-permute-start(s16[144,128]{1,0:T(8,128)(2,1)S(1)} %get-tuple-element.145), channel_id=1, source_target_pairs={{0,8},{1,9},{2,10},{3,11},{4,12},{5,13},{6,14},{7,15},{8,0},{9,1},... | collective-permute-start | bytes 110600 | tf_op jit(solution)/shard_map/ppermute | solution.py:24
  70.6 4.9 %collective-permute-start.26 = (s16[144,128]{1,0:T(8,128)(2,1)S(1)}, s16[144,128]{1,0:T(8,128)(2,1)S(1)}, u32[]{:S(2)}, u32[]{:S(2)}) collective-permute-start(s16[144,128]{1,0:T(8,128)(2,1)S(1)} %get-tuple-element.146), channel_id=1, source_target_pairs={{0,4},{1,5},{2,6},{3,7},{4,0},{5,1},{6,2},{7,3},{8,12},{9,13},{10,... | collective-permute-start | bytes 110600 | tf_op jit(solution)/shard_map/ppermute | solution.py:24
  75.6 5.7 %collective-permute-start.29 = (s16[304,128]{1,0:T(8,128)(2,1)S(1)}, s16[304,128]{1,0:T(8,128)(2,1)S(1)}, u32[]{:S(2)}, u32[]{:S(2)}) collective-permute-start(s16[304,128]{1,0:T(8,128)(2,1)S(1)} %sum_code.1), channel_id=1, source_target_pairs={{0,4},{1,5},{2,6},{3,7},{4,0},{5,1},{6,2},{7,3},{8,12},{9,13},{10,... | collective-permute-start | bytes 233480 | tf_op jit(solution)/shard_map/ppermute | solution.py:24
  76.5 6.6 %collective-permute-start.28 = (s16[304,128]{1,0:T(8,128)(2,1)S(1)}, s16[304,128]{1,0:T(8,128)(2,1)S(1)}, u32[]{:S(2)}, u32[]{:S(2)}) collective-permute-start(s16[304,128]{1,0:T(8,128)(2,1)S(1)} %sum_code.1), channel_id=1, source_target_pairs={{0,8},{1,9},{2,10},{3,11},{4,12},{5,13},{6,14},{7,15},{8,0},{9,1},... | collective-permute-start | bytes 233480 | tf_op jit(solution)/shard_map/ppermute | solution.py:24
  78.0 6.3 %collective-permute-start.27 = (s16[304,128]{1,0:T(8,128)(2,1)S(1)}, s16[304,128]{1,0:T(8,128)(2,1)S(1)}, u32[]{:S(2)}, u32[]{:S(2)}) collective-permute-start(s16[304,128]{1,0:T(8,128)(2,1)S(1)} %sum_code.1), channel_id=1, source_target_pairs={{0,12},{1,13},{2,14},{3,15},{4,8},{5,9},{6,10},{7,11},{8,4},{9,5},... | collective-permute-start | bytes 233480 | tf_op jit(solution)/shard_map/ppermute | solution.py:24
  80.0 5.3 %collective-permute-start.33 = (s16[304,128]{1,0:T(8,128)(2,1)S(1)}, s16[304,128]{1,0:T(8,128)(2,1)S(1)}, u32[]{:S(2)}, u32[]{:S(2)}) collective-permute-start(s16[304,128]{1,0:T(8,128)(2,1)S(1)} %sum_code.1), channel_id=1, source_target_pairs={{0,2},{1,3},{2,0},{3,1},{4,6},{5,7},{6,4},{7,5},{8,10},{9,11},{10,... | collective-permute-start | bytes 233480 | tf_op jit(solution)/shard_map/ppermute | solution.py:24
  81.3 4.8 %collective-permute-start.32 = (s16[304,128]{1,0:T(8,128)(2,1)S(1)}, s16[304,128]{1,0:T(8,128)(2,1)S(1)}, u32[]{:S(2)}, u32[]{:S(2)}) collective-permute-start(s16[304,128]{1,0:T(8,128)(2,1)S(1)} %collective-permute-done.29), channel_id=1, source_target_pairs={{0,2},{1,3},{2,0},{3,1},{4,6},{5,7},{6,4},{7,5},{8,10},{9,11},{10,... | collective-permute-start | bytes 233480 | tf_op jit(solution)/shard_map/ppermute | solution.py:24
  83.1 4.4 %collective-permute-start.31 = (s16[304,128]{1,0:T(8,128)(2,1)S(1)}, s16[304,128]{1,0:T(8,128)(2,1)S(1)}, u32[]{:S(2)}, u32[]{:S(2)}) collective-permute-start(s16[304,128]{1,0:T(8,128)(2,1)S(1)} %collective-permute-done.28), channel_id=1, source_target_pairs={{0,2},{1,3},{2,0},{3,1},{4,6},{5,7},{6,4},{7,5},{8,10},{9,11},{10,... | collective-permute-start | bytes 233480 | tf_op jit(solution)/shard_map/ppermute | solution.py:24
  84.4 4.4 %collective-permute-start.30 = (s16[304,128]{1,0:T(8,128)(2,1)S(1)}, s16[304,128]{1,0:T(8,128)(2,1)S(1)}, u32[]{:S(2)}, u32[]{:S(2)}) collective-permute-start(s16[304,128]{1,0:T(8,128)(2,1)S(1)} %collective-permute-done.27), channel_id=1, source_target_pairs={{0,2},{1,3},{2,0},{3,1},{4,6},{5,7},{6,4},{7,5},{8,10},{9,11},{10,... | collective-permute-start | bytes 233480 | tf_op jit(solution)/shard_map/ppermute | solution.py:24
  85.3 3.6 %collective-permute-start.34 = (s16[4,304,128]{2,1,0:T(8,128)(2,1)S(1)}, s16[4,304,128]{2,1,0:T(8,128)(2,1)S(1)}, u32[]{:S(2)}, u32[]{:S(2)}) collective-permute-start(s16[4,304,128]{2,1,0:T(8,128)(2,1)S(1)} %pad_add_fusion.a), channel_id=1, source_target_pairs={{0,1},{1,0},{2,3},{3,2},{4,5},{5,4},{6,7},{7,6},{8,9},{9,8},{10,11... | collective-permute-start | bytes 933896 | tf_op jit(solution)/shard_map/ppermute | solution.py:24
  88.8 2.0 %collective-permute-start.35 = (s16[4,304,128]{2,1,0:T(8,128)(2,1)S(1)}, s16[4,304,128]{2,1,0:T(8,128)(2,1)S(1)}, u32[]{:S(2)}, u32[]{:S(2)}) collective-permute-start(s16[4,304,128]{2,1,0:T(8,128)(2,1)S(1)} %pad_add_fusion.1.b), channel_id=1, source_target_pairs={{0,1},{1,0},{2,3},{3,2},{4,5},{5,4},{6,7},{7,6},{8,9},{9,8},{10,11... | collective-permute-start | bytes 933896 | tf_op jit(solution)/shard_map/ppermute | solution.py:24

commit v13 on v11

--- a/solution.py
+++ b/solution.py
@@ -388,7 +388,7 @@
 def unpack(src, which, side, z, packed):
     plane = packed.shape[0] // 2
     for t in range(4):
-        value = decode(src[t])
+        value = decode(src[3 - t])
         used = 0
         for first, n in ((which * (plane // 18) * 5, plane // 18 * 5), (plane // 18 * (10 + which * 4), plane // 18 * 4)):
             piece = n // 4
@@ -650,7 +650,7 @@
 
     column = [mine] + [swapped(mine, 4 * t) for t in (1, 2, 3)]
     across = [swapped(c, 2) for c in column]
-    a, b = jnp.stack(column), jnp.stack(across)
+    a, b = jnp.stack(column[::-1]), jnp.stack(across[::-1])
     sib_a, sib_b = swapped(a, 1), swapped(b, 1)
     whole = jax.ShapeDtypeStruct((aux, aux), F32)
     scratch = [dma(2 + aux // 2 // LANES), pltpu.VMEM((aux, aux), F32)]

time: 94.2 us -> 92.9 us (0.986)
  waiting for transfers between devices: 17.8 us -> 16.6 us
    ppermute x36, waiting for transfers between devices: 17.8 us -> 16.6 us  [move(): return lax.ppermute(x, 'dom', pairs)]
where the time goes in v13:
time: 92.9 us; the launch traced here: 92.6 us
  starting transfers between devices  41.8 us (45%)
  Pallas kernels  28.1 us (30%)
  waiting for transfers between devices  16.6 us (18%)
  local copies, waits for them, and re-layouts  4.53 us (5%)
  between operations  1.25 us (1%)
    ppermute x36, starting transfers between devices, move(): return lax.ppermute(x, 'dom', pairs)  41.8 us
    ppermute x36, waiting for transfers between devices, move(): return lax.ppermute(x, 'dom', pairs)  16.6 us
    pallas_call x4, Pallas kernels, pair_step(): kernel(functools.partial(body, plan, names, step), name, [smem] + [vmem]...  11.2 us
    unnamed x12, local copies, waits for them, and re-layouts  3.48 us
    pallas_call x1, Pallas kernels, shards(): kernel(own_kernel, 'own', [hbm, vmem, vmem], (jax.ShapeDtypeStruct((wide,...  3.01 us
    pallas_call x1, Pallas kernels, shards(): kernel(sib_kernel, 'sib', [vmem, vmem, hbm, vmem, vmem], total_t, vmem, [...  2.98 us
    pallas_call x1, Pallas kernels, shards(): kernel(near_metric_kernel, 'near_metric', [smem, vmem, vmem], (plain(uppe...  2.76 us
    pallas_call x1, Pallas kernels, shards(): kernel(unpack_kernel, 'unpack', [smem] + [vmem] * 3, (whole, plain(upper)...  1.87 us
  transfers between devices with their start and end apart: 36, of which 15 were waited for; matrix products, arithmetic and copies ran while one was open for 0% of the time, Pallas kernels for 24%

profile of v13, /device:TPU:0, one launch (start us, length us, event | category | flops | bytes accessed | tf_op | source)
XLA Modules:
  0.0 92.6 jit_solution(16414355900486050797)
XLA Ops:
  0.7 1.0 %slice.12 = bf16[416,384]{1,0:T(8,128)(2,1)S(1)} slice(bf16[2048,384]{1,0:T(8,128)(2,1)} %bitcast.13), slice={[0:416], [0:384]} | slice | bytes 638976 | tf_op jit(solution)/shard_map/slice | solution.py:502
  1.7 0.5 collective-permute-start.1
  2.2 2.6 %collective-permute-start = (bf16[416,384]{1,0:T(8,128)(2,1)S(1)}, bf16[416,384]{1,0:T(8,128)(2,1)S(1)}, u32[]{:S(2)}, u32[]{:S(2)}) collective-permute-start(bf16[416,384]{1,0:T(8,128)(2,1)S(1)} %slice.12), channel_id=1, source_target_pairs={{0,2},{1,3},{2,0},{3,1},{4,6},{5,7},{6,4},{7,5},{8,10},{9,11},{10,... | collective-permute-start | bytes 958472 | tf_op jit(solution)/shard_map/ppermute | solution.py:24
  4.8 0.2 collective-permute-start.2
  5.0 1.4 %copy-done = bf16[1,2,1024,384]{3,2,1,0:T(8,128)(2,1)S(1)} copy-done((bf16[1,2,1024,384]{3,2,1,0:T(8,128)(2,1)S(1)}, bf16[1,2,1024,384]{3,2,1,0:T(8,128)(2,1)}, u32[]{:S(2)}) %copy-start) | copy-done | bytes 1572888
  6.4 0.7 copy-done.4
  7.0 0.9 %split.1 = (bf16[384,384]{1,0:T(8,128)(2,1)S(1)}, bf16[432,384]{1,0:T(8,128)(2,1)S(1)}, bf16[416,384]{1,0:T(8,128)(2,1)S(1)}, bf16[416,384]{1,0:T(8,128)(2,1)S(1)}) custom-call(s32[1]{0:T(128)} %bitcast.me_ref.a_0_, s32[1,3]{1,0:T(1,128)S(1)} %copy-done.4, bf16[2048,384]{1,0:T(8,128)(2,1)S(1)} %bitcast.15), custom_call_target="tpu_custom_call" | custom-call | flops 1 | bytes 1 | tf_op jit(solution)/shard_map/split/pallas_call | solution.py:508
  8.0 1.3 %prep.1 = (f32[8,768]{1,0:T(8,128)S(1)}, f32[8,768]{1,0:T(8,128)S(1)}) custom-call(s32[1]{0:T(128)} %bitcast.me_ref.a_0_, s32[1,3]{1,0:T(1,128)S(1)} %copy-done.4, s32[1,3]{1,0:T(1,128)S(1)} %collective-permute-done.2.sib_pairs, f32[2,16]{1,0:T(2,128)S(1)} %bitcast.19, f32[64,128]{1,0:T(8,128)S(1)} %bitcast.18, s32[16,384]{1,0:T(8,128)S(1)} %copy-done.3), custom_call_target="tpu_custom_call" | custom-call | flops 1 | bytes 1 | tf_op jit(solution)/shard_map/prep/pallas_call | solution.py:516
  9.3 0.4 collective-permute-start.4
  9.7 1.4 %copy-done.1 = bf16[1,2,1024,384]{3,2,1,0:T(8,128)(2,1)S(1)} copy-done((bf16[1,2,1024,384]{3,2,1,0:T(8,128)(2,1)S(1)}, bf16[1,2,1024,384]{3,2,1,0:T(8,128)(2,1)}, u32[]{:S(2)}) %copy-start.1) | copy-done | bytes 1572888
  11.1 3.0 %own.1 = (bf16[768,1024]{1,0:T(8,128)(2,1)S(1)}, bf16[1024,768]{1,0:T(8,128)(2,1)S(1)}, f32[1024,768]{1,0:T(8,128)S(1)}) custom-call(bf16[2048,384]{1,0:T(8,128)(2,1)S(1)} %bitcast.16, f32[8,768]{1,0:T(8,128)S(1)} %get-tuple-element.79.levels.a_2_, f32[8,768]{1,0:T(8,128)S(1)} %get-tuple-element.80.weights.a_3_), custom_call_target="tpu_custom_call" | custom-call | flops 20000000000 | bytes 1 | tf_op jit(solution)/shard_map/own/pallas_call | solution.py:521
  14.1 3.7 %collective-permute-start.9 = (bf16[416,384]{1,0:T(8,128)(2,1)S(1)}, bf16[416,384]{1,0:T(8,128)(2,1)S(1)}, u32[]{:S(2)}, u32[]{:S(2)}) collective-permute-start(bf16[416,384]{1,0:T(8,128)(2,1)S(1)} %collective-permute-done.rest_0_), channel_id=1, source_target_pairs={{0,4},{1,5},{4,8},{5,9},{6,2},{7,3},{8,12},{9,13},{10,6},{11,7},{1... | collective-permute-start | bytes 958472 | tf_op jit(solution)/shard_map/ppermute | solution.py:24
  17.8 0.1 collective-permute-start.3
  17.9 3.0 %sib.1.total.near = f32[1024,768]{1,0:T(8,128)S(1)} custom-call(bf16[768,1024]{1,0:T(8,128)(2,1)S(1)} %get-tuple-element.115.own_t.a_1_, f32[1024,768]{1,0:T(8,128)S(1)} %get-tuple-element.91.total_in, bf16[2048,384]{1,0:T(8,128)(2,1)S(1)} %collective-permute-done.1.sib, f32[8,768]{1,0:T(8,128)S(1)} %get-tuple-element.79.levels.a_2_, ...), custom_call_target="tpu_custom_call", output_to_operand_aliasing={{}: (1, {})} | custom-call | flops 10000000000 | bytes 1 | tf_op jit(solution)/shard_map/sib/pallas_call | solution.py:531
  20.9 3.9 %collective-permute-start.12 = (bf16[384,384]{1,0:T(8,128)(2,1)S(1)}, bf16[384,384]{1,0:T(8,128)(2,1)S(1)}, u32[]{:S(2)}, u32[]{:S(2)}) collective-permute-start(bf16[384,384]{1,0:T(8,128)(2,1)S(1)} %collective-permute-done.4.rest_1_), channel_id=1, source_target_pairs={{0,4},{1,5},{4,8},{5,9},{6,2},{7,3},{8,12},{9,13},{10,6},{11,7},{1... | collective-permute-start | bytes 884744 | tf_op jit(solution)/shard_map/ppermute | solution.py:24
  24.7 0.1 collective-permute-start.8
  24.8 3.2 %collective-permute-done.3.rest_2_ = bf16[432,384]{1,0:T(8,128)(2,1)S(1)} collective-permute-done((bf16[432,384]{1,0:T(8,128)(2,1)S(1)}, bf16[432,384]{1,0:T(8,128)(2,1)S(1)}, u32[]{:S(2)}, u32[]{:S(2)}) %collective-permute-start.3) | collective-permute-done | bytes 331808 | tf_op jit(solution)/shard_map/ppermute | solution.py:24
  28.0 3.5 %collective-permute-start.13 = (bf16[432,384]{1,0:T(8,128)(2,1)S(1)}, bf16[432,384]{1,0:T(8,128)(2,1)S(1)}, u32[]{:S(2)}, u32[]{:S(2)}) collective-permute-start(bf16[432,384]{1,0:T(8,128)(2,1)S(1)} %collective-permute-done.3.rest_2_), channel_id=1, source_target_pairs={{0,4},{1,5},{4,8},{5,9},{6,2},{7,3},{8,12},{9,13},{10,6},{11,7},{1... | collective-permute-start | bytes 995336 | tf_op jit(solution)/shard_map/ppermute | solution.py:24
  31.5 0.1 collective-permute-start.5
  31.6 2.8 %near_metric.1 = (f32[1152,128]{1,0:T(8,128)S(1)}, f32[1152,128]{1,0:T(8,128)S(1)}, s16[1216,128]{1,0:T(8,128)(2,1)S(1)}, s16[1216,128]{1,0:T(8,128)(2,1)S(1)}) custom-call(s32[1]{0:T(128)} %bitcast.me_ref.a_0_, f32[1024,768]{1,0:T(8,128)S(1)} %sib.1.total.near, bf16[1024,768]{1,0:T(8,128)(2,1)S(1)} %get-tuple-element.99.own_s), custom_call_target="tpu_custom_call" | custom-call | flops 10000000000 | bytes 1 | tf_op jit(solution)/shard_map/near_metric/pallas_call | solution.py:543
  34.4 0.9 collective-permute-done.8.rest_3_
  35.3 3.5 %collective-permute-start.10 = (bf16[416,384]{1,0:T(8,128)(2,1)S(1)}, bf16[416,384]{1,0:T(8,128)(2,1)S(1)}, u32[]{:S(2)}, u32[]{:S(2)}) collective-permute-start(bf16[416,384]{1,0:T(8,128)(2,1)S(1)} %collective-permute-done.8.rest_3_), channel_id=1, source_target_pairs={{0,4},{1,5},{4,8},{5,9},{6,2},{7,3},{8,12},{9,13},{10,6},{11,7},{1... | collective-permute-start | bytes 958472 | tf_op jit(solution)/shard_map/ppermute | solution.py:24
  38.8 0.5 collective-permute-start.7
  39.3 0.2 collective-permute-done.13.rest_2_.a_5_
  39.6 0.2 maximum_select_fusion
  39.9 0.5 collective-permute-done.6.got_away
  40.4 0.4 collective-permute-done.7.got_keep
  40.9 0.2 collective-permute-done.5.rest_4_
  41.0 3.7 %collective-permute-start.11 = (bf16[416,384]{1,0:T(8,128)(2,1)S(1)}, bf16[416,384]{1,0:T(8,128)(2,1)S(1)}, u32[]{:S(2)}, u32[]{:S(2)}) collective-permute-start(bf16[416,384]{1,0:T(8,128)(2,1)S(1)} %collective-permute-done.5.rest_4_), channel_id=1, source_target_pairs={{0,4},{1,5},{4,8},{5,9},{6,2},{7,3},{8,12},{9,13},{10,6},{11,7},{1... | collective-permute-start | bytes 958472 | tf_op jit(solution)/shard_map/ppermute | solution.py:24
  44.7 0.4 chip.1
  45.2 2.7 %far2.1.total_in = f32[1024,768]{1,0:T(8,128)S(1)} custom-call(s32[1]{0:T(128)} %bitcast.me_ref.a_0_, bf16[768,1024]{1,0:T(8,128)(2,1)S(1)} %get-tuple-element.115.own_t.a_1_, f32[8,768]{1,0:T(8,128)S(1)} %get-tuple-element.79.levels.a_2_, f32[8,768]{1,0:T(8,128)S(1)} %get-tuple-element.80.weights.a_3_, bf16[416,384]{1,0:T(8,128)(2,1)S(1)} %collective-permute-done.rest_0_, ...), custom_call_target="tpu_custom_call" | custom-call | flops 10000000000 | bytes 1 | tf_op jit(solution)/shard_map/far2/pallas_call | solution.py:589
  47.9 2.7 %far3.1.a_4_ = f32[1024,768]{1,0:T(8,128)S(1)} custom-call(s32[1]{0:T(128)} %bitcast.me_ref.a_0_, bf16[768,1024]{1,0:T(8,128)(2,1)S(1)} %get-tuple-element.115.own_t.a_1_, f32[8,768]{1,0:T(8,128)S(1)} %get-tuple-element.79.levels.a_2_, f32[8,768]{1,0:T(8,128)S(1)} %get-tuple-element.80.weights.a_3_, ...), custom_call_target="tpu_custom_call", output_to_operand_aliasing={{}: (4, {})} | custom-call | flops 1 | bytes 1 | tf_op jit(solution)/shard_map/far3/pallas_call | solution.py:589
  50.8 0.5 collective-permute-start.15
  51.3 3.2 %collective-permute-done.17.across = s16[1216,128]{1,0:T(8,128)(2,1)S(1)} collective-permute-done((s16[1216,128]{1,0:T(8,128)(2,1)S(1)}, s16[1216,128]{1,0:T(8,128)(2,1)S(1)}, u32[]{:S(2)}, u32[]{:S(2)}) %collective-permute-start.17) | collective-permute-done | bytes 311328 | tf_op jit(solution)/shard_map/ppermute | solution.py:24
  54.6 1.9 %half.1.total_in = f32[1024,768]{1,0:T(8,128)S(1)} custom-call(s32[1]{0:T(128)} %bitcast.me_ref.a_0_, bf16[768,1024]{1,0:T(8,128)(2,1)S(1)} %get-tuple-element.115.own_t.a_1_, f32[8,768]{1,0:T(8,128)S(1)} %get-tuple-element.79.levels.a_2_, f32[8,768]{1,0:T(8,128)S(1)} %get-tuple-element.80.weights.a_3_, ...), custom_call_target="tpu_custom_call", output_to_operand_aliasing={{}: (4, {})} | custom-call | flops 1000000000 | bytes 1 | tf_op jit(solution)/shard_map/half/pallas_call | solution.py:589
  56.5 4.0 %last.1 = (f32[1024,768]{1,0:T(8,128)S(1)}, f32[2,1024,384]{2,1,0:T(8,128)}, f32[640,128]{1,0:T(8,128)S(1)}, f32[640,128]{1,0:T(8,128)S(1)}, bf16[1024,768]{1,0:...) custom-call(s32[1]{0:T(128)} %bitcast.me_ref.a_0_, ...), custom_call_target="tpu_custom_call", output_to_operand_aliasing={{0}: (4, {})} | custom-call | flops 1 | bytes 1 | tf_op jit(solution)/shard_map/last/pallas_call | solution.py:589
  60.5 0.6 collective-permute-start.19
  61.1 1.1 %corner.1 = (f32[512,128]{1,0:T(8,128)S(1)}, f32[512,128]{1,0:T(8,128)S(1)}) custom-call(s32[1]{0:T(128)} %bitcast.me_ref.a_0_, bf16[1024,768]{1,0:T(8,128)(2,1)S(1)} %get-tuple-element.132.high, bf16[1024,768]{1,0:T(8,128)(2,1)S(1)} %get-tuple-element.133.low, bf16[1024,768]{1,0:T(8,128)(2,1)S(1)} %get-tuple-element.99.own_s), custom_call_target="tpu_custom_call" | custom-call | flops 2000000000 | bytes 1 | tf_op jit(solution)/shard_map/corner/pallas_call | solution.py:629
  62.2 0.2 collective-permute-done.19.theirs
  62.3 0.4 collective-permute-start.23
  62.7 0.3 column.2
  63.0 2.7 %collective-permute-start.20 = (s16[160,128]{1,0:T(8,128)(2,1)S(1)}, s16[160,128]{1,0:T(8,128)(2,1)S(1)}, u32[]{:S(2)}, u32[]{:S(2)}) collective-permute-start(s16[160,128]{1,0:T(8,128)(2,1)S(1)} %get-tuple-element.139), channel_id=1, source_target_pairs={{0,12},{1,13},{2,14},{3,15},{4,8},{5,9},{6,10},{7,11},{8,4},{9,5},... | collective-permute-start | bytes 122888 | tf_op jit(solution)/shard_map/ppermute | solution.py:24
  65.6 0.4 collective-permute-start.21
  66.1 1.4 %collective-permute-start.22 = (s16[160,128]{1,0:T(8,128)(2,1)S(1)}, s16[160,128]{1,0:T(8,128)(2,1)S(1)}, u32[]{:S(2)}, u32[]{:S(2)}) collective-permute-start(s16[160,128]{1,0:T(8,128)(2,1)S(1)} %get-tuple-element.141), channel_id=1, source_target_pairs={{0,4},{1,5},{2,6},{3,7},{4,0},{5,1},{6,2},{7,3},{8,12},{9,13},{10,... | collective-permute-start | bytes 122888 | tf_op jit(solution)/shard_map/ppermute | solution.py:24
  67.4 0.5 column.3
  67.9 2.7 %collective-permute-start.24 = (s16[144,128]{1,0:T(8,128)(2,1)S(1)}, s16[144,128]{1,0:T(8,128)(2,1)S(1)}, u32[]{:S(2)}, u32[]{:S(2)}) collective-permute-start(s16[144,128]{1,0:T(8,128)(2,1)S(1)} %get-tuple-element.146), channel_id=1, source_target_pairs={{0,12},{1,13},{2,14},{3,15},{4,8},{5,9},{6,10},{7,11},{8,4},{9,5},... | collective-permute-start | bytes 110600 | tf_op jit(solution)/shard_map/ppermute | solution.py:24
  70.6 1.8 %collective-permute-start.26 = (s16[144,128]{1,0:T(8,128)(2,1)S(1)}, s16[144,128]{1,0:T(8,128)(2,1)S(1)}, u32[]{:S(2)}, u32[]{:S(2)}) collective-permute-start(s16[144,128]{1,0:T(8,128)(2,1)S(1)} %get-tuple-element.148), channel_id=1, source_target_pairs={{0,4},{1,5},{2,6},{3,7},{4,0},{5,1},{6,2},{7,3},{8,12},{9,13},{10,... | collective-permute-start | bytes 110600 | tf_op jit(solution)/shard_map/ppermute | solution.py:24
  72.4 1.5 %collective-permute-done.24.rest_5_ = s16[144,128]{1,0:T(8,128)(2,1)S(1)} collective-permute-done((s16[144,128]{1,0:T(8,128)(2,1)S(1)}, s16[144,128]{1,0:T(8,128)(2,1)S(1)}, u32[]{:S(2)}, u32[]{:S(2)}) %collective-permute-start.24) | collective-permute-done | bytes 36896 | tf_op jit(solution)/shard_map/ppermute | solution.py:24
  73.8 1.6 %collective-permute-done.25.rest_6_ = s16[144,128]{1,0:T(8,128)(2,1)S(1)} collective-permute-done((s16[144,128]{1,0:T(8,128)(2,1)S(1)}, s16[144,128]{1,0:T(8,128)(2,1)S(1)}, u32[]{:S(2)}, u32[]{:S(2)}) %collective-permute-start.25) | collective-permute-done | bytes 36896 | tf_op jit(solution)/shard_map/ppermute | solution.py:24
  75.4 0.2 sum_code.1
  75.6 0.9 %collective-permute-start.29 = (s16[304,128]{1,0:T(8,128)(2,1)S(1)}, s16[304,128]{1,0:T(8,128)(2,1)S(1)}, u32[]{:S(2)}, u32[]{:S(2)}) collective-permute-start(s16[304,128]{1,0:T(8,128)(2,1)S(1)} %sum_code.1), channel_id=1, source_target_pairs={{0,4},{1,5},{2,6},{3,7},{4,0},{5,1},{6,2},{7,3},{8,12},{9,13},{10,... | collective-permute-start | bytes 233480 | tf_op jit(solution)/shard_map/ppermute | solution.py:24
  76.5 1.5 %collective-permute-start.28 = (s16[304,128]{1,0:T(8,128)(2,1)S(1)}, s16[304,128]{1,0:T(8,128)(2,1)S(1)}, u32[]{:S(2)}, u32[]{:S(2)}) collective-permute-start(s16[304,128]{1,0:T(8,128)(2,1)S(1)} %sum_code.1), channel_id=1, source_target_pairs={{0,8},{1,9},{2,10},{3,11},{4,12},{5,13},{6,14},{7,15},{8,0},{9,1},... | collective-permute-start | bytes 233480 | tf_op jit(solution)/shard_map/ppermute | solution.py:24
  78.1 2.0 %collective-permute-start.27 = (s16[304,128]{1,0:T(8,128)(2,1)S(1)}, s16[304,128]{1,0:T(8,128)(2,1)S(1)}, u32[]{:S(2)}, u32[]{:S(2)}) collective-permute-start(s16[304,128]{1,0:T(8,128)(2,1)S(1)} %sum_code.1), channel_id=1, source_target_pairs={{0,12},{1,13},{2,14},{3,15},{4,8},{5,9},{6,10},{7,11},{8,4},{9,5},... | collective-permute-start | bytes 233480 | tf_op jit(solution)/shard_map/ppermute | solution.py:24
  80.0 1.2 %collective-permute-start.33 = (s16[304,128]{1,0:T(8,128)(2,1)S(1)}, s16[304,128]{1,0:T(8,128)(2,1)S(1)}, u32[]{:S(2)}, u32[]{:S(2)}) collective-permute-start(s16[304,128]{1,0:T(8,128)(2,1)S(1)} %sum_code.1), channel_id=1, source_target_pairs={{0,2},{1,3},{2,0},{3,1},{4,6},{5,7},{6,4},{7,5},{8,10},{9,11},{10,... | collective-permute-start | bytes 233480 | tf_op jit(solution)/shard_map/ppermute | solution.py:24
  81.3 1.7 %collective-permute-start.32 = (s16[304,128]{1,0:T(8,128)(2,1)S(1)}, s16[304,128]{1,0:T(8,128)(2,1)S(1)}, u32[]{:S(2)}, u32[]{:S(2)}) collective-permute-start(s16[304,128]{1,0:T(8,128)(2,1)S(1)} %collective-permute-done.29), channel_id=1, source_target_pairs={{0,2},{1,3},{2,0},{3,1},{4,6},{5,7},{6,4},{7,5},{8,10},{9,11},{10,... | collective-permute-start | bytes 233480 | tf_op jit(solution)/shard_map/ppermute | solution.py:24
  82.9 0.2 collective-permute-done.28
  83.1 0.2 collective-permute-start.31
  83.3 1.1 %collective-permute-done.27 = s16[304,128]{1,0:T(8,128)(2,1)S(1)} collective-permute-done((s16[304,128]{1,0:T(8,128)(2,1)S(1)}, s16[304,128]{1,0:T(8,128)(2,1)S(1)}, u32[]{:S(2)}, u32[]{:S(2)}) %collective-permute-start.27) | collective-permute-done | bytes 77856 | tf_op jit(solution)/shard_map/ppermute | solution.py:24
  84.4 0.9 collective-permute-start.30
  85.4 0.7 collective-permute-done.32
  86.1 1.5 %collective-permute-done.31 = s16[304,128]{1,0:T(8,128)(2,1)S(1)} collective-permute-done((s16[304,128]{1,0:T(8,128)(2,1)S(1)}, s16[304,128]{1,0:T(8,128)(2,1)S(1)}, u32[]{:S(2)}, u32[]{:S(2)}) %collective-permute-start.31) | collective-permute-done | bytes 77856 | tf_op jit(solution)/shard_map/ppermute | solution.py:24
  87.5 1.2 %collective-permute-done.30 = s16[304,128]{1,0:T(8,128)(2,1)S(1)} collective-permute-done((s16[304,128]{1,0:T(8,128)(2,1)S(1)}, s16[304,128]{1,0:T(8,128)(2,1)S(1)}, u32[]{:S(2)}, u32[]{:S(2)}) %collective-permute-start.30) | collective-permute-done | bytes 77856 | tf_op jit(solution)/shard_map/ppermute | solution.py:24
  88.9 1.9 %unpack.1 = (f32[1024,1024]{1,0:T(8,128)}, f32[4608,128]{1,0:T(8,128)S(1)}) custom-call(s32[1]{0:T(128)} %bitcast.me_ref.a_0_, s16[4,304,128]{2,1,0:T(8,128)(2,1)S(1)} %pad_add_fusion.a, s16[4,304,128]{2,1,0:T(8,128)(2,1)S(1)} %pad_add_fusion.1.b, s16[4,304,128]{2,1,0:T(8,128)(2,1)S(1)} %collective-permute-done.34.sib_a), custom_call_target="tpu_custom_call" | custom-call | flops 1000000000 | bytes 1 | tf_op jit(solution)/shard_map/unpack/pallas_call | solution.py:657
  90.8 1.7 %spread.1 = (f32[1024,1024]{1,0:T(8,128)}, f32[4608,128]{1,0:T(8,128)S(1)}) custom-call(s32[1]{0:T(128)} %bitcast.me_ref.a_0_, f32[1024,1024]{1,0:T(8,128)} %get-tuple-element.149.out_in, f32[4608,128]{1,0:T(8,128)S(1)} %get-tuple-element.150.packed_in, ...), custom_call_target="tpu_custom_call", output_to_operand_aliasing={{0}: (1, {}), {1}: (2, {})} | custom-call | flops 1 | bytes 1 | tf_op jit(solution)/shard_map/spread/pallas_call | solution.py:660
  (43 shorter events, 0.8 us)
Async XLA Ops:
  0.6 7.3 %copy-start.3 = (s32[16,384]{1,0:T(8,128)S(1)}, s32[16,384]{1,0:T(8,128)}, u32[]{:S(2)}) copy-start(s32[16,384]{1,0:T(8,128)} %maps_in.1) | copy-start | bytes 73732
  0.6 7.3 %copy-start.2 = (f32[8192]{0:T(1024)S(1)}, f32[8192]{0:T(1024)}, u32[]{:S(2)}) copy-start(f32[8192]{0:T(1024)} %param.8) | copy-start | bytes 98308
  0.7 7.3 %copy-start.5 = (f32[16,2]{0,1:T(2,128)S(1)}, f32[16,2]{0,1:T(2,128)}, u32[]{:S(2)}) copy-start(f32[16,2]{0,1:T(2,128)} %param.7) | copy-start | bytes 388
  1.7 7.6 %collective-permute-start.1 = (bf16[2048,384]{1,0:T(8,128)(2,1)}, bf16[2048,384]{1,0:T(8,128)(2,1)S(1)}, u32[]{:S(2)}, u32[]{:S(2)}) collective-permute-start(bf16[2048,384]{1,0:T(8,128)(2,1)} %bitcast.14), channel_id=1, source_target_pairs={{0,1},{1,0},{2,3},{3,2},{4,5},{5,4},{6,7},{7,6},{8,9},{9,8},{10,11... | collective-permute-start | bytes 4718600 | tf_op jit(solution)/shard_map/ppermute | solution.py:24
  2.2 11.9 %collective-permute-start = (bf16[416,384]{1,0:T(8,128)(2,1)S(1)}, bf16[416,384]{1,0:T(8,128)(2,1)S(1)}, u32[]{:S(2)}, u32[]{:S(2)}) collective-permute-start(bf16[416,384]{1,0:T(8,128)(2,1)S(1)} %slice.12), channel_id=1, source_target_pairs={{0,2},{1,3},{2,0},{3,1},{4,6},{5,7},{6,4},{7,5},{8,10},{9,11},{10,... | collective-permute-start | bytes 958472 | tf_op jit(solution)/shard_map/ppermute | solution.py:24
  4.8 3.2 %collective-permute-start.2 = (s32[1,3]{1,0:T(1,128)}, s32[1,3]{1,0:T(1,128)S(1)}, u32[]{:S(2)}, u32[]{:S(2)}) collective-permute-start(s32[1,3]{1,0:T(1,128)} %pairs.3), channel_id=1, source_target_pairs={{0,1},{1,0},{2,3},{3,2},{4,5},{5,4},{6,7},{7,6},{8,9},{9,8},{10,11... | collective-permute-start | bytes 44 | tf_op jit(solution)/shard_map/ppermute | solution.py:24
  5.0 1.4 %copy-start = (bf16[1,2,1024,384]{3,2,1,0:T(8,128)(2,1)S(1)}, bf16[1,2,1024,384]{3,2,1,0:T(8,128)(2,1)}, u32[]{:S(2)}) copy-start(bf16[1,2,1024,384]{3,2,1,0:T(8,128)(2,1)} %param.5) | copy-start | bytes 4718596
  6.4 0.7 copy-start.4
  9.3 11.6 %collective-permute-start.4 = (bf16[384,384]{1,0:T(8,128)(2,1)S(1)}, bf16[384,384]{1,0:T(8,128)(2,1)S(1)}, u32[]{:S(2)}, u32[]{:S(2)}) collective-permute-start(bf16[384,384]{1,0:T(8,128)(2,1)S(1)} %get-tuple-element.89), channel_id=1, source_target_pairs={{0,2},{1,3},{2,0},{3,1},{4,6},{5,7},{6,4},{7,5},{8,10},{9,11},{10,... | collective-permute-start | bytes 884744 | tf_op jit(solution)/shard_map/ppermute | solution.py:24
  9.7 1.4 %copy-start.1 = (bf16[1,2,1024,384]{3,2,1,0:T(8,128)(2,1)S(1)}, bf16[1,2,1024,384]{3,2,1,0:T(8,128)(2,1)}, u32[]{:S(2)}) copy-start(bf16[1,2,1024,384]{3,2,1,0:T(8,128)(2,1)} %param.5) | copy-start | bytes 4718596
  14.1 20.2 %collective-permute-start.9 = (bf16[416,384]{1,0:T(8,128)(2,1)S(1)}, bf16[416,384]{1,0:T(8,128)(2,1)S(1)}, u32[]{:S(2)}, u32[]{:S(2)}) collective-permute-start(bf16[416,384]{1,0:T(8,128)(2,1)S(1)} %collective-permute-done.rest_0_), channel_id=1, source_target_pairs={{0,4},{1,5},{4,8},{5,9},{6,2},{7,3},{8,12},{9,13},{10,6},{11,7},{1... | collective-permute-start | bytes 958472 | tf_op jit(solution)/shard_map/ppermute | solution.py:24
  17.8 10.2 %collective-permute-start.3 = (bf16[432,384]{1,0:T(8,128)(2,1)S(1)}, bf16[432,384]{1,0:T(8,128)(2,1)S(1)}, u32[]{:S(2)}, u32[]{:S(2)}) collective-permute-start(bf16[432,384]{1,0:T(8,128)(2,1)S(1)} %get-tuple-element.87), channel_id=1, source_target_pairs={{0,2},{1,3},{2,0},{3,1},{4,6},{5,7},{6,4},{7,5},{8,10},{9,11},{10,... | collective-permute-start | bytes 995336 | tf_op jit(solution)/shard_map/ppermute | solution.py:24
  20.9 18.0 %collective-permute-start.12 = (bf16[384,384]{1,0:T(8,128)(2,1)S(1)}, bf16[384,384]{1,0:T(8,128)(2,1)S(1)}, u32[]{:S(2)}, u32[]{:S(2)}) collective-permute-start(bf16[384,384]{1,0:T(8,128)(2,1)S(1)} %collective-permute-done.4.rest_1_), channel_id=1, source_target_pairs={{0,4},{1,5},{4,8},{5,9},{6,2},{7,3},{8,12},{9,13},{10,6},{11,7},{1... | collective-permute-start | bytes 884744 | tf_op jit(solution)/shard_map/ppermute | solution.py:24
  24.7 10.5 %collective-permute-start.8 = (bf16[416,384]{1,0:T(8,128)(2,1)S(1)}, bf16[416,384]{1,0:T(8,128)(2,1)S(1)}, u32[]{:S(2)}, u32[]{:S(2)}) collective-permute-start(bf16[416,384]{1,0:T(8,128)(2,1)S(1)} %get-tuple-element.103), channel_id=1, source_target_pairs={{0,2},{1,3},{2,0},{3,1},{4,6},{5,7},{6,4},{7,5},{8,10},{9,11},{10,... | collective-permute-start | bytes 958472 | tf_op jit(solution)/shard_map/ppermute | solution.py:24
  28.0 11.6 %collective-permute-start.13 = (bf16[432,384]{1,0:T(8,128)(2,1)S(1)}, bf16[432,384]{1,0:T(8,128)(2,1)S(1)}, u32[]{:S(2)}, u32[]{:S(2)}) collective-permute-start(bf16[432,384]{1,0:T(8,128)(2,1)S(1)} %collective-permute-done.3.rest_2_), channel_id=1, source_target_pairs={{0,4},{1,5},{4,8},{5,9},{6,2},{7,3},{8,12},{9,13},{10,6},{11,7},{1... | collective-permute-start | bytes 995336 | tf_op jit(solution)/shard_map/ppermute | solution.py:24
  31.5 9.5 %collective-permute-start.5 = (bf16[416,384]{1,0:T(8,128)(2,1)S(1)}, bf16[416,384]{1,0:T(8,128)(2,1)S(1)}, u32[]{:S(2)}, u32[]{:S(2)}) collective-permute-start(bf16[416,384]{1,0:T(8,128)(2,1)S(1)} %get-tuple-element.95), channel_id=1, source_target_pairs={{0,2},{1,3},{2,0},{3,1},{4,6},{5,7},{6,4},{7,5},{8,10},{9,11},{10,... | collective-permute-start | bytes 958472 | tf_op jit(solution)/shard_map/ppermute | solution.py:24
  35.3 9.9 %collective-permute-start.10 = (bf16[416,384]{1,0:T(8,128)(2,1)S(1)}, bf16[416,384]{1,0:T(8,128)(2,1)S(1)}, u32[]{:S(2)}, u32[]{:S(2)}) collective-permute-start(bf16[416,384]{1,0:T(8,128)(2,1)S(1)} %collective-permute-done.8.rest_3_), channel_id=1, source_target_pairs={{0,4},{1,5},{4,8},{5,9},{6,2},{7,3},{8,12},{9,13},{10,6},{11,7},{1... | collective-permute-start | bytes 958472 | tf_op jit(solution)/shard_map/ppermute | solution.py:24
  38.8 1.7 %collective-permute-start.6 = (s16[1216,128]{1,0:T(8,128)(2,1)S(1)}, s16[1216,128]{1,0:T(8,128)(2,1)S(1)}, u32[]{:S(2)}, u32[]{:S(2)}) collective-permute-start(s16[1216,128]{1,0:T(8,128)(2,1)S(1)} %get-tuple-element.100), channel_id=1, source_target_pairs={{0,1},{1,0},{2,3},{3,2},{4,5},{5,4},{6,7},{7,6},{8,9},{9,8},{10,11... | collective-permute-start | bytes 933896 | tf_op jit(solution)/shard_map/ppermute | solution.py:24
  38.8 2.0 %collective-permute-start.7 = (s16[1216,128]{1,0:T(8,128)(2,1)S(1)}, s16[1216,128]{1,0:T(8,128)(2,1)S(1)}, u32[]{:S(2)}, u32[]{:S(2)}) collective-permute-start(s16[1216,128]{1,0:T(8,128)(2,1)S(1)} %get-tuple-element.101), channel_id=1, source_target_pairs={{0,1},{1,0},{2,3},{3,2},{4,5},{5,4},{6,7},{7,6},{8,9},{9,8},{10,11... | collective-permute-start | bytes 933896 | tf_op jit(solution)/shard_map/ppermute | solution.py:24
  39.8 8.1 %collective-permute-start.14 = (bf16[1232,384]{1,0:T(8,128)(2,1)S(1)}, bf16[1232,384]{1,0:T(8,128)(2,1)S(1)}, u32[]{:S(2)}, u32[]{:S(2)}) collective-permute-start(bf16[1232,384]{1,0:T(8,128)(2,1)S(1)} %maximum_select_fusion), channel_id=1, source_target_pairs={{0,1},{1,0},{2,3},{3,2},{4,5},{5,4},{6,7},{7,6},{8,9},{9,8},{10,11... | collective-permute-start | bytes 2838536 | tf_op jit(solution)/shard_map/ppermute | solution.py:24
  41.0 13.4 %collective-permute-start.11 = (bf16[416,384]{1,0:T(8,128)(2,1)S(1)}, bf16[416,384]{1,0:T(8,128)(2,1)S(1)}, u32[]{:S(2)}, u32[]{:S(2)}) collective-permute-start(bf16[416,384]{1,0:T(8,128)(2,1)S(1)} %collective-permute-done.5.rest_4_), channel_id=1, source_target_pairs={{0,4},{1,5},{4,8},{5,9},{6,2},{7,3},{8,12},{9,13},{10,6},{11,7},{1... | collective-permute-start | bytes 958472 | tf_op jit(solution)/shard_map/ppermute | solution.py:24
  45.1 9.3 %collective-permute-start.17 = (s16[1216,128]{1,0:T(8,128)(2,1)S(1)}, s16[1216,128]{1,0:T(8,128)(2,1)S(1)}, u32[]{:S(2)}, u32[]{:S(2)}) collective-permute-start(s16[1216,128]{1,0:T(8,128)(2,1)S(1)} %get-tuple-element.124), channel_id=1, source_target_pairs={{0,2},{1,3},{2,0},{3,1},{4,6},{5,7},{6,4},{7,5},{8,10},{9,11},{10,... | collective-permute-start | bytes 933896 | tf_op jit(solution)/shard_map/ppermute | solution.py:24
  50.7 3.8 %collective-permute-start.16 = (bf16[208,384]{1,0:T(8,128)(2,1)S(1)}, bf16[208,384]{1,0:T(8,128)(2,1)S(1)}, u32[]{:S(2)}, u32[]{:S(2)}) collective-permute-start(bf16[208,384]{1,0:T(8,128)(2,1)S(1)} %get-tuple-element.152), channel_id=1, source_target_pairs={{0,1},{1,0},{2,3},{3,2},{4,5},{5,4},{6,7},{7,6},{8,9},{9,8},{10,11... | collective-permute-start | bytes 479240 | tf_op jit(solution)/shard_map/ppermute | solution.py:24
  50.8 3.7 %collective-permute-start.15 = (bf16[208,384]{1,0:T(8,128)(2,1)S(1)}, bf16[208,384]{1,0:T(8,128)(2,1)S(1)}, u32[]{:S(2)}, u32[]{:S(2)}) collective-permute-start(bf16[208,384]{1,0:T(8,128)(2,1)S(1)} %get-tuple-element.153), channel_id=1, source_target_pairs={{0,1},{1,0},{2,3},{3,2},{4,5},{5,4},{6,7},{7,6},{8,9},{9,8},{10,11... | collective-permute-start | bytes 479240 | tf_op jit(solution)/shard_map/ppermute | solution.py:24
  54.5 2.0 %collective-permute-start.18 = (bf16[416,384]{1,0:T(8,128)(2,1)S(1)}, bf16[416,384]{1,0:T(8,128)(2,1)S(1)}, u32[]{:S(2)}, u32[]{:S(2)}) collective-permute-start(bf16[416,384]{1,0:T(8,128)(2,1)S(1)} %broadcast_select_fusion), channel_id=1, source_target_pairs={{0,1},{1,0},{2,3},{3,2},{4,5},{5,4},{6,7},{7,6},{8,9},{9,8},{10,11... | collective-permute-start | bytes 958472 | tf_op jit(solution)/shard_map/ppermute | solution.py:24
  60.5 1.8 %collective-permute-start.19 = (f32[640,128]{1,0:T(8,128)S(1)}, f32[640,128]{1,0:T(8,128)S(1)}, u32[]{:S(2)}, u32[]{:S(2)}) collective-permute-start(f32[640,128]{1,0:T(8,128)S(1)} %get-tuple-element.131), channel_id=1, source_target_pairs={{0,1},{1,0},{2,3},{3,2},{4,5},{5,4},{6,7},{7,6},{8,9},{9,8},{10,11... | collective-permute-start | bytes 983048 | tf_op jit(solution)/shard_map/ppermute | solution.py:24
  62.3 5.1 %collective-permute-start.23 = (f32[512,128]{1,0:T(8,128)S(1)}, f32[512,128]{1,0:T(8,128)S(1)}, u32[]{:S(2)}, u32[]{:S(2)}) collective-permute-start(f32[512,128]{1,0:T(8,128)S(1)} %get-tuple-element.143), channel_id=1, source_target_pairs={{0,1},{1,0},{2,3},{3,2},{4,5},{5,4},{6,7},{7,6},{8,9},{9,8},{10,11... | collective-permute-start | bytes 786440 | tf_op jit(solution)/shard_map/ppermute | solution.py:24
  63.0 7.6 %collective-permute-start.20 = (s16[160,128]{1,0:T(8,128)(2,1)S(1)}, s16[160,128]{1,0:T(8,128)(2,1)S(1)}, u32[]{:S(2)}, u32[]{:S(2)}) collective-permute-start(s16[160,128]{1,0:T(8,128)(2,1)S(1)} %get-tuple-element.139), channel_id=1, source_target_pairs={{0,12},{1,13},{2,14},{3,15},{4,8},{5,9},{6,10},{7,11},{8,4},{9,5},... | collective-permute-start | bytes 122888 | tf_op jit(solution)/shard_map/ppermute | solution.py:24
  65.6 6.7 %collective-permute-start.21 = (s16[160,128]{1,0:T(8,128)(2,1)S(1)}, s16[160,128]{1,0:T(8,128)(2,1)S(1)}, u32[]{:S(2)}, u32[]{:S(2)}) collective-permute-start(s16[160,128]{1,0:T(8,128)(2,1)S(1)} %get-tuple-element.140), channel_id=1, source_target_pairs={{0,8},{1,9},{2,10},{3,11},{4,12},{5,13},{6,14},{7,15},{8,0},{9,1},... | collective-permute-start | bytes 122888 | tf_op jit(solution)/shard_map/ppermute | solution.py:24
  66.1 6.3 %collective-permute-start.22 = (s16[160,128]{1,0:T(8,128)(2,1)S(1)}, s16[160,128]{1,0:T(8,128)(2,1)S(1)}, u32[]{:S(2)}, u32[]{:S(2)}) collective-permute-start(s16[160,128]{1,0:T(8,128)(2,1)S(1)} %get-tuple-element.141), channel_id=1, source_target_pairs={{0,4},{1,5},{2,6},{3,7},{4,0},{5,1},{6,2},{7,3},{8,12},{9,13},{10,... | collective-permute-start | bytes 122888 | tf_op jit(solution)/shard_map/ppermute | solution.py:24
  67.9 5.9 %collective-permute-start.24 = (s16[144,128]{1,0:T(8,128)(2,1)S(1)}, s16[144,128]{1,0:T(8,128)(2,1)S(1)}, u32[]{:S(2)}, u32[]{:S(2)}) collective-permute-start(s16[144,128]{1,0:T(8,128)(2,1)S(1)} %get-tuple-element.146), channel_id=1, source_target_pairs={{0,12},{1,13},{2,14},{3,15},{4,8},{5,9},{6,10},{7,11},{8,4},{9,5},... | collective-permute-start | bytes 110600 | tf_op jit(solution)/shard_map/ppermute | solution.py:24
  70.6 4.9 %collective-permute-start.25 = (s16[144,128]{1,0:T(8,128)(2,1)S(1)}, s16[144,128]{1,0:T(8,128)(2,1)S(1)}, u32[]{:S(2)}, u32[]{:S(2)}) collective-permute-start(s16[144,128]{1,0:T(8,128)(2,1)S(1)} %get-tuple-element.147), channel_id=1, source_target_pairs={{0,8},{1,9},{2,10},{3,11},{4,12},{5,13},{6,14},{7,15},{8,0},{9,1},... | collective-permute-start | bytes 110600 | tf_op jit(solution)/shard_map/ppermute | solution.py:24
  70.6 4.9 %collective-permute-start.26 = (s16[144,128]{1,0:T(8,128)(2,1)S(1)}, s16[144,128]{1,0:T(8,128)(2,1)S(1)}, u32[]{:S(2)}, u32[]{:S(2)}) collective-permute-start(s16[144,128]{1,0:T(8,128)(2,1)S(1)} %get-tuple-element.148), channel_id=1, source_target_pairs={{0,4},{1,5},{2,6},{3,7},{4,0},{5,1},{6,2},{7,3},{8,12},{9,13},{10,... | collective-permute-start | bytes 110600 | tf_op jit(solution)/shard_map/ppermute | solution.py:24
  75.6 5.7 %collective-permute-start.29 = (s16[304,128]{1,0:T(8,128)(2,1)S(1)}, s16[304,128]{1,0:T(8,128)(2,1)S(1)}, u32[]{:S(2)}, u32[]{:S(2)}) collective-permute-start(s16[304,128]{1,0:T(8,128)(2,1)S(1)} %sum_code.1), channel_id=1, source_target_pairs={{0,4},{1,5},{2,6},{3,7},{4,0},{5,1},{6,2},{7,3},{8,12},{9,13},{10,... | collective-permute-start | bytes 233480 | tf_op jit(solution)/shard_map/ppermute | solution.py:24
  76.5 6.6 %collective-permute-start.28 = (s16[304,128]{1,0:T(8,128)(2,1)S(1)}, s16[304,128]{1,0:T(8,128)(2,1)S(1)}, u32[]{:S(2)}, u32[]{:S(2)}) collective-permute-start(s16[304,128]{1,0:T(8,128)(2,1)S(1)} %sum_code.1), channel_id=1, source_target_pairs={{0,8},{1,9},{2,10},{3,11},{4,12},{5,13},{6,14},{7,15},{8,0},{9,1},... | collective-permute-start | bytes 233480 | tf_op jit(solution)/shard_map/ppermute | solution.py:24
  78.1 6.3 %collective-permute-start.27 = (s16[304,128]{1,0:T(8,128)(2,1)S(1)}, s16[304,128]{1,0:T(8,128)(2,1)S(1)}, u32[]{:S(2)}, u32[]{:S(2)}) collective-permute-start(s16[304,128]{1,0:T(8,128)(2,1)S(1)} %sum_code.1), channel_id=1, source_target_pairs={{0,12},{1,13},{2,14},{3,15},{4,8},{5,9},{6,10},{7,11},{8,4},{9,5},... | collective-permute-start | bytes 233480 | tf_op jit(solution)/shard_map/ppermute | solution.py:24
  80.0 5.3 %collective-permute-start.33 = (s16[304,128]{1,0:T(8,128)(2,1)S(1)}, s16[304,128]{1,0:T(8,128)(2,1)S(1)}, u32[]{:S(2)}, u32[]{:S(2)}) collective-permute-start(s16[304,128]{1,0:T(8,128)(2,1)S(1)} %sum_code.1), channel_id=1, source_target_pairs={{0,2},{1,3},{2,0},{3,1},{4,6},{5,7},{6,4},{7,5},{8,10},{9,11},{10,... | collective-permute-start | bytes 233480 | tf_op jit(solution)/shard_map/ppermute | solution.py:24
  81.3 4.8 %collective-permute-start.32 = (s16[304,128]{1,0:T(8,128)(2,1)S(1)}, s16[304,128]{1,0:T(8,128)(2,1)S(1)}, u32[]{:S(2)}, u32[]{:S(2)}) collective-permute-start(s16[304,128]{1,0:T(8,128)(2,1)S(1)} %collective-permute-done.29), channel_id=1, source_target_pairs={{0,2},{1,3},{2,0},{3,1},{4,6},{5,7},{6,4},{7,5},{8,10},{9,11},{10,... | collective-permute-start | bytes 233480 | tf_op jit(solution)/shard_map/ppermute | solution.py:24
  83.1 4.4 %collective-permute-start.31 = (s16[304,128]{1,0:T(8,128)(2,1)S(1)}, s16[304,128]{1,0:T(8,128)(2,1)S(1)}, u32[]{:S(2)}, u32[]{:S(2)}) collective-permute-start(s16[304,128]{1,0:T(8,128)(2,1)S(1)} %collective-permute-done.28), channel_id=1, source_target_pairs={{0,2},{1,3},{2,0},{3,1},{4,6},{5,7},{6,4},{7,5},{8,10},{9,11},{10,... | collective-permute-start | bytes 233480 | tf_op jit(solution)/shard_map/ppermute | solution.py:24
  84.4 4.4 %collective-permute-start.30 = (s16[304,128]{1,0:T(8,128)(2,1)S(1)}, s16[304,128]{1,0:T(8,128)(2,1)S(1)}, u32[]{:S(2)}, u32[]{:S(2)}) collective-permute-start(s16[304,128]{1,0:T(8,128)(2,1)S(1)} %collective-permute-done.27), channel_id=1, source_target_pairs={{0,2},{1,3},{2,0},{3,1},{4,6},{5,7},{6,4},{7,5},{8,10},{9,11},{10,... | collective-permute-start | bytes 233480 | tf_op jit(solution)/shard_map/ppermute | solution.py:24
  85.3 3.6 %collective-permute-start.34 = (s16[4,304,128]{2,1,0:T(8,128)(2,1)S(1)}, s16[4,304,128]{2,1,0:T(8,128)(2,1)S(1)}, u32[]{:S(2)}, u32[]{:S(2)}) collective-permute-start(s16[4,304,128]{2,1,0:T(8,128)(2,1)S(1)} %pad_add_fusion.a), channel_id=1, source_target_pairs={{0,1},{1,0},{2,3},{3,2},{4,5},{5,4},{6,7},{7,6},{8,9},{9,8},{10,11... | collective-permute-start | bytes 933896 | tf_op jit(solution)/shard_map/ppermute | solution.py:24
  88.8 2.0 %collective-permute-start.35 = (s16[4,304,128]{2,1,0:T(8,128)(2,1)S(1)}, s16[4,304,128]{2,1,0:T(8,128)(2,1)S(1)}, u32[]{:S(2)}, u32[]{:S(2)}) collective-permute-start(s16[4,304,128]{2,1,0:T(8,128)(2,1)S(1)} %pad_add_fusion.1.b), channel_id=1, source_target_pairs={{0,1},{1,0},{2,3},{3,2},{4,5},{5,4},{6,7},{7,6},{8,9},{9,8},{10,11... | collective-permute-start | bytes 933896 | tf_op jit(solution)/shard_map/ppermute | solution.py:24
